TPU v7x, 32 devices: a whole 2x2x4 slice. The times are simulated.
32 devices in a mesh: dp: 2 (over x), sy: 4 (over z), sx: 4 (over y, core).
Axes of the slice: x: 2, y: 2, z: 4, core: 2. Of those that a mesh axis runs over, the one named last changes fastest.
Arguments:
- features: bfloat16 [2, 64, 256, 768], P('dp', 'sy', 'sx'), may hold values from -100 to 100
- depth_weight: float32 [7, 7, 768], replicated, may hold values from -0.875 to 0.875
- depth_bias: float32 [768], replicated, may hold values from -3 to 3
- reduce_weight: bfloat16 [768, 256], replicated, may hold values from -0.21875 to 0.21875
- reduce_bias: float32 [256], replicated, may hold values from -3 to 3
- class_weight: bfloat16 [10, 256, 256], replicated, may hold values from -0.375 to 0.375
- class_bias: float32 [10], replicated, may hold values from -4 to 4
- labels: int32 [2], P('dp'), may hold values from 0 to 9
Outputs:
- loss: float32 [], replicated
- depth_weight_grad: float32 [7, 7, 768], replicated
- depth_bias_grad: float32 [768], replicated
- reduce_weight_grad: float32 [768, 256], replicated
- reduce_bias_grad: float32 [256], replicated
- class_weight_grad: float32 [10, 256, 256], replicated
- class_bias_grad: float32 [10], replicated
All inputs are finite; a program needn't handle non-finite values.
Results may differ from a plain program's by a relative error of at most 0.006.
Values may be sent and summed in bfloat16 or wider, within the bound.
No kernel may reach another device: no remote copies, remote signals or barrier semaphores. Data moves between devices by JAX's collectives and lax.ppermute only.
A program may use at most 64 MiB of HBM per device.

v0:
```python
import jax
import jax.numpy as jnp
from jax import lax
from jax.sharding import PartitionSpec as P

KERNEL = 7
NEWTON_STEPS = 5


epsilon = 1e-05
loss_scale = 64.0
highest = lax.Precision.HIGHEST


def with_halo(block, sides, width):
    for axis, dim in sides:
        count = lax.axis_size(axis)
        forward = [(i, i + 1) for i in range(count - 1)]
        backward = [(target, source) for source, target in forward]
        low = lax.ppermute(
            lax.slice_in_dim(block, block.shape[dim] - width, None, axis=dim), axis, forward
        )
        high = lax.ppermute(lax.slice_in_dim(block, 0, width, axis=dim), axis, backward)
        block = jnp.concatenate([low, block, high], axis=dim)
    return block


def matrix_root(sigma):
    identity = jnp.eye(sigma.shape[0], dtype=sigma.dtype)
    trace_value = jnp.trace(sigma) + epsilon
    current = sigma / trace_value
    inverse = identity
    for iteration in range(NEWTON_STEPS):
        factor = 0.5 * (3.0 * identity - jnp.dot(inverse, current, precision=highest))
        current = jnp.dot(current, factor, precision=highest)
        inverse = jnp.dot(factor, inverse, precision=highest)
    return jnp.sqrt(trace_value) * current


def taps_conv(padded, tile_rows, tile_cols, depth_weight, depth_bias):
    total = jnp.zeros((tile_rows, tile_cols, padded.shape[2]), depth_weight.dtype) + depth_bias
    for row_tap in range(KERNEL):
        for col_tap in range(KERNEL):
            window = padded[row_tap : row_tap + tile_rows, col_tap : col_tap + tile_cols, :]
            total = total + window.astype(depth_weight.dtype) * depth_weight[row_tap, col_tap]
    return total.astype(jnp.bfloat16)


def body(
    features, depth_weight, depth_bias, reduce_weight, reduce_bias, class_weight, class_bias, labels
):
    tile_rows, tile_cols = (features.shape[1], features.shape[2])
    padded = with_halo(features, (("sy", 1), ("sx", 2)), KERNEL // 2)[0]
    conv_out = taps_conv(padded, tile_rows, tile_cols, depth_weight, depth_bias)
    flat_conv = conv_out.reshape(tile_rows * tile_cols, -1)
    before = jnp.dot(flat_conv, reduce_weight, preferred_element_type=jnp.float32) + reduce_bias
    feat = jax.nn.silu(before).astype(jnp.bfloat16)
    gram = lax.dot_general(feat, feat, (((0,), (0,)), ((), ())), preferred_element_type=jnp.float32)
    colsum = jnp.sum(feat.astype(jnp.float32), axis=0)
    gram, colsum = lax.psum((gram, colsum), ("sy", "sx"))
    count = tile_rows * tile_cols * lax.axis_size("sy") * lax.axis_size("sx")
    image_count = features.shape[0] * lax.axis_size("dp")
    mean_vec = colsum / count
    sigma = gram / count - jnp.outer(mean_vec, mean_vec)
    root, pullback = jax.vjp(matrix_root, sigma)
    weight_full = class_weight.astype(jnp.float32)
    logits = jnp.einsum("kij,ij->k", weight_full, root, precision=highest) + class_bias
    onehot = (jnp.arange(logits.shape[0], dtype=jnp.int32) == labels[0]).astype(jnp.float32)
    loss_part = jnp.sum(jax.nn.softplus(logits)) - jnp.sum(onehot * logits)
    logit_grad = loss_scale * (jax.nn.sigmoid(logits) - onehot) / image_count
    root_grad = jnp.einsum("k,kij->ij", logit_grad, weight_full, precision=highest)
    sigma_grad = pullback(root_grad)[0]
    class_local = logit_grad[:, None, None] * root[None, :, :]
    loss_total, class_weight_grad, class_bias_grad = lax.psum(
        (loss_part, class_local, logit_grad), "dp"
    )
    loss = loss_total / image_count
    symmetric = ((sigma_grad + sigma_grad.T) / count).astype(jnp.bfloat16)
    mean_term = jnp.dot(mean_vec, symmetric.astype(jnp.float32), precision=highest)
    feat_grad = jnp.dot(feat, symmetric, preferred_element_type=jnp.float32) - mean_term
    gate = jax.nn.sigmoid(before)
    pre_grad = (feat_grad * gate * (1.0 + before * (1.0 - gate))).astype(jnp.bfloat16)
    weight_grad = lax.dot_general(
        flat_conv, pre_grad, (((0,), (0,)), ((), ())), preferred_element_type=jnp.float32
    )
    bias_grad = jnp.sum(pre_grad.astype(jnp.float32), axis=0)
    conv_grad = lax.dot_general(
        pre_grad, reduce_weight, (((1,), (1,)), ((), ())), preferred_element_type=jnp.float32
    )
    conv_grad = conv_grad.astype(jnp.bfloat16).reshape(tile_rows, tile_cols, -1)
    depth_rows = []
    for row_tap in range(KERNEL):
        depth_cols = []
        for col_tap in range(KERNEL):
            window = padded[row_tap : row_tap + tile_rows, col_tap : col_tap + tile_cols, :]
            depth_cols.append(
                jnp.sum(window.astype(jnp.float32) * conv_grad.astype(jnp.float32), axis=(0, 1))
            )
        depth_rows.append(jnp.stack(depth_cols))
    depth_grad = jnp.stack(depth_rows)
    depth_bias_grad = jnp.sum(conv_grad.astype(jnp.float32), axis=(0, 1))
    weight_grad, depth_grad, depth_bias_grad, bias_grad = lax.psum(
        (weight_grad, depth_grad, depth_bias_grad, bias_grad), ("dp", "sy", "sx")
    )
    return (
        loss,
        depth_grad,
        depth_bias_grad,
        weight_grad,
        bias_grad,
        class_weight_grad,
        class_bias_grad,
    )


def solution(mesh):
    placed = (P("dp", "sy", "sx", None), P(), P(), P(), P(), P(), P(), P("dp"))
    return jax.shard_map(
        body,
        mesh=mesh,
        in_specs=placed,
        out_specs=(P(), P(), P(), P(), P(), P(), P()),
        check_vma=False,
    )
```

profile of v0, /device:TPU:0, one launch (start us, length us, event | category | flops | bytes accessed | tf_op | source)
XLA Modules:
  0.0 465.7 jit_solution(13198044370433280017)
XLA Ops:
  7.2 1.2 fusion.145
  8.4 4.9 %collective-permute-start = (bf16[1,3,64,768]{3,2,1,0:T(8,128)(2,1)S(1)}, bf16[1,3,64,768]{3,2,1,0:T(8,128)(2,1)S(1)}, u32[]{:S(2)}, u32[]{:S(2)}) collective-permute-start(bf16[1,3,64,768]{3,2,1,0:T(8,128)(2,1)S(1)} %get-tuple-element.118), channel_id=1, source_target_pairs={{0,4},{4,8},{8,12},{1,5},{5,9},{9,13},{2,6},{6,10},{10,14},{3,7},{... | collective-permute-start | bytes 884744 | tf_op jit(solution)/shard_map/ppermute | solution.py:20
  13.4 1.3 collective-permute-start.1
  14.7 1.4 slice_reduce_fusion.47
  16.1 1.4 slice_reduce_fusion.48
  18.1 1.5 collective-permute-done
  19.6 1.5 constant_dynamic-update-slice_fusion.1
  21.2 2.6 collective-permute-done.1
  23.9 1.3 collective-permute-start.2
  25.2 1.3 collective-permute-start.3
  26.5 1.1 slice_reduce_fusion.46
  27.6 2.6 collective-permute-done.3
  30.2 1.5 maximum_bitcast_fusion
  31.7 23.6 %fusion.98 = bf16[16,64,768]{2,1,0:T(8,128)(2,1)S(1)} fusion(f32[768]{0:T(1024)S(1)} %get-tuple-element.103, f32[768]{0:T(1024)S(1)} %get-tuple-element.104, f32[768]{0:T(1024)S(1)} %get-tuple-element.57, f32[768]{0:T(1024)S(1)} %get-tuple-element.58, f32[768]{0:T(1024)S(1)} %get-tuple-element.59, f32[768]{0:T(1024)S(1)} %get-tuple-element.60, ...), kind=kLoop, calls=%fused_computation.196 | loop fusion | flops 116391936 | bytes 78796800 | tf_op jit(solution)/shard_map/convert_element_type | solution.py:46
  55.3 1.6 convert_reduce_fusion.1
  56.9 33.1 %psum.64 = f32[256]{0:T(256)S(1)} all-reduce(f32[256]{0:T(256)S(1)} %get-tuple-element.113), channel_id=1, replica_groups=mesh['dp'=2,'sy'=4,'sx'=4] {'sy','sx'}, use_global_device_ids=true, to_apply=%region_2.3 | all-reduce | flops 256 | bytes 2048 | tf_op jit(solution)/shard_map/psum | solution.py:60
  89.9 1.0 fusion.146
  91.2 85.9 %all-reduce.7.cloned.1.call-done = f32[256,256]{1,0:T(8,128)} async-done(((f32[256,256]{1,0:T(8,128)}), f32[256,256]{1,0:T(8,128)}) %all-reduce.7.cloned.1.call-update) | async-done | bytes 262160 | tf_op jit(solution)/shard_map/psum | solution.py:60
  177.1 1.0 multiply_subtract_fusion
  178.3 0.6 select_reduce_fusion
  180.9 0.6 fusion.119
  181.5 0.6 fusion.148
  182.5 0.6 fusion.118
  183.1 0.6 fusion.150
  184.2 0.6 fusion.117
  185.2 0.6 fusion.152
  185.8 0.6 fusion.116
  186.4 1.1 broadcast_multiply_fusion.1
  187.5 4.2 fusion.139
  191.7 1.4 fusion.99
  193.5 0.8 fusion.115
  194.3 0.6 fusion.154
  195.3 0.4 fusion.155
  195.7 0.6 convolution_add_fusion.12
  196.7 0.6 fusion.114
  197.3 0.6 convolution_add_fusion.9
  198.8 0.6 convolution_add_fusion.10
  199.4 1.1 fusion.156
  200.4 0.6 fusion.112
  201.1 0.6 convolution_add_fusion.6
  201.7 1.1 fusion.163
  202.8 1.1 fusion.161
  203.9 1.7 fusion.130
  205.6 1.6 convolution_add_fusion.7
  207.6 1.6 fusion.110
  209.2 0.6 convolution_add_fusion.4
  209.8 0.6 convolution_add_fusion.3
  211.1 0.6 fusion.108
  211.8 0.9 multiply_reduce_fusion
  214.6 2.0 convert_reduce_fusion
  216.7 1.5 fusion.165
  218.7 7.5 %fusion.37 = (f32[768]{0:T(1024)S(1)}, f32[768]{0:T(1024)S(1)}, f32[768]{0:T(1024)S(1)}, f32[768]{0:T(1024)S(1)}, f32[768]{0:T(1024)S(1)}, /*index=5*/f32[768]{0...) fusion(bf16[22,70,768]{2,1,0:T(8,128)(2,1)S(1)} %copy-done.2, ...), kind=kOutput, calls=%fused_computation.135 | convolution fusion | flops 434886912 | bytes 24550400 | tf_op jit(solution)/shard_map/dot_general | solution.py:87
  226.2 7.6 %fusion.97 = (f32[768]{0:T(1024)S(1)}, f32[768]{0:T(1024)S(1)}, f32[768]{0:T(1024)S(1)}, f32[768]{0:T(1024)S(1)}, f32[768]{0:T(1024)S(1)}, /*index=5*/f32[768]{0...) fusion(bf16[22,70,768]{2,1,0:T(8,128)(2,1)S(1)} %copy-done.2, ...), kind=kLoop, calls=%fused_computation.195 | loop fusion | flops 42453504 | bytes 31512576 | tf_op jit(solution)/shard_map/reduce_sum | solution.py:97
  233.8 7.8 %fusion.79 = (f32[768]{0:T(1024)S(1)}, f32[768]{0:T(1024)S(1)}, f32[768]{0:T(1024)S(1)}, f32[768]{0:T(1024)S(1)}, f32[768]{0:T(1024)S(1)}, /*index=5*/f32[768]{0...) fusion(bf16[22,70,768]{2,1,0:T(8,128)(2,1)S(1)} %copy-done.2, ...), kind=kLoop, calls=%fused_computation.177 | loop fusion | flops 42453504 | bytes 31512576 | tf_op jit(solution)/shard_map/reduce_sum | solution.py:97
  242.7 0.7 copy-done.13
  243.4 1.8 broadcast_multiply_fusion
  246.5 5.5 %all-reduce.2 = (f32[]{:T(128)}, f32[10]{0:T(128)}) all-reduce(f32[]{:T(128)S(6)} %sub.41, f32[10]{0:T(128)S(1)} %get-tuple-element.121), channel_id=1, replica_groups=mesh['dp'=2,'sy'=4,'sx'=4] {'dp'}, use_global_device_ids=true, to_apply=%region_6.7 | all-reduce | flops 11 | bytes 88 | tf_op jit(solution)/shard_map/psum | solution.py:74
  252.6 2.2 reduce_sum.569
  254.8 40.9 %all-reduce = (f32[768]{0:T(1024)}, f32[256]{0:T(256)}) all-reduce(f32[768]{0:T(1024)S(1)} %reduce_sum.569, f32[256]{0:T(256)S(1)} %get-tuple-element.126), channel_id=1, replica_groups=mesh['dp'=2,'sy'=4,'sx'=4] {'dp','sy','sx'}, use_global_device_ids=true, to_apply=%region_60.61 | all-reduce | flops 1024 | bytes 8192 | tf_op jit(solution)/shard_map/psum | solution.py:102
  295.6 77.2 %all-reduce.11.cloned.1.call-done = (f32[7,7,768]{2,1,0:T(8,128)}, f32[768,256]{1,0:T(8,128)}) async-done(((f32[7,7,768]{2,1,0:T(8,128)}, f32[768,256]{1,0:T(8,128)}), (f32[7,7,768]{2,1,0:T(8,128)}, f32[768,256]{1,0:T(8,128)})) %all-reduce.11.cloned.1.call-update) | async-done | bytes 936976 | tf_op jit(solution)/shard_map/psum | solution.py:102
  372.9 77.6 %all-reduce.9.cloned.1.call-done = f32[10,256,256]{2,1,0:T(8,128)} async-done(((f32[10,256,256]{2,1,0:T(8,128)}), f32[10,256,256]{2,1,0:T(8,128)}) %all-reduce.9.cloned.1.call-update) | async-done | bytes 2621456 | tf_op jit(solution)/shard_map/psum | solution.py:74
  450.5 1.6 copy.81
  452.1 2.1 copy.82
  454.2 3.4 copy.83
  (129 shorter events, 7.6 us)
Async XLA Ops:
  7.2 180.4 %copy-start = (bf16[10,256,256]{2,1,0:T(8,128)(2,1)S(1)}, bf16[10,256,256]{2,1,0:T(8,128)(2,1)}, u32[]{:S(2)}) copy-start(bf16[10,256,256]{2,1,0:T(8,128)(2,1)} %param.13) | copy-start | bytes 3932164
  7.2 169.9 %all-reduce.7.cloned.1.call-start = ((), (), s32[]{:S(2)}) async-start(), calls=%async_computation | async-start | bytes 524288 | tf_op jit(solution)/shard_map/psum | solution.py:60
  8.4 11.2 %collective-permute-start = (bf16[1,3,64,768]{3,2,1,0:T(8,128)(2,1)S(1)}, bf16[1,3,64,768]{3,2,1,0:T(8,128)(2,1)S(1)}, u32[]{:S(2)}, u32[]{:S(2)}) collective-permute-start(bf16[1,3,64,768]{3,2,1,0:T(8,128)(2,1)S(1)} %get-tuple-element.118), channel_id=1, source_target_pairs={{0,4},{4,8},{8,12},{1,5},{5,9},{9,13},{2,6},{6,10},{10,14},{3,7},{... | collective-permute-start | bytes 884744 | tf_op jit(solution)/shard_map/ppermute | solution.py:20
  13.4 10.4 %collective-permute-start.1 = (bf16[1,3,64,768]{3,2,1,0:T(8,128)(2,1)S(1)}, bf16[1,3,64,768]{3,2,1,0:T(8,128)(2,1)S(1)}, u32[]{:S(2)}, u32[]{:S(2)}) collective-permute-start(bf16[1,3,64,768]{3,2,1,0:T(8,128)(2,1)S(1)} %get-tuple-element.117), channel_id=1, source_target_pairs={{4,0},{8,4},{12,8},{5,1},{9,5},{13,9},{6,2},{10,6},{14,10},{7,3},{... | collective-permute-start | bytes 884744 | tf_op jit(solution)/shard_map/ppermute | solution.py:23
  21.1 10.5 %copy-start.14 = (f32[768]{0:T(1024)S(1)}, f32[768]{0:T(1024)}, u32[]{:S(2)}) copy-start(f32[768]{0:T(1024)} %param.10) | copy-start | bytes 9220
  23.9 3.7 collective-permute-start.2
  25.2 5.0 %collective-permute-start.3 = (bf16[1,22,3,768]{3,2,1,0:T(4,128)(2,1)S(1)}, bf16[1,22,3,768]{3,2,1,0:T(4,128)(2,1)S(1)}, u32[]{:S(2)}, u32[]{:S(2)}) collective-permute-start(bf16[1,22,3,768]{3,2,1,0:T(4,128)(2,1)S(1)} %get-tuple-element.116), channel_id=1, source_target_pairs={{1,0},{2,1},{3,2},{5,4},{6,5},{7,6},{9,8},{10,9},{11,10},{13,12},{... | collective-permute-start | bytes 304136 | tf_op jit(solution)/shard_map/ppermute | solution.py:23
  31.6 23.6 %copy-start.1 = (bf16[22,70,768]{2,1,0:T(8,128)(2,1)}, bf16[22,70,768]{2,1,0:T(8,128)(2,1)S(1)}, u32[]{:S(2)}) copy-start(bf16[22,70,768]{2,1,0:T(8,128)(2,1)S(1)} %maximum_bitcast_fusion) | copy-start | bytes 7096324
  31.7 23.6 %copy-start.15 = (bf16[768,256]{1,0:T(8,128)(2,1)S(1)}, bf16[768,256]{1,0:T(8,128)(2,1)}, u32[]{:S(2)}) copy-start(bf16[768,256]{1,0:T(8,128)(2,1)} %param.11) | copy-start | bytes 1179652
  31.7 23.6 %copy-start.17 = (f32[256]{0:T(256)S(1)}, f32[256]{0:T(256)}, u32[]{:S(2)}) copy-start(f32[256]{0:T(256)} %param.12) | copy-start | bytes 3076
  55.3 1.6 copy-start.4
  91.0 281.9 %all-reduce.11.cloned.1.call-start = ((), (), s32[]{:S(2)}) async-start(), calls=%async_computation.2 | async-start | bytes 1916928 | tf_op jit(solution)/shard_map/psum | solution.py:102
  178.2 4.9 %copy-start.10 = (f32[256,256]{1,0:T(8,128)}, f32[256,256]{1,0:T(8,128)S(1)}, u32[]{:S(2)}) copy-start(f32[256,256]{1,0:T(8,128)S(1)} %multiply_subtract_fusion) | copy-start | bytes 786436
  180.1 4.7 %copy-start.6 = (f32[256,256]{0,1:T(8,128)}, f32[256,256]{0,1:T(8,128)S(1)}, u32[]{:S(2)}) copy-start(f32[256,256]{0,1:T(8,128)S(1)} %fusion.120) | copy-start | bytes 786436
  182.5 5.0 %copy-start.18 = (f32[10]{0:T(128)S(1)}, f32[10]{0:T(128)}, u32[]{:S(2)}) copy-start(f32[10]{0:T(128)} %param.14) | copy-start | bytes 124
  187.5 4.2 copy-start.8
  203.9 5.8 %copy-start.12 = (f32[256,256]{1,0:T(8,128)S(1)}, f32[256,256]{1,0:T(8,128)}, u32[]{:S(2)}) copy-start(f32[256,256]{1,0:T(8,128)} %fusion.163) | copy-start | bytes 786436
  203.9 6.8 %copy-start.7 = (f32[256,256]{0,1:T(8,128)S(1)}, f32[256,256]{0,1:T(8,128)}, u32[]{:S(2)}) copy-start(f32[256,256]{0,1:T(8,128)} %copy-done.6) | copy-start | bytes 786436
  205.6 5.5 %copy-start.11 = (f32[256,256]{1,0:T(8,128)S(1)}, f32[256,256]{1,0:T(8,128)}, u32[]{:S(2)}) copy-start(f32[256,256]{1,0:T(8,128)} %copy-done.10) | copy-start | bytes 786436
  214.6 2.1 copy-start.5
  216.7 1.9 copy-start.2
  216.7 2.0 copy-start.16
  226.2 7.6 %copy-start.3 = (f32[1024,768]{1,0:T(8,128)}, f32[1024,768]{1,0:T(8,128)S(1)}, u32[]{:S(2)}) copy-start(f32[1024,768]{1,0:T(8,128)S(1)} %get-tuple-element.125) | copy-start | bytes 9437188
  233.8 9.6 %copy-start.9 = (f32[256,256]{1,0:T(8,128)S(1)}, f32[256,256]{1,0:T(8,128)}, u32[]{:S(2)}) copy-start(f32[256,256]{1,0:T(8,128)} %copy-done.8) | copy-start | bytes 786436
  242.6 0.7 copy-start.13
  243.3 207.2 %all-reduce.9.cloned.1.call-start = ((), (), s32[]{:S(2)}) async-start(), calls=%async_computation.1 | async-start | bytes 5242880 | tf_op jit(solution)/shard_map/psum | solution.py:74
Sparse Core Ops, SparseCore 0:
  91.1 85.9 all-reduce.6
  243.5 129.3 all-reduce.10
  375.9 74.5 all-reduce.8
where the time goes:
time: 471 us; the launch traced here: 466 us
  waiting for transfers between devices  247 us (52%)
  blocking collectives  79.4 us (17%)
  other arithmetic  47.8 us (10%)
  matrix products  44.7 us (9%)
  between operations  21.4 us (5%)
  local copies, waits for them, and re-layouts  15.9 us (3%)
  starting transfers between devices  9.12 us (2%)
    psum x1, waiting for transfers between devices, body(): gram, colsum = lax.psum((gram, colsum), ('sy', 'sx'))  85.9 us
    psum x1, waiting for transfers between devices, body(): lax.psum((loss_part, class_local, logit_grad), 'dp')  77.6 us
    psum x1, waiting for transfers between devices, body(): lax.psum((weight_grad, depth_grad, depth_bias_grad, bias_grad), ('dp', 's...  77.2 us
    psum x1, blocking collectives, body(): lax.psum((weight_grad, depth_grad, depth_bias_grad, bias_grad), ('dp', 's...  40.9 us
    psum x1, blocking collectives, body(): gram, colsum = lax.psum((gram, colsum), ('sy', 'sx'))  33.1 us
    convert_element_type x1, other arithmetic, taps_conv(): return total.astype(jnp.bfloat16)  23.6 us
    reduce_sum x2, other arithmetic, body(): jnp.sum(window.astype(jnp.float32) * conv_grad.astype(jnp.float32), axis=...  15.4 us
    unnamed x49, local copies, waits for them, and re-layouts  9.89 us
  transfers between devices with their start and end apart: 7, of which 6 were waited for; matrix products, arithmetic and copies ran while one was open for 2% of the time, Pallas kernels for 0%

commit v1 on v0

v1 whole, which is shorter than its diff:
```python
import functools

import jax
import jax.numpy as jnp
from jax import lax
from jax.experimental import pallas as pl
from jax.experimental.pallas import tpu as pltpu
from jax.sharding import PartitionSpec as P

KERNEL = 7
HALF = KERNEL // 2
NEWTON_STEPS = 5
LANES = 128
GROUPS = 8
EDGE = 8

epsilon = 1e-05
loss_scale = 64.0
narrow = jnp.bfloat16
wide = jnp.float32


def params(megabytes, grid_axes=0):
    return pltpu.CompilerParams(
        vmem_limit_bytes=megabytes * 1024 * 1024,
        dimension_semantics=("arbitrary",) * grid_axes if grid_axes else None,
    )


def swap(value, axis, shift):
    count = lax.axis_size(axis)
    return lax.ppermute(value, axis, [(i, i ^ shift) for i in range(count)])


def is_upper(axis, shift):
    return (lax.axis_index(axis) & shift) != 0


def halve(value, axis, shift, sent_as):
    upper = is_upper(axis, shift)
    rows = value.shape[0] // 2
    low, high = value[:rows], value[rows:]
    kept = jnp.where(upper, high, low)
    sent = jnp.where(upper, low, high).astype(sent_as)
    return kept + swap(sent, axis, shift).astype(wide)


def unhalve(value, axis, shift):
    upper = is_upper(axis, shift)
    other = swap(value, axis, shift)
    return jnp.concatenate([jnp.where(upper, other, value), jnp.where(upper, value, other)])


def tree_sum(terms):
    while len(terms) > 1:
        terms = [terms[i] + terms[i + 1] for i in range(0, len(terms), 2)]
    return terms[0]


def exchange(value, axis, shift, sent_as):
    sent = value.astype(sent_as)
    return sent.astype(wide) + swap(sent, axis, shift).astype(wide)


def exchange_all(value, axis, sent_as):
    sent = value.astype(sent_as)
    moved = [sent] + [swap(sent, axis, shift) for shift in range(1, lax.axis_size(axis))]
    return tree_sum([part.astype(wide) for part in moved])


def doublings(axis, first=1):
    found = []
    shift = first
    while shift < lax.axis_size(axis):
        found.append(shift)
        shift *= 2
    return found


def next_along(value, axis):
    return lax.ppermute(value, axis, [(i, i + 1) for i in range(lax.axis_size(axis) - 1)])


def back_along(value, axis):
    return lax.ppermute(value, axis, [(i + 1, i) for i in range(lax.axis_size(axis) - 1)])


def spread_columns(source, target):
    for group in range(target.shape[0]):
        target[group] = source[pl.ds(EDGE - HALF + group, GROUPS, stride=GROUPS), :]


def fill_row(wide_row, middle, left, right):
    cols = middle.shape[0]
    wide_row[EDGE : EDGE + cols, :] = middle.astype(wide)
    wide_row[EDGE - HALF : EDGE, :] = left.astype(wide)
    wide_row[EDGE + cols : EDGE + cols + HALF, :] = right.astype(wide)


def spread_weights(weight_ref, spread_ref):
    for tap in range(KERNEL * KERNEL):
        spread_ref[tap] = jnp.broadcast_to(weight_ref[tap : tap + 1, :], spread_ref.shape[1:])


def conv_row(load, spread_ref, bias_ref, steps):
    total = [jnp.broadcast_to(bias_ref[0:1, :], (GROUPS, LANES))] * steps
    for row_tap in range(KERNEL):
        windows = [load(row_tap, group) for group in range(steps + KERNEL - 1)]
        for col_tap in range(KERNEL):
            scale = spread_ref[row_tap * KERNEL + col_tap]
            for step in range(steps):
                total[step] = total[step] + windows[step + col_tap] * scale
    return jnp.concatenate(total, axis=0).astype(narrow)


def reduce_part(tile, first, last, conv_out, reduce_ref, reduce_bias_ref, before, before_out, feat_out):
    product = jnp.dot(conv_out[...], reduce_ref[...], preferred_element_type=wide)

    @pl.when(first)
    def _():
        before[...] = product + reduce_bias_ref[...]

    @pl.when(jnp.logical_not(first))
    def _():
        before[...] += product

    @pl.when(last)
    def _():
        total = before[...]
        before_out[...] = total
        feat_out[...] = (total / (1.0 + jnp.exp(-total))).astype(narrow)


def feat_sums(feat):
    gram = lax.dot_general(feat, feat, (((0,), (0,)), ((), ())), preferred_element_type=wide)
    colsum = jnp.sum(feat.astype(wide), axis=0, keepdims=True)
    return gram, colsum


def inner_kernel(
    block, left, right, weight, bias, reduce_weight, reduce_bias,
    spread_out, conv_out, before_out, feat_out, gram_out, colsum_out,
    wide_row, spread_weight, before,
):
    tile = pl.program_id(0)
    first, last = tile == 0, tile == pl.num_programs(0) - 1
    rows, cols = block.shape[0], block.shape[1]
    steps = cols // GROUPS
    spread_weights(weight, spread_weight)

    def fill(row, _):
        fill_row(wide_row.at[row], block[row], left[row], right[row])
        spread_columns(wide_row.at[row], spread_out.at[0, row])
        return 0

    lax.fori_loop(0, rows, fill, 0)

    def one(index, _):
        def load(row_tap, group):
            return spread_out[0, index + row_tap, group]

        start = pl.multiple_of(index * cols, cols)
        conv_out[pl.ds(start, cols), :] = conv_row(load, spread_weight, bias, steps)
        return 0

    lax.fori_loop(0, rows - 2 * HALF, one, 0)
    reduce_part(
        tile, first, last, conv_out, reduce_weight, reduce_bias, before, before_out, feat_out
    )

    @pl.when(last)
    def _():
        gram_out[...], colsum_out[...] = feat_sums(feat_out[...])


def edge_kernel(
    spread_in, top, bottom, corners_top, corners_bottom, weight, bias, reduce_weight, reduce_bias,
    gram_in, colsum_in,
    spread_top, spread_bottom, conv_out, before_out, feat_out, sums_out,
    wide_row, spread_weight, before,
):
    tile = pl.program_id(0)
    first, last = tile == 0, tile == pl.num_programs(0) - 1
    rows, cols = spread_in.shape[1], top.shape[1]
    steps = cols // GROUPS
    spread_weights(weight, spread_weight)
    for row in range(HALF):
        fill_row(wide_row.at[row], top[row], corners_top[0, row], corners_top[1, row])
        spread_columns(wide_row.at[row], spread_top.at[0, row])
        fill_row(wide_row.at[row + HALF], bottom[row], corners_bottom[0, row], corners_bottom[1, row])
        spread_columns(wide_row.at[row + HALF], spread_bottom.at[0, row])

    def load_from(row):
        def load(row_tap, group):
            place = row + row_tap - HALF
            if place < 0:
                return spread_top[0, place + HALF, group]
            if place >= rows:
                return spread_bottom[0, place - rows, group]
            return spread_in[0, place, group]

        return load

    for index, row in enumerate(edge_rows(rows)):
        conv_out[index * cols : (index + 1) * cols, :] = conv_row(
            load_from(row), spread_weight, bias, steps
        )
    reduce_part(
        tile, first, last, conv_out, reduce_weight, reduce_bias, before, before_out, feat_out
    )

    @pl.when(last)
    def _():
        gram, colsum = feat_sums(feat_out[...])
        gram = gram + gram_in[...]
        colsum = colsum + colsum_in[...]
        width = gram.shape[0]
        half = width // 2
        quarter = half // 2
        sums_out[:half, :] = gram[:half, :]
        sums_out[half : half + quarter, :half] = gram[half : half + quarter, half:]
        sums_out[half : half + quarter, half:] = gram[half + quarter :, half:]
        sums_out[half + quarter :, :] = jnp.broadcast_to(
            colsum, (sums_out.shape[0] - half - quarter, width)
        )


def edge_rows(rows):
    return list(range(HALF)) + list(range(rows - HALF, rows))


def whole_spec(shape):
    return pl.BlockSpec(shape, lambda tile: (0,) * len(shape))


def tile_spec(shape):
    return pl.BlockSpec(shape, lambda tile: (0,) * (len(shape) - 1) + (tile,))


def lead_spec(shape):
    return pl.BlockSpec((1,) + shape[1:], lambda tile: (tile,) + (0,) * (len(shape) - 1))


def row_spec(shape):
    return pl.BlockSpec(shape, lambda tile: (tile, 0))


def shape_of(shape, dtype=wide):
    return jax.ShapeDtypeStruct(shape, dtype)


def conv_inner(block, left, right, weight, bias, reduce_weight, reduce_bias):
    rows, cols, channels = block.shape
    width = reduce_weight.shape[1]
    tiles = channels // LANES
    steps = cols // GROUPS
    pixels = (rows - 2 * HALF) * cols
    spread = (tiles, rows, steps + KERNEL - 1, GROUPS, LANES)
    return pl.pallas_call(
        inner_kernel,
        grid=(tiles,),
        in_specs=[
            tile_spec((rows, cols, LANES)),
            tile_spec((rows, HALF, LANES)),
            tile_spec((rows, HALF, LANES)),
            tile_spec((KERNEL * KERNEL, LANES)),
            tile_spec((1, LANES)),
            row_spec((LANES, width)),
            whole_spec((1, width)),
        ],
        out_specs=[
            lead_spec(spread),
            tile_spec((pixels, LANES)),
            whole_spec((pixels, width)),
            whole_spec((pixels, width)),
            whole_spec((width, width)),
            whole_spec((1, width)),
        ],
        out_shape=[
            shape_of(spread),
            shape_of((pixels, channels), narrow),
            shape_of((pixels, width)),
            shape_of((pixels, width), narrow),
            shape_of((width, width)),
            shape_of((1, width)),
        ],
        scratch_shapes=[
            pltpu.VMEM((rows, cols + 2 * EDGE, LANES), wide),
            pltpu.VMEM((KERNEL * KERNEL, GROUPS, LANES), wide),
            pltpu.VMEM((pixels, width), wide),
        ],
        compiler_params=params(32, 1),
        cost_estimate=pl.CostEstimate(
            flops=2 * KERNEL * KERNEL * pixels * channels,
            bytes_accessed=4 * rows * cols * channels * 2,
            transcendentals=pixels * width,
        ),
        name="conv_inner",
    )(block, left, right, weight, bias, reduce_weight, reduce_bias)


def conv_edge(spread, halos, weight, bias, reduce_weight, reduce_bias, gram, colsum):
    top, bottom, corners_top, corners_bottom = halos
    tiles, rows, groups = spread.shape[:3]
    cols, channels = top.shape[1:]
    width = reduce_weight.shape[1]
    pixels = 2 * HALF * cols
    side = (tiles, HALF, groups, GROUPS, LANES)
    sums_rows = 3 * width // 4 + 2 * GROUPS
    return pl.pallas_call(
        edge_kernel,
        grid=(tiles,),
        in_specs=[
            lead_spec(spread.shape),
            tile_spec((HALF, cols, LANES)),
            tile_spec((HALF, cols, LANES)),
            tile_spec((2, HALF, HALF, LANES)),
            tile_spec((2, HALF, HALF, LANES)),
            tile_spec((KERNEL * KERNEL, LANES)),
            tile_spec((1, LANES)),
            row_spec((LANES, width)),
            whole_spec((1, width)),
            whole_spec((width, width)),
            whole_spec((1, width)),
        ],
        out_specs=[
            lead_spec(side),
            lead_spec(side),
            tile_spec((pixels, LANES)),
            whole_spec((pixels, width)),
            whole_spec((pixels, width)),
            whole_spec((sums_rows, width)),
        ],
        out_shape=[
            shape_of(side),
            shape_of(side),
            shape_of((pixels, channels), narrow),
            shape_of((pixels, width)),
            shape_of((pixels, width), narrow),
            shape_of((sums_rows, width)),
        ],
        scratch_shapes=[
            pltpu.VMEM((2 * HALF, cols + 2 * EDGE, LANES), wide),
            pltpu.VMEM((KERNEL * KERNEL, GROUPS, LANES), wide),
            pltpu.VMEM((pixels, width), wide),
        ],
        compiler_params=params(32, 1),
        cost_estimate=pl.CostEstimate(
            flops=2 * KERNEL * KERNEL * pixels * channels,
            bytes_accessed=4 * rows * cols * channels * 2,
            transcendentals=pixels * width,
        ),
        name="conv_edge",
    )(
        spread, top, bottom, corners_top, corners_bottom,
        weight, bias, reduce_weight, reduce_bias, gram, colsum,
    )


def split(value):
    high = value.astype(narrow)
    return high, (value - high.astype(wide)).astype(narrow)


def product(left, right):
    def dot(a, b):
        return jnp.dot(a, b, preferred_element_type=wide)

    return dot(left[0], right[0]) + (dot(left[0], right[1]) + dot(left[1], right[0]))


def square_root(current):
    size = current.shape[0]
    row = lax.broadcasted_iota(jnp.int32, (size, size), 0)
    col = lax.broadcasted_iota(jnp.int32, (size, size), 1)
    triple = jnp.where(row == col, 3.0, 0.0)
    factor = split(0.5 * (triple - current))
    current = split(current)
    trail = [(current, None, factor)]
    inverse = factor
    current = split(product(current, factor))
    for step in range(1, NEWTON_STEPS):
        factor = split(0.5 * (triple - product(inverse, current)))
        trail.append((current, inverse, factor))
        last = step == NEWTON_STEPS - 1
        if not last:
            inverse = split(product(factor, inverse))
        current = product(current, factor)
        if not last:
            current = split(current)
    return current, trail


def square_root_change(change, trail):
    first, _, factor = trail[0]
    move = split(change)
    factor_move = split(-0.5 * change)
    change = product(move, factor) + product(first, factor_move)
    inverse_move = factor_move
    for step in range(1, NEWTON_STEPS):
        current, inverse, factor = trail[step]
        move = split(change)
        factor_move = split(
            -0.5 * (product(inverse_move, current) + product(inverse, move))
        )
        change = product(move, factor) + product(current, factor_move)
        if step < NEWTON_STEPS - 1:
            inverse_move = split(product(factor_move, inverse) + product(factor, inverse_move))
    return change


def head_kernel(
    flags, own, other, class_weight, class_bias, feat_inner, feat_edge, gate_inner, gate_edge,
    conv_turned, reduce_turned,
    root_out, facts_out, weight_grad_out, bias_grad_out, conv_inner_out, conv_edge_out,
    sums, root_grad_ref, pre, *, count, image_count,
):
    width = root_out.shape[0]
    half = width // 2
    quarter = half // 2
    rows = own.shape[0]
    upper = flags[0] != 0
    mine, theirs = own[...], other[...]
    sums[:rows, :] = jnp.where(upper, theirs, mine)
    sums[rows:, :] = jnp.where(upper, mine, theirs)
    low = jnp.concatenate(
        [sums[half : half + quarter, :half], sums[half : half + quarter, half:]], axis=0
    )
    cross = sums[:half, half:]
    gram = jnp.concatenate(
        [sums[:half, :], jnp.concatenate([cross.T, low], axis=1)], axis=0
    )
    mean_row = sums[half + quarter : half + quarter + 1, :] / count
    mean_col = jnp.broadcast_to(mean_row, (width, width)).T
    sigma = gram / count - mean_col * mean_row
    row = lax.broadcasted_iota(jnp.int32, (width, width), 0)
    col = lax.broadcasted_iota(jnp.int32, (width, width), 1)
    diagonal = row == col
    trace_value = jnp.sum(jnp.where(diagonal, sigma, 0.0), keepdims=True) + epsilon
    root_scale = jnp.sqrt(trace_value)
    unit, trail = square_root(sigma / trace_value)
    root = root_scale * unit
    root_out[...] = root

    classes = class_weight.shape[0]
    slots = class_bias.shape[0]
    place = lax.broadcasted_iota(jnp.int32, (slots, 1), 0)
    partial = [
        jnp.sum(class_weight[index].astype(wide) * root, axis=0, keepdims=True)
        for index in range(classes)
    ]
    partial.append(jnp.zeros((slots - classes, width), wide))
    logits = jnp.sum(jnp.concatenate(partial, axis=0), axis=1, keepdims=True) + class_bias[...]
    onehot = jnp.where(place == flags[1], 1.0, 0.0)
    soft = jnp.maximum(logits, 0.0) + jnp.log(1.0 + jnp.exp(-jnp.abs(logits)))
    share = 1.0 / (1.0 + jnp.exp(-logits))
    used = place < classes
    loss_part = jnp.sum(jnp.where(used, soft - onehot * logits, 0.0), keepdims=True)
    logit_grad = jnp.where(used, loss_scale * (share - onehot) / image_count, 0.0)
    facts_out[...] = jnp.broadcast_to(
        jnp.where(place == classes, loss_part, logit_grad), facts_out.shape
    )

    root_grad = jnp.zeros((width, width), wide)
    for index in range(classes):
        root_grad = root_grad + class_weight[index].astype(wide) * logit_grad[index : index + 1, :]
    root_grad = root_grad + root_grad.T
    change = square_root_change(root_scale * root_grad, trail)
    trace_grad = jnp.sum(root_grad * unit, keepdims=True) / (2.0 * root_scale) - jnp.sum(
        change * sigma, keepdims=True
    ) / (trace_value * trace_value)
    symmetric = (
        (change / trace_value + jnp.where(diagonal, trace_grad, 0.0)) / count
    ).astype(narrow)
    mean_term = jnp.sum(mean_col * symmetric.astype(wide), axis=0, keepdims=True)

    inner = feat_inner.shape[0]
    for feat, gate, start in ((feat_inner, gate_inner, 0), (feat_edge, gate_edge, inner)):
        grad = jnp.dot(feat[...], symmetric, preferred_element_type=wide) - mean_term
        pre[start : start + feat.shape[0], :] = (grad * gate[...]).astype(narrow)
    pre_grad = pre[...]
    bias_grad_out[...] = jnp.sum(pre_grad.astype(wide), axis=0, keepdims=True)
    weight_grad_out[...] = jnp.dot(conv_turned[...], pre_grad, preferred_element_type=wide)
    for out, start in ((conv_inner_out, 0), (conv_edge_out, inner)):
        out[...] = jnp.dot(
            pre[start : start + out.shape[0], :], reduce_turned[...], preferred_element_type=wide
        ).astype(narrow)


def head(flags, own, other, class_weight, class_bias, prepared, count, image_count):
    feat_inner, feat_edge, gate_inner, gate_edge, conv_turned, reduce_turned = prepared
    width, channels = reduce_turned.shape
    inner, edge = feat_inner.shape[0], feat_edge.shape[0]
    slots = class_bias.shape[0]
    in_vmem = pl.BlockSpec(memory_space=pltpu.VMEM)
    return pl.pallas_call(
        functools.partial(head_kernel, count=count, image_count=image_count),
        in_specs=[pl.BlockSpec(memory_space=pltpu.SMEM)] + [in_vmem] * 10,
        out_specs=[in_vmem] * 6,
        out_shape=[
            shape_of((width, width)),
            shape_of((slots, width)),
            shape_of((channels, width)),
            shape_of((1, width)),
            shape_of((inner, channels), narrow),
            shape_of((edge, channels), narrow),
        ],
        scratch_shapes=[
            pltpu.VMEM((2 * own.shape[0], width), wide),
            pltpu.VMEM((width, width), wide),
            pltpu.VMEM((inner + edge, width), narrow),
        ],
        compiler_params=params(48),
        cost_estimate=pl.CostEstimate(
            flops=200 * 2 * width**3, bytes_accessed=8 * 1024 * 1024, transcendentals=0
        ),
        name="head",
    )(
        flags, own, other, class_weight, class_bias,
        feat_inner, feat_edge, gate_inner, gate_edge, conv_turned, reduce_turned,
    )


def prepare_kernel(
    before_inner, before_edge, conv_inner_in, conv_edge_in, reduce_weight,
    gate_inner, gate_edge, conv_turned, reduce_turned,
):
    for before, gate in ((before_inner, gate_inner), (before_edge, gate_edge)):
        value = before[...]
        share = 1.0 / (1.0 + jnp.exp(-value))
        gate[...] = share * (1.0 + value * (1.0 - share))
    inner = conv_inner_in.shape[0]
    conv_turned[:, :inner] = conv_inner_in[...].T
    conv_turned[:, inner:] = conv_edge_in[...].T
    reduce_turned[...] = reduce_weight[...].T


def prepare(before_inner, before_edge, conv_in, conv_ed, reduce_weight):
    in_vmem = pl.BlockSpec(memory_space=pltpu.VMEM)
    channels, width = reduce_weight.shape
    inner, edge = before_inner.shape[0], before_edge.shape[0]
    return pl.pallas_call(
        prepare_kernel,
        in_specs=[in_vmem] * 5,
        out_specs=[in_vmem] * 4,
        out_shape=[
            shape_of((inner, width)),
            shape_of((edge, width)),
            shape_of((channels, inner + edge), narrow),
            shape_of((width, channels), narrow),
        ],
        compiler_params=params(32),
        cost_estimate=pl.CostEstimate(
            flops=10**9, bytes_accessed=6 * 1024 * 1024, transcendentals=(inner + edge) * width
        ),
        name="prepare",
    )(before_inner, before_edge, conv_in, conv_ed, reduce_weight)


def taps_kernel(spread_in, spread_top, spread_bottom, grad_inner, grad_edge, out, grads):
    rows = spread_in.shape[1]
    steps = grads.shape[1]
    cols = steps * GROUPS
    order = edge_rows(rows)
    for row in range(rows):
        if row in order:
            source, place = grad_edge, order.index(row)
        else:
            source, place = grad_inner, row - HALF
        values = source[place * cols : (place + 1) * cols, :].astype(wide)
        for step in range(steps):
            grads[row, step] = values[step * GROUPS : (step + 1) * GROUPS, :]

    def load(place, group):
        if place < 0:
            return spread_top[0, place + HALF, group]
        if place >= rows:
            return spread_bottom[0, place - rows, group]
        return spread_in[0, place, group]

    for first in range(0, KERNEL, 2):
        row_taps = [tap for tap in (first, first + 1) if tap < KERNEL]
        total = {
            (row_tap, col_tap): jnp.zeros((GROUPS, LANES), wide)
            for row_tap in row_taps
            for col_tap in range(KERNEL)
        }
        for place in range(first - HALF, rows + row_taps[-1] - HALF):
            windows = [load(place, group) for group in range(steps + KERNEL - 1)]
            for row_tap in row_taps:
                row = place - row_tap + HALF
                if not 0 <= row < rows:
                    continue
                for step in range(steps):
                    grad = grads[row, step]
                    for col_tap in range(KERNEL):
                        total[row_tap, col_tap] += windows[step + col_tap] * grad
        for (row_tap, col_tap), value in total.items():
            tap = row_tap * KERNEL + col_tap
            out[tap : tap + 1, :] = jnp.sum(value, axis=0, keepdims=True)
    total = [jnp.zeros((GROUPS, LANES), wide) for _ in range(KERNEL)]
    for index in range(rows * steps):
        slot = index % KERNEL
        total[slot] = total[slot] + grads[index // steps, index % steps]
    taps = KERNEL * KERNEL
    out[taps : taps + 1, :] = jnp.sum(sum(total), axis=0, keepdims=True)
    out[taps + 1 :, :] = jnp.zeros((out.shape[0] - taps - 1, LANES), wide)


def tap_grads(spread, spread_top, spread_bottom, grad_inner, grad_edge, first, many):
    tiles, rows, groups = spread.shape[:3]
    steps = groups - KERNEL + 1
    side = spread_top.shape

    def from_lead(shape):
        return pl.BlockSpec((1,) + shape[1:], lambda tile: (tile + first,) + (0,) * (len(shape) - 1))

    def from_tile(shape):
        return pl.BlockSpec((shape[0], LANES), lambda tile: (0, tile + first))

    return pl.pallas_call(
        taps_kernel,
        grid=(many,),
        in_specs=[
            from_lead(spread.shape),
            from_lead(side),
            from_lead(side),
            from_tile(grad_inner.shape),
            from_tile(grad_edge.shape),
        ],
        out_specs=pl.BlockSpec((KERNEL * KERNEL + 15, LANES), lambda tile: (0, tile)),
        out_shape=shape_of((KERNEL * KERNEL + 15, many * LANES)),
        scratch_shapes=[pltpu.VMEM((rows, steps, GROUPS, LANES), wide)],
        compiler_params=params(32, 1),
        cost_estimate=pl.CostEstimate(
            flops=2 * KERNEL * KERNEL * rows * steps * GROUPS * many * LANES,
            bytes_accessed=8 * 1024 * 1024 * many // tiles,
            transcendentals=0,
        ),
        name="tap_grads",
    )(spread, spread_top, spread_bottom, grad_inner, grad_edge)


def body(
    features, depth_weight, depth_bias, reduce_weight, reduce_bias, class_weight, class_bias, labels
):
    block = features[0]
    rows, cols, channels = block.shape
    width = reduce_weight.shape[1]
    classes = class_bias.shape[0]
    count = rows * cols * lax.axis_size("sy") * lax.axis_size("sx")
    image_count = features.shape[0] * lax.axis_size("dp")

    left = next_along(block[:, cols - HALF :], "sx")
    right = back_along(block[:, :HALF], "sx")
    top = next_along(block[rows - HALF :], "sy")
    bottom = back_along(block[:HALF], "sy")
    corners_top = next_along(jnp.stack([left[rows - HALF :], right[rows - HALF :]]), "sy")
    corners_bottom = back_along(jnp.stack([left[:HALF], right[:HALF]]), "sy")

    flat_weight = depth_weight.reshape(KERNEL * KERNEL, channels)
    flat_bias = depth_bias[None]
    reduce_row = reduce_bias[None]
    spread, conv_in, before_in, feat_in, gram, colsum = conv_inner(
        block, left, right, flat_weight, flat_bias, reduce_weight, reduce_row
    )
    spread_top, spread_bottom, conv_ed, before_ed, feat_ed, sums = conv_edge(
        spread,
        (top, bottom, corners_top, corners_bottom),
        flat_weight,
        flat_bias,
        reduce_weight,
        reduce_row,
        gram,
        colsum,
    )

    sums = halve(sums, "sx", 1, wide)
    gate_in, gate_ed, conv_turned, reduce_turned = prepare(
        before_in, before_ed, conv_in, conv_ed, reduce_weight
    )
    for shift in doublings("sx", 2):
        sums = exchange(sums, "sx", shift, wide)
    for shift in doublings("sy"):
        sums = exchange(sums, "sy", shift, wide)
    other = swap(sums, "sx", 1)

    flags = jnp.stack([is_upper("sx", 1).astype(jnp.int32), labels[0]])
    bias_column = jnp.pad(class_bias, (0, -classes % (2 * GROUPS)))[:, None]
    root, facts, weight_grad, bias_grad, conv_grad_in, conv_grad_ed = head(
        flags,
        sums,
        other,
        class_weight,
        bias_column,
        (feat_in, feat_ed, gate_in, gate_ed, conv_turned, reduce_turned),
        count,
        image_count,
    )

    sent = jnp.concatenate([root, facts])
    known = [sent] + [swap(sent, "dp", shift) for shift in range(1, lax.axis_size("dp"))]
    class_weight_grad = tree_sum(
        [part[width : width + classes, 0][:, None, None] * part[None, :width] for part in known]
    )
    totals = tree_sum([part[width:, 0] for part in known])
    class_bias_grad = totals[:classes]
    loss = totals[classes] / image_count

    tiles = channels // LANES
    many = tiles // 3 if tiles % 3 == 0 else tiles
    parts = [
        tap_grads(spread, spread_top, spread_bottom, conv_grad_in, conv_grad_ed, first, many)
        for first in range(0, tiles, many)
    ]
    weight_grad = halve(weight_grad, "sx", 1, wide)
    for shift in doublings("sx", 2):
        weight_grad = halve(weight_grad, "sx", shift, narrow)
    for shift in doublings("dp"):
        weight_grad = exchange(weight_grad, "dp", shift, narrow)
    weight_grad = exchange_all(weight_grad, "sy", narrow)
    for shift in reversed(doublings("sx")):
        weight_grad = unhalve(weight_grad, "sx", shift)

    taps = KERNEL * KERNEL
    small = jnp.concatenate(parts, axis=1)
    row = jnp.arange(small.shape[0])[:, None]
    small = jnp.where(row == taps + 1, jnp.pad(bias_grad, ((0, 0), (0, channels - width))), small)
    small = halve(small, "sx", 1, wide)
    for shift in doublings("sx", 2):
        small = exchange(small, "sx", shift, narrow)
    for shift in doublings("dp"):
        small = exchange(small, "dp", shift, narrow)
    small = exchange_all(small, "sy", narrow)
    small = unhalve(small, "sx", 1)
    return (
        loss,
        small[:taps].reshape(depth_weight.shape),
        small[taps],
        weight_grad,
        small[taps + 1, :width],
        class_weight_grad,
        class_bias_grad,
    )


def solution(mesh):
    placed = (P("dp", "sy", "sx", None), P(), P(), P(), P(), P(), P(), P("dp"))
    return jax.shard_map(
        body,
        mesh=mesh,
        in_specs=placed,
        out_specs=(P(), P(), P(), P(), P(), P(), P()),
        check_vma=False,
    )
```

time: 471 us -> 147 us (0.31)
  waiting for transfers between devices: 247 us -> 31.4 us
  blocking collectives: 79.4 us -> 0 us
  Pallas kernels: 0 us -> 47 us
  matrix products: 44.7 us -> 0 us
  other arithmetic: 47.8 us -> 3.62 us
  starting transfers between devices: 9.12 us -> 42.5 us
  between operations: 21.4 us -> 3.55 us
    psum x3 -> x0, waiting for transfers between devices: 241 us -> none  [the longest x1 85.9 us: body(): gram, colsum = lax.psum((gram, colsum), ('sy', 'sx'))]
    psum x3 -> x0, blocking collectives: 79.4 us -> none  [the longest x1 40.9 us: body(): lax.psum((weight_grad, depth_grad, depth_bias_grad, bias_grad), ('dp', 's...]
    pallas_call x0 -> x7, Pallas kernels: none -> 47 us  [the longest x3 14.8 us: tap_grads(): pl.pallas_call(taps_kernel, grid=(many,), in_specs=[from_lead(spread.shap...]
    dot_general x48 -> x0, matrix products: 44.7 us -> none  [the longest x15 9.54 us: matrix_root(): current = jnp.dot(current, factor, precision=highest)]
    ppermute x4 -> x27, starting transfers between devices: 8.83 us -> 42.5 us  [the longest x21 27.4 us: swap(): return lax.ppermute(value, axis, [(i, i ^ shift) for i in range(count)])]
    ppermute x4 -> x27, waiting for transfers between devices: 6.67 us -> 31.4 us  [the longest x21 31.4 us: swap(): return lax.ppermute(value, axis, [(i, i ^ shift) for i in range(count)])]
    convert_element_type x2 -> x6, other arithmetic: 23.6 us -> 0.13 us  [the longest x3 0.07 us: exchange(): sent = value.astype(sent_as)]
    reduce_sum x5 -> x0, other arithmetic: 19.9 us -> none  [the longest x2 15.4 us: body(): jnp.sum(window.astype(jnp.float32) * conv_grad.astype(jnp.float32), axis=...]
  transfers between devices with their start and end apart: 7 -> 27, of which waited for: 6 -> 12; matrix products, arithmetic and copies ran while one was open for 2% -> 6% of each run, Pallas kernels for 0% -> 10%
where the time goes in v1:
time: 147 us; the launch traced here: 146 us
  Pallas kernels  47 us (32%)
  starting transfers between devices  42.5 us (29%)
  waiting for transfers between devices  31.4 us (21%)
  local copies, waits for them, and re-layouts  17.8 us (12%)
  other arithmetic  3.62 us (2%)
  between operations  3.55 us (2%)
    ppermute x21, waiting for transfers between devices, swap(): return lax.ppermute(value, axis, [(i, i ^ shift) for i in range(count)])  31.4 us
    ppermute x21, starting transfers between devices, swap(): return lax.ppermute(value, axis, [(i, i ^ shift) for i in range(count)])  27.4 us
    pallas_call x3, Pallas kernels, tap_grads(): pl.pallas_call(taps_kernel, grid=(many,), in_specs=[from_lead(spread.shap...  14.8 us
    pallas_call x1, Pallas kernels, conv_inner(): pl.pallas_call(inner_kernel, grid=(tiles,), in_specs=[tile_spec((rows, co...  13.7 us
    ppermute x3, starting transfers between devices, next_along(): lax.ppermute(value, axis, [(i, i + 1) for i in range(lax.axis_size(axis)...  11.2 us
    pallas_call x1, Pallas kernels, head(): pl.pallas_call(functools.partial(head_kernel, count=count, image_count=im...  10.9 us
    unnamed x40, local copies, waits for them, and re-layouts  9.62 us
    pallas_call x1, Pallas kernels, conv_edge(): pl.pallas_call(edge_kernel, grid=(tiles,), in_specs=[lead_spec(spread.sha...  6.67 us
  transfers between devices with their start and end apart: 27, of which 12 were waited for; matrix products, arithmetic and copies ran while one was open for 6% of the time, Pallas kernels for 10%

profile of v1, /device:TPU:0, one launch (start us, length us, event | category | flops | bytes accessed | tf_op | source)
XLA Modules:
  0.0 145.9 jit_solution(2777183455197861478)
XLA Ops:
  0.6 1.2 fusion
  1.9 2.4 %collective-permute-start = (bf16[16,3,768]{2,1,0:T(4,128)(2,1)S(1)}, bf16[16,3,768]{2,1,0:T(4,128)(2,1)S(1)}, u32[]{:S(2)}, u32[]{:S(2)}) collective-permute-start(bf16[16,3,768]{2,1,0:T(4,128)(2,1)S(1)} %get-tuple-element.54), channel_id=1, source_target_pairs={{0,1},{1,2},{2,3},{4,5},{5,6},{6,7},{8,9},{9,10},{10,11},{12,13},{... | collective-permute-start | bytes 221192 | tf_op jit(solution)/shard_map/ppermute | solution.py:81
  4.2 1.3 collective-permute-start.1
  5.5 1.9 %slice_bitcast_fusion = (bf16[3,64,768]{2,1,0:T(8,128)(2,1)}, bf16[3,64,768]{2,1,0:T(8,128)(2,1)}) fusion(bf16[1,16,64,768]{3,2,1,0:T(8,128)(2,1)} %param.8), kind=kLoop, calls=%fused_computation.5 | loop fusion | bytes 1179648 | tf_op jit(solution)/shard_map/slice | solution.py:657
  7.5 4.3 %collective-permute-start.2 = (bf16[3,64,768]{2,1,0:T(8,128)(2,1)}, bf16[3,64,768]{2,1,0:T(8,128)(2,1)S(1)}, u32[]{:S(2)}, u32[]{:S(2)}) collective-permute-start(bf16[3,64,768]{2,1,0:T(8,128)(2,1)} %get-tuple-element.52), channel_id=1, source_target_pairs={{0,4},{4,8},{8,12},{1,5},{5,9},{9,13},{2,6},{6,10},{10,14},{3,7},{... | collective-permute-start | bytes 884744 | tf_op jit(solution)/shard_map/ppermute | solution.py:81
  11.8 1.3 collective-permute-start.3
  13.2 4.5 %collective-permute-start.4 = (bf16[2,3,3,768]{3,2,1,0:T(4,128)(2,1)S(1)}, bf16[2,3,3,768]{3,2,1,0:T(4,128)(2,1)S(1)}, u32[]{:S(2)}, u32[]{:S(2)}) collective-permute-start(bf16[2,3,3,768]{3,2,1,0:T(4,128)(2,1)S(1)} %pad_maximum_fusion.4), channel_id=1, source_target_pairs={{0,4},{4,8},{8,12},{1,5},{5,9},{9,13},{2,6},{6,10},{10,14},{3,7},{... | collective-permute-start | bytes 82952 | tf_op jit(solution)/shard_map/ppermute | solution.py:81
  17.8 1.3 collective-permute-start.5
  19.1 0.9 reshape.39.weight
  20.0 0.7 broadcast_in_dim.30.bias
  20.7 1.0 copy-done.2
  21.7 0.7 copy-done.4
  22.4 13.7 %conv_inner.1 = (f32[6,16,14,8,128]{4,3,2,1,0:T(8,128)S(1)}, bf16[640,768]{1,0:T(8,128)(2,1)S(1)}, f32[640,256]{1,0:T(8,128)S(1)}, bf16[640,256]{1,0:T(8,128)(2,...) custom-call(bf16[16,64,768]{2,1,0:T(8,128)(2,1)S(1)} %bitcast.22, ...), custom_call_target="tpu_custom_call" | custom-call | flops 48168960 | bytes 6291456 | tf_op jit(solution)/shard_map/conv_inner/pallas_call | solution.py:259
  36.1 0.8 copy-done.8
  36.9 0.7 copy-done.14
  37.7 6.7 %conv_edge.1 = (f32[6,3,14,8,128]{4,3,2,1,0:T(8,128)S(1)}, f32[6,3,14,8,128]{4,3,2,1,0:T(8,128)S(1)}, bf16[384,768]{1,0:T(8,128)(2,1)S(1)}, f32[384,256]{1,0:T(8...) custom-call(f32[6,16,14,8,128]{4,3,2,1,0:T(8,128)S(1)} %get-tuple-element.29.spread_in, ...), custom_call_target="tpu_custom_call" | custom-call | flops 28901376 | bytes 6291456 | tf_op jit(solution)/shard_map/conv_edge/pallas_call | solution.py:310
  44.4 0.8 copy-done.12
  45.2 1.7 %collective-permute-start.6 = (f32[104,256]{1,0:T(8,128)S(1)}, f32[104,256]{1,0:T(8,128)S(1)}, u32[]{:S(2)}, u32[]{:S(2)}) collective-permute-start(f32[104,256]{1,0:T(8,128)S(1)} %slice_select_fusion.1), channel_id=1, source_target_pairs={{0,1},{1,0},{2,3},{3,2},{4,5},{5,4},{6,7},{7,6},{8,9},{9,8},{10,11... | collective-permute-start | bytes 319496 | tf_op jit(solution)/shard_map/ppermute | solution.py:32
  46.8 1.0 collective-permute-done.6
  47.8 2.9 %collective-permute-start.7 = (f32[104,256]{1,0:T(8,128)S(1)}, f32[104,256]{1,0:T(8,128)S(1)}, u32[]{:S(2)}, u32[]{:S(2)}) collective-permute-start(f32[104,256]{1,0:T(8,128)S(1)} %select_add_fusion.1), channel_id=1, source_target_pairs={{0,2},{1,3},{2,0},{3,1},{4,6},{5,7},{6,4},{7,5},{8,10},{9,11},{10,... | collective-permute-start | bytes 319496 | tf_op jit(solution)/shard_map/ppermute | solution.py:32
  51.4 2.6 %collective-permute-done.7 = f32[104,256]{1,0:T(8,128)S(1)} collective-permute-done((f32[104,256]{1,0:T(8,128)S(1)}, f32[104,256]{1,0:T(8,128)S(1)}, u32[]{:S(2)}, u32[]{:S(2)}) %collective-permute-start.7) | collective-permute-done | bytes 106528 | tf_op jit(solution)/shard_map/ppermute | solution.py:32
  54.0 2.7 %collective-permute-start.8 = (f32[104,256]{1,0:T(8,128)S(1)}, f32[104,256]{1,0:T(8,128)S(1)}, u32[]{:S(2)}, u32[]{:S(2)}) collective-permute-start(f32[104,256]{1,0:T(8,128)S(1)} %add.60), channel_id=1, source_target_pairs={{0,4},{4,0},{8,12},{12,8},{1,5},{5,1},{9,13},{13,9},{2,6},{6,2},{1... | collective-permute-start | bytes 319496 | tf_op jit(solution)/shard_map/ppermute | solution.py:32
  56.7 2.8 %collective-permute-done.8 = f32[104,256]{1,0:T(8,128)S(1)} collective-permute-done((f32[104,256]{1,0:T(8,128)S(1)}, f32[104,256]{1,0:T(8,128)S(1)}, u32[]{:S(2)}, u32[]{:S(2)}) %collective-permute-start.8) | collective-permute-done | bytes 106528 | tf_op jit(solution)/shard_map/ppermute | solution.py:32
  59.5 3.0 %collective-permute-start.9 = (f32[104,256]{1,0:T(8,128)S(1)}, f32[104,256]{1,0:T(8,128)S(1)}, u32[]{:S(2)}, u32[]{:S(2)}) collective-permute-start(f32[104,256]{1,0:T(8,128)S(1)} %add.61), channel_id=1, source_target_pairs={{0,8},{4,12},{8,0},{12,4},{1,9},{5,13},{9,1},{13,5},{2,10},{6,14},... | collective-permute-start | bytes 319496 | tf_op jit(solution)/shard_map/ppermute | solution.py:32
  62.5 4.2 %collective-permute-done.9 = f32[104,256]{1,0:T(8,128)S(1)} collective-permute-done((f32[104,256]{1,0:T(8,128)S(1)}, f32[104,256]{1,0:T(8,128)S(1)}, u32[]{:S(2)}, u32[]{:S(2)}) %collective-permute-start.9) | collective-permute-done | bytes 106528 | tf_op jit(solution)/shard_map/ppermute | solution.py:32
  67.0 1.3 copy-done.7
  68.3 1.1 copy-done.9
  69.4 1.1 copy-done.11
  70.4 1.0 copy-done.13
  71.4 0.9 prepare.1
  72.4 1.1 copy-done.16
  73.5 10.9 %head.1 = (f32[256,256]{1,0:T(8,128)S(1)}, f32[16,256]{1,0:T(8,128)S(1)}, f32[768,256]{1,0:T(8,128)S(1)}, f32[1,256]{1,0:T(1,128)S(1)}, bf16[640,768]{1,0:T(8,128)(2,1)S(1)}, /*index=5*/bf16[384,768]{1,0:T(8,128)(2,1)S(1)}) custom-call(s32[2]{0:T(128)S(1)} %pad_add_fusion.flags, f32[104,256]{1,0:T(8,128)S(1)} %add.62.own, ...), custom_call_target="tpu_custom_call" | custom-call | flops 6710886400 | bytes 8388608 | tf_op jit(solution)/shard_map/head/pallas_call | solution.py:496
  84.5 5.1 %tap_grads.3 = f32[64,256]{1,0:T(8,128)S(1)} custom-call(f32[6,16,14,8,128]{4,3,2,1,0:T(8,128)S(1)} %bitcast.20, f32[6,3,14,8,128]{4,3,2,1,0:T(8,128)S(1)} %get-tuple-element.46.spread_top, f32[6,3,14,8,128]{4,3,2,1,0:T(8,128)S(1)} %get-tuple-element.47.spread_bottom, bf16[640,768]{1,0:T(8,128)(2,1)S(1)} %get-tuple-element.48.grad_inner, ...), custom_call_target="tpu_custom_call" | custom-call | flops 25690112 | bytes 2796202 | tf_op jit(solution)/shard_map/tap_grads/pallas_call | solution.py:621
  89.5 4.9 %tap_grads.4 = f32[64,256]{1,0:T(8,128)S(1)} custom-call(f32[6,16,14,8,128]{4,3,2,1,0:T(8,128)S(1)} %bitcast.20, f32[6,3,14,8,128]{4,3,2,1,0:T(8,128)S(1)} %get-tuple-element.46.spread_top, f32[6,3,14,8,128]{4,3,2,1,0:T(8,128)S(1)} %get-tuple-element.47.spread_bottom, bf16[640,768]{1,0:T(8,128)(2,1)S(1)} %get-tuple-element.48.grad_inner, ...), custom_call_target="tpu_custom_call" | custom-call | flops 25690112 | bytes 2796202 | tf_op jit(solution)/shard_map/tap_grads/pallas_call | solution.py:621
  94.4 4.9 %tap_grads.5 = f32[64,256]{1,0:T(8,128)S(1)} custom-call(f32[6,16,14,8,128]{4,3,2,1,0:T(8,128)S(1)} %bitcast.20, f32[6,3,14,8,128]{4,3,2,1,0:T(8,128)S(1)} %get-tuple-element.46.spread_top, f32[6,3,14,8,128]{4,3,2,1,0:T(8,128)S(1)} %get-tuple-element.47.spread_bottom, bf16[640,768]{1,0:T(8,128)(2,1)S(1)} %get-tuple-element.48.grad_inner, ...), custom_call_target="tpu_custom_call" | custom-call | flops 25690112 | bytes 2796202 | tf_op jit(solution)/shard_map/tap_grads/pallas_call | solution.py:621
  99.5 0.6 collective-permute-start.12
  100.2 0.8 collective-permute-done.12
  101.0 0.3 collective-permute-start.13
  101.3 3.8 %collective-permute-done.13 = bf16[32,768]{1,0:T(8,128)(2,1)S(1)} collective-permute-done((bf16[32,768]{1,0:T(8,128)(2,1)S(1)}, bf16[32,768]{1,0:T(8,128)(2,1)S(1)}, u32[]{:S(2)}, u32[]{:S(2)}) %collective-permute-start.13) | collective-permute-done | bytes 49184 | tf_op jit(solution)/shard_map/ppermute | solution.py:32
  105.2 1.5 %collective-permute-start.14 = (bf16[32,768]{1,0:T(8,128)(2,1)S(1)}, bf16[32,768]{1,0:T(8,128)(2,1)S(1)}, u32[]{:S(2)}, u32[]{:S(2)}) collective-permute-start(bf16[32,768]{1,0:T(8,128)(2,1)S(1)} %add_convert_fusion.3), channel_id=1, source_target_pairs={{0,16},{16,0},{1,17},{17,1},{2,18},{18,2},{3,19},{19,3},{4,20},{20... | collective-permute-start | bytes 147464 | tf_op jit(solution)/shard_map/ppermute | solution.py:32
  106.7 0.1 slice_reduce_fusion.2
  106.8 0.6 collective-permute-start.11
  107.4 2.3 %collective-permute-done.14 = bf16[32,768]{1,0:T(8,128)(2,1)S(1)} collective-permute-done((bf16[32,768]{1,0:T(8,128)(2,1)S(1)}, bf16[32,768]{1,0:T(8,128)(2,1)S(1)}, u32[]{:S(2)}, u32[]{:S(2)}) %collective-permute-start.14) | collective-permute-done | bytes 49184 | tf_op jit(solution)/shard_map/ppermute | solution.py:32
  109.8 0.7 collective-permute-start.15
  110.5 3.4 %collective-permute-start.16 = (bf16[32,768]{1,0:T(8,128)(2,1)S(1)}, bf16[32,768]{1,0:T(8,128)(2,1)S(1)}, u32[]{:S(2)}, u32[]{:S(2)}) collective-permute-start(bf16[32,768]{1,0:T(8,128)(2,1)S(1)} %add_convert_fusion.2), channel_id=1, source_target_pairs={{0,8},{4,12},{8,0},{12,4},{1,9},{5,13},{9,1},{13,5},{2,10},{6,14},... | collective-permute-start | bytes 147464 | tf_op jit(solution)/shard_map/ppermute | solution.py:32
  113.9 0.4 collective-permute-start.17
  114.4 1.4 collective-permute-start.20
  115.8 1.1 collective-permute-done.16
  116.9 2.9 %collective-permute-done.17 = bf16[32,768]{1,0:T(8,128)(2,1)S(1)} collective-permute-done((bf16[32,768]{1,0:T(8,128)(2,1)S(1)}, bf16[32,768]{1,0:T(8,128)(2,1)S(1)}, u32[]{:S(2)}, u32[]{:S(2)}) %collective-permute-start.17) | collective-permute-done | bytes 49184 | tf_op jit(solution)/shard_map/ppermute | solution.py:32
  120.0 1.7 %collective-permute-start.21 = (bf16[192,256]{1,0:T(8,128)(2,1)S(1)}, bf16[192,256]{1,0:T(8,128)(2,1)S(1)}, u32[]{:S(2)}, u32[]{:S(2)}) collective-permute-start(bf16[192,256]{1,0:T(8,128)(2,1)S(1)} %add_convert_fusion.1), channel_id=1, source_target_pairs={{0,16},{16,0},{1,17},{17,1},{2,18},{18,2},{3,19},{19,3},{4,20},{20... | collective-permute-start | bytes 294920 | tf_op jit(solution)/shard_map/ppermute | solution.py:32
  121.7 0.1 slice_reduce_fusion.1
  121.8 3.4 %collective-permute-done.21 = bf16[192,256]{1,0:T(8,128)(2,1)S(1)} collective-permute-done((bf16[192,256]{1,0:T(8,128)(2,1)S(1)}, bf16[192,256]{1,0:T(8,128)(2,1)S(1)}, u32[]{:S(2)}, u32[]{:S(2)}) %collective-permute-start.21) | collective-permute-done | bytes 98336 | tf_op jit(solution)/shard_map/ppermute | solution.py:32
  125.3 2.6 %collective-permute-start.23 = (bf16[192,256]{1,0:T(8,128)(2,1)S(1)}, bf16[192,256]{1,0:T(8,128)(2,1)S(1)}, u32[]{:S(2)}, u32[]{:S(2)}) collective-permute-start(bf16[192,256]{1,0:T(8,128)(2,1)S(1)} %add_convert_fusion), channel_id=1, source_target_pairs={{0,8},{4,12},{8,0},{12,4},{1,9},{5,13},{9,1},{13,5},{2,10},{6,14},... | collective-permute-start | bytes 294920 | tf_op jit(solution)/shard_map/ppermute | solution.py:32
  127.9 1.8 %collective-permute-start.24 = (bf16[192,256]{1,0:T(8,128)(2,1)S(1)}, bf16[192,256]{1,0:T(8,128)(2,1)S(1)}, u32[]{:S(2)}, u32[]{:S(2)}) collective-permute-start(bf16[192,256]{1,0:T(8,128)(2,1)S(1)} %add_convert_fusion), channel_id=1, source_target_pairs={{0,12},{4,8},{8,4},{12,0},{1,13},{5,9},{9,5},{13,1},{2,14},{6,10},... | collective-permute-start | bytes 294920 | tf_op jit(solution)/shard_map/ppermute | solution.py:32
  129.7 1.9 %multiply_add_fusion = f32[10,256,256]{2,1,0:T(8,128)} fusion(f32[256,256]{1,0:T(8,128)S(1)} %slice.132, f32[10]{0:T(128)S(1)} %slice_reduce_fusion.1, f32[256,256]{1,0:T(8,128)S(1)} %get-tuple-element.44, f32[10]{0:T(128)S(1)} %slice_reduce_fusion.2), kind=kLoop, calls=%fused_computation | loop fusion | flops 1966080 | bytes 3145808 | tf_op jit(solution)/shard_map/add | solution.py:56
  131.6 4.4 %collective-permute-done.23 = bf16[192,256]{1,0:T(8,128)(2,1)S(1)} collective-permute-done((bf16[192,256]{1,0:T(8,128)(2,1)S(1)}, bf16[192,256]{1,0:T(8,128)(2,1)S(1)}, u32[]{:S(2)}, u32[]{:S(2)}) %collective-permute-start.23) | collective-permute-done | bytes 98336 | tf_op jit(solution)/shard_map/ppermute | solution.py:32
  136.0 1.8 %collective-permute-start.25 = (f32[192,256]{1,0:T(8,128)S(1)}, f32[192,256]{1,0:T(8,128)S(1)}, u32[]{:S(2)}, u32[]{:S(2)}) collective-permute-start(f32[192,256]{1,0:T(8,128)S(1)} %add_add_fusion), channel_id=1, source_target_pairs={{0,2},{1,3},{2,0},{3,1},{4,6},{5,7},{6,4},{7,5},{8,10},{9,11},{10,... | collective-permute-start | bytes 589832 | tf_op jit(solution)/shard_map/ppermute | solution.py:32
  137.8 0.5 slice.124
  139.0 0.6 slice_reduce_fusion
  139.6 2.1 %collective-permute-done.25 = f32[192,256]{1,0:T(8,128)S(1)} collective-permute-done((f32[192,256]{1,0:T(8,128)S(1)}, f32[192,256]{1,0:T(8,128)S(1)}, u32[]{:S(2)}, u32[]{:S(2)}) %collective-permute-start.25) | collective-permute-done | bytes 196640 | tf_op jit(solution)/shard_map/ppermute | solution.py:32
  141.9 0.6 slice.130
  142.5 0.7 reshape.40
  143.2 0.6 slice_reduce_fusion.3
  143.9 0.9 pad_maximum_fusion
  (85 shorter events, 1.5 us)
Async XLA Ops:
  0.6 20.1 %copy-start.1 = (bf16[1,16,64,768]{3,2,1,0:T(8,128)(2,1)S(1)}, bf16[1,16,64,768]{3,2,1,0:T(8,128)(2,1)}, u32[]{:S(2)}) copy-start(bf16[1,16,64,768]{3,2,1,0:T(8,128)(2,1)} %param.8) | copy-start | bytes 4718596
  1.9 11.2 %collective-permute-start = (bf16[16,3,768]{2,1,0:T(4,128)(2,1)S(1)}, bf16[16,3,768]{2,1,0:T(4,128)(2,1)S(1)}, u32[]{:S(2)}, u32[]{:S(2)}) collective-permute-start(bf16[16,3,768]{2,1,0:T(4,128)(2,1)S(1)} %get-tuple-element.54), channel_id=1, source_target_pairs={{0,1},{1,2},{2,3},{4,5},{5,6},{6,7},{8,9},{9,10},{10,11},{12,13},{... | collective-permute-start | bytes 221192 | tf_op jit(solution)/shard_map/ppermute | solution.py:81
  4.2 8.9 %collective-permute-start.1 = (bf16[16,3,768]{2,1,0:T(4,128)(2,1)S(1)}, bf16[16,3,768]{2,1,0:T(4,128)(2,1)S(1)}, u32[]{:S(2)}, u32[]{:S(2)}) collective-permute-start(bf16[16,3,768]{2,1,0:T(4,128)(2,1)S(1)} %get-tuple-element.53), channel_id=1, source_target_pairs={{1,0},{2,1},{3,2},{5,4},{6,5},{7,6},{9,8},{10,9},{11,10},{13,12},{... | collective-permute-start | bytes 221192 | tf_op jit(solution)/shard_map/ppermute | solution.py:85
  7.5 30.2 %collective-permute-start.2 = (bf16[3,64,768]{2,1,0:T(8,128)(2,1)}, bf16[3,64,768]{2,1,0:T(8,128)(2,1)S(1)}, u32[]{:S(2)}, u32[]{:S(2)}) collective-permute-start(bf16[3,64,768]{2,1,0:T(8,128)(2,1)} %get-tuple-element.52), channel_id=1, source_target_pairs={{0,4},{4,8},{8,12},{1,5},{5,9},{9,13},{2,6},{6,10},{10,14},{3,7},{... | collective-permute-start | bytes 884744 | tf_op jit(solution)/shard_map/ppermute | solution.py:81
  11.8 25.9 %collective-permute-start.3 = (bf16[3,64,768]{2,1,0:T(8,128)(2,1)}, bf16[3,64,768]{2,1,0:T(8,128)(2,1)S(1)}, u32[]{:S(2)}, u32[]{:S(2)}) collective-permute-start(bf16[3,64,768]{2,1,0:T(8,128)(2,1)} %get-tuple-element.51), channel_id=1, source_target_pairs={{4,0},{8,4},{12,8},{5,1},{9,5},{13,9},{6,2},{10,6},{14,10},{7,3},{... | collective-permute-start | bytes 884744 | tf_op jit(solution)/shard_map/ppermute | solution.py:85
  13.2 24.5 %collective-permute-start.4 = (bf16[2,3,3,768]{3,2,1,0:T(4,128)(2,1)S(1)}, bf16[2,3,3,768]{3,2,1,0:T(4,128)(2,1)S(1)}, u32[]{:S(2)}, u32[]{:S(2)}) collective-permute-start(bf16[2,3,3,768]{3,2,1,0:T(4,128)(2,1)S(1)} %pad_maximum_fusion.4), channel_id=1, source_target_pairs={{0,4},{4,8},{8,12},{1,5},{5,9},{9,13},{2,6},{6,10},{10,14},{3,7},{... | collective-permute-start | bytes 82952 | tf_op jit(solution)/shard_map/ppermute | solution.py:81
  17.8 19.9 %collective-permute-start.5 = (bf16[2,3,3,768]{3,2,1,0:T(4,128)(2,1)S(1)}, bf16[2,3,3,768]{3,2,1,0:T(4,128)(2,1)S(1)}, u32[]{:S(2)}, u32[]{:S(2)}) collective-permute-start(bf16[2,3,3,768]{3,2,1,0:T(4,128)(2,1)S(1)} %pad_maximum_fusion.5), channel_id=1, source_target_pairs={{4,0},{8,4},{12,8},{5,1},{9,5},{13,9},{6,2},{10,6},{14,10},{7,3},{... | collective-permute-start | bytes 82952 | tf_op jit(solution)/shard_map/ppermute | solution.py:85
  20.7 1.0 copy-start.2
  21.7 0.7 copy-start.4
  36.1 0.8 copy-start.8
  36.9 0.7 copy-start.14
  37.6 6.7 %copy-start = (f32[6,16,14,8,128]{4,3,2,1,0:T(8,128)}, f32[6,16,14,8,128]{4,3,2,1,0:T(8,128)S(1)}, u32[]{:S(2)}) copy-start(f32[6,16,14,8,128]{4,3,2,1,0:T(8,128)S(1)} %get-tuple-element.29.spread_in) | copy-start | bytes 16515076
  37.6 6.7 %copy-start.6 = (bf16[640,768]{1,0:T(8,128)(2,1)}, bf16[640,768]{1,0:T(8,128)(2,1)S(1)}, u32[]{:S(2)}) copy-start(bf16[640,768]{1,0:T(8,128)(2,1)S(1)} %get-tuple-element.37.conv_inner_in) | copy-start | bytes 2949124
  37.7 24.8 %copy-start.17 = (f32[10]{0:T(128)S(1)}, f32[10]{0:T(128)}, u32[]{:S(2)}) copy-start(f32[10]{0:T(128)} %param.14) | copy-start | bytes 124
  37.7 29.3 %copy-start.3 = (bf16[768,256]{1,0:T(8,128)(2,1)S(1)}, bf16[768,256]{1,0:T(8,128)(2,1)}, u32[]{:S(2)}) copy-start(bf16[768,256]{1,0:T(8,128)(2,1)} %reduce_weight.5) | copy-start | bytes 1179652
  44.4 0.8 copy-start.12
  45.2 2.7 %copy-start.10 = (bf16[384,768]{1,0:T(8,128)(2,1)}, bf16[384,768]{1,0:T(8,128)(2,1)S(1)}, u32[]{:S(2)}) copy-start(bf16[384,768]{1,0:T(8,128)(2,1)S(1)} %get-tuple-element.38.conv_edge_in) | copy-start | bytes 1769476
  45.2 28.4 %copy-start.15 = (bf16[640,256]{1,0:T(8,128)(2,1)S(1)}, bf16[640,256]{1,0:T(8,128)(2,1)}, u32[]{:S(2)}) copy-start(bf16[640,256]{1,0:T(8,128)(2,1)} %copy-done.14) | copy-start | bytes 983044
  45.2 2.6 %collective-permute-start.6 = (f32[104,256]{1,0:T(8,128)S(1)}, f32[104,256]{1,0:T(8,128)S(1)}, u32[]{:S(2)}, u32[]{:S(2)}) collective-permute-start(f32[104,256]{1,0:T(8,128)S(1)} %slice_select_fusion.1), channel_id=1, source_target_pairs={{0,1},{1,0},{2,3},{3,2},{4,5},{5,4},{6,7},{7,6},{8,9},{9,8},{10,11... | collective-permute-start | bytes 319496 | tf_op jit(solution)/shard_map/ppermute | solution.py:32
  47.8 6.2 %collective-permute-start.7 = (f32[104,256]{1,0:T(8,128)S(1)}, f32[104,256]{1,0:T(8,128)S(1)}, u32[]{:S(2)}, u32[]{:S(2)}) collective-permute-start(f32[104,256]{1,0:T(8,128)S(1)} %select_add_fusion.1), channel_id=1, source_target_pairs={{0,2},{1,3},{2,0},{3,1},{4,6},{5,7},{6,4},{7,5},{8,10},{9,11},{10,... | collective-permute-start | bytes 319496 | tf_op jit(solution)/shard_map/ppermute | solution.py:32
  54.0 5.5 %collective-permute-start.8 = (f32[104,256]{1,0:T(8,128)S(1)}, f32[104,256]{1,0:T(8,128)S(1)}, u32[]{:S(2)}, u32[]{:S(2)}) collective-permute-start(f32[104,256]{1,0:T(8,128)S(1)} %add.60), channel_id=1, source_target_pairs={{0,4},{4,0},{8,12},{12,8},{1,5},{5,1},{9,13},{13,9},{2,6},{6,2},{1... | collective-permute-start | bytes 319496 | tf_op jit(solution)/shard_map/ppermute | solution.py:32
  59.5 7.2 %collective-permute-start.9 = (f32[104,256]{1,0:T(8,128)S(1)}, f32[104,256]{1,0:T(8,128)S(1)}, u32[]{:S(2)}, u32[]{:S(2)}) collective-permute-start(f32[104,256]{1,0:T(8,128)S(1)} %add.61), channel_id=1, source_target_pairs={{0,8},{4,12},{8,0},{12,4},{1,9},{5,13},{9,1},{13,5},{2,10},{6,14},... | collective-permute-start | bytes 319496 | tf_op jit(solution)/shard_map/ppermute | solution.py:32
  66.7 6.8 %collective-permute-start.10 = (f32[104,256]{1,0:T(8,128)S(1)}, f32[104,256]{1,0:T(8,128)S(1)}, u32[]{:S(2)}, u32[]{:S(2)}) collective-permute-start(f32[104,256]{1,0:T(8,128)S(1)} %add.62.own), channel_id=1, source_target_pairs={{0,1},{1,0},{2,3},{3,2},{4,5},{5,4},{6,7},{7,6},{8,9},{9,8},{10,11... | collective-permute-start | bytes 319496 | tf_op jit(solution)/shard_map/ppermute | solution.py:32
  67.0 6.6 %copy-start.5 = (bf16[10,256,256]{2,1,0:T(8,128)(2,1)S(1)}, bf16[10,256,256]{2,1,0:T(8,128)(2,1)}, u32[]{:S(2)}) copy-start(bf16[10,256,256]{2,1,0:T(8,128)(2,1)} %class_weight.1) | copy-start | bytes 3932164
  67.0 1.3 copy-start.7
  68.3 1.1 copy-start.9
  69.4 1.1 copy-start.11
  70.4 1.0 copy-start.13
  72.4 1.1 copy-start.16
  73.5 10.9 %slice-start = ((s8[5505024]{0:T(1024)(128)(4,1)}), s8[4194304]{0:T(1024)(128)(4,1)S(1)}, s32[]{:S(2)}) async-start(s8[5505024]{0:T(1024)(128)(4,1)} %bitcast.19), calls=%async_computation | async-start | bytes 8388608
  73.5 10.9 %slice-start.1 = ((s8[5505024]{0:T(1024)(128)(4,1)}), s8[1310720]{0:T(1024)(128)(4,1)S(1)}, s32[]{:S(2)}) async-start(s8[5505024]{0:T(1024)(128)(4,1)} %bitcast.19), calls=%async_computation.1 | async-start | bytes 2621440
  99.5 1.5 %collective-permute-start.12 = (f32[32,768]{1,0:T(8,128)S(1)}, f32[32,768]{1,0:T(8,128)S(1)}, u32[]{:S(2)}, u32[]{:S(2)}) collective-permute-start(f32[32,768]{1,0:T(8,128)S(1)} %slice_select_fusion.2), channel_id=1, source_target_pairs={{0,1},{1,0},{2,3},{3,2},{4,5},{5,4},{6,7},{7,6},{8,9},{9,8},{10,11... | collective-permute-start | bytes 294920 | tf_op jit(solution)/shard_map/ppermute | solution.py:32
  100.1 14.2 %collective-permute-start.19 = (f32[384,256]{1,0:T(8,128)S(1)}, f32[384,256]{1,0:T(8,128)S(1)}, u32[]{:S(2)}, u32[]{:S(2)}) collective-permute-start(f32[384,256]{1,0:T(8,128)S(1)} %slice_select_fusion), channel_id=1, source_target_pairs={{0,1},{1,0},{2,3},{3,2},{4,5},{5,4},{6,7},{7,6},{8,9},{9,8},{10,11... | collective-permute-start | bytes 1179656 | tf_op jit(solution)/shard_map/ppermute | solution.py:32
  101.0 4.2 %collective-permute-start.13 = (bf16[32,768]{1,0:T(8,128)(2,1)S(1)}, bf16[32,768]{1,0:T(8,128)(2,1)S(1)}, u32[]{:S(2)}, u32[]{:S(2)}) collective-permute-start(bf16[32,768]{1,0:T(8,128)(2,1)S(1)} %add_convert_fusion.4), channel_id=1, source_target_pairs={{0,2},{1,3},{2,0},{3,1},{4,6},{5,7},{6,4},{7,5},{8,10},{9,11},{10,... | collective-permute-start | bytes 147464 | tf_op jit(solution)/shard_map/ppermute | solution.py:32
  105.2 4.6 %collective-permute-start.14 = (bf16[32,768]{1,0:T(8,128)(2,1)S(1)}, bf16[32,768]{1,0:T(8,128)(2,1)S(1)}, u32[]{:S(2)}, u32[]{:S(2)}) collective-permute-start(bf16[32,768]{1,0:T(8,128)(2,1)S(1)} %add_convert_fusion.3), channel_id=1, source_target_pairs={{0,16},{16,0},{1,17},{17,1},{2,18},{18,2},{3,19},{19,3},{4,20},{20... | collective-permute-start | bytes 147464 | tf_op jit(solution)/shard_map/ppermute | solution.py:32
  106.8 13.0 %collective-permute-start.11 = (f32[272,256]{1,0:T(8,128)S(1)}, f32[272,256]{1,0:T(8,128)S(1)}, u32[]{:S(2)}, u32[]{:S(2)}) collective-permute-start(f32[272,256]{1,0:T(8,128)S(1)} %pad_maximum_fusion.2), channel_id=1, source_target_pairs={{0,16},{16,0},{1,17},{17,1},{2,18},{18,2},{3,19},{19,3},{4,20},{20... | collective-permute-start | bytes 835592 | tf_op jit(solution)/shard_map/ppermute | solution.py:32
  109.8 6.0 %collective-permute-start.15 = (bf16[32,768]{1,0:T(8,128)(2,1)S(1)}, bf16[32,768]{1,0:T(8,128)(2,1)S(1)}, u32[]{:S(2)}, u32[]{:S(2)}) collective-permute-start(bf16[32,768]{1,0:T(8,128)(2,1)S(1)} %add_convert_fusion.2), channel_id=1, source_target_pairs={{0,4},{4,0},{8,12},{12,8},{1,5},{5,1},{9,13},{13,9},{2,6},{6,2},{1... | collective-permute-start | bytes 147464 | tf_op jit(solution)/shard_map/ppermute | solution.py:32
  110.5 6.4 %collective-permute-start.16 = (bf16[32,768]{1,0:T(8,128)(2,1)S(1)}, bf16[32,768]{1,0:T(8,128)(2,1)S(1)}, u32[]{:S(2)}, u32[]{:S(2)}) collective-permute-start(bf16[32,768]{1,0:T(8,128)(2,1)S(1)} %add_convert_fusion.2), channel_id=1, source_target_pairs={{0,8},{4,12},{8,0},{12,4},{1,9},{5,13},{9,1},{13,5},{2,10},{6,14},... | collective-permute-start | bytes 147464 | tf_op jit(solution)/shard_map/ppermute | solution.py:32
  113.9 5.9 %collective-permute-start.17 = (bf16[32,768]{1,0:T(8,128)(2,1)S(1)}, bf16[32,768]{1,0:T(8,128)(2,1)S(1)}, u32[]{:S(2)}, u32[]{:S(2)}) collective-permute-start(bf16[32,768]{1,0:T(8,128)(2,1)S(1)} %add_convert_fusion.2), channel_id=1, source_target_pairs={{0,12},{4,8},{8,4},{12,0},{1,13},{5,9},{9,5},{13,1},{2,14},{6,10},... | collective-permute-start | bytes 147464 | tf_op jit(solution)/shard_map/ppermute | solution.py:32
  114.4 5.5 %collective-permute-start.20 = (bf16[192,256]{1,0:T(8,128)(2,1)S(1)}, bf16[192,256]{1,0:T(8,128)(2,1)S(1)}, u32[]{:S(2)}, u32[]{:S(2)}) collective-permute-start(bf16[192,256]{1,0:T(8,128)(2,1)S(1)} %select_convert_fusion), channel_id=1, source_target_pairs={{0,2},{1,3},{2,0},{3,1},{4,6},{5,7},{6,4},{7,5},{8,10},{9,11},{10,... | collective-permute-start | bytes 294920 | tf_op jit(solution)/shard_map/ppermute | solution.py:32
  119.8 22.1 %collective-permute-start.18 = (f32[32,768]{1,0:T(8,128)S(1)}, f32[32,768]{1,0:T(8,128)S(1)}, u32[]{:S(2)}, u32[]{:S(2)}) collective-permute-start(f32[32,768]{1,0:T(8,128)S(1)} %add_add_fusion.1), channel_id=1, source_target_pairs={{0,1},{1,0},{2,3},{3,2},{4,5},{5,4},{6,7},{7,6},{8,9},{9,8},{10,11... | collective-permute-start | bytes 294920 | tf_op jit(solution)/shard_map/ppermute | solution.py:32
  120.0 5.2 %collective-permute-start.21 = (bf16[192,256]{1,0:T(8,128)(2,1)S(1)}, bf16[192,256]{1,0:T(8,128)(2,1)S(1)}, u32[]{:S(2)}, u32[]{:S(2)}) collective-permute-start(bf16[192,256]{1,0:T(8,128)(2,1)S(1)} %add_convert_fusion.1), channel_id=1, source_target_pairs={{0,16},{16,0},{1,17},{17,1},{2,18},{18,2},{3,19},{19,3},{4,20},{20... | collective-permute-start | bytes 294920 | tf_op jit(solution)/shard_map/ppermute | solution.py:32
  125.2 6.3 %collective-permute-start.22 = (bf16[192,256]{1,0:T(8,128)(2,1)S(1)}, bf16[192,256]{1,0:T(8,128)(2,1)S(1)}, u32[]{:S(2)}, u32[]{:S(2)}) collective-permute-start(bf16[192,256]{1,0:T(8,128)(2,1)S(1)} %add_convert_fusion), channel_id=1, source_target_pairs={{0,4},{4,0},{8,12},{12,8},{1,5},{5,1},{9,13},{13,9},{2,6},{6,2},{1... | collective-permute-start | bytes 294920 | tf_op jit(solution)/shard_map/ppermute | solution.py:32
  125.3 10.7 %collective-permute-start.23 = (bf16[192,256]{1,0:T(8,128)(2,1)S(1)}, bf16[192,256]{1,0:T(8,128)(2,1)S(1)}, u32[]{:S(2)}, u32[]{:S(2)}) collective-permute-start(bf16[192,256]{1,0:T(8,128)(2,1)S(1)} %add_convert_fusion), channel_id=1, source_target_pairs={{0,8},{4,12},{8,0},{12,4},{1,9},{5,13},{9,1},{13,5},{2,10},{6,14},... | collective-permute-start | bytes 294920 | tf_op jit(solution)/shard_map/ppermute | solution.py:32
  127.9 8.1 %collective-permute-start.24 = (bf16[192,256]{1,0:T(8,128)(2,1)S(1)}, bf16[192,256]{1,0:T(8,128)(2,1)S(1)}, u32[]{:S(2)}, u32[]{:S(2)}) collective-permute-start(bf16[192,256]{1,0:T(8,128)(2,1)S(1)} %add_convert_fusion), channel_id=1, source_target_pairs={{0,12},{4,8},{8,4},{12,0},{1,13},{5,9},{9,5},{13,1},{2,14},{6,10},... | collective-permute-start | bytes 294920 | tf_op jit(solution)/shard_map/ppermute | solution.py:32
  136.0 5.7 %collective-permute-start.25 = (f32[192,256]{1,0:T(8,128)S(1)}, f32[192,256]{1,0:T(8,128)S(1)}, u32[]{:S(2)}, u32[]{:S(2)}) collective-permute-start(f32[192,256]{1,0:T(8,128)S(1)} %add_add_fusion), channel_id=1, source_target_pairs={{0,2},{1,3},{2,0},{3,1},{4,6},{5,7},{6,4},{7,5},{8,10},{9,11},{10,... | collective-permute-start | bytes 589832 | tf_op jit(solution)/shard_map/ppermute | solution.py:32
  141.8 2.0 %collective-permute-start.26 = (f32[384,256]{1,0:T(8,128)S(1)}, f32[384,256]{1,0:T(8,128)S(1)}, u32[]{:S(2)}, u32[]{:S(2)}) collective-permute-start(f32[384,256]{1,0:T(8,128)S(1)} %pad_maximum_fusion.1), channel_id=1, source_target_pairs={{0,1},{1,0},{2,3},{3,2},{4,5},{5,4},{6,7},{7,6},{8,9},{9,8},{10,11... | collective-permute-start | bytes 1179656 | tf_op jit(solution)/shard_map/ppermute | solution.py:32

commit v2 on v1

--- a/solution.py
+++ b/solution.py
@@ -98,8 +98,10 @@
 
 
 def spread_weights(weight_ref, spread_ref):
-    for tap in range(KERNEL * KERNEL):
-        spread_ref[tap] = jnp.broadcast_to(weight_ref[tap : tap + 1, :], spread_ref.shape[1:])
+    for row_tap in range(KERNEL):
+        for col_tap in range(KERNEL):
+            scale = weight_ref[row_tap, col_tap : col_tap + 1, :]
+            spread_ref[row_tap * KERNEL + col_tap] = jnp.broadcast_to(scale, spread_ref.shape[1:])
 
 
 def conv_row(load, spread_ref, bias_ref, steps):
@@ -174,21 +176,23 @@
 
 
 def edge_kernel(
-    spread_in, top, bottom, corners_top, corners_bottom, weight, bias, reduce_weight, reduce_bias,
-    gram_in, colsum_in,
+    spread_in, top, bottom, weight, bias, reduce_weight, reduce_bias, gram_in, colsum_in,
     spread_top, spread_bottom, conv_out, before_out, feat_out, sums_out,
-    wide_row, spread_weight, before,
+    wide_row, corners, spread_weight, before,
 ):
     tile = pl.program_id(0)
     first, last = tile == 0, tile == pl.num_programs(0) - 1
-    rows, cols = spread_in.shape[1], top.shape[1]
+    rows, cols = spread_in.shape[1], wide_row.shape[1] - 2 * EDGE
     steps = cols // GROUPS
     spread_weights(weight, spread_weight)
-    for row in range(HALF):
-        fill_row(wide_row.at[row], top[row], corners_top[0, row], corners_top[1, row])
-        spread_columns(wide_row.at[row], spread_top.at[0, row])
-        fill_row(wide_row.at[row + HALF], bottom[row], corners_bottom[0, row], corners_bottom[1, row])
-        spread_columns(wide_row.at[row + HALF], spread_bottom.at[0, row])
+    for side, (strip, spread) in enumerate(((top, spread_top), (bottom, spread_bottom))):
+        corners[side] = strip[HALF * cols :, :].astype(wide)
+        for row in range(HALF):
+            place = wide_row.at[side * HALF + row]
+            left = corners[side, row * HALF : (row + 1) * HALF, :]
+            right = corners[side, (HALF + row) * HALF : (HALF + row + 1) * HALF, :]
+            fill_row(place, strip[row * cols : (row + 1) * cols, :], left, right)
+            spread_columns(place, spread.at[0, row])
 
     def load_from(row):
         def load(row_tap, group):
@@ -263,7 +267,7 @@
             tile_spec((rows, cols, LANES)),
             tile_spec((rows, HALF, LANES)),
             tile_spec((rows, HALF, LANES)),
-            tile_spec((KERNEL * KERNEL, LANES)),
+            tile_spec((KERNEL, KERNEL, LANES)),
             tile_spec((1, LANES)),
             row_spec((LANES, width)),
             whole_spec((1, width)),
@@ -289,7 +293,7 @@
             pltpu.VMEM((KERNEL * KERNEL, GROUPS, LANES), wide),
             pltpu.VMEM((pixels, width), wide),
         ],
-        compiler_params=params(32, 1),
+        compiler_params=params(56, 1),
         cost_estimate=pl.CostEstimate(
             flops=2 * KERNEL * KERNEL * pixels * channels,
             bytes_accessed=4 * rows * cols * channels * 2,
@@ -300,9 +304,9 @@
 
 
 def conv_edge(spread, halos, weight, bias, reduce_weight, reduce_bias, gram, colsum):
-    top, bottom, corners_top, corners_bottom = halos
+    top, bottom = halos
     tiles, rows, groups = spread.shape[:3]
-    cols, channels = top.shape[1:]
+    cols, channels = (groups - KERNEL + 1) * GROUPS, top.shape[1]
     width = reduce_weight.shape[1]
     pixels = 2 * HALF * cols
     side = (tiles, HALF, groups, GROUPS, LANES)
@@ -312,11 +316,9 @@
         grid=(tiles,),
         in_specs=[
             lead_spec(spread.shape),
-            tile_spec((HALF, cols, LANES)),
-            tile_spec((HALF, cols, LANES)),
-            tile_spec((2, HALF, HALF, LANES)),
-            tile_spec((2, HALF, HALF, LANES)),
-            tile_spec((KERNEL * KERNEL, LANES)),
+            tile_spec((top.shape[0], LANES)),
+            tile_spec((top.shape[0], LANES)),
+            tile_spec((KERNEL, KERNEL, LANES)),
             tile_spec((1, LANES)),
             row_spec((LANES, width)),
             whole_spec((1, width)),
@@ -341,10 +343,11 @@
         ],
         scratch_shapes=[
             pltpu.VMEM((2 * HALF, cols + 2 * EDGE, LANES), wide),
+            pltpu.VMEM((2, top.shape[0] - HALF * cols, LANES), wide),
             pltpu.VMEM((KERNEL * KERNEL, GROUPS, LANES), wide),
             pltpu.VMEM((pixels, width), wide),
         ],
-        compiler_params=params(32, 1),
+        compiler_params=params(56, 1),
         cost_estimate=pl.CostEstimate(
             flops=2 * KERNEL * KERNEL * pixels * channels,
             bytes_accessed=4 * rows * cols * channels * 2,
@@ -352,8 +355,7 @@
         ),
         name="conv_edge",
     )(
-        spread, top, bottom, corners_top, corners_bottom,
-        weight, bias, reduce_weight, reduce_bias, gram, colsum,
+        spread, top, bottom, weight, bias, reduce_weight, reduce_bias, gram, colsum,
     )
 
 
@@ -410,11 +412,18 @@
 
 
 def head_kernel(
-    flags, own, other, class_weight, class_bias, feat_inner, feat_edge, gate_inner, gate_edge,
-    conv_turned, reduce_turned,
-    root_out, facts_out, weight_grad_out, bias_grad_out, conv_inner_out, conv_edge_out,
-    sums, root_grad_ref, pre, *, count, image_count,
+    flags, own, other, class_bias, *refs, count, image_count,
 ):
+    stored, refs = refs[:7], refs[7:]
+    root_out, facts_out, weight_grad_out, bias_grad_out, conv_inner_out, conv_edge_out = refs[:6]
+    held, (sums, pre, arrived) = refs[6:13], refs[13:]
+    copies = [
+        pltpu.make_async_copy(source, target, arrived.at[index])
+        for index, (source, target) in enumerate(zip(stored, held))
+    ]
+    for copy in copies:
+        copy.start()
+    class_weight, feat_inner, feat_edge, gate_inner, gate_edge, conv_turned, reduce_turned = held
     width = root_out.shape[0]
     half = width // 2
     quarter = half // 2
@@ -442,6 +451,7 @@
     root = root_scale * unit
     root_out[...] = root
 
+    copies[0].wait()
     classes = class_weight.shape[0]
     slots = class_bias.shape[0]
     place = lax.broadcasted_iota(jnp.int32, (slots, 1), 0)
@@ -474,6 +484,8 @@
     ).astype(narrow)
     mean_term = jnp.sum(mean_col * symmetric.astype(wide), axis=0, keepdims=True)
 
+    for copy in copies[1:]:
+        copy.wait()
     inner = feat_inner.shape[0]
     for feat, gate, start in ((feat_inner, gate_inner, 0), (feat_edge, gate_edge, inner)):
         grad = jnp.dot(feat[...], symmetric, preferred_element_type=wide) - mean_term
@@ -492,10 +504,13 @@
     width, channels = reduce_turned.shape
     inner, edge = feat_inner.shape[0], feat_edge.shape[0]
     slots = class_bias.shape[0]
+    stored = (class_weight,) + tuple(prepared)
     in_vmem = pl.BlockSpec(memory_space=pltpu.VMEM)
     return pl.pallas_call(
         functools.partial(head_kernel, count=count, image_count=image_count),
-        in_specs=[pl.BlockSpec(memory_space=pltpu.SMEM)] + [in_vmem] * 10,
+        in_specs=[pl.BlockSpec(memory_space=pltpu.SMEM)]
+        + [in_vmem] * 3
+        + [pl.BlockSpec(memory_space=pltpu.HBM)] * len(stored),
         out_specs=[in_vmem] * 6,
         out_shape=[
             shape_of((width, width)),
@@ -505,19 +520,19 @@
             shape_of((inner, channels), narrow),
             shape_of((edge, channels), narrow),
         ],
-        scratch_shapes=[
+        scratch_shapes=[pltpu.VMEM(part.shape, part.dtype) for part in stored]
+        + [
             pltpu.VMEM((2 * own.shape[0], width), wide),
-            pltpu.VMEM((width, width), wide),
             pltpu.VMEM((inner + edge, width), narrow),
-        ],
-        compiler_params=params(48),
+            pltpu.SemaphoreType.DMA((len(stored),)),
+        ],
+        compiler_params=params(56),
         cost_estimate=pl.CostEstimate(
             flops=200 * 2 * width**3, bytes_accessed=8 * 1024 * 1024, transcendentals=0
         ),
         name="head",
     )(
-        flags, own, other, class_weight, class_bias,
-        feat_inner, feat_edge, gate_inner, gate_edge, conv_turned, reduce_turned,
+        flags, own, other, class_bias, *stored
     )
 
 
@@ -549,7 +564,7 @@
             shape_of((channels, inner + edge), narrow),
             shape_of((width, channels), narrow),
         ],
-        compiler_params=params(32),
+        compiler_params=params(56),
         cost_estimate=pl.CostEstimate(
             flops=10**9, bytes_accessed=6 * 1024 * 1024, transcendentals=(inner + edge) * width
         ),
@@ -631,7 +646,7 @@
         out_specs=pl.BlockSpec((KERNEL * KERNEL + 15, LANES), lambda tile: (0, tile)),
         out_shape=shape_of((KERNEL * KERNEL + 15, many * LANES)),
         scratch_shapes=[pltpu.VMEM((rows, steps, GROUPS, LANES), wide)],
-        compiler_params=params(32, 1),
+        compiler_params=params(56, 1),
         cost_estimate=pl.CostEstimate(
             flops=2 * KERNEL * KERNEL * rows * steps * GROUPS * many * LANES,
             bytes_accessed=8 * 1024 * 1024 * many // tiles,
@@ -639,6 +654,13 @@
         ),
         name="tap_grads",
     )(spread, spread_top, spread_bottom, grad_inner, grad_edge)
+
+
+def edge_strip(block, left, right, rows):
+    channels = block.shape[2]
+    parts = [part[rows].reshape(-1, channels) for part in (block, left, right)]
+    short = -(2 * HALF * HALF) % 16
+    return jnp.concatenate(parts + [jnp.zeros((short, channels), block.dtype)])
 
 
 def body(
@@ -653,21 +675,26 @@
 
     left = next_along(block[:, cols - HALF :], "sx")
     right = back_along(block[:, :HALF], "sx")
-    top = next_along(block[rows - HALF :], "sy")
-    bottom = back_along(block[:HALF], "sy")
-    corners_top = next_along(jnp.stack([left[rows - HALF :], right[rows - HALF :]]), "sy")
-    corners_bottom = back_along(jnp.stack([left[:HALF], right[:HALF]]), "sy")
-
-    flat_weight = depth_weight.reshape(KERNEL * KERNEL, channels)
+    low, high, left, right = lax.optimization_barrier(
+        (
+            edge_strip(block, left, right, slice(rows - HALF, rows)),
+            edge_strip(block, left, right, slice(0, HALF)),
+            left,
+            right,
+        )
+    )
+    top = next_along(low, "sy")
+    bottom = back_along(high, "sy")
+
     flat_bias = depth_bias[None]
     reduce_row = reduce_bias[None]
     spread, conv_in, before_in, feat_in, gram, colsum = conv_inner(
-        block, left, right, flat_weight, flat_bias, reduce_weight, reduce_row
+        block, left, right, depth_weight, flat_bias, reduce_weight, reduce_row
     )
     spread_top, spread_bottom, conv_ed, before_ed, feat_ed, sums = conv_edge(
         spread,
-        (top, bottom, corners_top, corners_bottom),
-        flat_weight,
+        (top, bottom),
+        depth_weight,
         flat_bias,
         reduce_weight,
         reduce_row,
@@ -676,6 +703,9 @@
     )
 
     sums = halve(sums, "sx", 1, wide)
+    sums, before_in, before_ed, conv_in, conv_ed = lax.optimization_barrier(
+        (sums, before_in, before_ed, conv_in, conv_ed)
+    )
     gate_in, gate_ed, conv_turned, reduce_turned = prepare(
         before_in, before_ed, conv_in, conv_ed, reduce_weight
     )
@@ -709,16 +739,31 @@
 
     tiles = channels // LANES
     many = tiles // 3 if tiles % 3 == 0 else tiles
-    parts = [
-        tap_grads(spread, spread_top, spread_bottom, conv_grad_in, conv_grad_ed, first, many)
-        for first in range(0, tiles, many)
-    ]
+    turns = list(range(0, tiles, many))
+    parts = []
+
+    def beside(sums):
+        nonlocal conv_grad_in, conv_grad_ed
+        if not turns:
+            return sums
+        sums, conv_grad_in, conv_grad_ed, *parts[:] = lax.optimization_barrier(
+            (sums, conv_grad_in, conv_grad_ed, *parts)
+        )
+        parts.append(
+            tap_grads(
+                spread, spread_top, spread_bottom, conv_grad_in, conv_grad_ed, turns.pop(0), many
+            )
+        )
+        return sums
+
     weight_grad = halve(weight_grad, "sx", 1, wide)
     for shift in doublings("sx", 2):
-        weight_grad = halve(weight_grad, "sx", shift, narrow)
+        weight_grad = halve(beside(weight_grad), "sx", shift, narrow)
     for shift in doublings("dp"):
-        weight_grad = exchange(weight_grad, "dp", shift, narrow)
-    weight_grad = exchange_all(weight_grad, "sy", narrow)
+        weight_grad = exchange(beside(weight_grad), "dp", shift, narrow)
+    weight_grad = exchange_all(beside(weight_grad), "sy", narrow)
+    while turns:
+        weight_grad = beside(weight_grad)
     for shift in reversed(doublings("sx")):
         weight_grad = unhalve(weight_grad, "sx", shift)
 

time: 147 us -> 150 us (1.020)
  Pallas kernels: 47 us -> 61.3 us
  local copies, waits for them, and re-layouts: 17.8 us -> 9.11 us
  starting transfers between devices: 42.5 us -> 33.9 us
  other arithmetic: 3.62 us -> 10.2 us
    unnamed x40 -> x28, local copies, waits for them, and re-layouts: 9.62 us -> 1.52 us
    pallas_call x3, Pallas kernels: 14.8 us -> 20.3 us  [tap_grads(): pl.pallas_call(taps_kernel, grid=(many,), in_specs=[from_lead(spread.shap...]
    ppermute x3 -> x2, starting transfers between devices: 11.2 us -> 5.86 us  [next_along(): lax.ppermute(value, axis, [(i, i + 1) for i in range(lax.axis_size(axis)...]
    ppermute x21, waiting for transfers between devices: 31.4 us -> 28 us  [swap(): return lax.ppermute(value, axis, [(i, i ^ shift) for i in range(count)])]
    pallas_call x1, Pallas kernels: 0.95 us -> 4.12 us  [prepare(): pl.pallas_call(prepare_kernel, in_specs=[in_vmem] * 5, out_specs=[in_vmem...]
    ppermute x3 -> x2, waiting for transfers between devices: 0.01 us -> 2.79 us  [back_along(): lax.ppermute(value, axis, [(i + 1, i) for i in range(lax.axis_size(axis)...]
    pallas_call x1, Pallas kernels: 6.67 us -> 9.39 us  [conv_edge(): pl.pallas_call(edge_kernel, grid=(tiles,), in_specs=[lead_spec(spread.sha...]
    pallas_call x1, Pallas kernels: 13.7 us -> 16 us  [conv_inner(): pl.pallas_call(inner_kernel, grid=(tiles,), in_specs=[tile_spec((rows, co...]
  transfers between devices with their start and end apart: 27 -> 25, of which waited for: 12 -> 10; matrix products, arithmetic and copies ran while one was open for 6% -> 8% of each run, Pallas kernels for 10% -> 23%
where the time goes in v2:
time: 150 us; the launch traced here: 149 us
  Pallas kernels  61.3 us (41%)
  starting transfers between devices  33.9 us (23%)
  waiting for transfers between devices  30.8 us (21%)
  other arithmetic  10.2 us (7%)
  local copies, waits for them, and re-layouts  9.11 us (6%)
  between operations  3.46 us (2%)
    ppermute x21, waiting for transfers between devices, swap(): return lax.ppermute(value, axis, [(i, i ^ shift) for i in range(count)])  28 us
    ppermute x21, starting transfers between devices, swap(): return lax.ppermute(value, axis, [(i, i ^ shift) for i in range(count)])  25.5 us
    pallas_call x3, Pallas kernels, tap_grads(): pl.pallas_call(taps_kernel, grid=(many,), in_specs=[from_lead(spread.shap...  20.3 us
    pallas_call x1, Pallas kernels, conv_inner(): pl.pallas_call(inner_kernel, grid=(tiles,), in_specs=[tile_spec((rows, co...  16 us
    pallas_call x1, Pallas kernels, head(): pl.pallas_call(functools.partial(head_kernel, count=count, image_count=im...  11.5 us
    pallas_call x1, Pallas kernels, conv_edge(): pl.pallas_call(edge_kernel, grid=(tiles,), in_specs=[lead_spec(spread.sha...  9.39 us
    ppermute x2, starting transfers between devices, next_along(): lax.ppermute(value, axis, [(i, i + 1) for i in range(lax.axis_size(axis)...  5.86 us
    pallas_call x1, Pallas kernels, prepare(): pl.pallas_call(prepare_kernel, in_specs=[in_vmem] * 5, out_specs=[in_vmem...  4.12 us
  transfers between devices with their start and end apart: 25, of which 10 were waited for; matrix products, arithmetic and copies ran while one was open for 8% of the time, Pallas kernels for 23%

profile of v2, /device:TPU:0, one launch (start us, length us, event | category | flops | bytes accessed | tf_op | source)
XLA Modules:
  0.0 148.8 jit_solution(8725612864261661116)
XLA Ops:
  0.6 1.1 fusion.1
  1.8 2.4 %collective-permute-start = (bf16[16,3,768]{2,1,0:T(4,128)(2,1)S(1)}, bf16[16,3,768]{2,1,0:T(4,128)(2,1)S(1)}, u32[]{:S(2)}, u32[]{:S(2)}) collective-permute-start(bf16[16,3,768]{2,1,0:T(4,128)(2,1)S(1)} %get-tuple-element.95), channel_id=1, source_target_pairs={{0,1},{1,2},{2,3},{4,5},{5,6},{6,7},{8,9},{9,10},{10,11},{12,13},{... | collective-permute-start | bytes 221192 | tf_op jit(solution)/shard_map/ppermute | solution.py:81
  4.1 1.3 collective-permute-start.1
  5.4 1.1 fusion
  6.5 0.1 pad.28.clone
  6.7 2.8 %collective-permute-done.1.right = bf16[16,3,768]{2,1,0:T(4,128)(2,1)S(1)} collective-permute-done((bf16[16,3,768]{2,1,0:T(4,128)(2,1)S(1)}, bf16[16,3,768]{2,1,0:T(4,128)(2,1)S(1)}, u32[]{:S(2)}, u32[]{:S(2)}) %collective-permute-start.1) | collective-permute-done | bytes 73760 | tf_op jit(solution)/shard_map/ppermute | solution.py:85
  9.5 0.2 maximum_maximum_fusion.1
  9.7 3.5 %collective-permute-start.2 = (bf16[224,768]{1,0:T(8,128)(2,1)S(1)}, bf16[224,768]{1,0:T(8,128)(2,1)S(1)}, u32[]{:S(2)}, u32[]{:S(2)}) collective-permute-start(bf16[224,768]{1,0:T(8,128)(2,1)S(1)} %get-tuple-element.53), channel_id=1, source_target_pairs={{0,4},{4,8},{8,12},{1,5},{5,9},{9,13},{2,6},{6,10},{10,14},{3,7},{... | collective-permute-start | bytes 1032200 | tf_op jit(solution)/shard_map/ppermute | solution.py:81
  13.3 1.3 collective-permute-start.3
  14.6 0.6 broadcast_in_dim.30.bias
  15.2 16.0 %conv_inner.1 = (f32[6,16,14,8,128]{4,3,2,1,0:T(8,128)}, bf16[640,768]{1,0:T(8,128)(2,1)}, f32[640,256]{1,0:T(8,128)}, bf16[640,256]{1,0:T(8,128)(2,1)}, f32[256,256]{1,0:T(8,128)}, /*index=5*/f32[1,256]{1,0:T(1,128)}) custom-call(bf16[16,64,768]{2,1,0:T(8,128)(2,1)} %bitcast.10, bf16[16,3,768]{2,1,0:T(4,128)(2,1)} %copy-done.7, ...), custom_call_target="tpu_custom_call" | custom-call | flops 48168960 | bytes 6291456 | tf_op jit(solution)/shard_map/conv_inner/pallas_call | solution.py:263
  31.2 0.7 copy-done.3
  31.9 0.1 copy-done.4
  32.0 9.4 %conv_edge.1 = (f32[6,3,14,8,128]{4,3,2,1,0:T(8,128)}, f32[6,3,14,8,128]{4,3,2,1,0:T(8,128)}, bf16[384,768]{1,0:T(8,128)(2,1)}, f32[384,256]{1,0:T(8,128)}, bf16...) custom-call(f32[6,16,14,8,128]{4,3,2,1,0:T(8,128)} %get-tuple-element.52.spread_in, bf16[224,768]{1,0:T(8,128)(2,1)} %copy-done.3, ...), custom_call_target="tpu_custom_call" | custom-call | flops 28901376 | bytes 6291456 | tf_op jit(solution)/shard_map/conv_edge/pallas_call | solution.py:314
  41.4 1.0 slice_select_fusion.1
  42.4 3.0 %collective-permute-start.4 = (f32[104,256]{1,0:T(8,128)S(1)}, f32[104,256]{1,0:T(8,128)S(1)}, u32[]{:S(2)}, u32[]{:S(2)}) collective-permute-start(f32[104,256]{1,0:T(8,128)S(1)} %slice_select_fusion.1), channel_id=1, source_target_pairs={{0,1},{1,0},{2,3},{3,2},{4,5},{5,4},{6,7},{7,6},{8,9},{9,8},{10,11... | collective-permute-start | bytes 319496 | tf_op jit(solution)/shard_map/ppermute | solution.py:32
  45.4 1.0 collective-permute-done.4
  46.4 1.0 select_add_fusion.1
  47.4 0.5 collective-permute-start.5
  47.9 4.8 %collective-permute-done.5 = f32[104,256]{1,0:T(8,128)S(1)} collective-permute-done((f32[104,256]{1,0:T(8,128)S(1)}, f32[104,256]{1,0:T(8,128)S(1)}, u32[]{:S(2)}, u32[]{:S(2)}) %collective-permute-start.5) | collective-permute-done | bytes 106528 | tf_op jit(solution)/shard_map/ppermute | solution.py:32
  52.7 2.4 %collective-permute-start.6 = (f32[104,256]{1,0:T(8,128)S(1)}, f32[104,256]{1,0:T(8,128)S(1)}, u32[]{:S(2)}, u32[]{:S(2)}) collective-permute-start(f32[104,256]{1,0:T(8,128)S(1)} %add.60), channel_id=1, source_target_pairs={{0,4},{4,0},{8,12},{12,8},{1,5},{5,1},{9,13},{13,9},{2,6},{6,2},{1... | collective-permute-start | bytes 319496 | tf_op jit(solution)/shard_map/ppermute | solution.py:32
  55.7 2.0 %collective-permute-done.6 = f32[104,256]{1,0:T(8,128)S(1)} collective-permute-done((f32[104,256]{1,0:T(8,128)S(1)}, f32[104,256]{1,0:T(8,128)S(1)}, u32[]{:S(2)}, u32[]{:S(2)}) %collective-permute-start.6) | collective-permute-done | bytes 106528 | tf_op jit(solution)/shard_map/ppermute | solution.py:32
  57.8 3.1 %collective-permute-start.7 = (f32[104,256]{1,0:T(8,128)S(1)}, f32[104,256]{1,0:T(8,128)S(1)}, u32[]{:S(2)}, u32[]{:S(2)}) collective-permute-start(f32[104,256]{1,0:T(8,128)S(1)} %add.61), channel_id=1, source_target_pairs={{0,8},{4,12},{8,0},{12,4},{1,9},{5,13},{9,1},{13,5},{2,10},{6,14},... | collective-permute-start | bytes 319496 | tf_op jit(solution)/shard_map/ppermute | solution.py:32
  60.9 2.7 %collective-permute-done.7 = f32[104,256]{1,0:T(8,128)S(1)} collective-permute-done((f32[104,256]{1,0:T(8,128)S(1)}, f32[104,256]{1,0:T(8,128)S(1)}, u32[]{:S(2)}, u32[]{:S(2)}) %collective-permute-start.7) | collective-permute-done | bytes 106528 | tf_op jit(solution)/shard_map/ppermute | solution.py:32
  63.7 0.6 pad_add_fusion.flags
  64.3 0.7 copy.16.class_bias
  64.9 4.1 %prepare.1 = (f32[640,256]{1,0:T(8,128)}, f32[384,256]{1,0:T(8,128)}, bf16[768,1024]{1,0:T(8,128)(2,1)}, bf16[256,768]{1,0:T(8,128)(2,1)}) custom-call(f32[640,256]{1,0:T(8,128)} %get-tuple-element.65.before_inner, f32[384,256]{1,0:T(8,128)} %get-tuple-element.66.before_edge, bf16[640,768]{1,0:T(8,128)(2,1)} %get-tuple-element.67.conv_inner_in, ...), custom_call_target="tpu_custom_call" | custom-call | flops 1000000000 | bytes 6291456 | tf_op jit(solution)/shard_map/prepare/pallas_call | solution.py:557
  69.1 0.6 copy-done.12
  69.7 11.5 %head.1 = (f32[256,256]{1,0:T(8,128)}, f32[16,256]{1,0:T(8,128)}, f32[768,256]{1,0:T(8,128)}, f32[1,256]{1,0:T(1,128)}, bf16[640,768]{1,0:T(8,128)(2,1)}, /*index=5*/bf16[384,768]{1,0:T(8,128)(2,1)}) custom-call(s32[2]{0:T(128)} %pad_add_fusion.flags, f32[104,256]{1,0:T(8,128)} %copy-done.9, f32[104,256]{1,0:T(8,128)} %copy-done.12, ...), custom_call_target="tpu_custom_call" | custom-call | flops 6710886400 | bytes 8388608 | tf_op jit(solution)/shard_map/head/pallas_call | solution.py:509
  81.2 1.2 slice_select_fusion
  82.4 0.6 collective-permute-start.10
  82.9 1.0 pad_maximum_fusion.2
  83.9 1.6 %collective-permute-start.9 = (f32[272,256]{1,0:T(8,128)S(1)}, f32[272,256]{1,0:T(8,128)S(1)}, u32[]{:S(2)}, u32[]{:S(2)}) collective-permute-start(f32[272,256]{1,0:T(8,128)S(1)} %pad_maximum_fusion.2), channel_id=1, source_target_pairs={{0,16},{16,0},{1,17},{17,1},{2,18},{18,2},{3,19},{19,3},{4,20},{20... | collective-permute-start | bytes 835592 | tf_op jit(solution)/shard_map/ppermute | solution.py:32
  85.5 0.7 pad_reduce_fusion
  86.2 1.2 select_add_fusion
  87.4 0.6 collective-permute-start.11
  88.0 0.1 slice_reduce_fusion.2
  88.1 4.5 %collective-permute-done.9 = f32[272,256]{1,0:T(8,128)S(1)} collective-permute-done((f32[272,256]{1,0:T(8,128)S(1)}, f32[272,256]{1,0:T(8,128)S(1)}, u32[]{:S(2)}, u32[]{:S(2)}) %collective-permute-start.9) | collective-permute-done | bytes 278560 | tf_op jit(solution)/shard_map/ppermute | solution.py:32
  92.6 6.8 %tap_grads.3 = f32[64,256]{1,0:T(8,128)} custom-call(f32[6,16,14,8,128]{4,3,2,1,0:T(8,128)} %get-tuple-element.52.spread_in, f32[6,3,14,8,128]{4,3,2,1,0:T(8,128)} %get-tuple-element.82.spread_top, f32[6,3,14,8,128]{4,3,2,1,0:T(8,128)} %get-tuple-element.83.spread_bottom, bf16[640,768]{1,0:T(8,128)(2,1)} %get-tuple-element.90.grad_inner, ...), custom_call_target="tpu_custom_call" | custom-call | flops 25690112 | bytes 2796202 | tf_op jit(solution)/shard_map/tap_grads/pallas_call | solution.py:636
  99.4 1.6 %collective-permute-start.12 = (bf16[192,256]{1,0:T(8,128)(2,1)S(1)}, bf16[192,256]{1,0:T(8,128)(2,1)S(1)}, u32[]{:S(2)}, u32[]{:S(2)}) collective-permute-start(bf16[192,256]{1,0:T(8,128)(2,1)S(1)} %convert_add_fusion.1), channel_id=1, source_target_pairs={{0,16},{16,0},{1,17},{17,1},{2,18},{18,2},{3,19},{19,3},{4,20},{20... | collective-permute-start | bytes 294920 | tf_op jit(solution)/shard_map/ppermute | solution.py:32
  101.0 0.1 slice_reduce_fusion.1
  101.1 6.7 %tap_grads.4 = f32[64,256]{1,0:T(8,128)} custom-call(f32[6,16,14,8,128]{4,3,2,1,0:T(8,128)} %get-tuple-element.52.spread_in, f32[6,3,14,8,128]{4,3,2,1,0:T(8,128)} %get-tuple-element.82.spread_top, f32[6,3,14,8,128]{4,3,2,1,0:T(8,128)} %get-tuple-element.83.spread_bottom, bf16[640,768]{1,0:T(8,128)(2,1)} %get-tuple-element.90.grad_inner, ...), custom_call_target="tpu_custom_call" | custom-call | flops 25690112 | bytes 2796202 | tf_op jit(solution)/shard_map/tap_grads/pallas_call | solution.py:636
  107.9 6.8 %tap_grads.5 = f32[64,256]{1,0:T(8,128)} custom-call(f32[6,16,14,8,128]{4,3,2,1,0:T(8,128)} %get-tuple-element.52.spread_in, f32[6,3,14,8,128]{4,3,2,1,0:T(8,128)} %get-tuple-element.82.spread_top, f32[6,3,14,8,128]{4,3,2,1,0:T(8,128)} %get-tuple-element.83.spread_bottom, bf16[640,768]{1,0:T(8,128)(2,1)} %get-tuple-element.90.grad_inner, ...), custom_call_target="tpu_custom_call" | custom-call | flops 25690112 | bytes 2796202 | tf_op jit(solution)/shard_map/tap_grads/pallas_call | solution.py:636
  114.7 1.0 maximum_select_fusion
  115.7 0.1 collective-permute-start.13
  115.8 1.9 %multiply_add_fusion = f32[10,256,256]{2,1,0:T(8,128)} fusion(f32[256,256]{1,0:T(8,128)S(1)} %slice-done, f32[10]{0:T(128)S(1)} %slice_reduce_fusion.1, f32[256,256]{1,0:T(8,128)S(1)} %copy-done, f32[10]{0:T(128)S(1)} %slice_reduce_fusion.2), kind=kLoop, calls=%fused_computation | loop fusion | flops 1966080 | bytes 3145808 | tf_op jit(solution)/shard_map/add | solution.py:56
  117.7 0.6 collective-permute-start.14
  118.3 3.6 %collective-permute-done.14 = bf16[32,768]{1,0:T(8,128)(2,1)S(1)} collective-permute-done((bf16[32,768]{1,0:T(8,128)(2,1)S(1)}, bf16[32,768]{1,0:T(8,128)(2,1)S(1)}, u32[]{:S(2)}, u32[]{:S(2)}) %collective-permute-start.14) | collective-permute-done | bytes 49184 | tf_op jit(solution)/shard_map/ppermute | solution.py:32
  121.9 0.6 collective-permute-start.15
  122.5 0.6 slice_reduce_fusion
  123.1 0.5 slice.118
  124.3 2.2 %collective-permute-start.20 = (bf16[192,256]{1,0:T(8,128)(2,1)S(1)}, bf16[192,256]{1,0:T(8,128)(2,1)S(1)}, u32[]{:S(2)}, u32[]{:S(2)}) collective-permute-start(bf16[192,256]{1,0:T(8,128)(2,1)S(1)} %convert_add_fusion), channel_id=1, source_target_pairs={{0,4},{4,0},{8,12},{12,8},{1,5},{5,1},{9,13},{13,9},{2,6},{6,2},{1... | collective-permute-start | bytes 294920 | tf_op jit(solution)/shard_map/ppermute | solution.py:32
  126.5 3.4 %collective-permute-start.21 = (bf16[192,256]{1,0:T(8,128)(2,1)S(1)}, bf16[192,256]{1,0:T(8,128)(2,1)S(1)}, u32[]{:S(2)}, u32[]{:S(2)}) collective-permute-start(bf16[192,256]{1,0:T(8,128)(2,1)S(1)} %convert_add_fusion), channel_id=1, source_target_pairs={{0,8},{4,12},{8,0},{12,4},{1,9},{5,13},{9,1},{13,5},{2,10},{6,14},... | collective-permute-start | bytes 294920 | tf_op jit(solution)/shard_map/ppermute | solution.py:32
  129.9 0.6 collective-permute-start.16
  130.5 3.8 %collective-permute-start.17 = (bf16[32,768]{1,0:T(8,128)(2,1)S(1)}, bf16[32,768]{1,0:T(8,128)(2,1)S(1)}, u32[]{:S(2)}, u32[]{:S(2)}) collective-permute-start(bf16[32,768]{1,0:T(8,128)(2,1)S(1)} %add_convert_fusion), channel_id=1, source_target_pairs={{0,8},{4,12},{8,0},{12,4},{1,9},{5,13},{9,1},{13,5},{2,10},{6,14},... | collective-permute-start | bytes 147464 | tf_op jit(solution)/shard_map/ppermute | solution.py:32
  134.3 0.1 collective-permute-start.18
  134.5 4.4 %collective-permute-done.21 = bf16[192,256]{1,0:T(8,128)(2,1)S(1)} collective-permute-done((bf16[192,256]{1,0:T(8,128)(2,1)S(1)}, bf16[192,256]{1,0:T(8,128)(2,1)S(1)}, u32[]{:S(2)}, u32[]{:S(2)}) %collective-permute-start.21) | collective-permute-done | bytes 98336 | tf_op jit(solution)/shard_map/ppermute | solution.py:32
  138.9 0.6 collective-permute-start.23
  139.5 2.5 %collective-permute-done.17 = bf16[32,768]{1,0:T(8,128)(2,1)S(1)} collective-permute-done((bf16[32,768]{1,0:T(8,128)(2,1)S(1)}, bf16[32,768]{1,0:T(8,128)(2,1)S(1)}, u32[]{:S(2)}, u32[]{:S(2)}) %collective-permute-start.17) | collective-permute-done | bytes 49184 | tf_op jit(solution)/shard_map/ppermute | solution.py:32
  142.1 2.6 %collective-permute-done.23 = f32[192,256]{1,0:T(8,128)S(1)} collective-permute-done((f32[192,256]{1,0:T(8,128)S(1)}, f32[192,256]{1,0:T(8,128)S(1)}, u32[]{:S(2)}, u32[]{:S(2)}) %collective-permute-start.23) | collective-permute-done | bytes 196640 | tf_op jit(solution)/shard_map/ppermute | solution.py:32
  144.8 0.6 slice.122
  145.4 0.7 reshape.62
  146.1 0.6 slice_reduce_fusion.3
  146.8 0.9 pad_maximum_fusion
  (73 shorter events, 0.9 us)
Async XLA Ops:
  0.6 13.9 %copy-start.11 = (f32[768]{0:T(1024)S(1)}, f32[768]{0:T(1024)}, u32[]{:S(2)}) copy-start(f32[768]{0:T(1024)} %param.10) | copy-start | bytes 9220
  1.8 4.9 %collective-permute-start = (bf16[16,3,768]{2,1,0:T(4,128)(2,1)S(1)}, bf16[16,3,768]{2,1,0:T(4,128)(2,1)S(1)}, u32[]{:S(2)}, u32[]{:S(2)}) collective-permute-start(bf16[16,3,768]{2,1,0:T(4,128)(2,1)S(1)} %get-tuple-element.95), channel_id=1, source_target_pairs={{0,1},{1,2},{2,3},{4,5},{5,6},{6,7},{8,9},{9,10},{10,11},{12,13},{... | collective-permute-start | bytes 221192 | tf_op jit(solution)/shard_map/ppermute | solution.py:81
  4.1 5.3 %collective-permute-start.1 = (bf16[16,3,768]{2,1,0:T(4,128)(2,1)S(1)}, bf16[16,3,768]{2,1,0:T(4,128)(2,1)S(1)}, u32[]{:S(2)}, u32[]{:S(2)}) collective-permute-start(bf16[16,3,768]{2,1,0:T(4,128)(2,1)S(1)} %get-tuple-element.96), channel_id=1, source_target_pairs={{1,0},{2,1},{3,2},{5,4},{6,5},{7,6},{9,8},{10,9},{11,10},{13,12},{... | collective-permute-start | bytes 221192 | tf_op jit(solution)/shard_map/ppermute | solution.py:85
  6.6 8.5 %copy-start.7 = (bf16[16,3,768]{2,1,0:T(4,128)(2,1)}, bf16[16,3,768]{2,1,0:T(4,128)(2,1)S(1)}, u32[]{:S(2)}) copy-start(bf16[16,3,768]{2,1,0:T(4,128)(2,1)S(1)} %collective-permute-done.left) | copy-start | bytes 221188
  9.4 5.7 %copy-start.8 = (bf16[16,3,768]{2,1,0:T(4,128)(2,1)}, bf16[16,3,768]{2,1,0:T(4,128)(2,1)S(1)}, u32[]{:S(2)}) copy-start(bf16[16,3,768]{2,1,0:T(4,128)(2,1)S(1)} %collective-permute-done.1.right) | copy-start | bytes 221188
  9.7 21.4 %collective-permute-start.2 = (bf16[224,768]{1,0:T(8,128)(2,1)S(1)}, bf16[224,768]{1,0:T(8,128)(2,1)S(1)}, u32[]{:S(2)}, u32[]{:S(2)}) collective-permute-start(bf16[224,768]{1,0:T(8,128)(2,1)S(1)} %get-tuple-element.53), channel_id=1, source_target_pairs={{0,4},{4,8},{8,12},{1,5},{5,9},{9,13},{2,6},{6,10},{10,14},{3,7},{... | collective-permute-start | bytes 1032200 | tf_op jit(solution)/shard_map/ppermute | solution.py:81
  13.3 17.9 %collective-permute-start.3 = (bf16[224,768]{1,0:T(8,128)(2,1)S(1)}, bf16[224,768]{1,0:T(8,128)(2,1)S(1)}, u32[]{:S(2)}, u32[]{:S(2)}) collective-permute-start(bf16[224,768]{1,0:T(8,128)(2,1)S(1)} %get-tuple-element.54), channel_id=1, source_target_pairs={{4,0},{8,4},{12,8},{5,1},{9,5},{13,9},{6,2},{10,6},{14,10},{7,3},{... | collective-permute-start | bytes 1032200 | tf_op jit(solution)/shard_map/ppermute | solution.py:85
  31.2 0.7 copy-start.3
  31.2 0.8 copy-start.4
  32.0 28.8 %copy-start.13 = (f32[10]{0:T(128)S(1)}, f32[10]{0:T(128)}, u32[]{:S(2)}) copy-start(f32[10]{0:T(128)} %param.14) | copy-start | bytes 124
  42.4 4.0 %collective-permute-start.4 = (f32[104,256]{1,0:T(8,128)S(1)}, f32[104,256]{1,0:T(8,128)S(1)}, u32[]{:S(2)}, u32[]{:S(2)}) collective-permute-start(f32[104,256]{1,0:T(8,128)S(1)} %slice_select_fusion.1), channel_id=1, source_target_pairs={{0,1},{1,0},{2,3},{3,2},{4,5},{5,4},{6,7},{7,6},{8,9},{9,8},{10,11... | collective-permute-start | bytes 319496 | tf_op jit(solution)/shard_map/ppermute | solution.py:32
  47.4 5.3 %collective-permute-start.5 = (f32[104,256]{1,0:T(8,128)S(1)}, f32[104,256]{1,0:T(8,128)S(1)}, u32[]{:S(2)}, u32[]{:S(2)}) collective-permute-start(f32[104,256]{1,0:T(8,128)S(1)} %select_add_fusion.1), channel_id=1, source_target_pairs={{0,2},{1,3},{2,0},{3,1},{4,6},{5,7},{6,4},{7,5},{8,10},{9,11},{10,... | collective-permute-start | bytes 319496 | tf_op jit(solution)/shard_map/ppermute | solution.py:32
  52.7 5.1 %collective-permute-start.6 = (f32[104,256]{1,0:T(8,128)S(1)}, f32[104,256]{1,0:T(8,128)S(1)}, u32[]{:S(2)}, u32[]{:S(2)}) collective-permute-start(f32[104,256]{1,0:T(8,128)S(1)} %add.60), channel_id=1, source_target_pairs={{0,4},{4,0},{8,12},{12,8},{1,5},{5,1},{9,13},{13,9},{2,6},{6,2},{1... | collective-permute-start | bytes 319496 | tf_op jit(solution)/shard_map/ppermute | solution.py:32
  57.8 5.8 %collective-permute-start.7 = (f32[104,256]{1,0:T(8,128)S(1)}, f32[104,256]{1,0:T(8,128)S(1)}, u32[]{:S(2)}, u32[]{:S(2)}) collective-permute-start(f32[104,256]{1,0:T(8,128)S(1)} %add.61), channel_id=1, source_target_pairs={{0,8},{4,12},{8,0},{12,4},{1,9},{5,13},{9,1},{13,5},{2,10},{6,14},... | collective-permute-start | bytes 319496 | tf_op jit(solution)/shard_map/ppermute | solution.py:32
  63.6 5.5 %copy-start.9 = (f32[104,256]{1,0:T(8,128)}, f32[104,256]{1,0:T(8,128)S(1)}, u32[]{:S(2)}) copy-start(f32[104,256]{1,0:T(8,128)S(1)} %add.62.own) | copy-start | bytes 319492
  63.6 5.5 %collective-permute-start.8 = (f32[104,256]{1,0:T(8,128)S(1)}, f32[104,256]{1,0:T(8,128)S(1)}, u32[]{:S(2)}, u32[]{:S(2)}) collective-permute-start(f32[104,256]{1,0:T(8,128)S(1)} %add.62.own), channel_id=1, source_target_pairs={{0,1},{1,0},{2,3},{3,2},{4,5},{5,4},{6,7},{7,6},{8,9},{9,8},{10,11... | collective-permute-start | bytes 319496 | tf_op jit(solution)/shard_map/ppermute | solution.py:32
  69.1 0.6 copy-start.12
  81.2 6.8 %copy-start.10 = (f32[16,256]{1,0:T(8,128)S(1)}, f32[16,256]{1,0:T(8,128)}, u32[]{:S(2)}) copy-start(f32[16,256]{1,0:T(8,128)} %get-tuple-element.73) | copy-start | bytes 49156
  82.4 3.8 %collective-permute-start.10 = (f32[384,256]{1,0:T(8,128)S(1)}, f32[384,256]{1,0:T(8,128)S(1)}, u32[]{:S(2)}, u32[]{:S(2)}) collective-permute-start(f32[384,256]{1,0:T(8,128)S(1)} %slice_select_fusion), channel_id=1, source_target_pairs={{0,1},{1,0},{2,3},{3,2},{4,5},{5,4},{6,7},{7,6},{8,9},{9,8},{10,11... | collective-permute-start | bytes 1179656 | tf_op jit(solution)/shard_map/ppermute | solution.py:32
  83.9 8.7 %collective-permute-start.9 = (f32[272,256]{1,0:T(8,128)S(1)}, f32[272,256]{1,0:T(8,128)S(1)}, u32[]{:S(2)}, u32[]{:S(2)}) collective-permute-start(f32[272,256]{1,0:T(8,128)S(1)} %pad_maximum_fusion.2), channel_id=1, source_target_pairs={{0,16},{16,0},{1,17},{17,1},{2,18},{18,2},{3,19},{19,3},{4,20},{20... | collective-permute-start | bytes 835592 | tf_op jit(solution)/shard_map/ppermute | solution.py:32
  87.4 12.0 %collective-permute-start.11 = (bf16[192,256]{1,0:T(8,128)(2,1)S(1)}, bf16[192,256]{1,0:T(8,128)(2,1)S(1)}, u32[]{:S(2)}, u32[]{:S(2)}) collective-permute-start(bf16[192,256]{1,0:T(8,128)(2,1)S(1)} %select_convert_fusion), channel_id=1, source_target_pairs={{0,2},{1,3},{2,0},{3,1},{4,6},{5,7},{6,4},{7,5},{8,10},{9,11},{10,... | collective-permute-start | bytes 294920 | tf_op jit(solution)/shard_map/ppermute | solution.py:32
  92.6 8.4 %copy-start.1 = (f32[272,256]{1,0:T(8,128)}, f32[272,256]{1,0:T(8,128)S(1)}, u32[]{:S(2)}) copy-start(f32[272,256]{1,0:T(8,128)S(1)} %collective-permute-done.9) | copy-start | bytes 835588
  99.4 8.4 %collective-permute-start.12 = (bf16[192,256]{1,0:T(8,128)(2,1)S(1)}, bf16[192,256]{1,0:T(8,128)(2,1)S(1)}, u32[]{:S(2)}, u32[]{:S(2)}) collective-permute-start(bf16[192,256]{1,0:T(8,128)(2,1)S(1)} %convert_add_fusion.1), channel_id=1, source_target_pairs={{0,16},{16,0},{1,17},{17,1},{2,18},{18,2},{3,19},{19,3},{4,20},{20... | collective-permute-start | bytes 294920 | tf_op jit(solution)/shard_map/ppermute | solution.py:32
  107.8 6.8 %copy-start.5 = (f32[64,256]{1,0:T(8,128)S(1)}, f32[64,256]{1,0:T(8,128)}, u32[]{:S(2)}) copy-start(f32[64,256]{1,0:T(8,128)} %tap_grads.3) | copy-start | bytes 196612
  107.9 6.8 %copy-start.6 = (f32[64,256]{1,0:T(8,128)S(1)}, f32[64,256]{1,0:T(8,128)}, u32[]{:S(2)}) copy-start(f32[64,256]{1,0:T(8,128)} %tap_grads.4) | copy-start | bytes 196612
  107.9 7.9 %copy-start = (f32[256,256]{1,0:T(8,128)S(1)}, f32[256,256]{1,0:T(8,128)}, u32[]{:S(2)}) copy-start(f32[256,256]{1,0:T(8,128)} %get-tuple-element.74) | copy-start | bytes 786436
  107.9 7.9 %slice-start = ((f32[272,256]{1,0:T(8,128)}), f32[256,256]{1,0:T(8,128)S(1)}, s32[]{:S(2)}) async-start(f32[272,256]{1,0:T(8,128)} %copy-done.1), calls=%async_computation | async-start | bytes 524288 | tf_op jit(solution)/shard_map/slice | solution.py:734
  114.7 3.6 %copy-start.2 = (f32[272,256]{1,0:T(8,128)S(1)}, f32[272,256]{1,0:T(8,128)}, u32[]{:S(2)}) copy-start(f32[272,256]{1,0:T(8,128)} %copy-done.1) | copy-start | bytes 835588
  115.7 2.0 %collective-permute-start.13 = (f32[32,768]{1,0:T(8,128)S(1)}, f32[32,768]{1,0:T(8,128)S(1)}, u32[]{:S(2)}, u32[]{:S(2)}) collective-permute-start(f32[32,768]{1,0:T(8,128)S(1)} %slice_select_fusion.2), channel_id=1, source_target_pairs={{0,1},{1,0},{2,3},{3,2},{4,5},{5,4},{6,7},{7,6},{8,9},{9,8},{10,11... | collective-permute-start | bytes 294920 | tf_op jit(solution)/shard_map/ppermute | solution.py:32
  117.7 4.2 %collective-permute-start.14 = (bf16[32,768]{1,0:T(8,128)(2,1)S(1)}, bf16[32,768]{1,0:T(8,128)(2,1)S(1)}, u32[]{:S(2)}, u32[]{:S(2)}) collective-permute-start(bf16[32,768]{1,0:T(8,128)(2,1)S(1)} %add_convert_fusion.2), channel_id=1, source_target_pairs={{0,2},{1,3},{2,0},{3,1},{4,6},{5,7},{6,4},{7,5},{8,10},{9,11},{10,... | collective-permute-start | bytes 147464 | tf_op jit(solution)/shard_map/ppermute | solution.py:32
  121.9 8.0 %collective-permute-start.15 = (bf16[32,768]{1,0:T(8,128)(2,1)S(1)}, bf16[32,768]{1,0:T(8,128)(2,1)S(1)}, u32[]{:S(2)}, u32[]{:S(2)}) collective-permute-start(bf16[32,768]{1,0:T(8,128)(2,1)S(1)} %add_convert_fusion.1), channel_id=1, source_target_pairs={{0,16},{16,0},{1,17},{17,1},{2,18},{18,2},{3,19},{19,3},{4,20},{20... | collective-permute-start | bytes 147464 | tf_op jit(solution)/shard_map/ppermute | solution.py:32
  124.3 10.1 %collective-permute-start.20 = (bf16[192,256]{1,0:T(8,128)(2,1)S(1)}, bf16[192,256]{1,0:T(8,128)(2,1)S(1)}, u32[]{:S(2)}, u32[]{:S(2)}) collective-permute-start(bf16[192,256]{1,0:T(8,128)(2,1)S(1)} %convert_add_fusion), channel_id=1, source_target_pairs={{0,4},{4,0},{8,12},{12,8},{1,5},{5,1},{9,13},{13,9},{2,6},{6,2},{1... | collective-permute-start | bytes 294920 | tf_op jit(solution)/shard_map/ppermute | solution.py:32
  126.5 12.4 %collective-permute-start.21 = (bf16[192,256]{1,0:T(8,128)(2,1)S(1)}, bf16[192,256]{1,0:T(8,128)(2,1)S(1)}, u32[]{:S(2)}, u32[]{:S(2)}) collective-permute-start(bf16[192,256]{1,0:T(8,128)(2,1)S(1)} %convert_add_fusion), channel_id=1, source_target_pairs={{0,8},{4,12},{8,0},{12,4},{1,9},{5,13},{9,1},{13,5},{2,10},{6,14},... | collective-permute-start | bytes 294920 | tf_op jit(solution)/shard_map/ppermute | solution.py:32
  129.9 9.0 %collective-permute-start.22 = (bf16[192,256]{1,0:T(8,128)(2,1)S(1)}, bf16[192,256]{1,0:T(8,128)(2,1)S(1)}, u32[]{:S(2)}, u32[]{:S(2)}) collective-permute-start(bf16[192,256]{1,0:T(8,128)(2,1)S(1)} %convert_add_fusion), channel_id=1, source_target_pairs={{0,12},{4,8},{8,4},{12,0},{1,13},{5,9},{9,5},{13,1},{2,14},{6,10},... | collective-permute-start | bytes 294920 | tf_op jit(solution)/shard_map/ppermute | solution.py:32
  129.9 9.6 %collective-permute-start.16 = (bf16[32,768]{1,0:T(8,128)(2,1)S(1)}, bf16[32,768]{1,0:T(8,128)(2,1)S(1)}, u32[]{:S(2)}, u32[]{:S(2)}) collective-permute-start(bf16[32,768]{1,0:T(8,128)(2,1)S(1)} %add_convert_fusion), channel_id=1, source_target_pairs={{0,4},{4,0},{8,12},{12,8},{1,5},{5,1},{9,13},{13,9},{2,6},{6,2},{1... | collective-permute-start | bytes 147464 | tf_op jit(solution)/shard_map/ppermute | solution.py:32
  130.5 11.4 %collective-permute-start.17 = (bf16[32,768]{1,0:T(8,128)(2,1)S(1)}, bf16[32,768]{1,0:T(8,128)(2,1)S(1)}, u32[]{:S(2)}, u32[]{:S(2)}) collective-permute-start(bf16[32,768]{1,0:T(8,128)(2,1)S(1)} %add_convert_fusion), channel_id=1, source_target_pairs={{0,8},{4,12},{8,0},{12,4},{1,9},{5,13},{9,1},{13,5},{2,10},{6,14},... | collective-permute-start | bytes 147464 | tf_op jit(solution)/shard_map/ppermute | solution.py:32
  134.3 7.6 %collective-permute-start.18 = (bf16[32,768]{1,0:T(8,128)(2,1)S(1)}, bf16[32,768]{1,0:T(8,128)(2,1)S(1)}, u32[]{:S(2)}, u32[]{:S(2)}) collective-permute-start(bf16[32,768]{1,0:T(8,128)(2,1)S(1)} %add_convert_fusion), channel_id=1, source_target_pairs={{0,12},{4,8},{8,4},{12,0},{1,13},{5,9},{9,5},{13,1},{2,14},{6,10},... | collective-permute-start | bytes 147464 | tf_op jit(solution)/shard_map/ppermute | solution.py:32
  138.9 5.7 %collective-permute-start.23 = (f32[192,256]{1,0:T(8,128)S(1)}, f32[192,256]{1,0:T(8,128)S(1)}, u32[]{:S(2)}, u32[]{:S(2)}) collective-permute-start(f32[192,256]{1,0:T(8,128)S(1)} %add_add_fusion), channel_id=1, source_target_pairs={{0,2},{1,3},{2,0},{3,1},{4,6},{5,7},{6,4},{7,5},{8,10},{9,11},{10,... | collective-permute-start | bytes 589832 | tf_op jit(solution)/shard_map/ppermute | solution.py:32
  142.0 2.8 %collective-permute-start.19 = (f32[32,768]{1,0:T(8,128)S(1)}, f32[32,768]{1,0:T(8,128)S(1)}, u32[]{:S(2)}, u32[]{:S(2)}) collective-permute-start(f32[32,768]{1,0:T(8,128)S(1)} %add_add_fusion.1), channel_id=1, source_target_pairs={{0,1},{1,0},{2,3},{3,2},{4,5},{5,4},{6,7},{7,6},{8,9},{9,8},{10,11... | collective-permute-start | bytes 294920 | tf_op jit(solution)/shard_map/ppermute | solution.py:32
  144.7 2.0 %collective-permute-start.24 = (f32[384,256]{1,0:T(8,128)S(1)}, f32[384,256]{1,0:T(8,128)S(1)}, u32[]{:S(2)}, u32[]{:S(2)}) collective-permute-start(f32[384,256]{1,0:T(8,128)S(1)} %pad_maximum_fusion.1), channel_id=1, source_target_pairs={{0,1},{1,0},{2,3},{3,2},{4,5},{5,4},{6,7},{7,6},{8,9},{9,8},{10,11... | collective-permute-start | bytes 1179656 | tf_op jit(solution)/shard_map/ppermute | solution.py:32

commit v3 on v2

v3 whole, which is shorter than its diff:
```python
import functools

import jax
import jax.numpy as jnp
from jax import lax
from jax.experimental import pallas as pl
from jax.experimental.pallas import tpu as pltpu
from jax.sharding import PartitionSpec as P

KERNEL = 7
HALF = KERNEL // 2
NEWTON_STEPS = 5
LANES = 128
GROUPS = 8
EDGE = 8

epsilon = 1e-05
loss_scale = 64.0
narrow = jnp.bfloat16
wide = jnp.float32


def params(megabytes):
    return pltpu.CompilerParams(vmem_limit_bytes=megabytes * 1024 * 1024)


def swap(value, axis, shift):
    count = lax.axis_size(axis)
    return lax.ppermute(value, axis, [(i, i ^ shift) for i in range(count)])


def is_upper(axis, shift):
    return (lax.axis_index(axis) & shift) != 0


def halve(value, axis, shift, sent_as):
    upper = is_upper(axis, shift)
    rows = value.shape[0] // 2
    low, high = value[:rows], value[rows:]
    kept = jnp.where(upper, high, low)
    sent = jnp.where(upper, low, high).astype(sent_as)
    return kept + swap(sent, axis, shift).astype(wide)


def unhalve(value, axis, shift):
    upper = is_upper(axis, shift)
    other = swap(value, axis, shift)
    return jnp.concatenate([jnp.where(upper, other, value), jnp.where(upper, value, other)])


def tree_sum(terms):
    while len(terms) > 1:
        terms = [terms[i] + terms[i + 1] for i in range(0, len(terms), 2)]
    return terms[0]


def exchange(value, axis, shift, sent_as):
    sent = value.astype(sent_as)
    return sent.astype(wide) + swap(sent, axis, shift).astype(wide)


def exchange_all(value, axis, sent_as):
    sent = value.astype(sent_as)
    moved = [sent] + [swap(sent, axis, shift) for shift in range(1, lax.axis_size(axis))]
    return tree_sum([part.astype(wide) for part in moved])


def doublings(axis, first=1):
    found = []
    shift = first
    while shift < lax.axis_size(axis):
        found.append(shift)
        shift *= 2
    return found


def next_along(value, axis):
    return lax.ppermute(value, axis, [(i, i + 1) for i in range(lax.axis_size(axis) - 1)])


def back_along(value, axis):
    return lax.ppermute(value, axis, [(i + 1, i) for i in range(lax.axis_size(axis) - 1)])


def spread_columns(source, target):
    for group in range(target.shape[0]):
        target[group] = source[pl.ds(EDGE - HALF + group, GROUPS, stride=GROUPS), :]


def fill_row(wide_row, middle, left, right):
    cols = middle.shape[0]
    wide_row[EDGE : EDGE + cols, :] = middle.astype(wide)
    wide_row[EDGE - HALF : EDGE, :] = left.astype(wide)
    wide_row[EDGE + cols : EDGE + cols + HALF, :] = right.astype(wide)


def lanes_of(tile):
    return pl.ds(pl.multiple_of(tile * LANES, LANES), LANES)


def spread_weights(weight_ref, spread_ref, lanes):
    for row_tap in range(KERNEL):
        for col_tap in range(KERNEL):
            scale = weight_ref[row_tap, col_tap : col_tap + 1, lanes]
            spread_ref[row_tap * KERNEL + col_tap] = jnp.broadcast_to(scale, spread_ref.shape[1:])


def conv_row(load, spread_ref, bias, steps):
    total = [bias] * steps
    for row_tap in range(KERNEL):
        windows = [load(row_tap, group) for group in range(steps + KERNEL - 1)]
        for col_tap in range(KERNEL):
            scale = spread_ref[row_tap * KERNEL + col_tap]
            for step in range(steps):
                total[step] = total[step] + windows[step + col_tap] * scale
    return jnp.concatenate(total, axis=0).astype(narrow)


def reduce_part(conv_out, reduce_ref, reduce_bias_ref, before_out, feat_out):
    before = jnp.dot(conv_out[...], reduce_ref[...], preferred_element_type=wide)
    before = before + reduce_bias_ref[...]
    before_out[...] = before
    feat_out[...] = (before / (1.0 + jnp.exp(-before))).astype(narrow)
    feat = feat_out[...]
    gram = lax.dot_general(feat, feat, (((0,), (0,)), ((), ())), preferred_element_type=wide)
    return gram, jnp.sum(feat.astype(wide), axis=0, keepdims=True)


def inner_kernel(
    block, left, right, weight, bias, reduce_weight, reduce_bias,
    spread_out, conv_out, before_out, feat_out, gram_out, colsum_out,
    wide_row, spread_weight,
):
    rows, cols = block.shape[0], block.shape[1]
    steps = cols // GROUPS

    def one_tile(tile, _):
        lanes = lanes_of(tile)
        spread_weights(weight, spread_weight, lanes)
        start_value = jnp.broadcast_to(bias[0:1, lanes], (GROUPS, LANES))

        def fill(row, _):
            place = wide_row.at[row]
            fill_row(place, block[row, :, lanes], left[row, :, lanes], right[row, :, lanes])
            spread_columns(place, spread_out.at[tile, row])
            return 0

        lax.fori_loop(0, rows, fill, 0)

        def one_row(index, _):
            def load(row_tap, group):
                return spread_out[tile, index + row_tap, group]

            start = pl.multiple_of(index * cols, cols)
            conv_out[pl.ds(start, cols), lanes] = conv_row(load, spread_weight, start_value, steps)
            return 0

        lax.fori_loop(0, rows - 2 * HALF, one_row, 0)
        return 0

    lax.fori_loop(0, spread_out.shape[0], one_tile, 0)
    gram_out[...], colsum_out[...] = reduce_part(
        conv_out, reduce_weight, reduce_bias, before_out, feat_out
    )


def edge_kernel(
    flag, spread_in, top, bottom, weight, bias, reduce_weight, reduce_bias, gram_in, colsum_in,
    spread_top, spread_bottom, conv_out, before_out, feat_out, kept_out, sent_out,
    wide_row, corners, spread_weight, sums,
):
    rows, cols = spread_in.shape[1], wide_row.shape[1] - 2 * EDGE
    steps = cols // GROUPS

    def one_tile(tile, _):
        lanes = lanes_of(tile)
        spread_weights(weight, spread_weight, lanes)
        start_value = jnp.broadcast_to(bias[0:1, lanes], (GROUPS, LANES))
        for side, (strip, spread) in enumerate(((top, spread_top), (bottom, spread_bottom))):
            corners[side] = strip[HALF * cols :, lanes].astype(wide)
            for row in range(HALF):
                place = wide_row.at[side * HALF + row]
                left = corners[side, row * HALF : (row + 1) * HALF, :]
                right = corners[side, (HALF + row) * HALF : (HALF + row + 1) * HALF, :]
                fill_row(place, strip[row * cols : (row + 1) * cols, lanes], left, right)
                spread_columns(place, spread.at[tile, row])

        def load_from(row):
            def load(row_tap, group):
                place = row + row_tap - HALF
                if place < 0:
                    return spread_top[tile, place + HALF, group]
                if place >= rows:
                    return spread_bottom[tile, place - rows, group]
                return spread_in[tile, place, group]

            return load

        for index, row in enumerate(edge_rows(rows)):
            conv_out[index * cols : (index + 1) * cols, lanes] = conv_row(
                load_from(row), spread_weight, start_value, steps
            )
        return 0

    lax.fori_loop(0, spread_in.shape[0], one_tile, 0)
    gram, colsum = reduce_part(conv_out, reduce_weight, reduce_bias, before_out, feat_out)
    gram = gram + gram_in[...]
    colsum = colsum + colsum_in[...]
    width = gram.shape[0]
    half = width // 2
    quarter = half // 2
    sums[:half, :] = gram[:half, :]
    sums[half : half + quarter, :half] = gram[half : half + quarter, half:]
    sums[half : half + quarter, half:] = gram[half + quarter :, half:]
    sums[half + quarter :, :] = jnp.broadcast_to(
        colsum, (sums.shape[0] - half - quarter, width)
    )
    part = kept_out.shape[0]
    keep_or_send(flag[0] != 0, sums[:part, :], sums[part:, :], kept_out, sent_out)


def keep_or_send(upper, low, high, kept_out, sent_out):
    kept_out[...] = jnp.where(upper, high, low)
    sent_out[...] = jnp.where(upper, low, high).astype(sent_out.dtype)


def edge_rows(rows):
    return list(range(HALF)) + list(range(rows - HALF, rows))


def shape_of(shape, dtype=wide):
    return jax.ShapeDtypeStruct(shape, dtype)


in_vmem = pl.BlockSpec(memory_space=pltpu.VMEM)
in_smem = pl.BlockSpec(memory_space=pltpu.SMEM)


def cost(microseconds):
    return pl.CostEstimate(
        flops=microseconds * 10**9, bytes_accessed=microseconds * 10**6, transcendentals=0
    )


def conv_inner(block, left, right, weight, bias, reduce_weight, reduce_bias):
    rows, cols, channels = block.shape
    width = reduce_weight.shape[1]
    tiles = channels // LANES
    steps = cols // GROUPS
    pixels = (rows - 2 * HALF) * cols
    return pl.pallas_call(
        inner_kernel,
        in_specs=[in_vmem] * 7,
        out_specs=[in_vmem] * 6,
        out_shape=[
            shape_of((tiles, rows, steps + KERNEL - 1, GROUPS, LANES)),
            shape_of((pixels, channels), narrow),
            shape_of((pixels, width)),
            shape_of((pixels, width), narrow),
            shape_of((width, width)),
            shape_of((1, width)),
        ],
        scratch_shapes=[
            pltpu.VMEM((rows, cols + 2 * EDGE, LANES), wide),
            pltpu.VMEM((KERNEL * KERNEL, GROUPS, LANES), wide),
        ],
        compiler_params=params(24),
        cost_estimate=cost(10),
        name="conv_inner",
    )(block, left, right, weight, bias, reduce_weight, reduce_bias)


def conv_edge(flag, spread, top, bottom, weight, bias, reduce_weight, reduce_bias, gram, colsum):
    tiles, rows, groups = spread.shape[:3]
    cols, channels = (groups - KERNEL + 1) * GROUPS, top.shape[1]
    width = reduce_weight.shape[1]
    pixels = 2 * HALF * cols
    side = (tiles, HALF, groups, GROUPS, LANES)
    sums_rows = 3 * width // 4 + 2 * GROUPS
    return pl.pallas_call(
        edge_kernel,
        in_specs=[in_smem] + [in_vmem] * 9,
        out_specs=[in_vmem] * 7,
        out_shape=[
            shape_of(side),
            shape_of(side),
            shape_of((pixels, channels), narrow),
            shape_of((pixels, width)),
            shape_of((pixels, width), narrow),
            shape_of((sums_rows // 2, width)),
            shape_of((sums_rows // 2, width)),
        ],
        scratch_shapes=[
            pltpu.VMEM((2 * HALF, cols + 2 * EDGE, LANES), wide),
            pltpu.VMEM((2, top.shape[0] - HALF * cols, LANES), wide),
            pltpu.VMEM((KERNEL * KERNEL, GROUPS, LANES), wide),
            pltpu.VMEM((sums_rows, width), wide),
        ],
        compiler_params=params(24),
        cost_estimate=cost(6),
        name="conv_edge",
    )(flag, spread, top, bottom, weight, bias, reduce_weight, reduce_bias, gram, colsum)


def split(value):
    high = value.astype(narrow)
    return high, (value - high.astype(wide)).astype(narrow)


def product(left, right):
    def dot(a, b):
        return jnp.dot(a, b, preferred_element_type=wide)

    return dot(left[0], right[0]) + (dot(left[0], right[1]) + dot(left[1], right[0]))


def square_root(current):
    size = current.shape[0]
    row = lax.broadcasted_iota(jnp.int32, (size, size), 0)
    col = lax.broadcasted_iota(jnp.int32, (size, size), 1)
    triple = jnp.where(row == col, 3.0, 0.0)
    factor = split(0.5 * (triple - current))
    current = split(current)
    trail = [(current, None, factor)]
    inverse = factor
    current = split(product(current, factor))
    for step in range(1, NEWTON_STEPS):
        factor = split(0.5 * (triple - product(inverse, current)))
        trail.append((current, inverse, factor))
        last = step == NEWTON_STEPS - 1
        if not last:
            inverse = split(product(factor, inverse))
        current = product(current, factor)
        if not last:
            current = split(current)
    return current, trail


def square_root_change(change, trail):
    first, _, factor = trail[0]
    move = split(change)
    factor_move = split(-0.5 * change)
    change = product(move, factor) + product(first, factor_move)
    inverse_move = factor_move
    for step in range(1, NEWTON_STEPS):
        current, inverse, factor = trail[step]
        move = split(change)
        factor_move = split(
            -0.5 * (product(inverse_move, current) + product(inverse, move))
        )
        change = product(move, factor) + product(current, factor_move)
        if step < NEWTON_STEPS - 1:
            inverse_move = split(product(factor_move, inverse) + product(factor, inverse_move))
    return change


def head_kernel(
    flag, label, class_bias, own, other, class_weight,
    feat_inner, feat_edge, gate_inner, gate_edge, conv_turned, reduce_turned,
    root_out, kept_out, sent_out, bias_grad_out, conv_inner_out, conv_edge_out,
    sums, pre, *, count, image_count,
):
    width = root_out.shape[1]
    half = width // 2
    quarter = half // 2
    rows = own.shape[0]
    upper = flag[0] != 0
    mine, theirs = own[...], other[...]
    sums[:rows, :] = jnp.where(upper, theirs, mine)
    sums[rows:, :] = jnp.where(upper, mine, theirs)
    low = jnp.concatenate(
        [sums[half : half + quarter, :half], sums[half : half + quarter, half:]], axis=0
    )
    cross = sums[:half, half:]
    gram = jnp.concatenate(
        [sums[:half, :], jnp.concatenate([cross.T, low], axis=1)], axis=0
    )
    mean_row = sums[half + quarter : half + quarter + 1, :] / count
    mean_col = jnp.broadcast_to(mean_row, (width, width)).T
    sigma = gram / count - mean_col * mean_row
    row = lax.broadcasted_iota(jnp.int32, (width, width), 0)
    col = lax.broadcasted_iota(jnp.int32, (width, width), 1)
    diagonal = row == col
    trace_value = jnp.sum(jnp.where(diagonal, sigma, 0.0), keepdims=True) + epsilon
    root_scale = jnp.sqrt(trace_value)
    unit, trail = square_root(sigma / trace_value)
    root = root_scale * unit
    root_out[:width, :] = root

    classes = class_weight.shape[0]
    slots = root_out.shape[0] - width
    place = lax.broadcasted_iota(jnp.int32, (slots, 1), 0)
    bias = jnp.zeros((slots, 1), wide)
    for index in range(classes):
        bias = jnp.where(place == index, class_bias[index], bias)
    partial = [
        jnp.sum(class_weight[index].astype(wide) * root, axis=0, keepdims=True)
        for index in range(classes)
    ]
    partial.append(jnp.zeros((slots - classes, width), wide))
    logits = jnp.sum(jnp.concatenate(partial, axis=0), axis=1, keepdims=True) + bias
    onehot = jnp.where(place == label[0], 1.0, 0.0)
    soft = jnp.maximum(logits, 0.0) + jnp.log(1.0 + jnp.exp(-jnp.abs(logits)))
    share = 1.0 / (1.0 + jnp.exp(-logits))
    used = place < classes
    loss_part = jnp.sum(jnp.where(used, soft - onehot * logits, 0.0), keepdims=True)
    logit_grad = jnp.where(used, loss_scale * (share - onehot) / image_count, 0.0)
    root_out[width:, :] = jnp.broadcast_to(
        jnp.where(place == classes, loss_part, logit_grad), (slots, width)
    )

    root_grad = jnp.zeros((width, width), wide)
    for index in range(classes):
        root_grad = root_grad + class_weight[index].astype(wide) * logit_grad[index : index + 1, :]
    root_grad = root_grad + root_grad.T
    change = square_root_change(root_scale * root_grad, trail)
    trace_grad = jnp.sum(root_grad * unit, keepdims=True) / (2.0 * root_scale) - jnp.sum(
        change * sigma, keepdims=True
    ) / (trace_value * trace_value)
    symmetric = (
        (change / trace_value + jnp.where(diagonal, trace_grad, 0.0)) / count
    ).astype(narrow)
    mean_term = jnp.sum(mean_col * symmetric.astype(wide), axis=0, keepdims=True)

    inner = feat_inner.shape[0]
    for feat, gate, start in ((feat_inner, gate_inner, 0), (feat_edge, gate_edge, inner)):
        grad = jnp.dot(feat[...], symmetric, preferred_element_type=wide) - mean_term
        pre[start : start + feat.shape[0], :] = (grad * gate[...]).astype(narrow)
    pre_grad = pre[...]
    bias_grad_out[...] = jnp.sum(pre_grad.astype(wide), axis=0, keepdims=True)
    weight_grad = jnp.dot(conv_turned[...], pre_grad, preferred_element_type=wide)
    part = kept_out.shape[0]
    keep_or_send(upper, weight_grad[:part, :], weight_grad[part:, :], kept_out, sent_out)
    for out, start in ((conv_inner_out, 0), (conv_edge_out, inner)):
        out[...] = jnp.dot(
            pre[start : start + out.shape[0], :], reduce_turned[...], preferred_element_type=wide
        ).astype(narrow)


def head(flag, label, class_bias, own, other, class_weight, prepared, count, image_count):
    feat_inner, feat_edge, gate_inner, gate_edge, conv_turned, reduce_turned = prepared
    width, channels = reduce_turned.shape
    inner, edge = feat_inner.shape[0], feat_edge.shape[0]
    slots = -(-(class_weight.shape[0] + 1) // GROUPS) * GROUPS
    return pl.pallas_call(
        functools.partial(head_kernel, count=count, image_count=image_count),
        in_specs=[in_smem] * 3 + [in_vmem] * 9,
        out_specs=[in_vmem] * 6,
        out_shape=[
            shape_of((width + slots, width)),
            shape_of((channels // 2, width)),
            shape_of((channels // 2, width)),
            shape_of((1, width)),
            shape_of((inner, channels), narrow),
            shape_of((edge, channels), narrow),
        ],
        scratch_shapes=[
            pltpu.VMEM((2 * own.shape[0], width), wide),
            pltpu.VMEM((inner + edge, width), narrow),
        ],
        compiler_params=params(24),
        cost_estimate=cost(10),
        name="head",
    )(
        flag, label, class_bias, own, other, class_weight,
        feat_inner, feat_edge, gate_inner, gate_edge, conv_turned, reduce_turned,
    )


def prepare_kernel(
    before_inner, before_edge, conv_inner_in, conv_edge_in, reduce_weight,
    gate_inner, gate_edge, conv_turned, reduce_turned,
):
    for before, gate in ((before_inner, gate_inner), (before_edge, gate_edge)):
        value = before[...]
        share = 1.0 / (1.0 + jnp.exp(-value))
        gate[...] = share * (1.0 + value * (1.0 - share))
    inner = conv_inner_in.shape[0]
    conv_turned[:, :inner] = conv_inner_in[...].T
    conv_turned[:, inner:] = conv_edge_in[...].T
    reduce_turned[...] = reduce_weight[...].T


def prepare(before_inner, before_edge, conv_in, conv_ed, reduce_weight):
    channels, width = reduce_weight.shape
    inner, edge = before_inner.shape[0], before_edge.shape[0]
    return pl.pallas_call(
        prepare_kernel,
        in_specs=[in_vmem] * 5,
        out_specs=[in_vmem] * 4,
        out_shape=[
            shape_of((inner, width)),
            shape_of((edge, width)),
            shape_of((channels, inner + edge), narrow),
            shape_of((width, channels), narrow),
        ],
        compiler_params=params(16),
        cost_estimate=cost(1),
        name="prepare",
    )(before_inner, before_edge, conv_in, conv_ed, reduce_weight)


def taps_kernel(
    flag, spread_in, spread_top, spread_bottom, grad_inner, grad_edge, bias_grad, *refs,
    first, many,
):
    kept_out, sent_out, grads, out = refs[-4:]
    rows = spread_in.shape[1]
    steps = grads.shape[1]
    cols = steps * GROUPS
    order = edge_rows(rows)
    taps = KERNEL * KERNEL
    part = kept_out.shape[0]
    upper = flag[0] != 0
    out[taps:, :] = jnp.zeros((out.shape[0] - taps, LANES), wide)

    def one_tile(tile, _):
        lanes = lanes_of(tile)

        for row in range(rows):
            if row in order:
                source, place = grad_edge, order.index(row)
            else:
                source, place = grad_inner, row - HALF
            values = source[place * cols : (place + 1) * cols, lanes].astype(wide)
            for step in range(steps):
                grads[row, step] = values[step * GROUPS : (step + 1) * GROUPS, :]

        def load(place, group):
            if place < 0:
                return spread_top[tile, place + HALF, group]
            if place >= rows:
                return spread_bottom[tile, place - rows, group]
            return spread_in[tile, place, group]

        for begin in range(0, KERNEL, 2):
            row_taps = [tap for tap in (begin, begin + 1) if tap < KERNEL]
            total = {
                (row_tap, col_tap): jnp.zeros((GROUPS, LANES), wide)
                for row_tap in row_taps
                for col_tap in range(KERNEL)
            }
            for place in range(begin - HALF, rows + row_taps[-1] - HALF):
                windows = [load(place, group) for group in range(steps + KERNEL - 1)]
                for row_tap in row_taps:
                    row = place - row_tap + HALF
                    if not 0 <= row < rows:
                        continue
                    for step in range(steps):
                        grad = grads[row, step]
                        for col_tap in range(KERNEL):
                            total[row_tap, col_tap] += windows[step + col_tap] * grad
            for (row_tap, col_tap), value in total.items():
                tap = row_tap * KERNEL + col_tap
                out[tap : tap + 1, :] = jnp.sum(value, axis=0, keepdims=True)
        total = [jnp.zeros((GROUPS, LANES), wide) for _ in range(KERNEL)]
        for index in range(rows * steps):
            slot = index % KERNEL
            total[slot] = total[slot] + grads[index // steps, index % steps]
        out[taps : taps + 1, :] = jnp.sum(sum(total), axis=0, keepdims=True)
        low, high = out[:part, :], out[part:, :]
        kept_out[:, lanes] = jnp.where(upper, high, low)
        sent_out[:, lanes] = jnp.where(upper, low, high)
        return 0

    lax.fori_loop(first, first + many, one_tile, 0)
    if first == 0:
        width = bias_grad.shape[1]
        place = taps + 1 - part
        row = jnp.broadcast_to(bias_grad[...], (1, width))

        @pl.when(upper)
        def _():
            kept_out[place : place + 1, :width] = row

        @pl.when(jnp.logical_not(upper))
        def _():
            sent_out[place : place + 1, :width] = row


def tap_grads(flag, spreads, grads, bias_grad, filled, first, many):
    tiles, rows, groups = spreads[0].shape[:3]
    steps = groups - KERNEL + 1
    taps_rows = -(-(KERNEL * KERNEL + 2) // 32) * 32
    part = (taps_rows // 2, tiles * LANES)
    return pl.pallas_call(
        functools.partial(taps_kernel, first=first, many=many),
        in_specs=[in_smem] + [in_vmem] * (6 + len(filled)),
        out_specs=[in_vmem] * 2,
        out_shape=[shape_of(part), shape_of(part)],
        input_output_aliases={7 + index: index for index in range(len(filled))},
        scratch_shapes=[
            pltpu.VMEM((rows, steps, GROUPS, LANES), wide),
            pltpu.VMEM((taps_rows, LANES), wide),
        ],
        compiler_params=params(16),
        cost_estimate=cost(5),
        name="tap_grads",
    )(flag, *spreads, *grads, bias_grad, *filled)


def edge_strip(block, left, right, rows):
    channels = block.shape[2]
    parts = [part[rows].reshape(-1, channels) for part in (block, left, right)]
    short = -(2 * HALF * HALF) % 16
    return jnp.concatenate(parts + [jnp.zeros((short, channels), block.dtype)])


def body(
    features, depth_weight, depth_bias, reduce_weight, reduce_bias, class_weight, class_bias, labels
):
    together = lax.optimization_barrier
    block = features[0]
    rows, cols, channels = block.shape
    width = reduce_weight.shape[1]
    classes = class_bias.shape[0]
    count = rows * cols * lax.axis_size("sy") * lax.axis_size("sx")
    image_count = features.shape[0] * lax.axis_size("dp")

    flag = is_upper("sx", 1).astype(jnp.int32)[None]
    bias_row = depth_bias[None]
    reduce_row = reduce_bias[None]
    left = next_along(block[:, cols - HALF :], "sx")
    right = back_along(block[:, :HALF], "sx")
    low, high, left, right, flag, bias_row, reduce_row = together(
        (
            edge_strip(block, left, right, slice(rows - HALF, rows)),
            edge_strip(block, left, right, slice(0, HALF)),
            left,
            right,
            flag,
            bias_row,
            reduce_row,
        )
    )
    top = next_along(low, "sy")
    bottom = back_along(high, "sy")
    spread, conv_in, before_in, feat_in, gram, colsum = conv_inner(
        block, left, right, depth_weight, bias_row, reduce_weight, reduce_row
    )
    spread_top, spread_bottom, conv_ed, before_ed, feat_ed, kept, sent = conv_edge(
        flag, spread, top, bottom, depth_weight, bias_row, reduce_weight, reduce_row, gram, colsum
    )

    sums = kept + swap(sent, "sx", 1)
    sums, before_in, before_ed, conv_in, conv_ed = together(
        (sums, before_in, before_ed, conv_in, conv_ed)
    )
    gate_in, gate_ed, conv_turned, reduce_turned = prepare(
        before_in, before_ed, conv_in, conv_ed, reduce_weight
    )
    for shift in doublings("sx", 2):
        sums = exchange(sums, "sx", shift, wide)
    sums, gate_in, gate_ed, conv_turned, reduce_turned = together(
        (sums, gate_in, gate_ed, conv_turned, reduce_turned)
    )
    for shift in doublings("sy"):
        sums = exchange(sums, "sy", shift, wide)
    other = swap(sums, "sx", 1)

    root, kept, sent, bias_grad, *grads = head(
        flag,
        labels,
        class_bias,
        sums,
        other,
        class_weight,
        (feat_in, feat_ed, gate_in, gate_ed, conv_turned, reduce_turned),
        count,
        image_count,
    )

    known = [root] + [swap(root, "dp", shift) for shift in range(1, lax.axis_size("dp"))]
    spreads = (spread, spread_top, spread_bottom)
    tiles = channels // LANES
    many = tiles // 3 if tiles % 3 == 0 else tiles
    turns = list(range(0, tiles, many))
    filled = []

    def beside(sums):
        if turns:
            sums, grads[:], filled[:] = together((sums, grads, filled))
            filled[:] = tap_grads(flag, spreads, grads, bias_grad, filled, turns.pop(0), many)
        return sums

    sums = kept + swap(sent, "sx", 1)
    for shift in doublings("sx", 2):
        sums = halve(beside(sums), "sx", shift, narrow)
    for shift in doublings("dp"):
        sums = exchange(beside(sums), "dp", shift, narrow)
    sums = exchange_all(beside(sums), "sy", narrow)
    while turns:
        sums = beside(sums)

    sums, (kept, sent), known = together((sums, filled, known))
    small = kept + swap(sent, "sx", 1)
    class_weight_grad = tree_sum(
        [part[width : width + classes, 0][:, None, None] * part[None, :width] for part in known]
    )
    totals = tree_sum([part[width:, 0] for part in known])
    class_bias_grad = totals[:classes]
    loss = totals[classes] / image_count
    small, sums = together((small, sums))
    for shift in reversed(doublings("sx", 2)):
        sums = unhalve(sums, "sx", shift)
    for shift in doublings("sx", 2):
        small = exchange(small, "sx", shift, narrow)
    for shift in doublings("dp"):
        small = exchange(small, "dp", shift, narrow)
    small, sums = together((small, sums))
    weight_grad = unhalve(sums, "sx", 1)
    small = exchange_all(small, "sy", narrow)
    small = unhalve(small, "sx", 1)

    taps = KERNEL * KERNEL
    return (
        loss,
        small[:taps].reshape(depth_weight.shape),
        small[taps],
        weight_grad,
        small[taps + 1, :width],
        class_weight_grad,
        class_bias_grad,
    )


def solution(mesh):
    placed = (P("dp", "sy", "sx", None), P(), P(), P(), P(), P(), P(), P("dp"))
    return jax.shard_map(
        body,
        mesh=mesh,
        in_specs=placed,
        out_specs=(P(), P(), P(), P(), P(), P(), P()),
        check_vma=False,
    )
```

time: 150 us -> 125 us (0.83)
  Pallas kernels: 61.3 us -> 38.2 us
  local copies, waits for them, and re-layouts: 9.11 us -> 15.4 us
  other arithmetic: 10.2 us -> 4.44 us
  waiting for transfers between devices: 30.8 us -> 26.8 us
  starting transfers between devices: 33.9 us -> 36.2 us
    pallas_call x5, Pallas kernels: 45.7 us -> 27.5 us  [the longest x1 11.9 us: conv_inner(): pl.pallas_call(inner_kernel, in_specs=[in_vmem] * 7, out_specs=[in_vmem]...]
    unnamed x28, local copies, waits for them, and re-layouts: 1.52 us -> 9.02 us
    ppermute x21, waiting for transfers between devices: 28 us -> 24.7 us  [swap(): return lax.ppermute(value, axis, [(i, i ^ shift) for i in range(count)])]
    pallas_call x1, Pallas kernels: 4.12 us -> 0.97 us  [prepare(): pl.pallas_call(prepare_kernel, in_specs=[in_vmem] * 5, out_specs=[in_vmem...]
    select_n x4 -> x0, other arithmetic: 3.11 us -> none  [the longest x3 2.15 us: halve(): sent = jnp.where(upper, low, high).astype(sent_as)]
    ppermute x21, starting transfers between devices: 25.5 us -> 27.7 us  [swap(): return lax.ppermute(value, axis, [(i, i ^ shift) for i in range(count)])]
    add x3 -> x1, other arithmetic: 2.2 us -> 0.04 us  [halve(): return kept + swap(sent, axis, shift).astype(wide)]
    pallas_call x1, Pallas kernels: 11.5 us -> 9.69 us  [head(): pl.pallas_call(functools.partial(head_kernel, count=count, image_count=im...]
  transfers between devices with their start and end apart: 25 -> 25, of which waited for: 10 -> 14; matrix products, arithmetic and copies ran while one was open for 8% -> 7% of each run, Pallas kernels for 23% -> 19%
where the time goes in v3:
time: 125 us; the launch traced here: 124 us
  Pallas kernels  38.2 us (31%)
  starting transfers between devices  36.2 us (29%)
  waiting for transfers between devices  26.8 us (21%)
  local copies, waits for them, and re-layouts  15.4 us (12%)
  other arithmetic  4.44 us (4%)
  between operations  3.45 us (3%)
    ppermute x21, starting transfers between devices, swap(): return lax.ppermute(value, axis, [(i, i ^ shift) for i in range(count)])  27.7 us
    ppermute x21, waiting for transfers between devices, swap(): return lax.ppermute(value, axis, [(i, i ^ shift) for i in range(count)])  24.7 us
    pallas_call x1, Pallas kernels, conv_inner(): pl.pallas_call(inner_kernel, in_specs=[in_vmem] * 7, out_specs=[in_vmem]...  11.9 us
    pallas_call x3, Pallas kernels, tap_grads(): pl.pallas_call(functools.partial(taps_kernel, first=first, many=many), in...  10.7 us
    pallas_call x1, Pallas kernels, head(): pl.pallas_call(functools.partial(head_kernel, count=count, image_count=im...  9.69 us
    unnamed x28, local copies, waits for them, and re-layouts  9.02 us
    ppermute x2, starting transfers between devices, next_along(): lax.ppermute(value, axis, [(i, i + 1) for i in range(lax.axis_size(axis)...  5.86 us
    pallas_call x1, Pallas kernels, conv_edge(): pl.pallas_call(edge_kernel, in_specs=[in_smem] + [in_vmem] * 9, out_specs...  4.85 us
  transfers between devices with their start and end apart: 25, of which 14 were waited for; matrix products, arithmetic and copies ran while one was open for 7% of the time, Pallas kernels for 19%

profile of v3, /device:TPU:0, one launch (start us, length us, event | category | flops | bytes accessed | tf_op | source)
XLA Modules:
  0.0 124.4 jit_solution(3748531975116778368)
XLA Ops:
  0.7 1.2 %fusion.1 = (bf16[16,3,768]{2,1,0:T(4,128)(2,1)S(1)}, bf16[16,3,768]{2,1,0:T(4,128)(2,1)S(1)}) fusion(bf16[16,64,768]{2,1,0:T(8,128)(2,1)} %bitcast.7), kind=kLoop, calls=%fused_computation.25 | loop fusion | bytes 294912 | tf_op jit(solution)/shard_map/slice | solution.py:623
  1.9 2.4 %collective-permute-start = (bf16[16,3,768]{2,1,0:T(4,128)(2,1)S(1)}, bf16[16,3,768]{2,1,0:T(4,128)(2,1)S(1)}, u32[]{:S(2)}, u32[]{:S(2)}) collective-permute-start(bf16[16,3,768]{2,1,0:T(4,128)(2,1)S(1)} %get-tuple-element.145), channel_id=1, source_target_pairs={{0,1},{1,2},{2,3},{4,5},{5,6},{6,7},{8,9},{9,10},{10,11},{12,13},{... | collective-permute-start | bytes 221192 | tf_op jit(solution)/shard_map/ppermute | solution.py:78
  4.3 1.3 %collective-permute-start.1 = (bf16[16,3,768]{2,1,0:T(4,128)(2,1)S(1)}, bf16[16,3,768]{2,1,0:T(4,128)(2,1)S(1)}, u32[]{:S(2)}, u32[]{:S(2)}) collective-permute-start(bf16[16,3,768]{2,1,0:T(4,128)(2,1)S(1)} %get-tuple-element.146), channel_id=1, source_target_pairs={{1,0},{2,1},{3,2},{5,4},{6,5},{7,6},{9,8},{10,9},{11,10},{13,12},{... | collective-permute-start | bytes 221192 | tf_op jit(solution)/shard_map/ppermute | solution.py:82
  5.6 1.1 fusion
  6.7 0.7 broadcast_in_dim.16.bias
  7.4 0.1 pad.13.clone
  7.5 2.1 %collective-permute-done.1.right = bf16[16,3,768]{2,1,0:T(4,128)(2,1)S(1)} collective-permute-done((bf16[16,3,768]{2,1,0:T(4,128)(2,1)S(1)}, bf16[16,3,768]{2,1,0:T(4,128)(2,1)S(1)}, u32[]{:S(2)}, u32[]{:S(2)}) %collective-permute-start.1) | collective-permute-done | bytes 73760 | tf_op jit(solution)/shard_map/ppermute | solution.py:82
  9.7 0.2 maximum_maximum_fusion.1
  9.9 3.5 %collective-permute-start.2 = (bf16[224,768]{1,0:T(8,128)(2,1)S(1)}, bf16[224,768]{1,0:T(8,128)(2,1)S(1)}, u32[]{:S(2)}, u32[]{:S(2)}) collective-permute-start(bf16[224,768]{1,0:T(8,128)(2,1)S(1)} %get-tuple-element.81), channel_id=1, source_target_pairs={{0,4},{4,8},{8,12},{1,5},{5,9},{9,13},{2,6},{6,10},{10,14},{3,7},{... | collective-permute-start | bytes 1032200 | tf_op jit(solution)/shard_map/ppermute | solution.py:78
  13.4 1.3 %collective-permute-start.3 = (bf16[224,768]{1,0:T(8,128)(2,1)S(1)}, bf16[224,768]{1,0:T(8,128)(2,1)S(1)}, u32[]{:S(2)}, u32[]{:S(2)}) collective-permute-start(bf16[224,768]{1,0:T(8,128)(2,1)S(1)} %get-tuple-element.82), channel_id=1, source_target_pairs={{4,0},{8,4},{12,8},{5,1},{9,5},{13,9},{6,2},{10,6},{14,10},{7,3},{... | collective-permute-start | bytes 1032200 | tf_op jit(solution)/shard_map/ppermute | solution.py:82
  14.7 11.9 %conv_inner.1 = (f32[6,16,14,8,128]{4,3,2,1,0:T(8,128)S(1)}, bf16[640,768]{1,0:T(8,128)(2,1)S(1)}, f32[640,256]{1,0:T(8,128)S(1)}, bf16[640,256]{1,0:T(8,128)(2,...) custom-call(bf16[16,64,768]{2,1,0:T(8,128)(2,1)S(1)} %bitcast.8, ...), custom_call_target="tpu_custom_call" | custom-call | flops 10000000000 | bytes 10000000 | tf_op jit(solution)/shard_map/conv_inner/pallas_call | solution.py:251
  26.7 4.8 %conv_edge.1 = (f32[6,3,14,8,128]{4,3,2,1,0:T(8,128)S(1)}, f32[6,3,14,8,128]{4,3,2,1,0:T(8,128)S(1)}, bf16[384,768]{1,0:T(8,128)(2,1)S(1)}, f32[384,256]{1,0:T(8...) custom-call(s32[1]{0:T(128)} %bitcast.3.flag, ...), custom_call_target="tpu_custom_call" | custom-call | flops 6000000000 | bytes 6000000 | tf_op jit(solution)/shard_map/conv_edge/pallas_call | solution.py:280
  31.6 2.4 %copy-done.6 = f32[6,16,14,8,128]{4,3,2,1,0:T(8,128)} copy-done((f32[6,16,14,8,128]{4,3,2,1,0:T(8,128)}, f32[6,16,14,8,128]{4,3,2,1,0:T(8,128)S(1)}, u32[]{:S(2)}) %copy-start.6) | copy-done | bytes 5505048
  34.0 3.0 %collective-permute-start.4 = (f32[104,256]{1,0:T(8,128)S(1)}, f32[104,256]{1,0:T(8,128)S(1)}, u32[]{:S(2)}, u32[]{:S(2)}) collective-permute-start(f32[104,256]{1,0:T(8,128)S(1)} %get-tuple-element.86), channel_id=1, source_target_pairs={{0,1},{1,0},{2,3},{3,2},{4,5},{5,4},{6,7},{7,6},{8,9},{9,8},{10,11... | collective-permute-start | bytes 319496 | tf_op jit(solution)/shard_map/ppermute | solution.py:29
  36.9 1.0 collective-permute-done.4
  37.9 0.5 collective-permute-start.5
  38.4 1.0 prepare.1
  39.4 3.8 %collective-permute-done.5 = f32[104,256]{1,0:T(8,128)S(1)} collective-permute-done((f32[104,256]{1,0:T(8,128)S(1)}, f32[104,256]{1,0:T(8,128)S(1)}, u32[]{:S(2)}, u32[]{:S(2)}) %collective-permute-start.5) | collective-permute-done | bytes 106528 | tf_op jit(solution)/shard_map/ppermute | solution.py:29
  43.2 2.4 %collective-permute-start.6 = (f32[104,256]{1,0:T(8,128)S(1)}, f32[104,256]{1,0:T(8,128)S(1)}, u32[]{:S(2)}, u32[]{:S(2)}) collective-permute-start(f32[104,256]{1,0:T(8,128)S(1)} %add.56), channel_id=1, source_target_pairs={{0,4},{4,0},{8,12},{12,8},{1,5},{5,1},{9,13},{13,9},{2,6},{6,2},{1... | collective-permute-start | bytes 319496 | tf_op jit(solution)/shard_map/ppermute | solution.py:29
  45.7 2.7 %collective-permute-done.6 = f32[104,256]{1,0:T(8,128)S(1)} collective-permute-done((f32[104,256]{1,0:T(8,128)S(1)}, f32[104,256]{1,0:T(8,128)S(1)}, u32[]{:S(2)}, u32[]{:S(2)}) %collective-permute-start.6) | collective-permute-done | bytes 106528 | tf_op jit(solution)/shard_map/ppermute | solution.py:29
  48.4 3.1 %collective-permute-start.7 = (f32[104,256]{1,0:T(8,128)S(1)}, f32[104,256]{1,0:T(8,128)S(1)}, u32[]{:S(2)}, u32[]{:S(2)}) collective-permute-start(f32[104,256]{1,0:T(8,128)S(1)} %add.57), channel_id=1, source_target_pairs={{0,8},{4,12},{8,0},{12,4},{1,9},{5,13},{9,1},{13,5},{2,10},{6,14},... | collective-permute-start | bytes 319496 | tf_op jit(solution)/shard_map/ppermute | solution.py:29
  51.4 2.7 %collective-permute-done.7 = f32[104,256]{1,0:T(8,128)S(1)} collective-permute-done((f32[104,256]{1,0:T(8,128)S(1)}, f32[104,256]{1,0:T(8,128)S(1)}, u32[]{:S(2)}, u32[]{:S(2)}) %collective-permute-start.7) | collective-permute-done | bytes 106528 | tf_op jit(solution)/shard_map/ppermute | solution.py:29
  54.9 0.7 collective-permute-done.8.other
  55.5 9.7 %head.1 = (f32[272,256]{1,0:T(8,128)S(1)}, f32[384,256]{1,0:T(8,128)S(1)}, f32[384,256]{1,0:T(8,128)S(1)}, f32[1,256]{1,0:T(1,128)S(1)}, bf16[640,768]{1,0:T(8,128)(2,1)S(1)}, /*index=5*/bf16[384,768]{1,0:T(8,128)(2,1)S(1)}) custom-call(s32[1]{0:T(128)} %bitcast.3.flag, s32[1]{0:T(128)S(6)} %copy.23.label, f32[10]{0:T(128)S(1)} %copy-done.5, ...), custom_call_target="tpu_custom_call" | custom-call | flops 10000000000 | bytes 10000000 | tf_op jit(solution)/shard_map/head/pallas_call | solution.py:445
  65.2 0.9 copy-done.10
  66.2 0.8 copy-done.12
  67.0 0.1 collective-permute-start.9
  67.1 1.5 %collective-permute-start.15 = (f32[272,256]{1,0:T(8,128)S(1)}, f32[272,256]{1,0:T(8,128)S(1)}, u32[]{:S(2)}, u32[]{:S(2)}) collective-permute-start(f32[272,256]{1,0:T(8,128)S(1)} %get-tuple-element.134), channel_id=1, source_target_pairs={{0,16},{16,0},{1,17},{17,1},{2,18},{18,2},{3,19},{19,3},{4,20},{20... | collective-permute-start | bytes 835592 | tf_op jit(solution)/shard_map/ppermute | solution.py:29
  68.6 0.2 collective-permute-done.9
  68.9 1.0 add.59
  69.9 0.6 collective-permute-start.10
  70.5 2.6 %copy-done.7 = f32[6,16,14,8,128]{4,3,2,1,0:T(8,128)S(1)} copy-done((f32[6,16,14,8,128]{4,3,2,1,0:T(8,128)S(1)}, f32[6,16,14,8,128]{4,3,2,1,0:T(8,128)}, u32[]{:S(2)}) %copy-start.7) | copy-done | bytes 5505048
  73.1 1.2 copy-done.11
  74.3 1.1 copy-done.13
  75.3 3.7 %tap_grads.3 = (f32[32,768]{1,0:T(8,128)S(1)}, f32[32,768]{1,0:T(8,128)S(1)}) custom-call(s32[1]{0:T(128)} %bitcast.3.flag, f32[6,16,14,8,128]{4,3,2,1,0:T(8,128)S(1)} %copy-done.7, f32[6,3,14,8,128]{4,3,2,1,0:T(8,128)S(1)} %get-tuple-element.114.spread_top, f32[6,3,14,8,128]{4,3,2,1,0:T(8,128)S(1)} %copy-done.9, bf16[640,768]{1,0:T(8,128)(2,1)S(1)} %copy-done.11, ...), custom_call_target="tpu_custom_call" | custom-call | flops 5000000000 | bytes 5000000 | tf_op jit(solution)/shard_map/tap_grads/pallas_call | solution.py:586
  79.1 1.6 %collective-permute-start.11 = (bf16[192,256]{1,0:T(8,128)(2,1)S(1)}, bf16[192,256]{1,0:T(8,128)(2,1)S(1)}, u32[]{:S(2)}, u32[]{:S(2)}) collective-permute-start(bf16[192,256]{1,0:T(8,128)(2,1)S(1)} %convert_add_fusion.1), channel_id=1, source_target_pairs={{0,16},{16,0},{1,17},{17,1},{2,18},{18,2},{3,19},{19,3},{4,20},{20... | collective-permute-start | bytes 294920 | tf_op jit(solution)/shard_map/ppermute | solution.py:29
  80.7 3.5 %tap_grads.4 = (f32[32,768]{1,0:T(8,128)S(1)}, f32[32,768]{1,0:T(8,128)S(1)}) custom-call(s32[1]{0:T(128)} %bitcast.3.flag, f32[6,16,14,8,128]{4,3,2,1,0:T(8,128)S(1)} %copy-done.7, f32[6,3,14,8,128]{4,3,2,1,0:T(8,128)S(1)} %get-tuple-element.114.spread_top, f32[6,3,14,8,128]{4,3,2,1,0:T(8,128)S(1)} %copy-done.9, ...), custom_call_target="tpu_custom_call", output_to_operand_aliasing={{0}: (7, {}), {1}: (8, {})} | custom-call | flops 5000000000 | bytes 5000000 | tf_op jit(solution)/shard_map/tap_grads/pallas_call | solution.py:586
  84.2 3.1 %collective-permute-start.13 = (bf16[192,256]{1,0:T(8,128)(2,1)S(1)}, bf16[192,256]{1,0:T(8,128)(2,1)S(1)}, u32[]{:S(2)}, u32[]{:S(2)}) collective-permute-start(bf16[192,256]{1,0:T(8,128)(2,1)S(1)} %convert_add_fusion), channel_id=1, source_target_pairs={{0,8},{4,12},{8,0},{12,4},{1,9},{5,13},{9,1},{13,5},{2,10},{6,14},... | collective-permute-start | bytes 294920 | tf_op jit(solution)/shard_map/ppermute | solution.py:29
  87.3 2.5 %collective-permute-start.12 = (bf16[192,256]{1,0:T(8,128)(2,1)S(1)}, bf16[192,256]{1,0:T(8,128)(2,1)S(1)}, u32[]{:S(2)}, u32[]{:S(2)}) collective-permute-start(bf16[192,256]{1,0:T(8,128)(2,1)S(1)} %convert_add_fusion), channel_id=1, source_target_pairs={{0,4},{4,0},{8,12},{12,8},{1,5},{5,1},{9,13},{13,9},{2,6},{6,2},{1... | collective-permute-start | bytes 294920 | tf_op jit(solution)/shard_map/ppermute | solution.py:29
  89.8 3.5 %tap_grads.5 = (f32[32,768]{1,0:T(8,128)S(1)}, f32[32,768]{1,0:T(8,128)S(1)}) custom-call(s32[1]{0:T(128)} %bitcast.3.flag, f32[6,16,14,8,128]{4,3,2,1,0:T(8,128)S(1)} %copy-done.7, f32[6,3,14,8,128]{4,3,2,1,0:T(8,128)S(1)} %get-tuple-element.114.spread_top, f32[6,3,14,8,128]{4,3,2,1,0:T(8,128)S(1)} %copy-done.9, ...), custom_call_target="tpu_custom_call", output_to_operand_aliasing={{0}: (7, {}), {1}: (8, {})} | custom-call | flops 5000000000 | bytes 5000000 | tf_op jit(solution)/shard_map/tap_grads/pallas_call | solution.py:586
  93.3 2.9 %collective-permute-done.14 = bf16[192,256]{1,0:T(8,128)(2,1)S(1)} collective-permute-done((bf16[192,256]{1,0:T(8,128)(2,1)S(1)}, bf16[192,256]{1,0:T(8,128)(2,1)S(1)}, u32[]{:S(2)}, u32[]{:S(2)}) %collective-permute-start.14) | collective-permute-done | bytes 98336 | tf_op jit(solution)/shard_map/ppermute | solution.py:29
  96.3 0.1 collective-permute-start.16
  96.4 1.3 %collective-permute-done.16 = f32[32,768]{1,0:T(8,128)S(1)} collective-permute-done((f32[32,768]{1,0:T(8,128)S(1)}, f32[32,768]{1,0:T(8,128)S(1)}, u32[]{:S(2)}, u32[]{:S(2)}) %collective-permute-start.16) | collective-permute-done | bytes 98336 | tf_op jit(solution)/shard_map/ppermute | solution.py:29
  97.7 1.6 %collective-permute-start.17 = (bf16[32,768]{1,0:T(8,128)(2,1)S(1)}, bf16[32,768]{1,0:T(8,128)(2,1)S(1)}, u32[]{:S(2)}, u32[]{:S(2)}) collective-permute-start(bf16[32,768]{1,0:T(8,128)(2,1)S(1)} %add.66), channel_id=1, source_target_pairs={{0,2},{1,3},{2,0},{3,1},{4,6},{5,7},{6,4},{7,5},{8,10},{9,11},{10,... | collective-permute-start | bytes 147464 | tf_op jit(solution)/shard_map/ppermute | solution.py:29
  99.3 0.1 slice_reduce_fusion.1
  99.4 2.4 %collective-permute-done.17 = bf16[32,768]{1,0:T(8,128)(2,1)S(1)} collective-permute-done((bf16[32,768]{1,0:T(8,128)(2,1)S(1)}, bf16[32,768]{1,0:T(8,128)(2,1)S(1)}, u32[]{:S(2)}, u32[]{:S(2)}) %collective-permute-start.17) | collective-permute-done | bytes 49184 | tf_op jit(solution)/shard_map/ppermute | solution.py:29
  101.9 1.1 collective-permute-start.18
  103.0 1.9 %multiply_add_fusion = f32[10,256,256]{2,1,0:T(8,128)} fusion(f32[256,256]{1,0:T(8,128)S(1)} %slice.88, f32[10]{0:T(128)S(1)} %get-tuple-element.159, f32[256,256]{1,0:T(8,128)S(1)} %slice.86, f32[10]{0:T(128)S(1)} %get-tuple-element.160), kind=kLoop, calls=%fused_computation | loop fusion | flops 1966080 | bytes 3145808 | tf_op jit(solution)/shard_map/add | solution.py:53
  104.9 1.5 %collective-permute-start.19 = (f32[192,256]{1,0:T(8,128)S(1)}, f32[192,256]{1,0:T(8,128)S(1)}, u32[]{:S(2)}, u32[]{:S(2)}) collective-permute-start(f32[192,256]{1,0:T(8,128)S(1)} %add_add_fusion), channel_id=1, source_target_pairs={{0,2},{1,3},{2,0},{3,1},{4,6},{5,7},{6,4},{7,5},{8,10},{9,11},{10,... | collective-permute-start | bytes 589832 | tf_op jit(solution)/shard_map/ppermute | solution.py:29
  106.4 4.1 %collective-permute-done.19 = f32[192,256]{1,0:T(8,128)S(1)} collective-permute-done((f32[192,256]{1,0:T(8,128)S(1)}, f32[192,256]{1,0:T(8,128)S(1)}, u32[]{:S(2)}, u32[]{:S(2)}) %collective-permute-start.19) | collective-permute-done | bytes 196640 | tf_op jit(solution)/shard_map/ppermute | solution.py:29
  110.6 2.1 %collective-permute-start.21 = (bf16[32,768]{1,0:T(8,128)(2,1)S(1)}, bf16[32,768]{1,0:T(8,128)(2,1)S(1)}, u32[]{:S(2)}, u32[]{:S(2)}) collective-permute-start(bf16[32,768]{1,0:T(8,128)(2,1)S(1)} %convert_add_fusion.2), channel_id=1, source_target_pairs={{0,8},{4,12},{8,0},{12,4},{1,9},{5,13},{9,1},{13,5},{2,10},{6,14},... | collective-permute-start | bytes 147464 | tf_op jit(solution)/shard_map/ppermute | solution.py:29
  112.7 0.4 collective-permute-start.20
  113.1 1.9 %collective-permute-start.22 = (bf16[32,768]{1,0:T(8,128)(2,1)S(1)}, bf16[32,768]{1,0:T(8,128)(2,1)S(1)}, u32[]{:S(2)}, u32[]{:S(2)}) collective-permute-start(bf16[32,768]{1,0:T(8,128)(2,1)S(1)} %convert_add_fusion.2), channel_id=1, source_target_pairs={{0,12},{4,8},{8,4},{12,0},{1,13},{5,9},{9,5},{13,1},{2,14},{6,10},... | collective-permute-start | bytes 147464 | tf_op jit(solution)/shard_map/ppermute | solution.py:29
  115.1 0.5 slice.97
  116.2 0.6 collective-permute-done.20
  116.8 2.2 %collective-permute-done.22 = bf16[32,768]{1,0:T(8,128)(2,1)S(1)} collective-permute-done((bf16[32,768]{1,0:T(8,128)(2,1)S(1)}, bf16[32,768]{1,0:T(8,128)(2,1)S(1)}, u32[]{:S(2)}, u32[]{:S(2)}) %collective-permute-start.22) | collective-permute-done | bytes 49184 | tf_op jit(solution)/shard_map/ppermute | solution.py:29
  119.0 0.1 collective-permute-start.23
  119.1 0.6 slice_reduce_fusion
  119.7 0.5 collective-permute-start.24
  120.2 0.2 collective-permute-done.23
  120.4 0.6 slice.99
  121.0 0.7 reshape.57
  121.7 0.6 slice_reduce_fusion.3
  122.4 0.9 pad_maximum_fusion
  (62 shorter events, 0.7 us)
Async XLA Ops:
  0.6 14.1 %copy-start = (bf16[1,16,64,768]{3,2,1,0:T(8,128)(2,1)S(1)}, bf16[1,16,64,768]{3,2,1,0:T(8,128)(2,1)}, u32[]{:S(2)}) copy-start(bf16[1,16,64,768]{3,2,1,0:T(8,128)(2,1)} %param.8) | copy-start | bytes 4718596
  0.6 14.1 %copy-start.4 = (f32[256]{0:T(256)S(1)}, f32[256]{0:T(256)}, u32[]{:S(2)}) copy-start(f32[256]{0:T(256)} %param.12) | copy-start | bytes 3076
  0.7 14.1 %copy-start.2 = (bf16[768,256]{1,0:T(8,128)(2,1)S(1)}, bf16[768,256]{1,0:T(8,128)(2,1)}, u32[]{:S(2)}) copy-start(bf16[768,256]{1,0:T(8,128)(2,1)} %reduce_weight.5) | copy-start | bytes 1179652
  0.7 14.1 %copy-start.3 = (f32[7,7,768]{2,1,0:T(8,128)S(1)}, f32[7,7,768]{2,1,0:T(8,128)}, u32[]{:S(2)}) copy-start(f32[7,7,768]{2,1,0:T(8,128)} %weight.3) | copy-start | bytes 451588
  1.9 5.5 %collective-permute-start = (bf16[16,3,768]{2,1,0:T(4,128)(2,1)S(1)}, bf16[16,3,768]{2,1,0:T(4,128)(2,1)S(1)}, u32[]{:S(2)}, u32[]{:S(2)}) collective-permute-start(bf16[16,3,768]{2,1,0:T(4,128)(2,1)S(1)} %get-tuple-element.145), channel_id=1, source_target_pairs={{0,1},{1,2},{2,3},{4,5},{5,6},{6,7},{8,9},{9,10},{10,11},{12,13},{... | collective-permute-start | bytes 221192 | tf_op jit(solution)/shard_map/ppermute | solution.py:78
  4.3 5.3 %collective-permute-start.1 = (bf16[16,3,768]{2,1,0:T(4,128)(2,1)S(1)}, bf16[16,3,768]{2,1,0:T(4,128)(2,1)S(1)}, u32[]{:S(2)}, u32[]{:S(2)}) collective-permute-start(bf16[16,3,768]{2,1,0:T(4,128)(2,1)S(1)} %get-tuple-element.146), channel_id=1, source_target_pairs={{1,0},{2,1},{3,2},{5,4},{6,5},{7,6},{9,8},{10,9},{11,10},{13,12},{... | collective-permute-start | bytes 221192 | tf_op jit(solution)/shard_map/ppermute | solution.py:82
  9.9 16.8 %collective-permute-start.2 = (bf16[224,768]{1,0:T(8,128)(2,1)S(1)}, bf16[224,768]{1,0:T(8,128)(2,1)S(1)}, u32[]{:S(2)}, u32[]{:S(2)}) collective-permute-start(bf16[224,768]{1,0:T(8,128)(2,1)S(1)} %get-tuple-element.81), channel_id=1, source_target_pairs={{0,4},{4,8},{8,12},{1,5},{5,9},{9,13},{2,6},{6,10},{10,14},{3,7},{... | collective-permute-start | bytes 1032200 | tf_op jit(solution)/shard_map/ppermute | solution.py:78
  13.4 13.3 %collective-permute-start.3 = (bf16[224,768]{1,0:T(8,128)(2,1)S(1)}, bf16[224,768]{1,0:T(8,128)(2,1)S(1)}, u32[]{:S(2)}, u32[]{:S(2)}) collective-permute-start(bf16[224,768]{1,0:T(8,128)(2,1)S(1)} %get-tuple-element.82), channel_id=1, source_target_pairs={{4,0},{8,4},{12,8},{5,1},{9,5},{13,9},{6,2},{10,6},{14,10},{7,3},{... | collective-permute-start | bytes 1032200 | tf_op jit(solution)/shard_map/ppermute | solution.py:82
  31.6 2.4 %copy-start.6 = (f32[6,16,14,8,128]{4,3,2,1,0:T(8,128)}, f32[6,16,14,8,128]{4,3,2,1,0:T(8,128)S(1)}, u32[]{:S(2)}) copy-start(f32[6,16,14,8,128]{4,3,2,1,0:T(8,128)S(1)} %get-tuple-element.80.spread_in) | copy-start | bytes 16515076
  34.0 21.5 %copy-start.8 = (f32[6,3,14,8,128]{4,3,2,1,0:T(8,128)}, f32[6,3,14,8,128]{4,3,2,1,0:T(8,128)S(1)}, u32[]{:S(2)}) copy-start(f32[6,3,14,8,128]{4,3,2,1,0:T(8,128)S(1)} %get-tuple-element.115.spread_bottom) | copy-start | bytes 3096580
  34.0 21.5 %copy-start.1 = (bf16[10,256,256]{2,1,0:T(8,128)(2,1)S(1)}, bf16[10,256,256]{2,1,0:T(8,128)(2,1)}, u32[]{:S(2)}) copy-start(bf16[10,256,256]{2,1,0:T(8,128)(2,1)} %class_weight.1) | copy-start | bytes 3932164
  34.0 21.5 %copy-start.5 = (f32[10]{0:T(128)S(1)}, f32[10]{0:T(128)}, u32[]{:S(2)}) copy-start(f32[10]{0:T(128)} %class_bias.1) | copy-start | bytes 124
  34.0 3.9 %collective-permute-start.4 = (f32[104,256]{1,0:T(8,128)S(1)}, f32[104,256]{1,0:T(8,128)S(1)}, u32[]{:S(2)}, u32[]{:S(2)}) collective-permute-start(f32[104,256]{1,0:T(8,128)S(1)} %get-tuple-element.86), channel_id=1, source_target_pairs={{0,1},{1,0},{2,3},{3,2},{4,5},{5,4},{6,7},{7,6},{8,9},{9,8},{10,11... | collective-permute-start | bytes 319496 | tf_op jit(solution)/shard_map/ppermute | solution.py:29
  37.9 5.3 %collective-permute-start.5 = (f32[104,256]{1,0:T(8,128)S(1)}, f32[104,256]{1,0:T(8,128)S(1)}, u32[]{:S(2)}, u32[]{:S(2)}) collective-permute-start(f32[104,256]{1,0:T(8,128)S(1)} %add.55), channel_id=1, source_target_pairs={{0,2},{1,3},{2,0},{3,1},{4,6},{5,7},{6,4},{7,5},{8,10},{9,11},{10,... | collective-permute-start | bytes 319496 | tf_op jit(solution)/shard_map/ppermute | solution.py:29
  43.2 5.1 %collective-permute-start.6 = (f32[104,256]{1,0:T(8,128)S(1)}, f32[104,256]{1,0:T(8,128)S(1)}, u32[]{:S(2)}, u32[]{:S(2)}) collective-permute-start(f32[104,256]{1,0:T(8,128)S(1)} %add.56), channel_id=1, source_target_pairs={{0,4},{4,0},{8,12},{12,8},{1,5},{5,1},{9,13},{13,9},{2,6},{6,2},{1... | collective-permute-start | bytes 319496 | tf_op jit(solution)/shard_map/ppermute | solution.py:29
  48.4 5.8 %collective-permute-start.7 = (f32[104,256]{1,0:T(8,128)S(1)}, f32[104,256]{1,0:T(8,128)S(1)}, u32[]{:S(2)}, u32[]{:S(2)}) collective-permute-start(f32[104,256]{1,0:T(8,128)S(1)} %add.57), channel_id=1, source_target_pairs={{0,8},{4,12},{8,0},{12,4},{1,9},{5,13},{9,1},{13,5},{2,10},{6,14},... | collective-permute-start | bytes 319496 | tf_op jit(solution)/shard_map/ppermute | solution.py:29
  54.1 1.4 %collective-permute-start.8 = (f32[104,256]{1,0:T(8,128)S(1)}, f32[104,256]{1,0:T(8,128)S(1)}, u32[]{:S(2)}, u32[]{:S(2)}) collective-permute-start(f32[104,256]{1,0:T(8,128)S(1)} %add.58.own), channel_id=1, source_target_pairs={{0,1},{1,0},{2,3},{3,2},{4,5},{5,4},{6,7},{7,6},{8,9},{9,8},{10,11... | collective-permute-start | bytes 319496 | tf_op jit(solution)/shard_map/ppermute | solution.py:29
  55.5 15.0 %copy-start.9 = (f32[6,3,14,8,128]{4,3,2,1,0:T(8,128)S(1)}, f32[6,3,14,8,128]{4,3,2,1,0:T(8,128)}, u32[]{:S(2)}) copy-start(f32[6,3,14,8,128]{4,3,2,1,0:T(8,128)} %copy-done.8) | copy-start | bytes 3096580
  65.2 1.0 copy-start.10
  66.2 0.8 copy-start.12
  67.0 1.9 %collective-permute-start.9 = (f32[384,256]{1,0:T(8,128)S(1)}, f32[384,256]{1,0:T(8,128)}, u32[]{:S(2)}, u32[]{:S(2)}) collective-permute-start(f32[384,256]{1,0:T(8,128)S(1)} %get-tuple-element.108), channel_id=1, source_target_pairs={{0,1},{1,0},{2,3},{3,2},{4,5},{5,4},{6,7},{7,6},{8,9},{9,8},{10,11... | collective-permute-start | bytes 1179656 | tf_op jit(solution)/shard_map/ppermute | solution.py:29
  67.1 29.2 %collective-permute-start.15 = (f32[272,256]{1,0:T(8,128)S(1)}, f32[272,256]{1,0:T(8,128)S(1)}, u32[]{:S(2)}, u32[]{:S(2)}) collective-permute-start(f32[272,256]{1,0:T(8,128)S(1)} %get-tuple-element.134), channel_id=1, source_target_pairs={{0,16},{16,0},{1,17},{17,1},{2,18},{18,2},{3,19},{19,3},{4,20},{20... | collective-permute-start | bytes 835592 | tf_op jit(solution)/shard_map/ppermute | solution.py:29
  69.9 9.1 %collective-permute-start.10 = (bf16[192,256]{1,0:T(8,128)(2,1)S(1)}, bf16[192,256]{1,0:T(8,128)(2,1)S(1)}, u32[]{:S(2)}, u32[]{:S(2)}) collective-permute-start(bf16[192,256]{1,0:T(8,128)(2,1)S(1)} %select_convert_fusion), channel_id=1, source_target_pairs={{0,2},{1,3},{2,0},{3,1},{4,6},{5,7},{6,4},{7,5},{8,10},{9,11},{10,... | collective-permute-start | bytes 294920 | tf_op jit(solution)/shard_map/ppermute | solution.py:29
  70.5 2.6 %copy-start.7 = (f32[6,16,14,8,128]{4,3,2,1,0:T(8,128)S(1)}, f32[6,16,14,8,128]{4,3,2,1,0:T(8,128)}, u32[]{:S(2)}) copy-start(f32[6,16,14,8,128]{4,3,2,1,0:T(8,128)} %copy-done.6) | copy-start | bytes 16515076
  73.1 1.2 copy-start.11
  74.3 1.1 copy-start.13
  79.1 5.1 %collective-permute-start.11 = (bf16[192,256]{1,0:T(8,128)(2,1)S(1)}, bf16[192,256]{1,0:T(8,128)(2,1)S(1)}, u32[]{:S(2)}, u32[]{:S(2)}) collective-permute-start(bf16[192,256]{1,0:T(8,128)(2,1)S(1)} %convert_add_fusion.1), channel_id=1, source_target_pairs={{0,16},{16,0},{1,17},{17,1},{2,18},{18,2},{3,19},{19,3},{4,20},{20... | collective-permute-start | bytes 294920 | tf_op jit(solution)/shard_map/ppermute | solution.py:29
  84.2 9.1 %collective-permute-start.13 = (bf16[192,256]{1,0:T(8,128)(2,1)S(1)}, bf16[192,256]{1,0:T(8,128)(2,1)S(1)}, u32[]{:S(2)}, u32[]{:S(2)}) collective-permute-start(bf16[192,256]{1,0:T(8,128)(2,1)S(1)} %convert_add_fusion), channel_id=1, source_target_pairs={{0,8},{4,12},{8,0},{12,4},{1,9},{5,13},{9,1},{13,5},{2,10},{6,14},... | collective-permute-start | bytes 294920 | tf_op jit(solution)/shard_map/ppermute | solution.py:29
  87.3 6.0 %collective-permute-start.12 = (bf16[192,256]{1,0:T(8,128)(2,1)S(1)}, bf16[192,256]{1,0:T(8,128)(2,1)S(1)}, u32[]{:S(2)}, u32[]{:S(2)}) collective-permute-start(bf16[192,256]{1,0:T(8,128)(2,1)S(1)} %convert_add_fusion), channel_id=1, source_target_pairs={{0,4},{4,0},{8,12},{12,8},{1,5},{5,1},{9,13},{13,9},{2,6},{6,2},{1... | collective-permute-start | bytes 294920 | tf_op jit(solution)/shard_map/ppermute | solution.py:29
  89.8 6.4 %collective-permute-start.14 = (bf16[192,256]{1,0:T(8,128)(2,1)S(1)}, bf16[192,256]{1,0:T(8,128)(2,1)S(1)}, u32[]{:S(2)}, u32[]{:S(2)}) collective-permute-start(bf16[192,256]{1,0:T(8,128)(2,1)S(1)} %convert_add_fusion), channel_id=1, source_target_pairs={{0,12},{4,8},{8,4},{12,0},{1,13},{5,9},{9,5},{13,1},{2,14},{6,10},... | collective-permute-start | bytes 294920 | tf_op jit(solution)/shard_map/ppermute | solution.py:29
  96.3 1.4 %collective-permute-start.16 = (f32[32,768]{1,0:T(8,128)S(1)}, f32[32,768]{1,0:T(8,128)S(1)}, u32[]{:S(2)}, u32[]{:S(2)}) collective-permute-start(f32[32,768]{1,0:T(8,128)S(1)} %get-tuple-element.137), channel_id=1, source_target_pairs={{0,1},{1,0},{2,3},{3,2},{4,5},{5,4},{6,7},{7,6},{8,9},{9,8},{10,11... | collective-permute-start | bytes 294920 | tf_op jit(solution)/shard_map/ppermute | solution.py:29
  97.7 4.2 %collective-permute-start.17 = (bf16[32,768]{1,0:T(8,128)(2,1)S(1)}, bf16[32,768]{1,0:T(8,128)(2,1)S(1)}, u32[]{:S(2)}, u32[]{:S(2)}) collective-permute-start(bf16[32,768]{1,0:T(8,128)(2,1)S(1)} %add.66), channel_id=1, source_target_pairs={{0,2},{1,3},{2,0},{3,1},{4,6},{5,7},{6,4},{7,5},{8,10},{9,11},{10,... | collective-permute-start | bytes 147464 | tf_op jit(solution)/shard_map/ppermute | solution.py:29
  101.9 4.5 %collective-permute-start.18 = (bf16[32,768]{1,0:T(8,128)(2,1)S(1)}, bf16[32,768]{1,0:T(8,128)(2,1)S(1)}, u32[]{:S(2)}, u32[]{:S(2)}) collective-permute-start(bf16[32,768]{1,0:T(8,128)(2,1)S(1)} %add_convert_fusion), channel_id=1, source_target_pairs={{0,16},{16,0},{1,17},{17,1},{2,18},{18,2},{3,19},{19,3},{4,20},{20... | collective-permute-start | bytes 147464 | tf_op jit(solution)/shard_map/ppermute | solution.py:29
  104.9 5.7 %collective-permute-start.19 = (f32[192,256]{1,0:T(8,128)S(1)}, f32[192,256]{1,0:T(8,128)S(1)}, u32[]{:S(2)}, u32[]{:S(2)}) collective-permute-start(f32[192,256]{1,0:T(8,128)S(1)} %add_add_fusion), channel_id=1, source_target_pairs={{0,2},{1,3},{2,0},{3,1},{4,6},{5,7},{6,4},{7,5},{8,10},{9,11},{10,... | collective-permute-start | bytes 589832 | tf_op jit(solution)/shard_map/ppermute | solution.py:29
  110.6 5.6 %collective-permute-start.21 = (bf16[32,768]{1,0:T(8,128)(2,1)S(1)}, bf16[32,768]{1,0:T(8,128)(2,1)S(1)}, u32[]{:S(2)}, u32[]{:S(2)}) collective-permute-start(bf16[32,768]{1,0:T(8,128)(2,1)S(1)} %convert_add_fusion.2), channel_id=1, source_target_pairs={{0,8},{4,12},{8,0},{12,4},{1,9},{5,13},{9,1},{13,5},{2,10},{6,14},... | collective-permute-start | bytes 147464 | tf_op jit(solution)/shard_map/ppermute | solution.py:29
  112.7 4.1 %collective-permute-start.20 = (bf16[32,768]{1,0:T(8,128)(2,1)S(1)}, bf16[32,768]{1,0:T(8,128)(2,1)S(1)}, u32[]{:S(2)}, u32[]{:S(2)}) collective-permute-start(bf16[32,768]{1,0:T(8,128)(2,1)S(1)} %convert_add_fusion.2), channel_id=1, source_target_pairs={{0,4},{4,0},{8,12},{12,8},{1,5},{5,1},{9,13},{13,9},{2,6},{6,2},{1... | collective-permute-start | bytes 147464 | tf_op jit(solution)/shard_map/ppermute | solution.py:29
  113.1 5.9 %collective-permute-start.22 = (bf16[32,768]{1,0:T(8,128)(2,1)S(1)}, bf16[32,768]{1,0:T(8,128)(2,1)S(1)}, u32[]{:S(2)}, u32[]{:S(2)}) collective-permute-start(bf16[32,768]{1,0:T(8,128)(2,1)S(1)} %convert_add_fusion.2), channel_id=1, source_target_pairs={{0,12},{4,8},{8,4},{12,0},{1,13},{5,9},{9,5},{13,1},{2,14},{6,10},... | collective-permute-start | bytes 147464 | tf_op jit(solution)/shard_map/ppermute | solution.py:29
  119.0 1.4 %collective-permute-start.23 = (f32[32,768]{1,0:T(8,128)S(1)}, f32[32,768]{1,0:T(8,128)S(1)}, u32[]{:S(2)}, u32[]{:S(2)}) collective-permute-start(f32[32,768]{1,0:T(8,128)S(1)} %add_add_fusion.1), channel_id=1, source_target_pairs={{0,1},{1,0},{2,3},{3,2},{4,5},{5,4},{6,7},{7,6},{8,9},{9,8},{10,11... | collective-permute-start | bytes 294920 | tf_op jit(solution)/shard_map/ppermute | solution.py:29
  119.7 2.6 %collective-permute-start.24 = (f32[384,256]{1,0:T(8,128)S(1)}, f32[384,256]{1,0:T(8,128)S(1)}, u32[]{:S(2)}, u32[]{:S(2)}) collective-permute-start(f32[384,256]{1,0:T(8,128)S(1)} %pad_maximum_fusion.1), channel_id=1, source_target_pairs={{0,1},{1,0},{2,3},{3,2},{4,5},{5,4},{6,7},{7,6},{8,9},{9,8},{10,11... | collective-permute-start | bytes 1179656 | tf_op jit(solution)/shard_map/ppermute | solution.py:29

commit v4 on v3

--- a/solution.py
+++ b/solution.py
@@ -33,8 +33,7 @@
     return (lax.axis_index(axis) & shift) != 0
 
 
-def halve(value, axis, shift, sent_as):
-    upper = is_upper(axis, shift)
+def halve(value, axis, shift, upper, sent_as):
     rows = value.shape[0] // 2
     low, high = value[:rows], value[rows:]
     kept = jnp.where(upper, high, low)
@@ -42,8 +41,7 @@
     return kept + swap(sent, axis, shift).astype(wide)
 
 
-def unhalve(value, axis, shift):
-    upper = is_upper(axis, shift)
+def unhalve(value, axis, shift, upper):
     other = swap(value, axis, shift)
     return jnp.concatenate([jnp.where(upper, other, value), jnp.where(upper, value, other)])
 
@@ -105,15 +103,19 @@
             spread_ref[row_tap * KERNEL + col_tap] = jnp.broadcast_to(scale, spread_ref.shape[1:])
 
 
-def conv_row(load, spread_ref, bias, steps):
-    total = [bias] * steps
-    for row_tap in range(KERNEL):
-        windows = [load(row_tap, group) for group in range(steps + KERNEL - 1)]
-        for col_tap in range(KERNEL):
-            scale = spread_ref[row_tap * KERNEL + col_tap]
-            for step in range(steps):
-                total[step] = total[step] + windows[step + col_tap] * scale
-    return jnp.concatenate(total, axis=0).astype(narrow)
+def conv_rows(load, spread_ref, bias, steps, count):
+    total = [[bias] * steps for _ in range(count)]
+    for place in range(KERNEL + count - 1):
+        windows = [load(place, group) for group in range(steps + KERNEL - 1)]
+        for row in range(count):
+            row_tap = place - row
+            if not 0 <= row_tap < KERNEL:
+                continue
+            for col_tap in range(KERNEL):
+                scale = spread_ref[row_tap * KERNEL + col_tap]
+                for step in range(steps):
+                    total[row][step] = total[row][step] + windows[step + col_tap] * scale
+    return jnp.concatenate([part for row in total for part in row], axis=0).astype(narrow)
 
 
 def reduce_part(conv_out, reduce_ref, reduce_bias_ref, before_out, feat_out):
@@ -133,6 +135,8 @@
 ):
     rows, cols = block.shape[0], block.shape[1]
     steps = cols // GROUPS
+    inner = rows - 2 * HALF
+    at_once = 2 if inner % 2 == 0 else 1
 
     def one_tile(tile, _):
         lanes = lanes_of(tile)
@@ -151,11 +155,13 @@
             def load(row_tap, group):
                 return spread_out[tile, index + row_tap, group]
 
-            start = pl.multiple_of(index * cols, cols)
-            conv_out[pl.ds(start, cols), lanes] = conv_row(load, spread_weight, start_value, steps)
+            start = pl.multiple_of(index * cols, at_once * cols)
+            conv_out[pl.ds(start, at_once * cols), lanes] = conv_rows(
+                load, spread_weight, start_value, steps, at_once
+            )
             return 0
 
-        lax.fori_loop(0, rows - 2 * HALF, one_row, 0)
+        lax.fori_loop(0, inner // at_once, lambda turn, _: one_row(turn * at_once, 0), 0)
         return 0
 
     lax.fori_loop(0, spread_out.shape[0], one_tile, 0)
@@ -196,9 +202,10 @@
 
             return load
 
-        for index, row in enumerate(edge_rows(rows)):
-            conv_out[index * cols : (index + 1) * cols, lanes] = conv_row(
-                load_from(row), spread_weight, start_value, steps
+        for side, row in enumerate((0, rows - HALF)):
+            start = side * HALF * cols
+            conv_out[start : start + HALF * cols, lanes] = conv_rows(
+                load_from(row), spread_weight, start_value, steps, HALF
             )
         return 0
 
@@ -599,6 +606,36 @@
     )(flag, *spreads, *grads, bias_grad, *filled)
 
 
+def finish_kernel(flag, own, other, depth_out, depth_bias_out, bias_out, sums):
+    part = own.shape[0]
+    upper = flag[0] != 0
+    sums[:part, :] = jnp.where(upper, other[...], own[...])
+    sums[part:, :] = jnp.where(upper, own[...], other[...])
+    for row_tap in range(KERNEL):
+        depth_out[row_tap] = sums[row_tap * KERNEL : (row_tap + 1) * KERNEL, :]
+    taps = KERNEL * KERNEL
+    depth_bias_out[...] = sums[taps : taps + 1, :]
+    bias_out[...] = sums[taps + 1 : taps + 2, : bias_out.shape[1]]
+
+
+def finish(flag, own, other, width):
+    part, channels = own.shape
+    return pl.pallas_call(
+        finish_kernel,
+        in_specs=[in_smem] + [in_vmem] * 2,
+        out_specs=[in_vmem] * 3,
+        out_shape=[
+            shape_of((KERNEL, KERNEL, channels)),
+            shape_of((1, channels)),
+            shape_of((1, width)),
+        ],
+        scratch_shapes=[pltpu.VMEM((2 * part, channels), wide)],
+        compiler_params=params(8),
+        cost_estimate=cost(1),
+        name="finish",
+    )(flag, own, other)
+
+
 def edge_strip(block, left, right, rows):
     channels = block.shape[2]
     parts = [part[rows].reshape(-1, channels) for part in (block, left, right)]
@@ -618,21 +655,24 @@
     image_count = features.shape[0] * lax.axis_size("dp")
 
     flag = is_upper("sx", 1).astype(jnp.int32)[None]
+    uppers = [is_upper("sx", shift) for shift in doublings("sx")]
     bias_row = depth_bias[None]
     reduce_row = reduce_bias[None]
     left = next_along(block[:, cols - HALF :], "sx")
     right = back_along(block[:, :HALF], "sx")
-    low, high, left, right, flag, bias_row, reduce_row = together(
+    low, high, left, right, flag, uppers, bias_row, reduce_row = together(
         (
             edge_strip(block, left, right, slice(rows - HALF, rows)),
             edge_strip(block, left, right, slice(0, HALF)),
             left,
             right,
             flag,
+            uppers,
             bias_row,
             reduce_row,
         )
     )
+    uppers = dict(zip(doublings("sx"), uppers))
     top = next_along(low, "sy")
     bottom = back_along(high, "sy")
     spread, conv_in, before_in, feat_in, gram, colsum = conv_inner(
@@ -685,7 +725,7 @@
 
     sums = kept + swap(sent, "sx", 1)
     for shift in doublings("sx", 2):
-        sums = halve(beside(sums), "sx", shift, narrow)
+        sums = halve(beside(sums), "sx", shift, uppers[shift], narrow)
     for shift in doublings("dp"):
         sums = exchange(beside(sums), "dp", shift, narrow)
     sums = exchange_all(beside(sums), "sy", narrow)
@@ -702,23 +742,24 @@
     loss = totals[classes] / image_count
     small, sums = together((small, sums))
     for shift in reversed(doublings("sx", 2)):
-        sums = unhalve(sums, "sx", shift)
+        sums = unhalve(sums, "sx", shift, uppers[shift])
     for shift in doublings("sx", 2):
         small = exchange(small, "sx", shift, narrow)
     for shift in doublings("dp"):
         small = exchange(small, "dp", shift, narrow)
     small, sums = together((small, sums))
-    weight_grad = unhalve(sums, "sx", 1)
+    weight_grad = unhalve(sums, "sx", 1, uppers[1])
     small = exchange_all(small, "sy", narrow)
-    small = unhalve(small, "sx", 1)
-
-    taps = KERNEL * KERNEL
+    small, weight_grad, class_weight_grad, class_bias_grad, loss = together(
+        (small, weight_grad, class_weight_grad, class_bias_grad, loss)
+    )
+    depth_grad, depth_bias_grad, bias_grad = finish(flag, small, swap(small, "sx", 1), width)
     return (
         loss,
-        small[:taps].reshape(depth_weight.shape),
-        small[taps],
+        depth_grad,
+        depth_bias_grad[0],
         weight_grad,
-        small[taps + 1, :width],
+        bias_grad[0],
         class_weight_grad,
         class_bias_grad,
     )

time: 125 us -> 114 us (0.912)
  local copies, waits for them, and re-layouts: 15.4 us -> 4.56 us
  waiting for transfers between devices: 26.8 us -> 28.4 us
  starting transfers between devices: 36.2 us -> 34.7 us
    unnamed x28 -> x12, local copies, waits for them, and re-layouts: 9.02 us -> 0.03 us
    ppermute x21, waiting for transfers between devices: 24.7 us -> 26.3 us  [swap(): return lax.ppermute(value, axis, [(i, i ^ shift) for i in range(count)])]
    ppermute x21, starting transfers between devices: 27.7 us -> 26.2 us  [swap(): return lax.ppermute(value, axis, [(i, i ^ shift) for i in range(count)])]
  transfers between devices with their start and end apart: 25 -> 25, of which waited for: 14 -> 16; matrix products, arithmetic and copies ran while one was open for 7% -> 5% of each run, Pallas kernels for 19% -> 21%
where the time goes in v4:
time: 114 us
  Pallas kernels  38.7 us (34%)
  starting transfers between devices  34.7 us (30%)
  waiting for transfers between devices  28.4 us (25%)
  local copies, waits for them, and re-layouts  4.56 us (4%)
  other arithmetic  4.03 us (4%)
  between operations  3.43 us (3%)
    ppermute x21, waiting for transfers between devices, swap(): return lax.ppermute(value, axis, [(i, i ^ shift) for i in range(count)])  26.3 us
    ppermute x21, starting transfers between devices, swap(): return lax.ppermute(value, axis, [(i, i ^ shift) for i in range(count)])  26.2 us
    pallas_call x1, Pallas kernels, conv_inner(): pl.pallas_call(inner_kernel, in_specs=[in_vmem] * 7, out_specs=[in_vmem]...  11.5 us
    pallas_call x3, Pallas kernels, tap_grads(): pl.pallas_call(functools.partial(taps_kernel, first=first, many=many), in...  11 us
    pallas_call x1, Pallas kernels, head(): pl.pallas_call(functools.partial(head_kernel, count=count, image_count=im...  9.67 us
    ppermute x2, starting transfers between devices, next_along(): lax.ppermute(value, axis, [(i, i + 1) for i in range(lax.axis_size(axis)...  5.86 us
    pallas_call x1, Pallas kernels, conv_edge(): pl.pallas_call(edge_kernel, in_specs=[in_smem] + [in_vmem] * 9, out_specs...  4.78 us
    ppermute x2, starting transfers between devices, back_along(): lax.ppermute(value, axis, [(i + 1, i) for i in range(lax.axis_size(axis)...  2.58 us
  transfers between devices with their start and end apart: 25, of which 16 were waited for; matrix products, arithmetic and copies ran while one was open for 5% of the time, Pallas kernels for 21%

profile of v4, /device:TPU:0, one launch (start us, length us, event | category | flops | bytes accessed | tf_op | source)
XLA Modules:
  0.0 113.8 jit_solution(6482082368682564792)
XLA Ops:
  0.6 0.0 copy-start
  0.7 1.2 %fusion.1 = (bf16[16,3,768]{2,1,0:T(4,128)(2,1)S(1)}, bf16[16,3,768]{2,1,0:T(4,128)(2,1)S(1)}) fusion(bf16[16,64,768]{2,1,0:T(8,128)(2,1)} %bitcast.7), kind=kLoop, calls=%fused_computation.21 | loop fusion | bytes 294912 | tf_op jit(solution)/shard_map/slice | solution.py:661
  1.9 2.4 %collective-permute-start = (bf16[16,3,768]{2,1,0:T(4,128)(2,1)S(1)}, bf16[16,3,768]{2,1,0:T(4,128)(2,1)S(1)}, u32[]{:S(2)}, u32[]{:S(2)}) collective-permute-start(bf16[16,3,768]{2,1,0:T(4,128)(2,1)S(1)} %get-tuple-element.165), channel_id=1, source_target_pairs={{0,1},{1,2},{2,3},{4,5},{5,6},{6,7},{8,9},{9,10},{10,11},{12,13},{... | collective-permute-start | bytes 221192 | tf_op jit(solution)/shard_map/ppermute | solution.py:76
  4.3 1.3 %collective-permute-start.1 = (bf16[16,3,768]{2,1,0:T(4,128)(2,1)S(1)}, bf16[16,3,768]{2,1,0:T(4,128)(2,1)S(1)}, u32[]{:S(2)}, u32[]{:S(2)}) collective-permute-start(bf16[16,3,768]{2,1,0:T(4,128)(2,1)S(1)} %get-tuple-element.166), channel_id=1, source_target_pairs={{1,0},{2,1},{3,2},{5,4},{6,5},{7,6},{9,8},{10,9},{11,10},{13,12},{... | collective-permute-start | bytes 221192 | tf_op jit(solution)/shard_map/ppermute | solution.py:80
  5.6 1.1 fusion
  6.7 0.7 broadcast_in_dim.16.bias
  7.4 0.1 pad.11.clone
  7.5 0.0 collective-permute-done.left
  7.6 2.1 %collective-permute-done.1.right = bf16[16,3,768]{2,1,0:T(4,128)(2,1)S(1)} collective-permute-done((bf16[16,3,768]{2,1,0:T(4,128)(2,1)S(1)}, bf16[16,3,768]{2,1,0:T(4,128)(2,1)S(1)}, u32[]{:S(2)}, u32[]{:S(2)}) %collective-permute-start.1) | collective-permute-done | bytes 73760 | tf_op jit(solution)/shard_map/ppermute | solution.py:80
  9.7 0.2 maximum_maximum_fusion.1
  9.9 3.5 %collective-permute-start.2 = (bf16[224,768]{1,0:T(8,128)(2,1)S(1)}, bf16[224,768]{1,0:T(8,128)(2,1)S(1)}, u32[]{:S(2)}, u32[]{:S(2)}) collective-permute-start(bf16[224,768]{1,0:T(8,128)(2,1)S(1)} %get-tuple-element.92), channel_id=1, source_target_pairs={{0,4},{4,8},{8,12},{1,5},{5,9},{9,13},{2,6},{6,10},{10,14},{3,7},{... | collective-permute-start | bytes 1032200 | tf_op jit(solution)/shard_map/ppermute | solution.py:76
  13.4 1.3 %collective-permute-start.3 = (bf16[224,768]{1,0:T(8,128)(2,1)S(1)}, bf16[224,768]{1,0:T(8,128)(2,1)S(1)}, u32[]{:S(2)}, u32[]{:S(2)}) collective-permute-start(bf16[224,768]{1,0:T(8,128)(2,1)S(1)} %get-tuple-element.93), channel_id=1, source_target_pairs={{4,0},{8,4},{12,8},{5,1},{9,5},{13,9},{6,2},{10,6},{14,10},{7,3},{... | collective-permute-start | bytes 1032200 | tf_op jit(solution)/shard_map/ppermute | solution.py:80
  14.7 11.5 %conv_inner.1 = (f32[6,16,14,8,128]{4,3,2,1,0:T(8,128)S(1)}, bf16[640,768]{1,0:T(8,128)(2,1)S(1)}, f32[640,256]{1,0:T(8,128)S(1)}, bf16[640,256]{1,0:T(8,128)(2,...) custom-call(bf16[16,64,768]{2,1,0:T(8,128)(2,1)S(1)} %bitcast.8, ...), custom_call_target="tpu_custom_call" | custom-call | flops 10000000000 | bytes 10000000 | tf_op jit(solution)/shard_map/conv_inner/pallas_call | solution.py:258
  26.3 4.8 %conv_edge.1 = (f32[6,3,14,8,128]{4,3,2,1,0:T(8,128)S(1)}, f32[6,3,14,8,128]{4,3,2,1,0:T(8,128)S(1)}, bf16[384,768]{1,0:T(8,128)(2,1)S(1)}, f32[384,256]{1,0:T(8...) custom-call(s32[1]{0:T(128)} %bitcast.3.flag, ...), custom_call_target="tpu_custom_call" | custom-call | flops 6000000000 | bytes 6000000 | tf_op jit(solution)/shard_map/conv_edge/pallas_call | solution.py:287
  31.1 0.0 copy-start.1
  31.1 0.0 copy-start.5
  31.1 3.0 %collective-permute-start.4 = (f32[104,256]{1,0:T(8,128)S(1)}, f32[104,256]{1,0:T(8,128)S(1)}, u32[]{:S(2)}, u32[]{:S(2)}) collective-permute-start(f32[104,256]{1,0:T(8,128)S(1)} %get-tuple-element.97), channel_id=1, source_target_pairs={{0,1},{1,0},{2,3},{3,2},{4,5},{5,4},{6,7},{7,6},{8,9},{9,8},{10,11... | collective-permute-start | bytes 319496 | tf_op jit(solution)/shard_map/ppermute | solution.py:29
  34.1 1.0 collective-permute-done.4
  35.1 0.5 collective-permute-start.5
  35.6 1.0 prepare.1
  36.6 3.8 %collective-permute-done.5 = f32[104,256]{1,0:T(8,128)S(1)} collective-permute-done((f32[104,256]{1,0:T(8,128)S(1)}, f32[104,256]{1,0:T(8,128)S(1)}, u32[]{:S(2)}, u32[]{:S(2)}) %collective-permute-start.5) | collective-permute-done | bytes 106528 | tf_op jit(solution)/shard_map/ppermute | solution.py:29
  40.4 2.4 %collective-permute-start.6 = (f32[104,256]{1,0:T(8,128)S(1)}, f32[104,256]{1,0:T(8,128)S(1)}, u32[]{:S(2)}, u32[]{:S(2)}) collective-permute-start(f32[104,256]{1,0:T(8,128)S(1)} %add.56), channel_id=1, source_target_pairs={{0,4},{4,0},{8,12},{12,8},{1,5},{5,1},{9,13},{13,9},{2,6},{6,2},{1... | collective-permute-start | bytes 319496 | tf_op jit(solution)/shard_map/ppermute | solution.py:29
  42.8 2.7 %collective-permute-done.6 = f32[104,256]{1,0:T(8,128)S(1)} collective-permute-done((f32[104,256]{1,0:T(8,128)S(1)}, f32[104,256]{1,0:T(8,128)S(1)}, u32[]{:S(2)}, u32[]{:S(2)}) %collective-permute-start.6) | collective-permute-done | bytes 106528 | tf_op jit(solution)/shard_map/ppermute | solution.py:29
  45.6 3.1 %collective-permute-start.7 = (f32[104,256]{1,0:T(8,128)S(1)}, f32[104,256]{1,0:T(8,128)S(1)}, u32[]{:S(2)}, u32[]{:S(2)}) collective-permute-start(f32[104,256]{1,0:T(8,128)S(1)} %add.57), channel_id=1, source_target_pairs={{0,8},{4,12},{8,0},{12,4},{1,9},{5,13},{9,1},{13,5},{2,10},{6,14},... | collective-permute-start | bytes 319496 | tf_op jit(solution)/shard_map/ppermute | solution.py:29
  48.6 2.7 %collective-permute-done.7 = f32[104,256]{1,0:T(8,128)S(1)} collective-permute-done((f32[104,256]{1,0:T(8,128)S(1)}, f32[104,256]{1,0:T(8,128)S(1)}, u32[]{:S(2)}, u32[]{:S(2)}) %collective-permute-start.7) | collective-permute-done | bytes 106528 | tf_op jit(solution)/shard_map/ppermute | solution.py:29
  51.3 0.1 collective-permute-start.8
  52.1 0.7 collective-permute-done.8.other
  52.7 9.7 %head.1 = (f32[272,256]{1,0:T(8,128)S(1)}, f32[384,256]{1,0:T(8,128)S(1)}, f32[384,256]{1,0:T(8,128)S(1)}, f32[1,256]{1,0:T(1,128)S(1)}, bf16[640,768]{1,0:T(8,128)(2,1)S(1)}, /*index=5*/bf16[384,768]{1,0:T(8,128)(2,1)S(1)}) custom-call(s32[1]{0:T(128)} %bitcast.3.flag, s32[1]{0:T(128)S(6)} %copy.23.label, f32[10]{0:T(128)S(1)} %copy-done.5, ...), custom_call_target="tpu_custom_call" | custom-call | flops 10000000000 | bytes 10000000 | tf_op jit(solution)/shard_map/head/pallas_call | solution.py:452
  62.4 0.2 collective-permute-start.9
  62.6 1.5 %collective-permute-start.15 = (f32[272,256]{1,0:T(8,128)S(1)}, f32[272,256]{1,0:T(8,128)S(1)}, u32[]{:S(2)}, u32[]{:S(2)}) collective-permute-start(f32[272,256]{1,0:T(8,128)S(1)} %get-tuple-element.153), channel_id=1, source_target_pairs={{0,16},{16,0},{1,17},{17,1},{2,18},{18,2},{3,19},{19,3},{4,20},{20... | collective-permute-start | bytes 835592 | tf_op jit(solution)/shard_map/ppermute | solution.py:29
  64.1 0.1 collective-permute-done.9
  64.2 0.1 add.59
  64.3 0.6 collective-permute-start.10
  64.9 3.8 %tap_grads.3 = (f32[32,768]{1,0:T(8,128)S(1)}, f32[32,768]{1,0:T(8,128)S(1)}) custom-call(s32[1]{0:T(128)} %bitcast.3.flag, f32[6,16,14,8,128]{4,3,2,1,0:T(8,128)S(1)} %get-tuple-element.91.spread_in, f32[6,3,14,8,128]{4,3,2,1,0:T(8,128)S(1)} %get-tuple-element.125.spread_top, f32[6,3,14,8,128]{4,3,2,1,0:T(8,128)S(1)} %get-tuple-element.126.spread_bottom, ...), custom_call_target="tpu_custom_call" | custom-call | flops 5000000000 | bytes 5000000 | tf_op jit(solution)/shard_map/tap_grads/pallas_call | solution.py:593
  68.7 0.5 collective-permute-done.10
  69.2 1.6 %collective-permute-start.11 = (bf16[192,256]{1,0:T(8,128)(2,1)S(1)}, bf16[192,256]{1,0:T(8,128)(2,1)S(1)}, u32[]{:S(2)}, u32[]{:S(2)}) collective-permute-start(bf16[192,256]{1,0:T(8,128)(2,1)S(1)} %convert_add_fusion.1), channel_id=1, source_target_pairs={{0,16},{16,0},{1,17},{17,1},{2,18},{18,2},{3,19},{19,3},{4,20},{20... | collective-permute-start | bytes 294920 | tf_op jit(solution)/shard_map/ppermute | solution.py:29
  70.8 3.6 %tap_grads.4 = (f32[32,768]{1,0:T(8,128)S(1)}, f32[32,768]{1,0:T(8,128)S(1)}) custom-call(s32[1]{0:T(128)} %bitcast.3.flag, f32[6,16,14,8,128]{4,3,2,1,0:T(8,128)S(1)} %get-tuple-element.91.spread_in, f32[6,3,14,8,128]{4,3,2,1,0:T(8,128)S(1)} %get-tuple-element.125.spread_top, ...), custom_call_target="tpu_custom_call", output_to_operand_aliasing={{0}: (7, {}), {1}: (8, {})} | custom-call | flops 5000000000 | bytes 5000000 | tf_op jit(solution)/shard_map/tap_grads/pallas_call | solution.py:593
  74.5 3.1 %collective-permute-start.13 = (bf16[192,256]{1,0:T(8,128)(2,1)S(1)}, bf16[192,256]{1,0:T(8,128)(2,1)S(1)}, u32[]{:S(2)}, u32[]{:S(2)}) collective-permute-start(bf16[192,256]{1,0:T(8,128)(2,1)S(1)} %convert_add_fusion), channel_id=1, source_target_pairs={{0,8},{4,12},{8,0},{12,4},{1,9},{5,13},{9,1},{13,5},{2,10},{6,14},... | collective-permute-start | bytes 294920 | tf_op jit(solution)/shard_map/ppermute | solution.py:29
  77.5 2.5 %collective-permute-start.12 = (bf16[192,256]{1,0:T(8,128)(2,1)S(1)}, bf16[192,256]{1,0:T(8,128)(2,1)S(1)}, u32[]{:S(2)}, u32[]{:S(2)}) collective-permute-start(bf16[192,256]{1,0:T(8,128)(2,1)S(1)} %convert_add_fusion), channel_id=1, source_target_pairs={{0,4},{4,0},{8,12},{12,8},{1,5},{5,1},{9,13},{13,9},{2,6},{6,2},{1... | collective-permute-start | bytes 294920 | tf_op jit(solution)/shard_map/ppermute | solution.py:29
  80.0 3.6 %tap_grads.5 = (f32[32,768]{1,0:T(8,128)S(1)}, f32[32,768]{1,0:T(8,128)S(1)}) custom-call(s32[1]{0:T(128)} %bitcast.3.flag, f32[6,16,14,8,128]{4,3,2,1,0:T(8,128)S(1)} %get-tuple-element.91.spread_in, f32[6,3,14,8,128]{4,3,2,1,0:T(8,128)S(1)} %get-tuple-element.125.spread_top, ...), custom_call_target="tpu_custom_call", output_to_operand_aliasing={{0}: (7, {}), {1}: (8, {})} | custom-call | flops 5000000000 | bytes 5000000 | tf_op jit(solution)/shard_map/tap_grads/pallas_call | solution.py:593
  83.7 2.8 %collective-permute-done.14 = bf16[192,256]{1,0:T(8,128)(2,1)S(1)} collective-permute-done((bf16[192,256]{1,0:T(8,128)(2,1)S(1)}, bf16[192,256]{1,0:T(8,128)(2,1)S(1)}, u32[]{:S(2)}, u32[]{:S(2)}) %collective-permute-start.14) | collective-permute-done | bytes 98336 | tf_op jit(solution)/shard_map/ppermute | solution.py:29
  86.5 0.1 collective-permute-start.16
  86.6 1.3 %collective-permute-done.16 = f32[32,768]{1,0:T(8,128)S(1)} collective-permute-done((f32[32,768]{1,0:T(8,128)S(1)}, f32[32,768]{1,0:T(8,128)S(1)}, u32[]{:S(2)}, u32[]{:S(2)}) %collective-permute-start.16) | collective-permute-done | bytes 98336 | tf_op jit(solution)/shard_map/ppermute | solution.py:29
  87.9 1.1 collective-permute-start.17
  89.0 0.1 slice_reduce_fusion.1
  89.1 2.9 %collective-permute-done.17 = bf16[32,768]{1,0:T(8,128)(2,1)S(1)} collective-permute-done((bf16[32,768]{1,0:T(8,128)(2,1)S(1)}, bf16[32,768]{1,0:T(8,128)(2,1)S(1)}, u32[]{:S(2)}, u32[]{:S(2)}) %collective-permute-start.17) | collective-permute-done | bytes 49184 | tf_op jit(solution)/shard_map/ppermute | solution.py:29
  92.1 1.0 collective-permute-start.18
  93.1 1.9 %multiply_add_fusion = f32[10,256,256]{2,1,0:T(8,128)} fusion(f32[256,256]{1,0:T(8,128)S(1)} %slice.73, f32[10]{0:T(128)S(1)} %get-tuple-element.177, f32[256,256]{1,0:T(8,128)S(1)} %slice.71, f32[10]{0:T(128)S(1)} %get-tuple-element.178), kind=kLoop, calls=%fused_computation | loop fusion | flops 1966080 | bytes 3145808 | tf_op jit(solution)/shard_map/add | solution.py:51
  95.0 1.0 collective-permute-start.19
  96.0 0.3 collective-permute-done.18
  96.2 4.4 %collective-permute-done.19 = f32[192,256]{1,0:T(8,128)S(1)} collective-permute-done((f32[192,256]{1,0:T(8,128)S(1)}, f32[192,256]{1,0:T(8,128)S(1)}, u32[]{:S(2)}, u32[]{:S(2)}) %collective-permute-start.19) | collective-permute-done | bytes 196640 | tf_op jit(solution)/shard_map/ppermute | solution.py:29
  100.7 0.1 collective-permute-start.23
  100.8 1.8 %collective-permute-start.21 = (bf16[32,768]{1,0:T(8,128)(2,1)S(1)}, bf16[32,768]{1,0:T(8,128)(2,1)S(1)}, u32[]{:S(2)}, u32[]{:S(2)}) collective-permute-start(bf16[32,768]{1,0:T(8,128)(2,1)S(1)} %convert_add_fusion.2), channel_id=1, source_target_pairs={{0,8},{4,12},{8,0},{12,4},{1,9},{5,13},{9,1},{13,5},{2,10},{6,14},... | collective-permute-start | bytes 147464 | tf_op jit(solution)/shard_map/ppermute | solution.py:29
  102.6 0.6 collective-permute-start.20
  103.1 2.1 %collective-permute-start.22 = (bf16[32,768]{1,0:T(8,128)(2,1)S(1)}, bf16[32,768]{1,0:T(8,128)(2,1)S(1)}, u32[]{:S(2)}, u32[]{:S(2)}) collective-permute-start(bf16[32,768]{1,0:T(8,128)(2,1)S(1)} %convert_add_fusion.2), channel_id=1, source_target_pairs={{0,12},{4,8},{8,4},{12,0},{1,13},{5,9},{9,5},{13,1},{2,14},{6,10},... | collective-permute-start | bytes 147464 | tf_op jit(solution)/shard_map/ppermute | solution.py:29
  105.3 0.6 slice_reduce_fusion
  105.9 0.5 slice.86
  107.1 0.1 collective-permute-done.20
  107.2 1.9 %collective-permute-done.22 = bf16[32,768]{1,0:T(8,128)(2,1)S(1)} collective-permute-done((bf16[32,768]{1,0:T(8,128)(2,1)S(1)}, bf16[32,768]{1,0:T(8,128)(2,1)S(1)}, u32[]{:S(2)}, u32[]{:S(2)}) %collective-permute-start.22) | collective-permute-done | bytes 49184 | tf_op jit(solution)/shard_map/ppermute | solution.py:29
  109.1 0.1 broadcast_select_fusion.1
  109.1 0.9 pad_maximum_fusion
  110.1 1.3 %collective-permute-done.24.other = f32[32,768]{1,0:T(8,128)S(1)} collective-permute-done((f32[32,768]{1,0:T(8,128)S(1)}, f32[32,768]{1,0:T(8,128)S(1)}, u32[]{:S(2)}, u32[]{:S(2)}) %collective-permute-start.24) | collective-permute-done | bytes 98336 | tf_op jit(solution)/shard_map/ppermute | solution.py:29
  111.4 0.7 finish.1
  112.1 0.6 reduce.3
  (43 shorter events, 0.5 us)
Async XLA Ops:
  0.6 14.1 %copy-start = (bf16[1,16,64,768]{3,2,1,0:T(8,128)(2,1)S(1)}, bf16[1,16,64,768]{3,2,1,0:T(8,128)(2,1)}, u32[]{:S(2)}) copy-start(bf16[1,16,64,768]{3,2,1,0:T(8,128)(2,1)} %param.8) | copy-start | bytes 4718596
  0.6 14.1 %copy-start.4 = (f32[256]{0:T(256)S(1)}, f32[256]{0:T(256)}, u32[]{:S(2)}) copy-start(f32[256]{0:T(256)} %param.12) | copy-start | bytes 3076
  0.7 14.1 %copy-start.2 = (bf16[768,256]{1,0:T(8,128)(2,1)S(1)}, bf16[768,256]{1,0:T(8,128)(2,1)}, u32[]{:S(2)}) copy-start(bf16[768,256]{1,0:T(8,128)(2,1)} %reduce_weight.5) | copy-start | bytes 1179652
  0.7 14.1 %copy-start.3 = (f32[7,7,768]{2,1,0:T(8,128)S(1)}, f32[7,7,768]{2,1,0:T(8,128)}, u32[]{:S(2)}) copy-start(f32[7,7,768]{2,1,0:T(8,128)} %weight.3) | copy-start | bytes 451588
  1.9 5.6 %collective-permute-start = (bf16[16,3,768]{2,1,0:T(4,128)(2,1)S(1)}, bf16[16,3,768]{2,1,0:T(4,128)(2,1)S(1)}, u32[]{:S(2)}, u32[]{:S(2)}) collective-permute-start(bf16[16,3,768]{2,1,0:T(4,128)(2,1)S(1)} %get-tuple-element.165), channel_id=1, source_target_pairs={{0,1},{1,2},{2,3},{4,5},{5,6},{6,7},{8,9},{9,10},{10,11},{12,13},{... | collective-permute-start | bytes 221192 | tf_op jit(solution)/shard_map/ppermute | solution.py:76
  4.3 5.3 %collective-permute-start.1 = (bf16[16,3,768]{2,1,0:T(4,128)(2,1)S(1)}, bf16[16,3,768]{2,1,0:T(4,128)(2,1)S(1)}, u32[]{:S(2)}, u32[]{:S(2)}) collective-permute-start(bf16[16,3,768]{2,1,0:T(4,128)(2,1)S(1)} %get-tuple-element.166), channel_id=1, source_target_pairs={{1,0},{2,1},{3,2},{5,4},{6,5},{7,6},{9,8},{10,9},{11,10},{13,12},{... | collective-permute-start | bytes 221192 | tf_op jit(solution)/shard_map/ppermute | solution.py:80
  9.9 16.4 %collective-permute-start.2 = (bf16[224,768]{1,0:T(8,128)(2,1)S(1)}, bf16[224,768]{1,0:T(8,128)(2,1)S(1)}, u32[]{:S(2)}, u32[]{:S(2)}) collective-permute-start(bf16[224,768]{1,0:T(8,128)(2,1)S(1)} %get-tuple-element.92), channel_id=1, source_target_pairs={{0,4},{4,8},{8,12},{1,5},{5,9},{9,13},{2,6},{6,10},{10,14},{3,7},{... | collective-permute-start | bytes 1032200 | tf_op jit(solution)/shard_map/ppermute | solution.py:76
  13.4 12.9 %collective-permute-start.3 = (bf16[224,768]{1,0:T(8,128)(2,1)S(1)}, bf16[224,768]{1,0:T(8,128)(2,1)S(1)}, u32[]{:S(2)}, u32[]{:S(2)}) collective-permute-start(bf16[224,768]{1,0:T(8,128)(2,1)S(1)} %get-tuple-element.93), channel_id=1, source_target_pairs={{4,0},{8,4},{12,8},{5,1},{9,5},{13,9},{6,2},{10,6},{14,10},{7,3},{... | collective-permute-start | bytes 1032200 | tf_op jit(solution)/shard_map/ppermute | solution.py:80
  31.1 21.6 %copy-start.1 = (bf16[10,256,256]{2,1,0:T(8,128)(2,1)S(1)}, bf16[10,256,256]{2,1,0:T(8,128)(2,1)}, u32[]{:S(2)}) copy-start(bf16[10,256,256]{2,1,0:T(8,128)(2,1)} %class_weight.1) | copy-start | bytes 3932164
  31.1 21.6 %copy-start.5 = (f32[10]{0:T(128)S(1)}, f32[10]{0:T(128)}, u32[]{:S(2)}) copy-start(f32[10]{0:T(128)} %class_bias.1) | copy-start | bytes 124
  31.1 4.0 %collective-permute-start.4 = (f32[104,256]{1,0:T(8,128)S(1)}, f32[104,256]{1,0:T(8,128)S(1)}, u32[]{:S(2)}, u32[]{:S(2)}) collective-permute-start(f32[104,256]{1,0:T(8,128)S(1)} %get-tuple-element.97), channel_id=1, source_target_pairs={{0,1},{1,0},{2,3},{3,2},{4,5},{5,4},{6,7},{7,6},{8,9},{9,8},{10,11... | collective-permute-start | bytes 319496 | tf_op jit(solution)/shard_map/ppermute | solution.py:29
  35.1 5.3 %collective-permute-start.5 = (f32[104,256]{1,0:T(8,128)S(1)}, f32[104,256]{1,0:T(8,128)S(1)}, u32[]{:S(2)}, u32[]{:S(2)}) collective-permute-start(f32[104,256]{1,0:T(8,128)S(1)} %add.55), channel_id=1, source_target_pairs={{0,2},{1,3},{2,0},{3,1},{4,6},{5,7},{6,4},{7,5},{8,10},{9,11},{10,... | collective-permute-start | bytes 319496 | tf_op jit(solution)/shard_map/ppermute | solution.py:29
  40.4 5.1 %collective-permute-start.6 = (f32[104,256]{1,0:T(8,128)S(1)}, f32[104,256]{1,0:T(8,128)S(1)}, u32[]{:S(2)}, u32[]{:S(2)}) collective-permute-start(f32[104,256]{1,0:T(8,128)S(1)} %add.56), channel_id=1, source_target_pairs={{0,4},{4,0},{8,12},{12,8},{1,5},{5,1},{9,13},{13,9},{2,6},{6,2},{1... | collective-permute-start | bytes 319496 | tf_op jit(solution)/shard_map/ppermute | solution.py:29
  45.6 5.8 %collective-permute-start.7 = (f32[104,256]{1,0:T(8,128)S(1)}, f32[104,256]{1,0:T(8,128)S(1)}, u32[]{:S(2)}, u32[]{:S(2)}) collective-permute-start(f32[104,256]{1,0:T(8,128)S(1)} %add.57), channel_id=1, source_target_pairs={{0,8},{4,12},{8,0},{12,4},{1,9},{5,13},{9,1},{13,5},{2,10},{6,14},... | collective-permute-start | bytes 319496 | tf_op jit(solution)/shard_map/ppermute | solution.py:29
  51.3 1.4 %collective-permute-start.8 = (f32[104,256]{1,0:T(8,128)S(1)}, f32[104,256]{1,0:T(8,128)S(1)}, u32[]{:S(2)}, u32[]{:S(2)}) collective-permute-start(f32[104,256]{1,0:T(8,128)S(1)} %add.58.own), channel_id=1, source_target_pairs={{0,1},{1,0},{2,3},{3,2},{4,5},{5,4},{6,7},{7,6},{8,9},{9,8},{10,11... | collective-permute-start | bytes 319496 | tf_op jit(solution)/shard_map/ppermute | solution.py:29
  62.4 1.8 %collective-permute-start.9 = (f32[384,256]{1,0:T(8,128)S(1)}, f32[384,256]{1,0:T(8,128)S(1)}, u32[]{:S(2)}, u32[]{:S(2)}) collective-permute-start(f32[384,256]{1,0:T(8,128)S(1)} %get-tuple-element.119), channel_id=1, source_target_pairs={{0,1},{1,0},{2,3},{3,2},{4,5},{5,4},{6,7},{7,6},{8,9},{9,8},{10,11... | collective-permute-start | bytes 1179656 | tf_op jit(solution)/shard_map/ppermute | solution.py:29
  62.6 23.9 %collective-permute-start.15 = (f32[272,256]{1,0:T(8,128)S(1)}, f32[272,256]{1,0:T(8,128)S(1)}, u32[]{:S(2)}, u32[]{:S(2)}) collective-permute-start(f32[272,256]{1,0:T(8,128)S(1)} %get-tuple-element.153), channel_id=1, source_target_pairs={{0,16},{16,0},{1,17},{17,1},{2,18},{18,2},{3,19},{19,3},{4,20},{20... | collective-permute-start | bytes 835592 | tf_op jit(solution)/shard_map/ppermute | solution.py:29
  64.3 4.9 %collective-permute-start.10 = (bf16[192,256]{1,0:T(8,128)(2,1)S(1)}, bf16[192,256]{1,0:T(8,128)(2,1)S(1)}, u32[]{:S(2)}, u32[]{:S(2)}) collective-permute-start(bf16[192,256]{1,0:T(8,128)(2,1)S(1)} %select_convert_fusion), channel_id=1, source_target_pairs={{0,2},{1,3},{2,0},{3,1},{4,6},{5,7},{6,4},{7,5},{8,10},{9,11},{10,... | collective-permute-start | bytes 294920 | tf_op jit(solution)/shard_map/ppermute | solution.py:29
  69.2 5.2 %collective-permute-start.11 = (bf16[192,256]{1,0:T(8,128)(2,1)S(1)}, bf16[192,256]{1,0:T(8,128)(2,1)S(1)}, u32[]{:S(2)}, u32[]{:S(2)}) collective-permute-start(bf16[192,256]{1,0:T(8,128)(2,1)S(1)} %convert_add_fusion.1), channel_id=1, source_target_pairs={{0,16},{16,0},{1,17},{17,1},{2,18},{18,2},{3,19},{19,3},{4,20},{20... | collective-permute-start | bytes 294920 | tf_op jit(solution)/shard_map/ppermute | solution.py:29
  74.5 9.2 %collective-permute-start.13 = (bf16[192,256]{1,0:T(8,128)(2,1)S(1)}, bf16[192,256]{1,0:T(8,128)(2,1)S(1)}, u32[]{:S(2)}, u32[]{:S(2)}) collective-permute-start(bf16[192,256]{1,0:T(8,128)(2,1)S(1)} %convert_add_fusion), channel_id=1, source_target_pairs={{0,8},{4,12},{8,0},{12,4},{1,9},{5,13},{9,1},{13,5},{2,10},{6,14},... | collective-permute-start | bytes 294920 | tf_op jit(solution)/shard_map/ppermute | solution.py:29
  77.5 6.1 %collective-permute-start.12 = (bf16[192,256]{1,0:T(8,128)(2,1)S(1)}, bf16[192,256]{1,0:T(8,128)(2,1)S(1)}, u32[]{:S(2)}, u32[]{:S(2)}) collective-permute-start(bf16[192,256]{1,0:T(8,128)(2,1)S(1)} %convert_add_fusion), channel_id=1, source_target_pairs={{0,4},{4,0},{8,12},{12,8},{1,5},{5,1},{9,13},{13,9},{2,6},{6,2},{1... | collective-permute-start | bytes 294920 | tf_op jit(solution)/shard_map/ppermute | solution.py:29
  80.0 6.4 %collective-permute-start.14 = (bf16[192,256]{1,0:T(8,128)(2,1)S(1)}, bf16[192,256]{1,0:T(8,128)(2,1)S(1)}, u32[]{:S(2)}, u32[]{:S(2)}) collective-permute-start(bf16[192,256]{1,0:T(8,128)(2,1)S(1)} %convert_add_fusion), channel_id=1, source_target_pairs={{0,12},{4,8},{8,4},{12,0},{1,13},{5,9},{9,5},{13,1},{2,14},{6,10},... | collective-permute-start | bytes 294920 | tf_op jit(solution)/shard_map/ppermute | solution.py:29
  86.5 1.4 %collective-permute-start.16 = (f32[32,768]{1,0:T(8,128)S(1)}, f32[32,768]{1,0:T(8,128)S(1)}, u32[]{:S(2)}, u32[]{:S(2)}) collective-permute-start(f32[32,768]{1,0:T(8,128)S(1)} %get-tuple-element.146), channel_id=1, source_target_pairs={{0,1},{1,0},{2,3},{3,2},{4,5},{5,4},{6,7},{7,6},{8,9},{9,8},{10,11... | collective-permute-start | bytes 294920 | tf_op jit(solution)/shard_map/ppermute | solution.py:29
  87.9 4.2 %collective-permute-start.17 = (bf16[32,768]{1,0:T(8,128)(2,1)S(1)}, bf16[32,768]{1,0:T(8,128)(2,1)S(1)}, u32[]{:S(2)}, u32[]{:S(2)}) collective-permute-start(bf16[32,768]{1,0:T(8,128)(2,1)S(1)} %add.65), channel_id=1, source_target_pairs={{0,2},{1,3},{2,0},{3,1},{4,6},{5,7},{6,4},{7,5},{8,10},{9,11},{10,... | collective-permute-start | bytes 147464 | tf_op jit(solution)/shard_map/ppermute | solution.py:29
  92.1 4.2 %collective-permute-start.18 = (bf16[32,768]{1,0:T(8,128)(2,1)S(1)}, bf16[32,768]{1,0:T(8,128)(2,1)S(1)}, u32[]{:S(2)}, u32[]{:S(2)}) collective-permute-start(bf16[32,768]{1,0:T(8,128)(2,1)S(1)} %add_convert_fusion), channel_id=1, source_target_pairs={{0,16},{16,0},{1,17},{17,1},{2,18},{18,2},{3,19},{19,3},{4,20},{20... | collective-permute-start | bytes 147464 | tf_op jit(solution)/shard_map/ppermute | solution.py:29
  95.0 5.7 %collective-permute-start.19 = (f32[192,256]{1,0:T(8,128)S(1)}, f32[192,256]{1,0:T(8,128)S(1)}, u32[]{:S(2)}, u32[]{:S(2)}) collective-permute-start(f32[192,256]{1,0:T(8,128)S(1)} %add_add_fusion), channel_id=1, source_target_pairs={{0,2},{1,3},{2,0},{3,1},{4,6},{5,7},{6,4},{7,5},{8,10},{9,11},{10,... | collective-permute-start | bytes 589832 | tf_op jit(solution)/shard_map/ppermute | solution.py:29
  100.7 8.3 %collective-permute-start.23 = (f32[384,256]{1,0:T(8,128)S(1)}, f32[384,256]{1,0:T(8,128)S(1)}, u32[]{:S(2)}, u32[]{:S(2)}) collective-permute-start(f32[384,256]{1,0:T(8,128)S(1)} %pad_maximum_fusion.1), channel_id=1, source_target_pairs={{0,1},{1,0},{2,3},{3,2},{4,5},{5,4},{6,7},{7,6},{8,9},{9,8},{10,11... | collective-permute-start | bytes 1179656 | tf_op jit(solution)/shard_map/ppermute | solution.py:29
  100.8 6.2 %collective-permute-start.21 = (bf16[32,768]{1,0:T(8,128)(2,1)S(1)}, bf16[32,768]{1,0:T(8,128)(2,1)S(1)}, u32[]{:S(2)}, u32[]{:S(2)}) collective-permute-start(bf16[32,768]{1,0:T(8,128)(2,1)S(1)} %convert_add_fusion.2), channel_id=1, source_target_pairs={{0,8},{4,12},{8,0},{12,4},{1,9},{5,13},{9,1},{13,5},{2,10},{6,14},... | collective-permute-start | bytes 147464 | tf_op jit(solution)/shard_map/ppermute | solution.py:29
  102.6 4.6 %collective-permute-start.20 = (bf16[32,768]{1,0:T(8,128)(2,1)S(1)}, bf16[32,768]{1,0:T(8,128)(2,1)S(1)}, u32[]{:S(2)}, u32[]{:S(2)}) collective-permute-start(bf16[32,768]{1,0:T(8,128)(2,1)S(1)} %convert_add_fusion.2), channel_id=1, source_target_pairs={{0,4},{4,0},{8,12},{12,8},{1,5},{5,1},{9,13},{13,9},{2,6},{6,2},{1... | collective-permute-start | bytes 147464 | tf_op jit(solution)/shard_map/ppermute | solution.py:29
  103.1 5.9 %collective-permute-start.22 = (bf16[32,768]{1,0:T(8,128)(2,1)S(1)}, bf16[32,768]{1,0:T(8,128)(2,1)S(1)}, u32[]{:S(2)}, u32[]{:S(2)}) collective-permute-start(bf16[32,768]{1,0:T(8,128)(2,1)S(1)} %convert_add_fusion.2), channel_id=1, source_target_pairs={{0,12},{4,8},{8,4},{12,0},{1,13},{5,9},{9,5},{13,1},{2,14},{6,10},... | collective-permute-start | bytes 147464 | tf_op jit(solution)/shard_map/ppermute | solution.py:29
  110.1 1.3 %collective-permute-start.24 = (f32[32,768]{1,0:T(8,128)S(1)}, f32[32,768]{1,0:T(8,128)S(1)}, u32[]{:S(2)}, u32[]{:S(2)}) collective-permute-start(f32[32,768]{1,0:T(8,128)S(1)} %add_add_fusion.1.own), channel_id=1, source_target_pairs={{0,1},{1,0},{2,3},{3,2},{4,5},{5,4},{6,7},{7,6},{8,9},{9,8},{10,11... | collective-permute-start | bytes 294920 | tf_op jit(solution)/shard_map/ppermute | solution.py:29

commit v5 on v4

--- a/solution.py
+++ b/solution.py
@@ -60,6 +60,20 @@
 def exchange_all(value, axis, sent_as):
     sent = value.astype(sent_as)
     moved = [sent] + [swap(sent, axis, shift) for shift in range(1, lax.axis_size(axis))]
+    return tree_sum([part.astype(wide) for part in moved])
+
+
+def exchange_square(value, axes, shifts, sent_as):
+    counts = [lax.axis_size(axis) for axis in axes]
+    sent = value.astype(sent_as)
+    moved = [sent]
+    for first, second in ((0, 1), (1, 0), (1, 1)):
+        pairs = [
+            (i * counts[1] + j, (i ^ (first * shifts[0])) * counts[1] + (j ^ (second * shifts[1])))
+            for i in range(counts[0])
+            for j in range(counts[1])
+        ]
+        moved.append(lax.ppermute(sent, axes, pairs))
     return tree_sum([part.astype(wide) for part in moved])
 
 
@@ -70,6 +84,11 @@
         found.append(shift)
         shift *= 2
     return found
+
+
+def pair_up(first, second):
+    many = min(len(first), len(second))
+    return list(zip(second, first)), first[many:], second[many:]
 
 
 def next_along(value, axis):
@@ -614,8 +633,8 @@
     for row_tap in range(KERNEL):
         depth_out[row_tap] = sums[row_tap * KERNEL : (row_tap + 1) * KERNEL, :]
     taps = KERNEL * KERNEL
-    depth_bias_out[...] = sums[taps : taps + 1, :]
-    bias_out[...] = sums[taps + 1 : taps + 2, : bias_out.shape[1]]
+    depth_bias_out[...] = sums[taps, :]
+    bias_out[...] = sums[taps + 1, : bias_out.shape[0]]
 
 
 def finish(flag, own, other, width):
@@ -626,8 +645,8 @@
         out_specs=[in_vmem] * 3,
         out_shape=[
             shape_of((KERNEL, KERNEL, channels)),
-            shape_of((1, channels)),
-            shape_of((1, width)),
+            shape_of((channels,)),
+            shape_of((width,)),
         ],
         scratch_shapes=[pltpu.VMEM((2 * part, channels), wide)],
         compiler_params=params(8),
@@ -728,7 +747,7 @@
         sums = halve(beside(sums), "sx", shift, uppers[shift], narrow)
     for shift in doublings("dp"):
         sums = exchange(beside(sums), "dp", shift, narrow)
-    sums = exchange_all(beside(sums), "sy", narrow)
+    sums = exchange_all(beside(sums), "sy", narrow).astype(narrow)
     while turns:
         sums = beside(sums)
 
@@ -743,23 +762,23 @@
     small, sums = together((small, sums))
     for shift in reversed(doublings("sx", 2)):
         sums = unhalve(sums, "sx", shift, uppers[shift])
-    for shift in doublings("sx", 2):
+    squares, left_x, left_dp = pair_up(doublings("sx", 2), doublings("dp"))
+    for pair in squares:
+        small = exchange_square(small, ("dp", "sx"), pair, narrow)
+    for shift in left_x:
         small = exchange(small, "sx", shift, narrow)
-    for shift in doublings("dp"):
+    for shift in left_dp:
         small = exchange(small, "dp", shift, narrow)
     small, sums = together((small, sums))
-    weight_grad = unhalve(sums, "sx", 1, uppers[1])
+    weight_grad = unhalve(sums, "sx", 1, uppers[1]).astype(wide)
     small = exchange_all(small, "sy", narrow)
-    small, weight_grad, class_weight_grad, class_bias_grad, loss = together(
-        (small, weight_grad, class_weight_grad, class_bias_grad, loss)
-    )
     depth_grad, depth_bias_grad, bias_grad = finish(flag, small, swap(small, "sx", 1), width)
     return (
         loss,
         depth_grad,
-        depth_bias_grad[0],
+        depth_bias_grad,
         weight_grad,
-        bias_grad[0],
+        bias_grad,
         class_weight_grad,
         class_bias_grad,
     )

time: 114 us -> 111 us (0.974)
  waiting for transfers between devices: 28.4 us -> 24.4 us
  starting transfers between devices: 34.7 us -> 36.2 us
    ppermute x21 -> x19, waiting for transfers between devices: 26.3 us -> 21.7 us  [swap(): return lax.ppermute(value, axis, [(i, i ^ shift) for i in range(count)])]
    ppermute x0 -> x3, starting transfers between devices: none -> 3.55 us  [exchange_square(): moved.append(lax.ppermute(sent, axes, pairs))]
    ppermute x21 -> x19, starting transfers between devices: 26.2 us -> 24.2 us  [swap(): return lax.ppermute(value, axis, [(i, i ^ shift) for i in range(count)])]
  transfers between devices with their start and end apart: 25 -> 26, of which waited for: 16 -> 16; matrix products, arithmetic and copies ran while one was open for 5% -> 5% of each run, Pallas kernels for 21% -> 22%
where the time goes in v5:
time: 111 us
  Pallas kernels  38.7 us (35%)
  starting transfers between devices  36.2 us (33%)
  waiting for transfers between devices  24.4 us (22%)
  local copies, waits for them, and re-layouts  4.57 us (4%)
  between operations  3.41 us (3%)
  other arithmetic  3.38 us (3%)
    ppermute x19, starting transfers between devices, swap(): return lax.ppermute(value, axis, [(i, i ^ shift) for i in range(count)])  24.2 us
    ppermute x19, waiting for transfers between devices, swap(): return lax.ppermute(value, axis, [(i, i ^ shift) for i in range(count)])  21.7 us
    pallas_call x1, Pallas kernels, conv_inner(): pl.pallas_call(inner_kernel, in_specs=[in_vmem] * 7, out_specs=[in_vmem]...  11.5 us
    pallas_call x3, Pallas kernels, tap_grads(): pl.pallas_call(functools.partial(taps_kernel, first=first, many=many), in...  11 us
    pallas_call x1, Pallas kernels, head(): pl.pallas_call(functools.partial(head_kernel, count=count, image_count=im...  9.67 us
    ppermute x2, starting transfers between devices, next_along(): lax.ppermute(value, axis, [(i, i + 1) for i in range(lax.axis_size(axis)...  5.86 us
    pallas_call x1, Pallas kernels, conv_edge(): pl.pallas_call(edge_kernel, in_specs=[in_smem] + [in_vmem] * 9, out_specs...  4.78 us
    ppermute x3, starting transfers between devices, exchange_square(): moved.append(lax.ppermute(sent, axes, pairs))  3.55 us
  transfers between devices with their start and end apart: 26, of which 16 were waited for; matrix products, arithmetic and copies ran while one was open for 5% of the time, Pallas kernels for 22%

profile of v5, /device:TPU:0, one launch (start us, length us, event | category | flops | bytes accessed | tf_op | source)
XLA Modules:
  0.0 110.7 jit_solution(18222165745242525306)
XLA Ops:
  0.6 0.0 copy-start
  0.7 1.2 %fusion.1 = (bf16[16,3,768]{2,1,0:T(4,128)(2,1)S(1)}, bf16[16,3,768]{2,1,0:T(4,128)(2,1)S(1)}) fusion(bf16[16,64,768]{2,1,0:T(8,128)(2,1)} %bitcast.6), kind=kLoop, calls=%fused_computation.20 | loop fusion | bytes 294912 | tf_op jit(solution)/shard_map/slice | solution.py:680
  1.9 2.4 %collective-permute-start = (bf16[16,3,768]{2,1,0:T(4,128)(2,1)S(1)}, bf16[16,3,768]{2,1,0:T(4,128)(2,1)S(1)}, u32[]{:S(2)}, u32[]{:S(2)}) collective-permute-start(bf16[16,3,768]{2,1,0:T(4,128)(2,1)S(1)} %get-tuple-element.155), channel_id=1, source_target_pairs={{0,1},{1,2},{2,3},{4,5},{5,6},{6,7},{8,9},{9,10},{10,11},{12,13},{... | collective-permute-start | bytes 221192 | tf_op jit(solution)/shard_map/ppermute | solution.py:95
  4.3 1.3 %collective-permute-start.1 = (bf16[16,3,768]{2,1,0:T(4,128)(2,1)S(1)}, bf16[16,3,768]{2,1,0:T(4,128)(2,1)S(1)}, u32[]{:S(2)}, u32[]{:S(2)}) collective-permute-start(bf16[16,3,768]{2,1,0:T(4,128)(2,1)S(1)} %get-tuple-element.156), channel_id=1, source_target_pairs={{1,0},{2,1},{3,2},{5,4},{6,5},{7,6},{9,8},{10,9},{11,10},{13,12},{... | collective-permute-start | bytes 221192 | tf_op jit(solution)/shard_map/ppermute | solution.py:99
  5.6 1.1 fusion
  6.7 0.7 broadcast_in_dim.16.bias
  7.4 0.1 pad.11.clone
  7.5 2.1 %collective-permute-done.1.right = bf16[16,3,768]{2,1,0:T(4,128)(2,1)S(1)} collective-permute-done((bf16[16,3,768]{2,1,0:T(4,128)(2,1)S(1)}, bf16[16,3,768]{2,1,0:T(4,128)(2,1)S(1)}, u32[]{:S(2)}, u32[]{:S(2)}) %collective-permute-start.1) | collective-permute-done | bytes 73760 | tf_op jit(solution)/shard_map/ppermute | solution.py:99
  9.7 0.2 maximum_maximum_fusion.1
  9.9 3.5 %collective-permute-start.2 = (bf16[224,768]{1,0:T(8,128)(2,1)S(1)}, bf16[224,768]{1,0:T(8,128)(2,1)S(1)}, u32[]{:S(2)}, u32[]{:S(2)}) collective-permute-start(bf16[224,768]{1,0:T(8,128)(2,1)S(1)} %get-tuple-element.87), channel_id=1, source_target_pairs={{0,4},{4,8},{8,12},{1,5},{5,9},{9,13},{2,6},{6,10},{10,14},{3,7},{... | collective-permute-start | bytes 1032200 | tf_op jit(solution)/shard_map/ppermute | solution.py:95
  13.4 1.3 %collective-permute-start.3 = (bf16[224,768]{1,0:T(8,128)(2,1)S(1)}, bf16[224,768]{1,0:T(8,128)(2,1)S(1)}, u32[]{:S(2)}, u32[]{:S(2)}) collective-permute-start(bf16[224,768]{1,0:T(8,128)(2,1)S(1)} %get-tuple-element.88), channel_id=1, source_target_pairs={{4,0},{8,4},{12,8},{5,1},{9,5},{13,9},{6,2},{10,6},{14,10},{7,3},{... | collective-permute-start | bytes 1032200 | tf_op jit(solution)/shard_map/ppermute | solution.py:99
  14.7 11.5 %conv_inner.1 = (f32[6,16,14,8,128]{4,3,2,1,0:T(8,128)S(1)}, bf16[640,768]{1,0:T(8,128)(2,1)S(1)}, f32[640,256]{1,0:T(8,128)S(1)}, bf16[640,256]{1,0:T(8,128)(2,...) custom-call(bf16[16,64,768]{2,1,0:T(8,128)(2,1)S(1)} %bitcast.7, ...), custom_call_target="tpu_custom_call" | custom-call | flops 10000000000 | bytes 10000000 | tf_op jit(solution)/shard_map/conv_inner/pallas_call | solution.py:277
  26.3 4.8 %conv_edge.1 = (f32[6,3,14,8,128]{4,3,2,1,0:T(8,128)S(1)}, f32[6,3,14,8,128]{4,3,2,1,0:T(8,128)S(1)}, bf16[384,768]{1,0:T(8,128)(2,1)S(1)}, f32[384,256]{1,0:T(8...) custom-call(s32[1]{0:T(128)} %bitcast.3.flag, ...), custom_call_target="tpu_custom_call" | custom-call | flops 6000000000 | bytes 6000000 | tf_op jit(solution)/shard_map/conv_edge/pallas_call | solution.py:306
  31.1 0.0 copy-start.1
  31.1 0.0 copy-start.5
  31.1 3.0 %collective-permute-start.4 = (f32[104,256]{1,0:T(8,128)S(1)}, f32[104,256]{1,0:T(8,128)S(1)}, u32[]{:S(2)}, u32[]{:S(2)}) collective-permute-start(f32[104,256]{1,0:T(8,128)S(1)} %get-tuple-element.92), channel_id=1, source_target_pairs={{0,1},{1,0},{2,3},{3,2},{4,5},{5,4},{6,7},{7,6},{8,9},{9,8},{10,11... | collective-permute-start | bytes 319496 | tf_op jit(solution)/shard_map/ppermute | solution.py:29
  34.1 1.0 collective-permute-done.4
  35.1 0.5 collective-permute-start.5
  35.6 1.0 prepare.1
  36.6 3.8 %collective-permute-done.5 = f32[104,256]{1,0:T(8,128)S(1)} collective-permute-done((f32[104,256]{1,0:T(8,128)S(1)}, f32[104,256]{1,0:T(8,128)S(1)}, u32[]{:S(2)}, u32[]{:S(2)}) %collective-permute-start.5) | collective-permute-done | bytes 106528 | tf_op jit(solution)/shard_map/ppermute | solution.py:29
  40.4 2.4 %collective-permute-start.6 = (f32[104,256]{1,0:T(8,128)S(1)}, f32[104,256]{1,0:T(8,128)S(1)}, u32[]{:S(2)}, u32[]{:S(2)}) collective-permute-start(f32[104,256]{1,0:T(8,128)S(1)} %add.59), channel_id=1, source_target_pairs={{0,4},{4,0},{8,12},{12,8},{1,5},{5,1},{9,13},{13,9},{2,6},{6,2},{1... | collective-permute-start | bytes 319496 | tf_op jit(solution)/shard_map/ppermute | solution.py:29
  42.8 2.7 %collective-permute-done.6 = f32[104,256]{1,0:T(8,128)S(1)} collective-permute-done((f32[104,256]{1,0:T(8,128)S(1)}, f32[104,256]{1,0:T(8,128)S(1)}, u32[]{:S(2)}, u32[]{:S(2)}) %collective-permute-start.6) | collective-permute-done | bytes 106528 | tf_op jit(solution)/shard_map/ppermute | solution.py:29
  45.6 3.1 %collective-permute-start.7 = (f32[104,256]{1,0:T(8,128)S(1)}, f32[104,256]{1,0:T(8,128)S(1)}, u32[]{:S(2)}, u32[]{:S(2)}) collective-permute-start(f32[104,256]{1,0:T(8,128)S(1)} %add.60), channel_id=1, source_target_pairs={{0,8},{4,12},{8,0},{12,4},{1,9},{5,13},{9,1},{13,5},{2,10},{6,14},... | collective-permute-start | bytes 319496 | tf_op jit(solution)/shard_map/ppermute | solution.py:29
  48.6 2.7 %collective-permute-done.7 = f32[104,256]{1,0:T(8,128)S(1)} collective-permute-done((f32[104,256]{1,0:T(8,128)S(1)}, f32[104,256]{1,0:T(8,128)S(1)}, u32[]{:S(2)}, u32[]{:S(2)}) %collective-permute-start.7) | collective-permute-done | bytes 106528 | tf_op jit(solution)/shard_map/ppermute | solution.py:29
  51.3 0.1 collective-permute-start.8
  52.1 0.7 collective-permute-done.8.other
  52.7 9.7 %head.1 = (f32[272,256]{1,0:T(8,128)S(1)}, f32[384,256]{1,0:T(8,128)S(1)}, f32[384,256]{1,0:T(8,128)S(1)}, f32[1,256]{1,0:T(1,128)S(1)}, bf16[640,768]{1,0:T(8,128)(2,1)S(1)}, /*index=5*/bf16[384,768]{1,0:T(8,128)(2,1)S(1)}) custom-call(s32[1]{0:T(128)} %bitcast.3.flag, s32[1]{0:T(128)S(6)} %copy.23.label, f32[10]{0:T(128)S(1)} %copy-done.5, ...), custom_call_target="tpu_custom_call" | custom-call | flops 10000000000 | bytes 10000000 | tf_op jit(solution)/shard_map/head/pallas_call | solution.py:471
  62.4 0.2 collective-permute-start.9
  62.6 1.5 %collective-permute-start.15 = (f32[272,256]{1,0:T(8,128)S(1)}, f32[272,256]{1,0:T(8,128)S(1)}, u32[]{:S(2)}, u32[]{:S(2)}) collective-permute-start(f32[272,256]{1,0:T(8,128)S(1)} %get-tuple-element.140), channel_id=1, source_target_pairs={{0,16},{16,0},{1,17},{17,1},{2,18},{18,2},{3,19},{19,3},{4,20},{20... | collective-permute-start | bytes 835592 | tf_op jit(solution)/shard_map/ppermute | solution.py:29
  64.1 0.1 collective-permute-done.9
  64.2 0.1 add.62
  64.3 0.6 collective-permute-start.10
  64.9 3.8 %tap_grads.3 = (f32[32,768]{1,0:T(8,128)S(1)}, f32[32,768]{1,0:T(8,128)S(1)}) custom-call(s32[1]{0:T(128)} %bitcast.3.flag, f32[6,16,14,8,128]{4,3,2,1,0:T(8,128)S(1)} %get-tuple-element.86.spread_in, f32[6,3,14,8,128]{4,3,2,1,0:T(8,128)S(1)} %get-tuple-element.120.spread_top, f32[6,3,14,8,128]{4,3,2,1,0:T(8,128)S(1)} %get-tuple-element.121.spread_bottom, ...), custom_call_target="tpu_custom_call" | custom-call | flops 5000000000 | bytes 5000000 | tf_op jit(solution)/shard_map/tap_grads/pallas_call | solution.py:612
  68.7 0.5 collective-permute-done.10
  69.2 1.6 %collective-permute-start.11 = (bf16[192,256]{1,0:T(8,128)(2,1)S(1)}, bf16[192,256]{1,0:T(8,128)(2,1)S(1)}, u32[]{:S(2)}, u32[]{:S(2)}) collective-permute-start(bf16[192,256]{1,0:T(8,128)(2,1)S(1)} %convert_add_fusion.1), channel_id=1, source_target_pairs={{0,16},{16,0},{1,17},{17,1},{2,18},{18,2},{3,19},{19,3},{4,20},{20... | collective-permute-start | bytes 294920 | tf_op jit(solution)/shard_map/ppermute | solution.py:29
  70.8 3.6 %tap_grads.4 = (f32[32,768]{1,0:T(8,128)S(1)}, f32[32,768]{1,0:T(8,128)S(1)}) custom-call(s32[1]{0:T(128)} %bitcast.3.flag, f32[6,16,14,8,128]{4,3,2,1,0:T(8,128)S(1)} %get-tuple-element.86.spread_in, f32[6,3,14,8,128]{4,3,2,1,0:T(8,128)S(1)} %get-tuple-element.120.spread_top, ...), custom_call_target="tpu_custom_call", output_to_operand_aliasing={{0}: (7, {}), {1}: (8, {})} | custom-call | flops 5000000000 | bytes 5000000 | tf_op jit(solution)/shard_map/tap_grads/pallas_call | solution.py:612
  74.5 3.1 %collective-permute-start.13 = (bf16[192,256]{1,0:T(8,128)(2,1)S(1)}, bf16[192,256]{1,0:T(8,128)(2,1)S(1)}, u32[]{:S(2)}, u32[]{:S(2)}) collective-permute-start(bf16[192,256]{1,0:T(8,128)(2,1)S(1)} %convert_add_fusion), channel_id=1, source_target_pairs={{0,8},{4,12},{8,0},{12,4},{1,9},{5,13},{9,1},{13,5},{2,10},{6,14},... | collective-permute-start | bytes 294920 | tf_op jit(solution)/shard_map/ppermute | solution.py:29
  77.5 2.5 %collective-permute-start.12 = (bf16[192,256]{1,0:T(8,128)(2,1)S(1)}, bf16[192,256]{1,0:T(8,128)(2,1)S(1)}, u32[]{:S(2)}, u32[]{:S(2)}) collective-permute-start(bf16[192,256]{1,0:T(8,128)(2,1)S(1)} %convert_add_fusion), channel_id=1, source_target_pairs={{0,4},{4,0},{8,12},{12,8},{1,5},{5,1},{9,13},{13,9},{2,6},{6,2},{1... | collective-permute-start | bytes 294920 | tf_op jit(solution)/shard_map/ppermute | solution.py:29
  80.0 3.6 %tap_grads.5 = (f32[32,768]{1,0:T(8,128)S(1)}, f32[32,768]{1,0:T(8,128)S(1)}) custom-call(s32[1]{0:T(128)} %bitcast.3.flag, f32[6,16,14,8,128]{4,3,2,1,0:T(8,128)S(1)} %get-tuple-element.86.spread_in, f32[6,3,14,8,128]{4,3,2,1,0:T(8,128)S(1)} %get-tuple-element.120.spread_top, ...), custom_call_target="tpu_custom_call", output_to_operand_aliasing={{0}: (7, {}), {1}: (8, {})} | custom-call | flops 5000000000 | bytes 5000000 | tf_op jit(solution)/shard_map/tap_grads/pallas_call | solution.py:612
  83.7 2.8 %collective-permute-done.14 = bf16[192,256]{1,0:T(8,128)(2,1)S(1)} collective-permute-done((bf16[192,256]{1,0:T(8,128)(2,1)S(1)}, bf16[192,256]{1,0:T(8,128)(2,1)S(1)}, u32[]{:S(2)}, u32[]{:S(2)}) %collective-permute-start.14) | collective-permute-done | bytes 98336 | tf_op jit(solution)/shard_map/ppermute | solution.py:29
  86.5 0.1 add_convert_fusion
  86.6 0.1 collective-permute-start.16
  86.7 0.1 slice_reduce_fusion.1
  86.8 1.2 %collective-permute-done.16 = f32[32,768]{1,0:T(8,128)S(1)} collective-permute-done((f32[32,768]{1,0:T(8,128)S(1)}, f32[32,768]{1,0:T(8,128)S(1)}, u32[]{:S(2)}, u32[]{:S(2)}) %collective-permute-start.16) | collective-permute-done | bytes 98336 | tf_op jit(solution)/shard_map/ppermute | solution.py:29
  88.0 1.0 collective-permute-start.18
  89.0 1.0 collective-permute-start.17
  90.0 1.5 %collective-permute-start.19 = (bf16[32,768]{1,0:T(8,128)(2,1)S(1)}, bf16[32,768]{1,0:T(8,128)(2,1)S(1)}, u32[]{:S(2)}, u32[]{:S(2)}) collective-permute-start(bf16[32,768]{1,0:T(8,128)(2,1)S(1)} %add.69), channel_id=1, source_target_pairs={{0,18},{1,19},{2,16},{3,17},{16,2},{17,3},{18,0},{19,1},{4,22},{5,... | collective-permute-start | bytes 147464 | tf_op jit(solution)/shard_map/ppermute | solution.py:76
  91.5 1.9 %multiply_add_fusion = f32[10,256,256]{2,1,0:T(8,128)} fusion(f32[256,256]{1,0:T(8,128)S(1)} %slice.76, f32[10]{0:T(128)S(1)} %get-tuple-element.167, f32[256,256]{1,0:T(8,128)S(1)} %slice.74, f32[10]{0:T(128)S(1)} %get-tuple-element.168), kind=kLoop, calls=%fused_computation | loop fusion | flops 1966080 | bytes 3145808 | tf_op jit(solution)/shard_map/add | solution.py:51
  93.4 1.0 collective-permute-start.20
  94.4 0.6 collective-permute-done.19
  95.0 3.0 %collective-permute-done.20 = bf16[192,256]{1,0:T(8,128)(2,1)S(1)} collective-permute-done((bf16[192,256]{1,0:T(8,128)(2,1)S(1)}, bf16[192,256]{1,0:T(8,128)(2,1)S(1)}, u32[]{:S(2)}, u32[]{:S(2)}) %collective-permute-start.20) | collective-permute-done | bytes 98336 | tf_op jit(solution)/shard_map/ppermute | solution.py:29
  98.0 2.1 %collective-permute-start.22 = (bf16[32,768]{1,0:T(8,128)(2,1)S(1)}, bf16[32,768]{1,0:T(8,128)(2,1)S(1)}, u32[]{:S(2)}, u32[]{:S(2)}) collective-permute-start(bf16[32,768]{1,0:T(8,128)(2,1)S(1)} %add_add_fusion.1), channel_id=1, source_target_pairs={{0,8},{4,12},{8,0},{12,4},{1,9},{5,13},{9,1},{13,5},{2,10},{6,14},... | collective-permute-start | bytes 147464 | tf_op jit(solution)/shard_map/ppermute | solution.py:29
  100.2 0.4 collective-permute-start.21
  100.6 1.9 %collective-permute-start.23 = (bf16[32,768]{1,0:T(8,128)(2,1)S(1)}, bf16[32,768]{1,0:T(8,128)(2,1)S(1)}, u32[]{:S(2)}, u32[]{:S(2)}) collective-permute-start(bf16[32,768]{1,0:T(8,128)(2,1)S(1)} %add_add_fusion.1), channel_id=1, source_target_pairs={{0,12},{4,8},{8,4},{12,0},{1,13},{5,9},{9,5},{13,1},{2,14},{6,10},... | collective-permute-start | bytes 147464 | tf_op jit(solution)/shard_map/ppermute | solution.py:29
  102.5 0.5 slice.85
  103.7 0.1 collective-permute-start.25
  103.7 0.2 collective-permute-done.22
  104.0 0.5 collective-permute-done.21
  104.5 2.0 %collective-permute-done.23 = bf16[32,768]{1,0:T(8,128)(2,1)S(1)} collective-permute-done((bf16[32,768]{1,0:T(8,128)(2,1)S(1)}, bf16[32,768]{1,0:T(8,128)(2,1)S(1)}, u32[]{:S(2)}, u32[]{:S(2)}) %collective-permute-start.23) | collective-permute-done | bytes 49184 | tf_op jit(solution)/shard_map/ppermute | solution.py:29
  106.5 0.1 collective-permute-start.24
  106.6 0.6 slice_reduce_fusion
  107.2 0.7 collective-permute-done.24.other
  107.9 0.7 finish.1
  108.6 0.9 maximum_convert_fusion
  (43 shorter events, 0.5 us)
Async XLA Ops:
  0.6 14.1 %copy-start = (bf16[1,16,64,768]{3,2,1,0:T(8,128)(2,1)S(1)}, bf16[1,16,64,768]{3,2,1,0:T(8,128)(2,1)}, u32[]{:S(2)}) copy-start(bf16[1,16,64,768]{3,2,1,0:T(8,128)(2,1)} %param.8) | copy-start | bytes 4718596
  0.6 14.1 %copy-start.4 = (f32[256]{0:T(256)S(1)}, f32[256]{0:T(256)}, u32[]{:S(2)}) copy-start(f32[256]{0:T(256)} %param.12) | copy-start | bytes 3076
  0.7 14.1 %copy-start.2 = (bf16[768,256]{1,0:T(8,128)(2,1)S(1)}, bf16[768,256]{1,0:T(8,128)(2,1)}, u32[]{:S(2)}) copy-start(bf16[768,256]{1,0:T(8,128)(2,1)} %reduce_weight.5) | copy-start | bytes 1179652
  0.7 14.1 %copy-start.3 = (f32[7,7,768]{2,1,0:T(8,128)S(1)}, f32[7,7,768]{2,1,0:T(8,128)}, u32[]{:S(2)}) copy-start(f32[7,7,768]{2,1,0:T(8,128)} %weight.3) | copy-start | bytes 451588
  1.9 5.6 %collective-permute-start = (bf16[16,3,768]{2,1,0:T(4,128)(2,1)S(1)}, bf16[16,3,768]{2,1,0:T(4,128)(2,1)S(1)}, u32[]{:S(2)}, u32[]{:S(2)}) collective-permute-start(bf16[16,3,768]{2,1,0:T(4,128)(2,1)S(1)} %get-tuple-element.155), channel_id=1, source_target_pairs={{0,1},{1,2},{2,3},{4,5},{5,6},{6,7},{8,9},{9,10},{10,11},{12,13},{... | collective-permute-start | bytes 221192 | tf_op jit(solution)/shard_map/ppermute | solution.py:95
  4.3 5.3 %collective-permute-start.1 = (bf16[16,3,768]{2,1,0:T(4,128)(2,1)S(1)}, bf16[16,3,768]{2,1,0:T(4,128)(2,1)S(1)}, u32[]{:S(2)}, u32[]{:S(2)}) collective-permute-start(bf16[16,3,768]{2,1,0:T(4,128)(2,1)S(1)} %get-tuple-element.156), channel_id=1, source_target_pairs={{1,0},{2,1},{3,2},{5,4},{6,5},{7,6},{9,8},{10,9},{11,10},{13,12},{... | collective-permute-start | bytes 221192 | tf_op jit(solution)/shard_map/ppermute | solution.py:99
  9.9 16.4 %collective-permute-start.2 = (bf16[224,768]{1,0:T(8,128)(2,1)S(1)}, bf16[224,768]{1,0:T(8,128)(2,1)S(1)}, u32[]{:S(2)}, u32[]{:S(2)}) collective-permute-start(bf16[224,768]{1,0:T(8,128)(2,1)S(1)} %get-tuple-element.87), channel_id=1, source_target_pairs={{0,4},{4,8},{8,12},{1,5},{5,9},{9,13},{2,6},{6,10},{10,14},{3,7},{... | collective-permute-start | bytes 1032200 | tf_op jit(solution)/shard_map/ppermute | solution.py:95
  13.4 12.9 %collective-permute-start.3 = (bf16[224,768]{1,0:T(8,128)(2,1)S(1)}, bf16[224,768]{1,0:T(8,128)(2,1)S(1)}, u32[]{:S(2)}, u32[]{:S(2)}) collective-permute-start(bf16[224,768]{1,0:T(8,128)(2,1)S(1)} %get-tuple-element.88), channel_id=1, source_target_pairs={{4,0},{8,4},{12,8},{5,1},{9,5},{13,9},{6,2},{10,6},{14,10},{7,3},{... | collective-permute-start | bytes 1032200 | tf_op jit(solution)/shard_map/ppermute | solution.py:99
  31.1 21.6 %copy-start.1 = (bf16[10,256,256]{2,1,0:T(8,128)(2,1)S(1)}, bf16[10,256,256]{2,1,0:T(8,128)(2,1)}, u32[]{:S(2)}) copy-start(bf16[10,256,256]{2,1,0:T(8,128)(2,1)} %class_weight.1) | copy-start | bytes 3932164
  31.1 21.6 %copy-start.5 = (f32[10]{0:T(128)S(1)}, f32[10]{0:T(128)}, u32[]{:S(2)}) copy-start(f32[10]{0:T(128)} %class_bias.1) | copy-start | bytes 124
  31.1 4.0 %collective-permute-start.4 = (f32[104,256]{1,0:T(8,128)S(1)}, f32[104,256]{1,0:T(8,128)S(1)}, u32[]{:S(2)}, u32[]{:S(2)}) collective-permute-start(f32[104,256]{1,0:T(8,128)S(1)} %get-tuple-element.92), channel_id=1, source_target_pairs={{0,1},{1,0},{2,3},{3,2},{4,5},{5,4},{6,7},{7,6},{8,9},{9,8},{10,11... | collective-permute-start | bytes 319496 | tf_op jit(solution)/shard_map/ppermute | solution.py:29
  35.1 5.3 %collective-permute-start.5 = (f32[104,256]{1,0:T(8,128)S(1)}, f32[104,256]{1,0:T(8,128)S(1)}, u32[]{:S(2)}, u32[]{:S(2)}) collective-permute-start(f32[104,256]{1,0:T(8,128)S(1)} %add.58), channel_id=1, source_target_pairs={{0,2},{1,3},{2,0},{3,1},{4,6},{5,7},{6,4},{7,5},{8,10},{9,11},{10,... | collective-permute-start | bytes 319496 | tf_op jit(solution)/shard_map/ppermute | solution.py:29
  40.4 5.1 %collective-permute-start.6 = (f32[104,256]{1,0:T(8,128)S(1)}, f32[104,256]{1,0:T(8,128)S(1)}, u32[]{:S(2)}, u32[]{:S(2)}) collective-permute-start(f32[104,256]{1,0:T(8,128)S(1)} %add.59), channel_id=1, source_target_pairs={{0,4},{4,0},{8,12},{12,8},{1,5},{5,1},{9,13},{13,9},{2,6},{6,2},{1... | collective-permute-start | bytes 319496 | tf_op jit(solution)/shard_map/ppermute | solution.py:29
  45.6 5.8 %collective-permute-start.7 = (f32[104,256]{1,0:T(8,128)S(1)}, f32[104,256]{1,0:T(8,128)S(1)}, u32[]{:S(2)}, u32[]{:S(2)}) collective-permute-start(f32[104,256]{1,0:T(8,128)S(1)} %add.60), channel_id=1, source_target_pairs={{0,8},{4,12},{8,0},{12,4},{1,9},{5,13},{9,1},{13,5},{2,10},{6,14},... | collective-permute-start | bytes 319496 | tf_op jit(solution)/shard_map/ppermute | solution.py:29
  51.3 1.4 %collective-permute-start.8 = (f32[104,256]{1,0:T(8,128)S(1)}, f32[104,256]{1,0:T(8,128)S(1)}, u32[]{:S(2)}, u32[]{:S(2)}) collective-permute-start(f32[104,256]{1,0:T(8,128)S(1)} %add.61.own), channel_id=1, source_target_pairs={{0,1},{1,0},{2,3},{3,2},{4,5},{5,4},{6,7},{7,6},{8,9},{9,8},{10,11... | collective-permute-start | bytes 319496 | tf_op jit(solution)/shard_map/ppermute | solution.py:29
  62.4 1.8 %collective-permute-start.9 = (f32[384,256]{1,0:T(8,128)S(1)}, f32[384,256]{1,0:T(8,128)S(1)}, u32[]{:S(2)}, u32[]{:S(2)}) collective-permute-start(f32[384,256]{1,0:T(8,128)S(1)} %get-tuple-element.114), channel_id=1, source_target_pairs={{0,1},{1,0},{2,3},{3,2},{4,5},{5,4},{6,7},{7,6},{8,9},{9,8},{10,11... | collective-permute-start | bytes 1179656 | tf_op jit(solution)/shard_map/ppermute | solution.py:29
  62.6 23.9 %collective-permute-start.15 = (f32[272,256]{1,0:T(8,128)S(1)}, f32[272,256]{1,0:T(8,128)S(1)}, u32[]{:S(2)}, u32[]{:S(2)}) collective-permute-start(f32[272,256]{1,0:T(8,128)S(1)} %get-tuple-element.140), channel_id=1, source_target_pairs={{0,16},{16,0},{1,17},{17,1},{2,18},{18,2},{3,19},{19,3},{4,20},{20... | collective-permute-start | bytes 835592 | tf_op jit(solution)/shard_map/ppermute | solution.py:29
  64.3 4.9 %collective-permute-start.10 = (bf16[192,256]{1,0:T(8,128)(2,1)S(1)}, bf16[192,256]{1,0:T(8,128)(2,1)S(1)}, u32[]{:S(2)}, u32[]{:S(2)}) collective-permute-start(bf16[192,256]{1,0:T(8,128)(2,1)S(1)} %select_convert_fusion), channel_id=1, source_target_pairs={{0,2},{1,3},{2,0},{3,1},{4,6},{5,7},{6,4},{7,5},{8,10},{9,11},{10,... | collective-permute-start | bytes 294920 | tf_op jit(solution)/shard_map/ppermute | solution.py:29
  69.2 5.2 %collective-permute-start.11 = (bf16[192,256]{1,0:T(8,128)(2,1)S(1)}, bf16[192,256]{1,0:T(8,128)(2,1)S(1)}, u32[]{:S(2)}, u32[]{:S(2)}) collective-permute-start(bf16[192,256]{1,0:T(8,128)(2,1)S(1)} %convert_add_fusion.1), channel_id=1, source_target_pairs={{0,16},{16,0},{1,17},{17,1},{2,18},{18,2},{3,19},{19,3},{4,20},{20... | collective-permute-start | bytes 294920 | tf_op jit(solution)/shard_map/ppermute | solution.py:29
  74.5 9.2 %collective-permute-start.13 = (bf16[192,256]{1,0:T(8,128)(2,1)S(1)}, bf16[192,256]{1,0:T(8,128)(2,1)S(1)}, u32[]{:S(2)}, u32[]{:S(2)}) collective-permute-start(bf16[192,256]{1,0:T(8,128)(2,1)S(1)} %convert_add_fusion), channel_id=1, source_target_pairs={{0,8},{4,12},{8,0},{12,4},{1,9},{5,13},{9,1},{13,5},{2,10},{6,14},... | collective-permute-start | bytes 294920 | tf_op jit(solution)/shard_map/ppermute | solution.py:29
  77.5 6.1 %collective-permute-start.12 = (bf16[192,256]{1,0:T(8,128)(2,1)S(1)}, bf16[192,256]{1,0:T(8,128)(2,1)S(1)}, u32[]{:S(2)}, u32[]{:S(2)}) collective-permute-start(bf16[192,256]{1,0:T(8,128)(2,1)S(1)} %convert_add_fusion), channel_id=1, source_target_pairs={{0,4},{4,0},{8,12},{12,8},{1,5},{5,1},{9,13},{13,9},{2,6},{6,2},{1... | collective-permute-start | bytes 294920 | tf_op jit(solution)/shard_map/ppermute | solution.py:29
  80.0 6.4 %collective-permute-start.14 = (bf16[192,256]{1,0:T(8,128)(2,1)S(1)}, bf16[192,256]{1,0:T(8,128)(2,1)S(1)}, u32[]{:S(2)}, u32[]{:S(2)}) collective-permute-start(bf16[192,256]{1,0:T(8,128)(2,1)S(1)} %convert_add_fusion), channel_id=1, source_target_pairs={{0,12},{4,8},{8,4},{12,0},{1,13},{5,9},{9,5},{13,1},{2,14},{6,10},... | collective-permute-start | bytes 294920 | tf_op jit(solution)/shard_map/ppermute | solution.py:29
  86.6 1.4 %collective-permute-start.16 = (f32[32,768]{1,0:T(8,128)S(1)}, f32[32,768]{1,0:T(8,128)S(1)}, u32[]{:S(2)}, u32[]{:S(2)}) collective-permute-start(f32[32,768]{1,0:T(8,128)S(1)} %get-tuple-element.143), channel_id=1, source_target_pairs={{0,1},{1,0},{2,3},{3,2},{4,5},{5,4},{6,7},{7,6},{8,9},{9,8},{10,11... | collective-permute-start | bytes 294920 | tf_op jit(solution)/shard_map/ppermute | solution.py:29
  88.0 6.4 %collective-permute-start.18 = (bf16[32,768]{1,0:T(8,128)(2,1)S(1)}, bf16[32,768]{1,0:T(8,128)(2,1)S(1)}, u32[]{:S(2)}, u32[]{:S(2)}) collective-permute-start(bf16[32,768]{1,0:T(8,128)(2,1)S(1)} %add.69), channel_id=1, source_target_pairs={{0,16},{1,17},{2,18},{3,19},{16,0},{17,1},{18,2},{19,3},{4,20},{5,... | collective-permute-start | bytes 147464 | tf_op jit(solution)/shard_map/ppermute | solution.py:76
  89.0 5.4 %collective-permute-start.17 = (bf16[32,768]{1,0:T(8,128)(2,1)S(1)}, bf16[32,768]{1,0:T(8,128)(2,1)S(1)}, u32[]{:S(2)}, u32[]{:S(2)}) collective-permute-start(bf16[32,768]{1,0:T(8,128)(2,1)S(1)} %add.69), channel_id=1, source_target_pairs={{0,2},{1,3},{2,0},{3,1},{16,18},{17,19},{18,16},{19,17},{4,6},{5,7... | collective-permute-start | bytes 147464 | tf_op jit(solution)/shard_map/ppermute | solution.py:76
  90.0 5.0 %collective-permute-start.19 = (bf16[32,768]{1,0:T(8,128)(2,1)S(1)}, bf16[32,768]{1,0:T(8,128)(2,1)S(1)}, u32[]{:S(2)}, u32[]{:S(2)}) collective-permute-start(bf16[32,768]{1,0:T(8,128)(2,1)S(1)} %add.69), channel_id=1, source_target_pairs={{0,18},{1,19},{2,16},{3,17},{16,2},{17,3},{18,0},{19,1},{4,22},{5,... | collective-permute-start | bytes 147464 | tf_op jit(solution)/shard_map/ppermute | solution.py:76
  93.4 4.6 %collective-permute-start.20 = (bf16[192,256]{1,0:T(8,128)(2,1)S(1)}, bf16[192,256]{1,0:T(8,128)(2,1)S(1)}, u32[]{:S(2)}, u32[]{:S(2)}) collective-permute-start(bf16[192,256]{1,0:T(8,128)(2,1)S(1)} %add_convert_fusion), channel_id=1, source_target_pairs={{0,2},{1,3},{2,0},{3,1},{4,6},{5,7},{6,4},{7,5},{8,10},{9,11},{10,... | collective-permute-start | bytes 294920 | tf_op jit(solution)/shard_map/ppermute | solution.py:29
  98.0 5.9 %collective-permute-start.22 = (bf16[32,768]{1,0:T(8,128)(2,1)S(1)}, bf16[32,768]{1,0:T(8,128)(2,1)S(1)}, u32[]{:S(2)}, u32[]{:S(2)}) collective-permute-start(bf16[32,768]{1,0:T(8,128)(2,1)S(1)} %add_add_fusion.1), channel_id=1, source_target_pairs={{0,8},{4,12},{8,0},{12,4},{1,9},{5,13},{9,1},{13,5},{2,10},{6,14},... | collective-permute-start | bytes 147464 | tf_op jit(solution)/shard_map/ppermute | solution.py:29
  100.2 4.3 %collective-permute-start.21 = (bf16[32,768]{1,0:T(8,128)(2,1)S(1)}, bf16[32,768]{1,0:T(8,128)(2,1)S(1)}, u32[]{:S(2)}, u32[]{:S(2)}) collective-permute-start(bf16[32,768]{1,0:T(8,128)(2,1)S(1)} %add_add_fusion.1), channel_id=1, source_target_pairs={{0,4},{4,0},{8,12},{12,8},{1,5},{5,1},{9,13},{13,9},{2,6},{6,2},{1... | collective-permute-start | bytes 147464 | tf_op jit(solution)/shard_map/ppermute | solution.py:29
  100.6 5.9 %collective-permute-start.23 = (bf16[32,768]{1,0:T(8,128)(2,1)S(1)}, bf16[32,768]{1,0:T(8,128)(2,1)S(1)}, u32[]{:S(2)}, u32[]{:S(2)}) collective-permute-start(bf16[32,768]{1,0:T(8,128)(2,1)S(1)} %add_add_fusion.1), channel_id=1, source_target_pairs={{0,12},{4,8},{8,4},{12,0},{1,13},{5,9},{9,5},{13,1},{2,14},{6,10},... | collective-permute-start | bytes 147464 | tf_op jit(solution)/shard_map/ppermute | solution.py:29
  103.7 4.9 %collective-permute-start.25 = (bf16[384,256]{1,0:T(8,128)(2,1)S(1)}, bf16[384,256]{1,0:T(8,128)(2,1)S(1)}, u32[]{:S(2)}, u32[]{:S(2)}) collective-permute-start(bf16[384,256]{1,0:T(8,128)(2,1)S(1)} %pad_maximum_fusion), channel_id=1, source_target_pairs={{0,1},{1,0},{2,3},{3,2},{4,5},{5,4},{6,7},{7,6},{8,9},{9,8},{10,11... | collective-permute-start | bytes 589832 | tf_op jit(solution)/shard_map/ppermute | solution.py:29
  106.5 1.4 %collective-permute-start.24 = (f32[32,768]{1,0:T(8,128)S(1)}, f32[32,768]{1,0:T(8,128)S(1)}, u32[]{:S(2)}, u32[]{:S(2)}) collective-permute-start(f32[32,768]{1,0:T(8,128)S(1)} %add_add_fusion.own), channel_id=1, source_target_pairs={{0,1},{1,0},{2,3},{3,2},{4,5},{5,4},{6,7},{7,6},{8,9},{9,8},{10,11... | collective-permute-start | bytes 294920 | tf_op jit(solution)/shard_map/ppermute | solution.py:29

commit v6 on v5

--- a/solution.py
+++ b/solution.py
@@ -13,6 +13,7 @@
 LANES = 128
 GROUPS = 8
 EDGE = 8
+TAPS_ROWS = 64
 
 epsilon = 1e-05
 loss_scale = 64.0
@@ -33,19 +34,6 @@
     return (lax.axis_index(axis) & shift) != 0
 
 
-def halve(value, axis, shift, upper, sent_as):
-    rows = value.shape[0] // 2
-    low, high = value[:rows], value[rows:]
-    kept = jnp.where(upper, high, low)
-    sent = jnp.where(upper, low, high).astype(sent_as)
-    return kept + swap(sent, axis, shift).astype(wide)
-
-
-def unhalve(value, axis, shift, upper):
-    other = swap(value, axis, shift)
-    return jnp.concatenate([jnp.where(upper, other, value), jnp.where(upper, value, other)])
-
-
 def tree_sum(terms):
     while len(terms) > 1:
         terms = [terms[i] + terms[i + 1] for i in range(0, len(terms), 2)]
@@ -63,18 +51,37 @@
     return tree_sum([part.astype(wide) for part in moved])
 
 
-def exchange_square(value, axes, shifts, sent_as):
+def square_pairs(axes, shifts):
     counts = [lax.axis_size(axis) for axis in axes]
-    sent = value.astype(sent_as)
-    moved = [sent]
-    for first, second in ((0, 1), (1, 0), (1, 1)):
-        pairs = [
+    return {
+        2 * first + second: [
             (i * counts[1] + j, (i ^ (first * shifts[0])) * counts[1] + (j ^ (second * shifts[1])))
             for i in range(counts[0])
             for j in range(counts[1])
         ]
-        moved.append(lax.ppermute(sent, axes, pairs))
-    return tree_sum([part.astype(wide) for part in moved])
+        for first, second in ((0, 1), (1, 0), (1, 1))
+    }
+
+
+def square_scatter(value, axes, pairs, places, sent_as):
+    pieces = value.reshape((4, value.shape[0] // 4) + value.shape[1:])
+
+    def piece(turn):
+        return lax.dynamic_index_in_dim(pieces, places[turn], 0, keepdims=False)
+
+    moved = [
+        lax.ppermute(piece(turn).astype(sent_as), axes, pairs[turn]).astype(wide)
+        for turn in (1, 2, 3)
+    ]
+    return tree_sum([piece(0)] + moved)
+
+
+def square_gather(value, axes, pairs, places):
+    whole = jnp.zeros((4,) + value.shape, value.dtype)
+    for turn in range(4):
+        part = lax.ppermute(value, axes, pairs[turn]) if turn else value
+        whole = lax.dynamic_update_index_in_dim(whole, part, places[turn], 0)
+    return whole.reshape((-1,) + value.shape[1:])
 
 
 def doublings(axis, first=1):
@@ -84,11 +91,6 @@
         found.append(shift)
         shift *= 2
     return found
-
-
-def pair_up(first, second):
-    many = min(len(first), len(second))
-    return list(zip(second, first)), first[many:], second[many:]
 
 
 def next_along(value, axis):
@@ -383,7 +385,7 @@
 def head_kernel(
     flag, label, class_bias, own, other, class_weight,
     feat_inner, feat_edge, gate_inner, gate_edge, conv_turned, reduce_turned,
-    root_out, kept_out, sent_out, bias_grad_out, conv_inner_out, conv_edge_out,
+    root_out, payload, conv_inner_out, conv_edge_out,
     sums, pre, *, count, image_count,
 ):
     width = root_out.shape[1]
@@ -453,10 +455,15 @@
         grad = jnp.dot(feat[...], symmetric, preferred_element_type=wide) - mean_term
         pre[start : start + feat.shape[0], :] = (grad * gate[...]).astype(narrow)
     pre_grad = pre[...]
-    bias_grad_out[...] = jnp.sum(pre_grad.astype(wide), axis=0, keepdims=True)
-    weight_grad = jnp.dot(conv_turned[...], pre_grad, preferred_element_type=wide)
-    part = kept_out.shape[0]
-    keep_or_send(upper, weight_grad[:part, :], weight_grad[part:, :], kept_out, sent_out)
+    payload[width:, :] = jnp.zeros((payload.shape[0] - width, payload.shape[1]), wide)
+    taps = KERNEL * KERNEL
+    payload[width + taps + 1 : width + taps + 2, :width] = jnp.sum(
+        pre_grad.astype(wide), axis=0, keepdims=True
+    )
+    for first in range(0, conv_turned.shape[0], width):
+        payload[:width, first : first + width] = jnp.dot(
+            conv_turned[first : first + width, :], pre_grad, preferred_element_type=wide
+        )
     for out, start in ((conv_inner_out, 0), (conv_edge_out, inner)):
         out[...] = jnp.dot(
             pre[start : start + out.shape[0], :], reduce_turned[...], preferred_element_type=wide
@@ -471,12 +478,10 @@
     return pl.pallas_call(
         functools.partial(head_kernel, count=count, image_count=image_count),
         in_specs=[in_smem] * 3 + [in_vmem] * 9,
-        out_specs=[in_vmem] * 6,
+        out_specs=[in_vmem] * 4,
         out_shape=[
             shape_of((width + slots, width)),
-            shape_of((channels // 2, width)),
-            shape_of((channels // 2, width)),
-            shape_of((1, width)),
+            shape_of((width + TAPS_ROWS, channels)),
             shape_of((inner, channels), narrow),
             shape_of((edge, channels), narrow),
         ],
@@ -527,18 +532,15 @@
 
 
 def taps_kernel(
-    flag, spread_in, spread_top, spread_bottom, grad_inner, grad_edge, bias_grad, *refs,
-    first, many,
+    spread_in, spread_top, spread_bottom, grad_inner, grad_edge, payload_in, payload, grads, *,
+    first, last,
 ):
-    kept_out, sent_out, grads, out = refs[-4:]
     rows = spread_in.shape[1]
     steps = grads.shape[1]
     cols = steps * GROUPS
     order = edge_rows(rows)
     taps = KERNEL * KERNEL
-    part = kept_out.shape[0]
-    upper = flag[0] != 0
-    out[taps:, :] = jnp.zeros((out.shape[0] - taps, LANES), wide)
+    base = payload.shape[0] - TAPS_ROWS
 
     def one_tile(tile, _):
         lanes = lanes_of(tile)
@@ -578,63 +580,50 @@
                             total[row_tap, col_tap] += windows[step + col_tap] * grad
             for (row_tap, col_tap), value in total.items():
                 tap = row_tap * KERNEL + col_tap
-                out[tap : tap + 1, :] = jnp.sum(value, axis=0, keepdims=True)
+                payload[base + tap : base + tap + 1, lanes] = jnp.sum(value, axis=0, keepdims=True)
         total = [jnp.zeros((GROUPS, LANES), wide) for _ in range(KERNEL)]
         for index in range(rows * steps):
             slot = index % KERNEL
             total[slot] = total[slot] + grads[index // steps, index % steps]
-        out[taps : taps + 1, :] = jnp.sum(sum(total), axis=0, keepdims=True)
-        low, high = out[:part, :], out[part:, :]
-        kept_out[:, lanes] = jnp.where(upper, high, low)
-        sent_out[:, lanes] = jnp.where(upper, low, high)
+        payload[base + taps : base + taps + 1, lanes] = jnp.sum(sum(total), axis=0, keepdims=True)
         return 0
 
-    lax.fori_loop(first, first + many, one_tile, 0)
-    if first == 0:
-        width = bias_grad.shape[1]
-        place = taps + 1 - part
-        row = jnp.broadcast_to(bias_grad[...], (1, width))
-
-        @pl.when(upper)
-        def _():
-            kept_out[place : place + 1, :width] = row
-
-        @pl.when(jnp.logical_not(upper))
-        def _():
-            sent_out[place : place + 1, :width] = row
-
-
-def tap_grads(flag, spreads, grads, bias_grad, filled, first, many):
-    tiles, rows, groups = spreads[0].shape[:3]
+    lax.fori_loop(first, last, one_tile, 0)
+
+
+def tap_grads(spreads, grads, payload, first, last):
+    rows, groups = spreads[0].shape[1:3]
     steps = groups - KERNEL + 1
-    taps_rows = -(-(KERNEL * KERNEL + 2) // 32) * 32
-    part = (taps_rows // 2, tiles * LANES)
     return pl.pallas_call(
-        functools.partial(taps_kernel, first=first, many=many),
-        in_specs=[in_smem] + [in_vmem] * (6 + len(filled)),
-        out_specs=[in_vmem] * 2,
-        out_shape=[shape_of(part), shape_of(part)],
-        input_output_aliases={7 + index: index for index in range(len(filled))},
-        scratch_shapes=[
-            pltpu.VMEM((rows, steps, GROUPS, LANES), wide),
-            pltpu.VMEM((taps_rows, LANES), wide),
-        ],
+        functools.partial(taps_kernel, first=first, last=last),
+        in_specs=[in_vmem] * 6,
+        out_specs=in_vmem,
+        out_shape=shape_of(payload.shape),
+        input_output_aliases={5: 0},
+        scratch_shapes=[pltpu.VMEM((rows, steps, GROUPS, LANES), wide)],
         compiler_params=params(16),
-        cost_estimate=cost(5),
+        cost_estimate=cost(2 * (last - first)),
         name="tap_grads",
-    )(flag, *spreads, *grads, bias_grad, *filled)
-
-
-def finish_kernel(flag, own, other, depth_out, depth_bias_out, bias_out, sums):
+    )(*spreads, *grads, payload)
+
+
+def finish_kernel(
+    flag, own, other, weight_out, depth_out, depth_bias_out, bias_out, payload,
+):
     part = own.shape[0]
     upper = flag[0] != 0
-    sums[:part, :] = jnp.where(upper, other[...], own[...])
-    sums[part:, :] = jnp.where(upper, own[...], other[...])
+    mine, theirs = own[...].astype(wide), other[...].astype(wide)
+    payload[:part, :] = jnp.where(upper, theirs, mine)
+    payload[part:, :] = jnp.where(upper, mine, theirs)
+    width = weight_out.shape[1]
+    for first in range(0, weight_out.shape[0], width):
+        weight_out[first : first + width, :] = payload[:width, first : first + width]
     for row_tap in range(KERNEL):
-        depth_out[row_tap] = sums[row_tap * KERNEL : (row_tap + 1) * KERNEL, :]
+        start = width + row_tap * KERNEL
+        depth_out[row_tap] = payload[start : start + KERNEL, :]
     taps = KERNEL * KERNEL
-    depth_bias_out[...] = sums[taps, :]
-    bias_out[...] = sums[taps + 1, : bias_out.shape[0]]
+    depth_bias_out[...] = payload[width + taps, :]
+    bias_out[...] = payload[width + taps + 1, :width]
 
 
 def finish(flag, own, other, width):
@@ -642,8 +631,9 @@
     return pl.pallas_call(
         finish_kernel,
         in_specs=[in_smem] + [in_vmem] * 2,
-        out_specs=[in_vmem] * 3,
+        out_specs=[in_vmem] * 4,
         out_shape=[
+            shape_of((channels, width)),
             shape_of((KERNEL, KERNEL, channels)),
             shape_of((channels,)),
             shape_of((width,)),
@@ -674,24 +664,26 @@
     image_count = features.shape[0] * lax.axis_size("dp")
 
     flag = is_upper("sx", 1).astype(jnp.int32)[None]
-    uppers = [is_upper("sx", shift) for shift in doublings("sx")]
+    upper = is_upper("sx", 1)
+    corner = 2 * (lax.axis_index("dp") & 1) + ((lax.axis_index("sx") & 2) >> 1)
+    places = [corner ^ turn for turn in range(4)]
     bias_row = depth_bias[None]
     reduce_row = reduce_bias[None]
     left = next_along(block[:, cols - HALF :], "sx")
     right = back_along(block[:, :HALF], "sx")
-    low, high, left, right, flag, uppers, bias_row, reduce_row = together(
+    low, high, left, right, flag, upper, places, bias_row, reduce_row = together(
         (
             edge_strip(block, left, right, slice(rows - HALF, rows)),
             edge_strip(block, left, right, slice(0, HALF)),
             left,
             right,
             flag,
-            uppers,
+            upper,
+            places,
             bias_row,
             reduce_row,
         )
     )
-    uppers = dict(zip(doublings("sx"), uppers))
     top = next_along(low, "sy")
     bottom = back_along(high, "sy")
     spread, conv_in, before_in, feat_in, gram, colsum = conv_inner(
@@ -717,7 +709,7 @@
         sums = exchange(sums, "sy", shift, wide)
     other = swap(sums, "sx", 1)
 
-    root, kept, sent, bias_grad, *grads = head(
+    root, payload, *grads = head(
         flag,
         labels,
         class_bias,
@@ -728,51 +720,36 @@
         count,
         image_count,
     )
-
     known = [root] + [swap(root, "dp", shift) for shift in range(1, lax.axis_size("dp"))]
     spreads = (spread, spread_top, spread_bottom)
     tiles = channels // LANES
-    many = tiles // 3 if tiles % 3 == 0 else tiles
-    turns = list(range(0, tiles, many))
-    filled = []
-
-    def beside(sums):
-        if turns:
-            sums, grads[:], filled[:] = together((sums, grads, filled))
-            filled[:] = tap_grads(flag, spreads, grads, bias_grad, filled, turns.pop(0), many)
-        return sums
-
-    sums = kept + swap(sent, "sx", 1)
-    for shift in doublings("sx", 2):
-        sums = halve(beside(sums), "sx", shift, uppers[shift], narrow)
-    for shift in doublings("dp"):
-        sums = exchange(beside(sums), "dp", shift, narrow)
-    sums = exchange_all(beside(sums), "sy", narrow).astype(narrow)
-    while turns:
-        sums = beside(sums)
-
-    sums, (kept, sent), known = together((sums, filled, known))
-    small = kept + swap(sent, "sx", 1)
+    payload = tap_grads(spreads, grads, payload, 0, tiles // 2)
+    payload, known = together((payload, known))
+    payload = tap_grads(spreads, grads, payload, tiles // 2, tiles)
+
+    part = payload.shape[0] // 2
+    low, high = payload[:part], payload[part:]
+    kept, sent = jnp.where(upper, high, low), jnp.where(upper, low, high)
+    payload = kept + swap(sent.astype(narrow), "sx", 1).astype(wide)
+    axes = ("dp", "sx")
+    pairs = square_pairs(axes, (1, 2))
+    payload = square_scatter(payload, axes, pairs, places, narrow)
     class_weight_grad = tree_sum(
         [part[width : width + classes, 0][:, None, None] * part[None, :width] for part in known]
     )
     totals = tree_sum([part[width:, 0] for part in known])
     class_bias_grad = totals[:classes]
     loss = totals[classes] / image_count
-    small, sums = together((small, sums))
-    for shift in reversed(doublings("sx", 2)):
-        sums = unhalve(sums, "sx", shift, uppers[shift])
-    squares, left_x, left_dp = pair_up(doublings("sx", 2), doublings("dp"))
-    for pair in squares:
-        small = exchange_square(small, ("dp", "sx"), pair, narrow)
-    for shift in left_x:
-        small = exchange(small, "sx", shift, narrow)
-    for shift in left_dp:
-        small = exchange(small, "dp", shift, narrow)
-    small, sums = together((small, sums))
-    weight_grad = unhalve(sums, "sx", 1, uppers[1]).astype(wide)
-    small = exchange_all(small, "sy", narrow)
-    depth_grad, depth_bias_grad, bias_grad = finish(flag, small, swap(small, "sx", 1), width)
+    for shift in doublings("dp", 2):
+        payload = exchange(payload, "dp", shift, narrow)
+    payload = exchange_all(payload, "sy", narrow).astype(narrow)
+    payload, class_weight_grad, class_bias_grad, loss = together(
+        (payload, class_weight_grad, class_bias_grad, loss)
+    )
+    payload = square_gather(payload, axes, pairs, places)
+    weight_grad, depth_grad, depth_bias_grad, bias_grad = finish(
+        flag, payload, swap(payload, "sx", 1), width
+    )
     return (
         loss,
         depth_grad,

time: 111 us -> 116 us (1.045)
  Pallas kernels: 38.7 us -> 45.6 us
  local copies, waits for them, and re-layouts: 4.57 us -> 9.97 us
  waiting for transfers between devices: 24.4 us -> 20.4 us
  starting transfers between devices: 36.2 us -> 33.7 us
    ppermute x19 -> x11, starting transfers between devices: 24.2 us -> 16 us  [swap(): return lax.ppermute(value, axis, [(i, i ^ shift) for i in range(count)])]
    pallas_call x3 -> x2, Pallas kernels: 11 us -> 17.6 us  [tap_grads(): pl.pallas_call(functools.partial(taps_kernel, first=first, last=last), in...]
    ppermute x19 -> x11, waiting for transfers between devices: 21.7 us -> 15.2 us  [swap(): return lax.ppermute(value, axis, [(i, i ^ shift) for i in range(count)])]
    unnamed x12 -> x36, local copies, waits for them, and re-layouts: 0.03 us -> 5.35 us
    ppermute x3 -> x6, waiting for transfers between devices: 0.6 us -> 5.15 us  [the longest x3 3.19 us: square_gather(): part = lax.ppermute(value, axes, pairs[turn]) if turn else value]
    ppermute x3 -> x6, starting transfers between devices: 3.55 us -> 7.11 us  [the longest x3 3.55 us: square_scatter(): lax.ppermute(piece(turn).astype(sent_as), axes, pairs[turn]).astype(wide)]
    ppermute x2, starting transfers between devices: 5.86 us -> 7.98 us  [next_along(): lax.ppermute(value, axis, [(i, i + 1) for i in range(lax.axis_size(axis)...]
    ppermute x2, waiting for transfers between devices: 2.07 us -> 0.01 us  [back_along(): lax.ppermute(value, axis, [(i + 1, i) for i in range(lax.axis_size(axis)...]
  transfers between devices with their start and end apart: 26 -> 21, of which waited for: 16 -> 14; matrix products, arithmetic and copies ran while one was open for 5% -> 4% of each run, Pallas kernels for 22% -> 19%
where the time goes in v6:
time: 116 us
  Pallas kernels  45.6 us (39%)
  starting transfers between devices  33.7 us (29%)
  waiting for transfers between devices  20.4 us (18%)
  local copies, waits for them, and re-layouts  9.97 us (9%)
  between operations  3.47 us (3%)
  other arithmetic  2.32 us (2%)
    pallas_call x2, Pallas kernels, tap_grads(): pl.pallas_call(functools.partial(taps_kernel, first=first, last=last), in...  17.6 us
    ppermute x11, starting transfers between devices, swap(): return lax.ppermute(value, axis, [(i, i ^ shift) for i in range(count)])  16 us
    ppermute x11, waiting for transfers between devices, swap(): return lax.ppermute(value, axis, [(i, i ^ shift) for i in range(count)])  15.2 us
    pallas_call x1, Pallas kernels, conv_inner(): pl.pallas_call(inner_kernel, in_specs=[in_vmem] * 7, out_specs=[in_vmem]...  11.5 us
    pallas_call x1, Pallas kernels, head(): pl.pallas_call(functools.partial(head_kernel, count=count, image_count=im...  9.7 us
    ppermute x2, starting transfers between devices, next_along(): lax.ppermute(value, axis, [(i, i + 1) for i in range(lax.axis_size(axis)...  7.98 us
    unnamed x36, local copies, waits for them, and re-layouts  5.35 us
    pallas_call x1, Pallas kernels, conv_edge(): pl.pallas_call(edge_kernel, in_specs=[in_smem] + [in_vmem] * 9, out_specs...  4.78 us
  transfers between devices with their start and end apart: 21, of which 14 were waited for; matrix products, arithmetic and copies ran while one was open for 4% of the time, Pallas kernels for 19%

profile of v6, /device:TPU:0, one launch (start us, length us, event | category | flops | bytes accessed | tf_op | source)
XLA Modules:
  0.0 115.5 jit_solution(14070467033777886444)
XLA Ops:
  0.6 0.0 copy-start
  0.7 1.2 %fusion.6 = (bf16[16,3,768]{2,1,0:T(4,128)(2,1)S(1)}, bf16[16,3,768]{2,1,0:T(4,128)(2,1)S(1)}) fusion(bf16[16,64,768]{2,1,0:T(8,128)(2,1)} %bitcast.28), kind=kLoop, calls=%fused_computation.24 | loop fusion | bytes 294912 | tf_op jit(solution)/shard_map/slice | solution.py:672
  1.9 1.3 %collective-permute-start.1 = (bf16[16,3,768]{2,1,0:T(4,128)(2,1)S(1)}, bf16[16,3,768]{2,1,0:T(4,128)(2,1)S(1)}, u32[]{:S(2)}, u32[]{:S(2)}) collective-permute-start(bf16[16,3,768]{2,1,0:T(4,128)(2,1)S(1)} %get-tuple-element.118), channel_id=1, source_target_pairs={{1,0},{2,1},{3,2},{5,4},{6,5},{7,6},{9,8},{10,9},{11,10},{13,12},{... | collective-permute-start | bytes 221192 | tf_op jit(solution)/shard_map/ppermute | solution.py:101
  3.2 3.0 %collective-permute-start = (bf16[16,3,768]{2,1,0:T(4,128)(2,1)S(1)}, bf16[16,3,768]{2,1,0:T(4,128)(2,1)S(1)}, u32[]{:S(2)}, u32[]{:S(2)}) collective-permute-start(bf16[16,3,768]{2,1,0:T(4,128)(2,1)S(1)} %get-tuple-element.117), channel_id=1, source_target_pairs={{0,1},{1,2},{2,3},{4,5},{5,6},{6,7},{8,9},{9,10},{10,11},{12,13},{... | collective-permute-start | bytes 221192 | tf_op jit(solution)/shard_map/ppermute | solution.py:97
  6.3 1.1 fusion.5
  7.4 0.7 broadcast_in_dim.32.bias
  8.1 0.1 pad.7.clone
  8.2 0.0 collective-permute-done.1.right
  8.2 0.0 collective-permute-done.left
  8.3 0.2 maximum_maximum_fusion.1
  8.5 4.9 %collective-permute-start.2 = (bf16[224,768]{1,0:T(8,128)(2,1)S(1)}, bf16[224,768]{1,0:T(8,128)(2,1)S(1)}, u32[]{:S(2)}, u32[]{:S(2)}) collective-permute-start(bf16[224,768]{1,0:T(8,128)(2,1)S(1)} %get-tuple-element.68), channel_id=1, source_target_pairs={{0,4},{4,8},{8,12},{1,5},{5,9},{9,13},{2,6},{6,10},{10,14},{3,7},{... | collective-permute-start | bytes 1032200 | tf_op jit(solution)/shard_map/ppermute | solution.py:97
  13.5 1.3 %collective-permute-start.3 = (bf16[224,768]{1,0:T(8,128)(2,1)S(1)}, bf16[224,768]{1,0:T(8,128)(2,1)S(1)}, u32[]{:S(2)}, u32[]{:S(2)}) collective-permute-start(bf16[224,768]{1,0:T(8,128)(2,1)S(1)} %get-tuple-element.69), channel_id=1, source_target_pairs={{4,0},{8,4},{12,8},{5,1},{9,5},{13,9},{6,2},{10,6},{14,10},{7,3},{... | collective-permute-start | bytes 1032200 | tf_op jit(solution)/shard_map/ppermute | solution.py:101
  14.8 11.5 %conv_inner.1 = (f32[6,16,14,8,128]{4,3,2,1,0:T(8,128)S(1)}, bf16[640,768]{1,0:T(8,128)(2,1)S(1)}, f32[640,256]{1,0:T(8,128)S(1)}, bf16[640,256]{1,0:T(8,128)(2,...) custom-call(bf16[16,64,768]{2,1,0:T(8,128)(2,1)S(1)} %bitcast.29, ...), custom_call_target="tpu_custom_call" | custom-call | flops 10000000000 | bytes 10000000 | tf_op jit(solution)/shard_map/conv_inner/pallas_call | solution.py:279
  26.4 0.8 copy-done.16
  27.1 0.0 collective-permute-done.2.top
  27.1 0.0 collective-permute-done.3.bottom
  27.1 4.8 %conv_edge.1 = (f32[6,3,14,8,128]{4,3,2,1,0:T(8,128)S(1)}, f32[6,3,14,8,128]{4,3,2,1,0:T(8,128)S(1)}, bf16[384,768]{1,0:T(8,128)(2,1)S(1)}, f32[384,256]{1,0:T(8...) custom-call(s32[1]{0:T(128)} %bitcast.3.flag, ...), custom_call_target="tpu_custom_call" | custom-call | flops 6000000000 | bytes 6000000 | tf_op jit(solution)/shard_map/conv_edge/pallas_call | solution.py:308
  32.0 0.0 copy-start.1
  32.0 0.0 copy-start.5
  32.0 0.9 collective-permute-start.4
  32.9 1.0 collective-permute-done.4
  33.9 2.7 %collective-permute-start.5 = (f32[104,256]{1,0:T(8,128)S(1)}, f32[104,256]{1,0:T(8,128)S(1)}, u32[]{:S(2)}, u32[]{:S(2)}) collective-permute-start(f32[104,256]{1,0:T(8,128)S(1)} %add.62), channel_id=1, source_target_pairs={{0,2},{1,3},{2,0},{3,1},{4,6},{5,7},{6,4},{7,5},{8,10},{9,11},{10,... | collective-permute-start | bytes 319496 | tf_op jit(solution)/shard_map/ppermute | solution.py:30
  36.5 1.0 prepare.1
  37.5 0.0 copy-start.6
  37.5 1.1 copy-done.6
  38.7 1.2 %collective-permute-done.5 = f32[104,256]{1,0:T(8,128)S(1)} collective-permute-done((f32[104,256]{1,0:T(8,128)S(1)}, f32[104,256]{1,0:T(8,128)S(1)}, u32[]{:S(2)}, u32[]{:S(2)}) %collective-permute-start.5) | collective-permute-done | bytes 106528 | tf_op jit(solution)/shard_map/ppermute | solution.py:30
  39.8 2.7 %collective-permute-start.6 = (f32[104,256]{1,0:T(8,128)S(1)}, f32[104,256]{1,0:T(8,128)S(1)}, u32[]{:S(2)}, u32[]{:S(2)}) collective-permute-start(f32[104,256]{1,0:T(8,128)S(1)} %add.63), channel_id=1, source_target_pairs={{0,4},{4,0},{8,12},{12,8},{1,5},{5,1},{9,13},{13,9},{2,6},{6,2},{1... | collective-permute-start | bytes 319496 | tf_op jit(solution)/shard_map/ppermute | solution.py:30
  42.6 2.8 %collective-permute-done.6 = f32[104,256]{1,0:T(8,128)S(1)} collective-permute-done((f32[104,256]{1,0:T(8,128)S(1)}, f32[104,256]{1,0:T(8,128)S(1)}, u32[]{:S(2)}, u32[]{:S(2)}) %collective-permute-start.6) | collective-permute-done | bytes 106528 | tf_op jit(solution)/shard_map/ppermute | solution.py:30
  45.3 3.0 %collective-permute-start.7 = (f32[104,256]{1,0:T(8,128)S(1)}, f32[104,256]{1,0:T(8,128)S(1)}, u32[]{:S(2)}, u32[]{:S(2)}) collective-permute-start(f32[104,256]{1,0:T(8,128)S(1)} %add.64), channel_id=1, source_target_pairs={{0,8},{4,12},{8,0},{12,4},{1,9},{5,13},{9,1},{13,5},{2,10},{6,14},... | collective-permute-start | bytes 319496 | tf_op jit(solution)/shard_map/ppermute | solution.py:30
  48.3 4.2 %collective-permute-done.7 = f32[104,256]{1,0:T(8,128)S(1)} collective-permute-done((f32[104,256]{1,0:T(8,128)S(1)}, f32[104,256]{1,0:T(8,128)S(1)}, u32[]{:S(2)}, u32[]{:S(2)}) %collective-permute-start.7) | collective-permute-done | bytes 106528 | tf_op jit(solution)/shard_map/ppermute | solution.py:30
  52.6 0.1 collective-permute-start.8
  53.3 0.6 collective-permute-done.8.other
  53.9 1.4 %copy-done.7 = bf16[768,1024]{1,0:T(8,128)(2,1)S(1)} copy-done((bf16[768,1024]{1,0:T(8,128)(2,1)S(1)}, bf16[768,1024]{1,0:T(8,128)(2,1)}, u32[]{:S(2)}) %copy-start.7) | copy-done | bytes 1572888
  55.3 1.0 copy-done.9
  56.3 1.0 copy-done.17
  57.3 9.7 %head.1 = (f32[272,256]{1,0:T(8,128)S(1)}, f32[320,768]{1,0:T(8,128)S(1)}, bf16[640,768]{1,0:T(8,128)(2,1)S(1)}, bf16[384,768]{1,0:T(8,128)(2,1)S(1)}) custom-call(s32[1]{0:T(128)} %bitcast.3.flag, s32[1]{0:T(128)S(6)} %copy.23.label, f32[10]{0:T(128)S(1)} %copy-done.5, f32[104,256]{1,0:T(8,128)S(1)} %add.65.own, ...), custom_call_target="tpu_custom_call" | custom-call | flops 10000000000 | bytes 10000000 | tf_op jit(solution)/shard_map/head/pallas_call | solution.py:478
  67.0 1.6 %collective-permute-start.9 = (f32[272,256]{1,0:T(8,128)S(1)}, f32[272,256]{1,0:T(8,128)S(1)}, u32[]{:S(2)}, u32[]{:S(2)}) collective-permute-start(f32[272,256]{1,0:T(8,128)S(1)} %get-tuple-element.105), channel_id=1, source_target_pairs={{0,16},{16,0},{1,17},{17,1},{2,18},{18,2},{3,19},{19,3},{4,20},{20... | collective-permute-start | bytes 835592 | tf_op jit(solution)/shard_map/ppermute | solution.py:30
  68.6 8.9 %tap_grads.2.payload_in = f32[320,768]{1,0:T(8,128)S(1)} custom-call(f32[6,16,14,8,128]{4,3,2,1,0:T(8,128)S(1)} %copy-done.11, f32[6,3,14,8,128]{4,3,2,1,0:T(8,128)S(1)} %copy-done.13, f32[6,3,14,8,128]{4,3,2,1,0:T(8,128)S(1)} %copy-done.15, bf16[640,768]{1,0:T(8,128)(2,1)S(1)} %get-tuple-element.96.grad_inner, ...), custom_call_target="tpu_custom_call", output_to_operand_aliasing={{}: (5, {})} | custom-call | flops 6000000000 | bytes 6000000 | tf_op jit(solution)/shard_map/tap_grads/pallas_call | solution.py:597
  77.5 0.1 slice_reduce_fusion.1
  77.7 8.7 %tap_grads.3 = f32[320,768]{1,0:T(8,128)S(1)} custom-call(f32[6,16,14,8,128]{4,3,2,1,0:T(8,128)S(1)} %copy-done.11, f32[6,3,14,8,128]{4,3,2,1,0:T(8,128)S(1)} %copy-done.13, f32[6,3,14,8,128]{4,3,2,1,0:T(8,128)S(1)} %copy-done.15, bf16[640,768]{1,0:T(8,128)(2,1)S(1)} %get-tuple-element.96.grad_inner, ...), custom_call_target="tpu_custom_call", output_to_operand_aliasing={{}: (5, {})} | custom-call | flops 6000000000 | bytes 6000000 | tf_op jit(solution)/shard_map/tap_grads/pallas_call | solution.py:597
  86.5 0.1 collective-permute-start.10
  86.5 1.9 %multiply_add_fusion = f32[10,256,256]{2,1,0:T(8,128)} fusion(f32[256,256]{1,0:T(8,128)S(1)} %slice.73, f32[10]{0:T(128)S(1)} %get-tuple-element.128, f32[256,256]{1,0:T(8,128)S(1)} %slice.71, f32[10]{0:T(128)S(1)} %get-tuple-element.129), kind=kLoop, calls=%fused_computation | loop fusion | flops 1966080 | bytes 3145808 | tf_op jit(solution)/shard_map/add | solution.py:39
  88.4 0.1 convert_add_fusion
  88.5 0.3 collective-permute-start.13
  88.8 1.5 %collective-permute-start.12 = (bf16[40,768]{1,0:T(8,128)(2,1)S(1)}, bf16[40,768]{1,0:T(8,128)(2,1)S(1)}, u32[]{:S(2)}, u32[]{:S(2)}) collective-permute-start(bf16[40,768]{1,0:T(8,128)(2,1)S(1)} %get-tuple-element.121), channel_id=1, source_target_pairs={{0,16},{1,17},{2,18},{3,19},{16,0},{17,1},{18,2},{19,3},{4,20},{5,... | collective-permute-start | bytes 184328 | tf_op jit(solution)/shard_map/ppermute | solution.py:73
  90.3 1.8 %collective-permute-start.11 = (bf16[40,768]{1,0:T(8,128)(2,1)S(1)}, bf16[40,768]{1,0:T(8,128)(2,1)S(1)}, u32[]{:S(2)}, u32[]{:S(2)}) collective-permute-start(bf16[40,768]{1,0:T(8,128)(2,1)S(1)} %get-tuple-element.119), channel_id=1, source_target_pairs={{0,2},{1,3},{2,0},{3,1},{16,18},{17,19},{18,16},{19,17},{4,6},{5,7... | collective-permute-start | bytes 184328 | tf_op jit(solution)/shard_map/ppermute | solution.py:73
  92.1 0.5 slice.88
  93.3 1.0 collective-permute-done.13
  94.3 0.9 collective-permute-done.11
  95.3 4.3 %collective-permute-start.16 = (bf16[40,768]{1,0:T(8,128)(2,1)S(1)}, bf16[40,768]{1,0:T(8,128)(2,1)S(1)}, u32[]{:S(2)}, u32[]{:S(2)}) collective-permute-start(bf16[40,768]{1,0:T(8,128)(2,1)S(1)} %fusion.1), channel_id=1, source_target_pairs={{0,12},{4,8},{8,4},{12,0},{1,13},{5,9},{9,5},{13,1},{2,14},{6,10},... | collective-permute-start | bytes 184328 | tf_op jit(solution)/shard_map/ppermute | solution.py:30
  99.6 0.6 collective-permute-start.14
  100.2 0.6 slice_reduce_fusion
  100.9 1.0 collective-permute-done.16
  101.9 2.9 %collective-permute-done.15 = bf16[40,768]{1,0:T(8,128)(2,1)S(1)} collective-permute-done((bf16[40,768]{1,0:T(8,128)(2,1)S(1)}, bf16[40,768]{1,0:T(8,128)(2,1)S(1)}, u32[]{:S(2)}, u32[]{:S(2)}) %collective-permute-start.15) | collective-permute-done | bytes 61472 | tf_op jit(solution)/shard_map/ppermute | solution.py:30
  104.8 0.1 collective-permute-done.14
  104.9 1.1 collective-permute-start.17
  106.1 0.6 collective-permute-start.18
  106.6 1.9 %collective-permute-start.19 = (bf16[40,768]{1,0:T(8,128)(2,1)S(1)}, bf16[40,768]{1,0:T(8,128)(2,1)S(1)}, u32[]{:S(2)}, u32[]{:S(2)}) collective-permute-start(bf16[40,768]{1,0:T(8,128)(2,1)S(1)} %add_convert_fusion), channel_id=1, source_target_pairs={{0,18},{1,19},{2,16},{3,17},{16,2},{17,3},{18,0},{19,1},{4,22},{5,... | collective-permute-start | bytes 184328 | tf_op jit(solution)/shard_map/ppermute | solution.py:82
  108.5 0.9 collective-permute-done.17
  109.5 0.8 collective-permute-done.18
  110.3 1.5 %collective-permute-done.19 = bf16[40,768]{1,0:T(8,128)(2,1)S(1)} collective-permute-done((bf16[40,768]{1,0:T(8,128)(2,1)S(1)}, bf16[40,768]{1,0:T(8,128)(2,1)S(1)}, u32[]{:S(2)}, u32[]{:S(2)}) %collective-permute-start.19) | collective-permute-done | bytes 61472 | tf_op jit(solution)/shard_map/ppermute | solution.py:82
  111.8 0.1 collective-permute-start.20
  111.8 1.5 %collective-permute-done.20.other = bf16[160,768]{1,0:T(8,128)(2,1)S(1)} collective-permute-done((bf16[160,768]{1,0:T(8,128)(2,1)S(1)}, bf16[160,768]{1,0:T(8,128)(2,1)S(1)}, u32[]{:S(2)}, u32[]{:S(2)}) %collective-permute-start.20) | collective-permute-done | bytes 245792 | tf_op jit(solution)/shard_map/ppermute | solution.py:30
  113.3 1.0 finish.1
  (54 shorter events, 0.5 us)
Async XLA Ops:
  0.6 14.1 %copy-start = (bf16[1,16,64,768]{3,2,1,0:T(8,128)(2,1)S(1)}, bf16[1,16,64,768]{3,2,1,0:T(8,128)(2,1)}, u32[]{:S(2)}) copy-start(bf16[1,16,64,768]{3,2,1,0:T(8,128)(2,1)} %param.8) | copy-start | bytes 4718596
  0.6 14.1 %copy-start.4 = (f32[256]{0:T(256)S(1)}, f32[256]{0:T(256)}, u32[]{:S(2)}) copy-start(f32[256]{0:T(256)} %param.12) | copy-start | bytes 3076
  0.7 14.1 %copy-start.3 = (f32[7,7,768]{2,1,0:T(8,128)S(1)}, f32[7,7,768]{2,1,0:T(8,128)}, u32[]{:S(2)}) copy-start(f32[7,7,768]{2,1,0:T(8,128)} %weight.3) | copy-start | bytes 451588
  0.7 14.1 %copy-start.2 = (bf16[768,256]{1,0:T(8,128)(2,1)S(1)}, bf16[768,256]{1,0:T(8,128)(2,1)}, u32[]{:S(2)}) copy-start(bf16[768,256]{1,0:T(8,128)(2,1)} %reduce_weight.5) | copy-start | bytes 1179652
  1.9 6.2 %collective-permute-start.1 = (bf16[16,3,768]{2,1,0:T(4,128)(2,1)S(1)}, bf16[16,3,768]{2,1,0:T(4,128)(2,1)S(1)}, u32[]{:S(2)}, u32[]{:S(2)}) collective-permute-start(bf16[16,3,768]{2,1,0:T(4,128)(2,1)S(1)} %get-tuple-element.118), channel_id=1, source_target_pairs={{1,0},{2,1},{3,2},{5,4},{6,5},{7,6},{9,8},{10,9},{11,10},{13,12},{... | collective-permute-start | bytes 221192 | tf_op jit(solution)/shard_map/ppermute | solution.py:101
  3.2 5.0 %collective-permute-start = (bf16[16,3,768]{2,1,0:T(4,128)(2,1)S(1)}, bf16[16,3,768]{2,1,0:T(4,128)(2,1)S(1)}, u32[]{:S(2)}, u32[]{:S(2)}) collective-permute-start(bf16[16,3,768]{2,1,0:T(4,128)(2,1)S(1)} %get-tuple-element.117), channel_id=1, source_target_pairs={{0,1},{1,2},{2,3},{4,5},{5,6},{6,7},{8,9},{9,10},{10,11},{12,13},{... | collective-permute-start | bytes 221192 | tf_op jit(solution)/shard_map/ppermute | solution.py:97
  8.5 18.6 %collective-permute-start.2 = (bf16[224,768]{1,0:T(8,128)(2,1)S(1)}, bf16[224,768]{1,0:T(8,128)(2,1)S(1)}, u32[]{:S(2)}, u32[]{:S(2)}) collective-permute-start(bf16[224,768]{1,0:T(8,128)(2,1)S(1)} %get-tuple-element.68), channel_id=1, source_target_pairs={{0,4},{4,8},{8,12},{1,5},{5,9},{9,13},{2,6},{6,10},{10,14},{3,7},{... | collective-permute-start | bytes 1032200 | tf_op jit(solution)/shard_map/ppermute | solution.py:97
  13.5 13.7 %collective-permute-start.3 = (bf16[224,768]{1,0:T(8,128)(2,1)S(1)}, bf16[224,768]{1,0:T(8,128)(2,1)S(1)}, u32[]{:S(2)}, u32[]{:S(2)}) collective-permute-start(bf16[224,768]{1,0:T(8,128)(2,1)S(1)} %get-tuple-element.69), channel_id=1, source_target_pairs={{4,0},{8,4},{12,8},{5,1},{9,5},{13,9},{6,2},{10,6},{14,10},{7,3},{... | collective-permute-start | bytes 1032200 | tf_op jit(solution)/shard_map/ppermute | solution.py:101
  26.3 0.8 copy-start.16
  27.1 4.8 %copy-start.10 = (f32[6,16,14,8,128]{4,3,2,1,0:T(8,128)}, f32[6,16,14,8,128]{4,3,2,1,0:T(8,128)S(1)}, u32[]{:S(2)}) copy-start(f32[6,16,14,8,128]{4,3,2,1,0:T(8,128)S(1)} %get-tuple-element.66.spread_in) | copy-start | bytes 16515076
  31.9 20.6 %copy-start.12 = (f32[6,3,14,8,128]{4,3,2,1,0:T(8,128)}, f32[6,3,14,8,128]{4,3,2,1,0:T(8,128)S(1)}, u32[]{:S(2)}) copy-start(f32[6,3,14,8,128]{4,3,2,1,0:T(8,128)S(1)} %get-tuple-element.72.spread_top) | copy-start | bytes 3096580
  32.0 20.7 %copy-start.14 = (f32[6,3,14,8,128]{4,3,2,1,0:T(8,128)}, f32[6,3,14,8,128]{4,3,2,1,0:T(8,128)S(1)}, u32[]{:S(2)}) copy-start(f32[6,3,14,8,128]{4,3,2,1,0:T(8,128)S(1)} %get-tuple-element.73.spread_bottom) | copy-start | bytes 3096580
  32.0 22.0 %copy-start.1 = (bf16[10,256,256]{2,1,0:T(8,128)(2,1)S(1)}, bf16[10,256,256]{2,1,0:T(8,128)(2,1)}, u32[]{:S(2)}) copy-start(bf16[10,256,256]{2,1,0:T(8,128)(2,1)} %class_weight.1) | copy-start | bytes 3932164
  32.0 22.0 %copy-start.5 = (f32[10]{0:T(128)S(1)}, f32[10]{0:T(128)}, u32[]{:S(2)}) copy-start(f32[10]{0:T(128)} %class_bias.1) | copy-start | bytes 124
  32.0 1.9 %collective-permute-start.4 = (f32[104,256]{1,0:T(8,128)S(1)}, f32[104,256]{1,0:T(8,128)S(1)}, u32[]{:S(2)}, u32[]{:S(2)}) collective-permute-start(f32[104,256]{1,0:T(8,128)S(1)} %get-tuple-element.75), channel_id=1, source_target_pairs={{0,1},{1,0},{2,3},{3,2},{4,5},{5,4},{6,7},{7,6},{8,9},{9,8},{10,11... | collective-permute-start | bytes 319496 | tf_op jit(solution)/shard_map/ppermute | solution.py:30
  33.9 5.9 %collective-permute-start.5 = (f32[104,256]{1,0:T(8,128)S(1)}, f32[104,256]{1,0:T(8,128)S(1)}, u32[]{:S(2)}, u32[]{:S(2)}) collective-permute-start(f32[104,256]{1,0:T(8,128)S(1)} %add.62), channel_id=1, source_target_pairs={{0,2},{1,3},{2,0},{3,1},{4,6},{5,7},{6,4},{7,5},{8,10},{9,11},{10,... | collective-permute-start | bytes 319496 | tf_op jit(solution)/shard_map/ppermute | solution.py:30
  37.5 1.1 copy-start.6
  38.7 13.9 %copy-start.8 = (bf16[256,768]{1,0:T(8,128)(2,1)}, bf16[256,768]{1,0:T(8,128)(2,1)S(1)}, u32[]{:S(2)}) copy-start(bf16[256,768]{1,0:T(8,128)(2,1)S(1)} %get-tuple-element.95.reduce_turned) | copy-start | bytes 1179652
  39.8 5.5 %collective-permute-start.6 = (f32[104,256]{1,0:T(8,128)S(1)}, f32[104,256]{1,0:T(8,128)S(1)}, u32[]{:S(2)}, u32[]{:S(2)}) collective-permute-start(f32[104,256]{1,0:T(8,128)S(1)} %add.63), channel_id=1, source_target_pairs={{0,4},{4,0},{8,12},{12,8},{1,5},{5,1},{9,13},{13,9},{2,6},{6,2},{1... | collective-permute-start | bytes 319496 | tf_op jit(solution)/shard_map/ppermute | solution.py:30
  45.3 7.2 %collective-permute-start.7 = (f32[104,256]{1,0:T(8,128)S(1)}, f32[104,256]{1,0:T(8,128)S(1)}, u32[]{:S(2)}, u32[]{:S(2)}) collective-permute-start(f32[104,256]{1,0:T(8,128)S(1)} %add.64), channel_id=1, source_target_pairs={{0,8},{4,12},{8,0},{12,4},{1,9},{5,13},{9,1},{13,5},{2,10},{6,14},... | collective-permute-start | bytes 319496 | tf_op jit(solution)/shard_map/ppermute | solution.py:30
  52.6 1.4 %collective-permute-start.8 = (f32[104,256]{1,0:T(8,128)S(1)}, f32[104,256]{1,0:T(8,128)S(1)}, u32[]{:S(2)}, u32[]{:S(2)}) collective-permute-start(f32[104,256]{1,0:T(8,128)S(1)} %add.65.own), channel_id=1, source_target_pairs={{0,1},{1,0},{2,3},{3,2},{4,5},{5,4},{6,7},{7,6},{8,9},{9,8},{10,11... | collective-permute-start | bytes 319496 | tf_op jit(solution)/shard_map/ppermute | solution.py:30
  53.9 1.4 %copy-start.7 = (bf16[768,1024]{1,0:T(8,128)(2,1)S(1)}, bf16[768,1024]{1,0:T(8,128)(2,1)}, u32[]{:S(2)}) copy-start(bf16[768,1024]{1,0:T(8,128)(2,1)} %copy-done.6) | copy-start | bytes 4718596
  55.3 1.0 copy-start.9
  56.3 1.0 copy-start.17
  57.3 11.3 %copy-start.11 = (f32[6,16,14,8,128]{4,3,2,1,0:T(8,128)S(1)}, f32[6,16,14,8,128]{4,3,2,1,0:T(8,128)}, u32[]{:S(2)}) copy-start(f32[6,16,14,8,128]{4,3,2,1,0:T(8,128)} %copy-done.10) | copy-start | bytes 16515076
  57.3 11.3 %copy-start.13 = (f32[6,3,14,8,128]{4,3,2,1,0:T(8,128)S(1)}, f32[6,3,14,8,128]{4,3,2,1,0:T(8,128)}, u32[]{:S(2)}) copy-start(f32[6,3,14,8,128]{4,3,2,1,0:T(8,128)} %copy-done.12) | copy-start | bytes 3096580
  57.3 11.3 %copy-start.15 = (f32[6,3,14,8,128]{4,3,2,1,0:T(8,128)S(1)}, f32[6,3,14,8,128]{4,3,2,1,0:T(8,128)}, u32[]{:S(2)}) copy-start(f32[6,3,14,8,128]{4,3,2,1,0:T(8,128)} %copy-done.14) | copy-start | bytes 3096580
  67.0 10.5 %collective-permute-start.9 = (f32[272,256]{1,0:T(8,128)S(1)}, f32[272,256]{1,0:T(8,128)S(1)}, u32[]{:S(2)}, u32[]{:S(2)}) collective-permute-start(f32[272,256]{1,0:T(8,128)S(1)} %get-tuple-element.105), channel_id=1, source_target_pairs={{0,16},{16,0},{1,17},{17,1},{2,18},{18,2},{3,19},{19,3},{4,20},{20... | collective-permute-start | bytes 835592 | tf_op jit(solution)/shard_map/ppermute | solution.py:30
  86.5 1.9 %collective-permute-start.10 = (bf16[160,768]{1,0:T(8,128)(2,1)S(1)}, bf16[160,768]{1,0:T(8,128)(2,1)S(1)}, u32[]{:S(2)}, u32[]{:S(2)}) collective-permute-start(bf16[160,768]{1,0:T(8,128)(2,1)S(1)} %select_convert_fusion), channel_id=1, source_target_pairs={{0,1},{1,0},{2,3},{3,2},{4,5},{5,4},{6,7},{7,6},{8,9},{9,8},{10,11... | collective-permute-start | bytes 737288 | tf_op jit(solution)/shard_map/ppermute | solution.py:30
  88.5 5.8 %collective-permute-start.13 = (bf16[40,768]{1,0:T(8,128)(2,1)S(1)}, bf16[40,768]{1,0:T(8,128)(2,1)S(1)}, u32[]{:S(2)}, u32[]{:S(2)}) collective-permute-start(bf16[40,768]{1,0:T(8,128)(2,1)S(1)} %get-tuple-element.120), channel_id=1, source_target_pairs={{0,18},{1,19},{2,16},{3,17},{16,2},{17,3},{18,0},{19,1},{4,22},{5,... | collective-permute-start | bytes 184328 | tf_op jit(solution)/shard_map/ppermute | solution.py:73
  88.8 5.5 %collective-permute-start.12 = (bf16[40,768]{1,0:T(8,128)(2,1)S(1)}, bf16[40,768]{1,0:T(8,128)(2,1)S(1)}, u32[]{:S(2)}, u32[]{:S(2)}) collective-permute-start(bf16[40,768]{1,0:T(8,128)(2,1)S(1)} %get-tuple-element.121), channel_id=1, source_target_pairs={{0,16},{1,17},{2,18},{3,19},{16,0},{17,1},{18,2},{19,3},{4,20},{5,... | collective-permute-start | bytes 184328 | tf_op jit(solution)/shard_map/ppermute | solution.py:73
  90.3 4.9 %collective-permute-start.11 = (bf16[40,768]{1,0:T(8,128)(2,1)S(1)}, bf16[40,768]{1,0:T(8,128)(2,1)S(1)}, u32[]{:S(2)}, u32[]{:S(2)}) collective-permute-start(bf16[40,768]{1,0:T(8,128)(2,1)S(1)} %get-tuple-element.119), channel_id=1, source_target_pairs={{0,2},{1,3},{2,0},{3,1},{16,18},{17,19},{18,16},{19,17},{4,6},{5,7... | collective-permute-start | bytes 184328 | tf_op jit(solution)/shard_map/ppermute | solution.py:73
  95.3 6.6 %collective-permute-start.16 = (bf16[40,768]{1,0:T(8,128)(2,1)S(1)}, bf16[40,768]{1,0:T(8,128)(2,1)S(1)}, u32[]{:S(2)}, u32[]{:S(2)}) collective-permute-start(bf16[40,768]{1,0:T(8,128)(2,1)S(1)} %fusion.1), channel_id=1, source_target_pairs={{0,12},{4,8},{8,4},{12,0},{1,13},{5,9},{9,5},{13,1},{2,14},{6,10},... | collective-permute-start | bytes 184328 | tf_op jit(solution)/shard_map/ppermute | solution.py:30
  99.6 5.2 %collective-permute-start.15 = (bf16[40,768]{1,0:T(8,128)(2,1)S(1)}, bf16[40,768]{1,0:T(8,128)(2,1)S(1)}, u32[]{:S(2)}, u32[]{:S(2)}) collective-permute-start(bf16[40,768]{1,0:T(8,128)(2,1)S(1)} %fusion.1), channel_id=1, source_target_pairs={{0,8},{4,12},{8,0},{12,4},{1,9},{5,13},{9,1},{13,5},{2,10},{6,14},... | collective-permute-start | bytes 184328 | tf_op jit(solution)/shard_map/ppermute | solution.py:30
  99.6 5.3 %collective-permute-start.14 = (bf16[40,768]{1,0:T(8,128)(2,1)S(1)}, bf16[40,768]{1,0:T(8,128)(2,1)S(1)}, u32[]{:S(2)}, u32[]{:S(2)}) collective-permute-start(bf16[40,768]{1,0:T(8,128)(2,1)S(1)} %fusion.1), channel_id=1, source_target_pairs={{0,4},{4,0},{8,12},{12,8},{1,5},{5,1},{9,13},{13,9},{2,6},{6,2},{1... | collective-permute-start | bytes 184328 | tf_op jit(solution)/shard_map/ppermute | solution.py:30
  104.9 4.5 %collective-permute-start.17 = (bf16[40,768]{1,0:T(8,128)(2,1)S(1)}, bf16[40,768]{1,0:T(8,128)(2,1)S(1)}, u32[]{:S(2)}, u32[]{:S(2)}) collective-permute-start(bf16[40,768]{1,0:T(8,128)(2,1)S(1)} %add_convert_fusion), channel_id=1, source_target_pairs={{0,2},{1,3},{2,0},{3,1},{16,18},{17,19},{18,16},{19,17},{4,6},{5,7... | collective-permute-start | bytes 184328 | tf_op jit(solution)/shard_map/ppermute | solution.py:82
  106.1 4.2 %collective-permute-start.18 = (bf16[40,768]{1,0:T(8,128)(2,1)S(1)}, bf16[40,768]{1,0:T(8,128)(2,1)S(1)}, u32[]{:S(2)}, u32[]{:S(2)}) collective-permute-start(bf16[40,768]{1,0:T(8,128)(2,1)S(1)} %add_convert_fusion), channel_id=1, source_target_pairs={{0,16},{1,17},{2,18},{3,19},{16,0},{17,1},{18,2},{19,3},{4,20},{5,... | collective-permute-start | bytes 184328 | tf_op jit(solution)/shard_map/ppermute | solution.py:82
  106.6 5.1 %collective-permute-start.19 = (bf16[40,768]{1,0:T(8,128)(2,1)S(1)}, bf16[40,768]{1,0:T(8,128)(2,1)S(1)}, u32[]{:S(2)}, u32[]{:S(2)}) collective-permute-start(bf16[40,768]{1,0:T(8,128)(2,1)S(1)} %add_convert_fusion), channel_id=1, source_target_pairs={{0,18},{1,19},{2,16},{3,17},{16,2},{17,3},{18,0},{19,1},{4,22},{5,... | collective-permute-start | bytes 184328 | tf_op jit(solution)/shard_map/ppermute | solution.py:82
  111.8 1.6 %collective-permute-start.20 = (bf16[160,768]{1,0:T(8,128)(2,1)S(1)}, bf16[160,768]{1,0:T(8,128)(2,1)S(1)}, u32[]{:S(2)}, u32[]{:S(2)}) collective-permute-start(bf16[160,768]{1,0:T(8,128)(2,1)S(1)} %bitcast.30), channel_id=1, source_target_pairs={{0,1},{1,0},{2,3},{3,2},{4,5},{5,4},{6,7},{7,6},{8,9},{9,8},{10,11... | collective-permute-start | bytes 737288 | tf_op jit(solution)/shard_map/ppermute | solution.py:30

commit v7 on v6

--- a/solution.py
+++ b/solution.py
@@ -67,7 +67,9 @@
     pieces = value.reshape((4, value.shape[0] // 4) + value.shape[1:])
 
     def piece(turn):
-        return lax.dynamic_index_in_dim(pieces, places[turn], 0, keepdims=False)
+        starts = (places[turn],) + (0,) * value.ndim
+        sizes = (1,) + pieces.shape[1:]
+        return lax.dynamic_slice(pieces, starts, sizes, allow_negative_indices=False)[0]
 
     moved = [
         lax.ppermute(piece(turn).astype(sent_as), axes, pairs[turn]).astype(wide)
@@ -80,7 +82,8 @@
     whole = jnp.zeros((4,) + value.shape, value.dtype)
     for turn in range(4):
         part = lax.ppermute(value, axes, pairs[turn]) if turn else value
-        whole = lax.dynamic_update_index_in_dim(whole, part, places[turn], 0)
+        starts = (places[turn],) + (0,) * value.ndim
+        whole = lax.dynamic_update_slice(whole, part[None], starts, allow_negative_indices=False)
     return whole.reshape((-1,) + value.shape[1:])
 
 
@@ -532,7 +535,7 @@
 
 
 def taps_kernel(
-    spread_in, spread_top, spread_bottom, grad_inner, grad_edge, payload_in, payload, grads, *,
+    spread_in, spread_top, spread_bottom, grad_inner, grad_edge, payload_in, payload, grads, out, *,
     first, last,
 ):
     rows = spread_in.shape[1]
@@ -580,12 +583,13 @@
                             total[row_tap, col_tap] += windows[step + col_tap] * grad
             for (row_tap, col_tap), value in total.items():
                 tap = row_tap * KERNEL + col_tap
-                payload[base + tap : base + tap + 1, lanes] = jnp.sum(value, axis=0, keepdims=True)
+                out[tap : tap + 1, :] = jnp.sum(value, axis=0, keepdims=True)
         total = [jnp.zeros((GROUPS, LANES), wide) for _ in range(KERNEL)]
         for index in range(rows * steps):
             slot = index % KERNEL
             total[slot] = total[slot] + grads[index // steps, index % steps]
-        payload[base + taps : base + taps + 1, lanes] = jnp.sum(sum(total), axis=0, keepdims=True)
+        out[taps : taps + 1, :] = jnp.sum(sum(total), axis=0, keepdims=True)
+        payload[pl.ds(base, taps + 1), lanes] = out[: taps + 1, :]
         return 0
 
     lax.fori_loop(first, last, one_tile, 0)
@@ -600,7 +604,10 @@
         out_specs=in_vmem,
         out_shape=shape_of(payload.shape),
         input_output_aliases={5: 0},
-        scratch_shapes=[pltpu.VMEM((rows, steps, GROUPS, LANES), wide)],
+        scratch_shapes=[
+            pltpu.VMEM((rows, steps, GROUPS, LANES), wide),
+            pltpu.VMEM((TAPS_ROWS, LANES), wide),
+        ],
         compiler_params=params(16),
         cost_estimate=cost(2 * (last - first)),
         name="tap_grads",
@@ -734,6 +741,7 @@
     axes = ("dp", "sx")
     pairs = square_pairs(axes, (1, 2))
     payload = square_scatter(payload, axes, pairs, places, narrow)
+    payload, known = together((payload, known))
     class_weight_grad = tree_sum(
         [part[width : width + classes, 0][:, None, None] * part[None, :width] for part in known]
     )

time: 116 us -> 107 us (0.922)
  Pallas kernels: 45.6 us -> 38.9 us
  local copies, waits for them, and re-layouts: 9.97 us -> 4.65 us
  waiting for transfers between devices: 20.4 us -> 23 us
    pallas_call x2, Pallas kernels: 17.6 us -> 10.9 us  [tap_grads(): pl.pallas_call(functools.partial(taps_kernel, first=first, last=last), in...]
    unnamed x36 -> x12, local copies, waits for them, and re-layouts: 5.35 us -> 0.03 us
  transfers between devices with their start and end apart: 21 -> 21, of which waited for: 14 -> 14; matrix products, arithmetic and copies ran while one was open for 4% -> 5% of each run, Pallas kernels for 19% -> 17%
where the time goes in v7:
time: 107 us; the launch traced here: 106 us
  Pallas kernels  38.9 us (36%)
  starting transfers between devices  34.1 us (32%)
  waiting for transfers between devices  23 us (21%)
  local copies, waits for them, and re-layouts  4.65 us (4%)
  between operations  3.38 us (3%)
  other arithmetic  2.31 us (2%)
    ppermute x11, starting transfers between devices, swap(): return lax.ppermute(value, axis, [(i, i ^ shift) for i in range(count)])  16.4 us
    ppermute x11, waiting for transfers between devices, swap(): return lax.ppermute(value, axis, [(i, i ^ shift) for i in range(count)])  16.3 us
    pallas_call x1, Pallas kernels, conv_inner(): pl.pallas_call(inner_kernel, in_specs=[in_vmem] * 7, out_specs=[in_vmem]...  11.5 us
    pallas_call x2, Pallas kernels, tap_grads(): pl.pallas_call(functools.partial(taps_kernel, first=first, last=last), in...  10.9 us
    pallas_call x1, Pallas kernels, head(): pl.pallas_call(functools.partial(head_kernel, count=count, image_count=im...  9.7 us
    ppermute x2, starting transfers between devices, next_along(): lax.ppermute(value, axis, [(i, i + 1) for i in range(lax.axis_size(axis)...  7.98 us
    pallas_call x1, Pallas kernels, conv_edge(): pl.pallas_call(edge_kernel, in_specs=[in_smem] + [in_vmem] * 9, out_specs...  4.78 us
    ppermute x3, waiting for transfers between devices, square_gather(): part = lax.ppermute(value, axes, pairs[turn]) if turn else value  3.9 us
  transfers between devices with their start and end apart: 21, of which 14 were waited for; matrix products, arithmetic and copies ran while one was open for 5% of the time, Pallas kernels for 17%

profile of v7, /device:TPU:0, one launch (start us, length us, event | category | flops | bytes accessed | tf_op | source)
XLA Modules:
  0.0 106.3 jit_solution(11404472739255135032)
XLA Ops:
  0.6 0.0 copy-start
  0.6 0.0 copy-start.4
  0.7 0.0 copy-start.3
  0.7 1.2 %fusion.5 = (bf16[16,3,768]{2,1,0:T(4,128)(2,1)S(1)}, bf16[16,3,768]{2,1,0:T(4,128)(2,1)S(1)}) fusion(bf16[16,64,768]{2,1,0:T(8,128)(2,1)} %bitcast.26), kind=kLoop, calls=%fused_computation.23 | loop fusion | bytes 294912 | tf_op jit(solution)/shard_map/slice | solution.py:679
  1.9 1.3 %collective-permute-start.1 = (bf16[16,3,768]{2,1,0:T(4,128)(2,1)S(1)}, bf16[16,3,768]{2,1,0:T(4,128)(2,1)S(1)}, u32[]{:S(2)}, u32[]{:S(2)}) collective-permute-start(bf16[16,3,768]{2,1,0:T(4,128)(2,1)S(1)} %get-tuple-element.124), channel_id=1, source_target_pairs={{1,0},{2,1},{3,2},{5,4},{6,5},{7,6},{9,8},{10,9},{11,10},{13,12},{... | collective-permute-start | bytes 221192 | tf_op jit(solution)/shard_map/ppermute | solution.py:104
  3.2 3.0 %collective-permute-start = (bf16[16,3,768]{2,1,0:T(4,128)(2,1)S(1)}, bf16[16,3,768]{2,1,0:T(4,128)(2,1)S(1)}, u32[]{:S(2)}, u32[]{:S(2)}) collective-permute-start(bf16[16,3,768]{2,1,0:T(4,128)(2,1)S(1)} %get-tuple-element.123), channel_id=1, source_target_pairs={{0,1},{1,2},{2,3},{4,5},{5,6},{6,7},{8,9},{9,10},{10,11},{12,13},{... | collective-permute-start | bytes 221192 | tf_op jit(solution)/shard_map/ppermute | solution.py:100
  6.3 1.1 %fusion.4 = (bf16[1,3,64,768]{3,2,1,0:T(8,128)(2,1)S(1)}, bf16[1,3,64,768]{3,2,1,0:T(8,128)(2,1)S(1)}) fusion(bf16[1,16,64,768]{3,2,1,0:T(8,128)(2,1)} %param.8), kind=kLoop, calls=%fused_computation.22 | loop fusion | bytes 1179648 | tf_op jit(solution)/shard_map/slice | solution.py:657
  7.4 0.7 broadcast_in_dim.31.bias
  8.1 0.1 pad.7.clone
  8.1 0.0 collective-permute-done.1.right
  8.2 0.0 collective-permute-done.left
  8.3 0.2 maximum_maximum_fusion.1
  8.5 4.9 %collective-permute-start.2 = (bf16[224,768]{1,0:T(8,128)(2,1)S(1)}, bf16[224,768]{1,0:T(8,128)(2,1)S(1)}, u32[]{:S(2)}, u32[]{:S(2)}) collective-permute-start(bf16[224,768]{1,0:T(8,128)(2,1)S(1)} %get-tuple-element.71), channel_id=1, source_target_pairs={{0,4},{4,8},{8,12},{1,5},{5,9},{9,13},{2,6},{6,10},{10,14},{3,7},{... | collective-permute-start | bytes 1032200 | tf_op jit(solution)/shard_map/ppermute | solution.py:100
  13.5 1.3 %collective-permute-start.3 = (bf16[224,768]{1,0:T(8,128)(2,1)S(1)}, bf16[224,768]{1,0:T(8,128)(2,1)S(1)}, u32[]{:S(2)}, u32[]{:S(2)}) collective-permute-start(bf16[224,768]{1,0:T(8,128)(2,1)S(1)} %get-tuple-element.72), channel_id=1, source_target_pairs={{4,0},{8,4},{12,8},{5,1},{9,5},{13,9},{6,2},{10,6},{14,10},{7,3},{... | collective-permute-start | bytes 1032200 | tf_op jit(solution)/shard_map/ppermute | solution.py:104
  14.8 11.5 %conv_inner.1 = (f32[6,16,14,8,128]{4,3,2,1,0:T(8,128)S(1)}, bf16[640,768]{1,0:T(8,128)(2,1)S(1)}, f32[640,256]{1,0:T(8,128)S(1)}, bf16[640,256]{1,0:T(8,128)(2,...) custom-call(bf16[16,64,768]{2,1,0:T(8,128)(2,1)S(1)} %bitcast.27, ...), custom_call_target="tpu_custom_call" | custom-call | flops 10000000000 | bytes 10000000 | tf_op jit(solution)/shard_map/conv_inner/pallas_call | solution.py:282
  26.3 0.0 collective-permute-done.2.top
  26.3 0.0 collective-permute-done.3.bottom
  26.4 4.8 %conv_edge.1 = (f32[6,3,14,8,128]{4,3,2,1,0:T(8,128)S(1)}, f32[6,3,14,8,128]{4,3,2,1,0:T(8,128)S(1)}, bf16[384,768]{1,0:T(8,128)(2,1)S(1)}, f32[384,256]{1,0:T(8...) custom-call(s32[1]{0:T(128)} %bitcast.3.flag, ...), custom_call_target="tpu_custom_call" | custom-call | flops 6000000000 | bytes 6000000 | tf_op jit(solution)/shard_map/conv_edge/pallas_call | solution.py:311
  31.1 0.0 copy-start.1
  31.2 0.0 copy-start.5
  31.2 0.9 collective-permute-start.4
  32.1 1.0 collective-permute-done.4
  33.1 2.7 %collective-permute-start.5 = (f32[104,256]{1,0:T(8,128)S(1)}, f32[104,256]{1,0:T(8,128)S(1)}, u32[]{:S(2)}, u32[]{:S(2)}) collective-permute-start(f32[104,256]{1,0:T(8,128)S(1)} %add.44), channel_id=1, source_target_pairs={{0,2},{1,3},{2,0},{3,1},{4,6},{5,7},{6,4},{7,5},{8,10},{9,11},{10,... | collective-permute-start | bytes 319496 | tf_op jit(solution)/shard_map/ppermute | solution.py:30
  35.7 1.0 prepare.1
  36.7 2.3 %collective-permute-done.5 = f32[104,256]{1,0:T(8,128)S(1)} collective-permute-done((f32[104,256]{1,0:T(8,128)S(1)}, f32[104,256]{1,0:T(8,128)S(1)}, u32[]{:S(2)}, u32[]{:S(2)}) %collective-permute-start.5) | collective-permute-done | bytes 106528 | tf_op jit(solution)/shard_map/ppermute | solution.py:30
  39.0 2.7 %collective-permute-start.6 = (f32[104,256]{1,0:T(8,128)S(1)}, f32[104,256]{1,0:T(8,128)S(1)}, u32[]{:S(2)}, u32[]{:S(2)}) collective-permute-start(f32[104,256]{1,0:T(8,128)S(1)} %add.45), channel_id=1, source_target_pairs={{0,4},{4,0},{8,12},{12,8},{1,5},{5,1},{9,13},{13,9},{2,6},{6,2},{1... | collective-permute-start | bytes 319496 | tf_op jit(solution)/shard_map/ppermute | solution.py:30
  41.7 2.8 %collective-permute-done.6 = f32[104,256]{1,0:T(8,128)S(1)} collective-permute-done((f32[104,256]{1,0:T(8,128)S(1)}, f32[104,256]{1,0:T(8,128)S(1)}, u32[]{:S(2)}, u32[]{:S(2)}) %collective-permute-start.6) | collective-permute-done | bytes 106528 | tf_op jit(solution)/shard_map/ppermute | solution.py:30
  44.5 3.0 %collective-permute-start.7 = (f32[104,256]{1,0:T(8,128)S(1)}, f32[104,256]{1,0:T(8,128)S(1)}, u32[]{:S(2)}, u32[]{:S(2)}) collective-permute-start(f32[104,256]{1,0:T(8,128)S(1)} %add.46), channel_id=1, source_target_pairs={{0,8},{4,12},{8,0},{12,4},{1,9},{5,13},{9,1},{13,5},{2,10},{6,14},... | collective-permute-start | bytes 319496 | tf_op jit(solution)/shard_map/ppermute | solution.py:30
  47.5 4.2 %collective-permute-done.7 = f32[104,256]{1,0:T(8,128)S(1)} collective-permute-done((f32[104,256]{1,0:T(8,128)S(1)}, f32[104,256]{1,0:T(8,128)S(1)}, u32[]{:S(2)}, u32[]{:S(2)}) %collective-permute-start.7) | collective-permute-done | bytes 106528 | tf_op jit(solution)/shard_map/ppermute | solution.py:30
  51.7 0.1 collective-permute-start.8
  52.5 0.7 collective-permute-done.8.other
  53.1 9.7 %head.1 = (f32[272,256]{1,0:T(8,128)S(1)}, f32[320,768]{1,0:T(8,128)S(1)}, bf16[640,768]{1,0:T(8,128)(2,1)S(1)}, bf16[384,768]{1,0:T(8,128)(2,1)S(1)}) custom-call(s32[1]{0:T(128)} %bitcast.3.flag, s32[1]{0:T(128)S(6)} %copy.23.label, f32[10]{0:T(128)S(1)} %copy-done.5, f32[104,256]{1,0:T(8,128)S(1)} %add.47.own, ...), custom_call_target="tpu_custom_call" | custom-call | flops 10000000000 | bytes 10000000 | tf_op jit(solution)/shard_map/head/pallas_call | solution.py:481
  62.8 1.6 %collective-permute-start.9 = (f32[272,256]{1,0:T(8,128)S(1)}, f32[272,256]{1,0:T(8,128)S(1)}, u32[]{:S(2)}, u32[]{:S(2)}) collective-permute-start(f32[272,256]{1,0:T(8,128)S(1)} %get-tuple-element.111), channel_id=1, source_target_pairs={{0,16},{16,0},{1,17},{17,1},{2,18},{18,2},{3,19},{19,3},{4,20},{20... | collective-permute-start | bytes 835592 | tf_op jit(solution)/shard_map/ppermute | solution.py:30
  64.4 5.4 %tap_grads.2.payload_in = f32[320,768]{1,0:T(8,128)S(1)} custom-call(f32[6,16,14,8,128]{4,3,2,1,0:T(8,128)S(1)} %get-tuple-element.69.spread_in, f32[6,3,14,8,128]{4,3,2,1,0:T(8,128)S(1)} %get-tuple-element.75.spread_top, f32[6,3,14,8,128]{4,3,2,1,0:T(8,128)S(1)} %get-tuple-element.76.spread_bottom, ...), custom_call_target="tpu_custom_call", output_to_operand_aliasing={{}: (5, {})} | custom-call | flops 6000000000 | bytes 6000000 | tf_op jit(solution)/shard_map/tap_grads/pallas_call | solution.py:601
  69.8 1.8 %collective-permute-done.9 = f32[272,256]{1,0:T(8,128)S(1)} collective-permute-done((f32[272,256]{1,0:T(8,128)S(1)}, f32[272,256]{1,0:T(8,128)S(1)}, u32[]{:S(2)}, u32[]{:S(2)}) %collective-permute-start.9) | collective-permute-done | bytes 278560 | tf_op jit(solution)/shard_map/ppermute | solution.py:30
  71.6 5.4 %tap_grads.3 = f32[320,768]{1,0:T(8,128)S(1)} custom-call(f32[6,16,14,8,128]{4,3,2,1,0:T(8,128)S(1)} %get-tuple-element.69.spread_in, f32[6,3,14,8,128]{4,3,2,1,0:T(8,128)S(1)} %get-tuple-element.75.spread_top, f32[6,3,14,8,128]{4,3,2,1,0:T(8,128)S(1)} %get-tuple-element.76.spread_bottom, ...), custom_call_target="tpu_custom_call", output_to_operand_aliasing={{}: (5, {})} | custom-call | flops 6000000000 | bytes 6000000 | tf_op jit(solution)/shard_map/tap_grads/pallas_call | solution.py:601
  77.1 0.1 collective-permute-start.10
  77.2 1.5 %collective-permute-done.10 = bf16[160,768]{1,0:T(8,128)(2,1)S(1)} collective-permute-done((bf16[160,768]{1,0:T(8,128)(2,1)S(1)}, bf16[160,768]{1,0:T(8,128)(2,1)S(1)}, u32[]{:S(2)}, u32[]{:S(2)}) %collective-permute-start.10) | collective-permute-done | bytes 245792 | tf_op jit(solution)/shard_map/ppermute | solution.py:30
  78.7 0.1 convert_add_fusion
  78.8 1.2 %collective-permute-start.13 = (bf16[40,768]{1,0:T(8,128)(2,1)S(1)}, bf16[40,768]{1,0:T(8,128)(2,1)S(1)}, u32[]{:S(2)}, u32[]{:S(2)}) collective-permute-start(bf16[40,768]{1,0:T(8,128)(2,1)S(1)} %get-tuple-element.126), channel_id=1, source_target_pairs={{0,18},{1,19},{2,16},{3,17},{16,2},{17,3},{18,0},{19,1},{4,22},{5,... | collective-permute-start | bytes 184328 | tf_op jit(solution)/shard_map/ppermute | solution.py:75
  80.0 0.5 collective-permute-start.12
  80.6 1.8 %collective-permute-start.11 = (bf16[40,768]{1,0:T(8,128)(2,1)S(1)}, bf16[40,768]{1,0:T(8,128)(2,1)S(1)}, u32[]{:S(2)}, u32[]{:S(2)}) collective-permute-start(bf16[40,768]{1,0:T(8,128)(2,1)S(1)} %get-tuple-element.125), channel_id=1, source_target_pairs={{0,2},{1,3},{2,0},{3,1},{16,18},{17,19},{18,16},{19,17},{4,6},{5,7... | collective-permute-start | bytes 184328 | tf_op jit(solution)/shard_map/ppermute | solution.py:75
  82.3 2.0 %collective-permute-done.13 = bf16[40,768]{1,0:T(8,128)(2,1)S(1)} collective-permute-done((bf16[40,768]{1,0:T(8,128)(2,1)S(1)}, bf16[40,768]{1,0:T(8,128)(2,1)S(1)}, u32[]{:S(2)}, u32[]{:S(2)}) %collective-permute-start.13) | collective-permute-done | bytes 61472 | tf_op jit(solution)/shard_map/ppermute | solution.py:75
  84.3 0.0 collective-permute-done.12
  84.3 0.8 collective-permute-done.11
  85.1 4.7 %collective-permute-start.16 = (bf16[40,768]{1,0:T(8,128)(2,1)S(1)}, bf16[40,768]{1,0:T(8,128)(2,1)S(1)}, u32[]{:S(2)}, u32[]{:S(2)}) collective-permute-start(bf16[40,768]{1,0:T(8,128)(2,1)S(1)} %fusion), channel_id=1, source_target_pairs={{0,12},{4,8},{8,4},{12,0},{1,13},{5,9},{9,5},{13,1},{2,14},{6,10},... | collective-permute-start | bytes 184328 | tf_op jit(solution)/shard_map/ppermute | solution.py:30
  89.8 0.0 collective-permute-start.15
  89.8 0.6 collective-permute-start.14
  90.5 0.1 slice_reduce_fusion.1
  90.7 0.5 slice.88
  91.8 1.9 %multiply_add_fusion = f32[10,256,256]{2,1,0:T(8,128)} fusion(f32[256,256]{1,0:T(8,128)S(1)} %slice.73, f32[10]{0:T(128)S(1)} %get-tuple-element.134, f32[256,256]{1,0:T(8,128)S(1)} %slice.71, f32[10]{0:T(128)S(1)} %get-tuple-element.135), kind=kLoop, calls=%fused_computation | loop fusion | flops 1966080 | bytes 3145808 | tf_op jit(solution)/shard_map/add | solution.py:39
  93.7 0.6 slice_reduce_fusion
  94.3 0.0 collective-permute-done.16
  94.3 0.6 collective-permute-done.15
  95.0 0.0 collective-permute-done.14
  95.0 0.9 collective-permute-start.17
  95.9 1.5 %collective-permute-start.18 = (bf16[40,768]{1,0:T(8,128)(2,1)S(1)}, bf16[40,768]{1,0:T(8,128)(2,1)S(1)}, u32[]{:S(2)}, u32[]{:S(2)}) collective-permute-start(bf16[40,768]{1,0:T(8,128)(2,1)S(1)} %add_convert_fusion), channel_id=1, source_target_pairs={{0,16},{1,17},{2,18},{3,19},{16,0},{17,1},{18,2},{19,3},{4,20},{5,... | collective-permute-start | bytes 184328 | tf_op jit(solution)/shard_map/ppermute | solution.py:84
  97.4 1.2 %collective-permute-start.19 = (bf16[40,768]{1,0:T(8,128)(2,1)S(1)}, bf16[40,768]{1,0:T(8,128)(2,1)S(1)}, u32[]{:S(2)}, u32[]{:S(2)}) collective-permute-start(bf16[40,768]{1,0:T(8,128)(2,1)S(1)} %add_convert_fusion), channel_id=1, source_target_pairs={{0,18},{1,19},{2,16},{3,17},{16,2},{17,3},{18,0},{19,1},{4,22},{5,... | collective-permute-start | bytes 184328 | tf_op jit(solution)/shard_map/ppermute | solution.py:84
  98.6 1.3 %collective-permute-done.17 = bf16[40,768]{1,0:T(8,128)(2,1)S(1)} collective-permute-done((bf16[40,768]{1,0:T(8,128)(2,1)S(1)}, bf16[40,768]{1,0:T(8,128)(2,1)S(1)}, u32[]{:S(2)}, u32[]{:S(2)}) %collective-permute-start.17) | collective-permute-done | bytes 61472 | tf_op jit(solution)/shard_map/ppermute | solution.py:84
  100.0 0.2 collective-permute-done.18
  100.2 2.4 %collective-permute-done.19 = bf16[40,768]{1,0:T(8,128)(2,1)S(1)} collective-permute-done((bf16[40,768]{1,0:T(8,128)(2,1)S(1)}, bf16[40,768]{1,0:T(8,128)(2,1)S(1)}, u32[]{:S(2)}, u32[]{:S(2)}) %collective-permute-start.19) | collective-permute-done | bytes 61472 | tf_op jit(solution)/shard_map/ppermute | solution.py:84
  102.5 0.1 collective-permute-start.20
  102.6 1.5 %collective-permute-done.20.other = bf16[160,768]{1,0:T(8,128)(2,1)S(1)} collective-permute-done((bf16[160,768]{1,0:T(8,128)(2,1)S(1)}, bf16[160,768]{1,0:T(8,128)(2,1)S(1)}, u32[]{:S(2)}, u32[]{:S(2)}) %collective-permute-start.20) | collective-permute-done | bytes 245792 | tf_op jit(solution)/shard_map/ppermute | solution.py:30
  104.1 1.0 finish.1
  (30 shorter events, 0.5 us)
Async XLA Ops:
  0.6 14.1 %copy-start = (bf16[1,16,64,768]{3,2,1,0:T(8,128)(2,1)S(1)}, bf16[1,16,64,768]{3,2,1,0:T(8,128)(2,1)}, u32[]{:S(2)}) copy-start(bf16[1,16,64,768]{3,2,1,0:T(8,128)(2,1)} %param.8) | copy-start | bytes 4718596
  0.6 14.1 %copy-start.4 = (f32[256]{0:T(256)S(1)}, f32[256]{0:T(256)}, u32[]{:S(2)}) copy-start(f32[256]{0:T(256)} %param.12) | copy-start | bytes 3076
  0.7 14.1 %copy-start.3 = (f32[7,7,768]{2,1,0:T(8,128)S(1)}, f32[7,7,768]{2,1,0:T(8,128)}, u32[]{:S(2)}) copy-start(f32[7,7,768]{2,1,0:T(8,128)} %weight.3) | copy-start | bytes 451588
  0.7 14.1 %copy-start.2 = (bf16[768,256]{1,0:T(8,128)(2,1)S(1)}, bf16[768,256]{1,0:T(8,128)(2,1)}, u32[]{:S(2)}) copy-start(bf16[768,256]{1,0:T(8,128)(2,1)} %reduce_weight.5) | copy-start | bytes 1179652
  1.9 6.2 %collective-permute-start.1 = (bf16[16,3,768]{2,1,0:T(4,128)(2,1)S(1)}, bf16[16,3,768]{2,1,0:T(4,128)(2,1)S(1)}, u32[]{:S(2)}, u32[]{:S(2)}) collective-permute-start(bf16[16,3,768]{2,1,0:T(4,128)(2,1)S(1)} %get-tuple-element.124), channel_id=1, source_target_pairs={{1,0},{2,1},{3,2},{5,4},{6,5},{7,6},{9,8},{10,9},{11,10},{13,12},{... | collective-permute-start | bytes 221192 | tf_op jit(solution)/shard_map/ppermute | solution.py:104
  3.2 5.0 %collective-permute-start = (bf16[16,3,768]{2,1,0:T(4,128)(2,1)S(1)}, bf16[16,3,768]{2,1,0:T(4,128)(2,1)S(1)}, u32[]{:S(2)}, u32[]{:S(2)}) collective-permute-start(bf16[16,3,768]{2,1,0:T(4,128)(2,1)S(1)} %get-tuple-element.123), channel_id=1, source_target_pairs={{0,1},{1,2},{2,3},{4,5},{5,6},{6,7},{8,9},{9,10},{10,11},{12,13},{... | collective-permute-start | bytes 221192 | tf_op jit(solution)/shard_map/ppermute | solution.py:100
  8.5 17.8 %collective-permute-start.2 = (bf16[224,768]{1,0:T(8,128)(2,1)S(1)}, bf16[224,768]{1,0:T(8,128)(2,1)S(1)}, u32[]{:S(2)}, u32[]{:S(2)}) collective-permute-start(bf16[224,768]{1,0:T(8,128)(2,1)S(1)} %get-tuple-element.71), channel_id=1, source_target_pairs={{0,4},{4,8},{8,12},{1,5},{5,9},{9,13},{2,6},{6,10},{10,14},{3,7},{... | collective-permute-start | bytes 1032200 | tf_op jit(solution)/shard_map/ppermute | solution.py:100
  13.5 12.9 %collective-permute-start.3 = (bf16[224,768]{1,0:T(8,128)(2,1)S(1)}, bf16[224,768]{1,0:T(8,128)(2,1)S(1)}, u32[]{:S(2)}, u32[]{:S(2)}) collective-permute-start(bf16[224,768]{1,0:T(8,128)(2,1)S(1)} %get-tuple-element.72), channel_id=1, source_target_pairs={{4,0},{8,4},{12,8},{5,1},{9,5},{13,9},{6,2},{10,6},{14,10},{7,3},{... | collective-permute-start | bytes 1032200 | tf_op jit(solution)/shard_map/ppermute | solution.py:104
  31.1 22.0 %copy-start.1 = (bf16[10,256,256]{2,1,0:T(8,128)(2,1)S(1)}, bf16[10,256,256]{2,1,0:T(8,128)(2,1)}, u32[]{:S(2)}) copy-start(bf16[10,256,256]{2,1,0:T(8,128)(2,1)} %class_weight.1) | copy-start | bytes 3932164
  31.2 22.0 %copy-start.5 = (f32[10]{0:T(128)S(1)}, f32[10]{0:T(128)}, u32[]{:S(2)}) copy-start(f32[10]{0:T(128)} %class_bias.1) | copy-start | bytes 124
  31.2 1.9 %collective-permute-start.4 = (f32[104,256]{1,0:T(8,128)S(1)}, f32[104,256]{1,0:T(8,128)S(1)}, u32[]{:S(2)}, u32[]{:S(2)}) collective-permute-start(f32[104,256]{1,0:T(8,128)S(1)} %get-tuple-element.78), channel_id=1, source_target_pairs={{0,1},{1,0},{2,3},{3,2},{4,5},{5,4},{6,7},{7,6},{8,9},{9,8},{10,11... | collective-permute-start | bytes 319496 | tf_op jit(solution)/shard_map/ppermute | solution.py:30
  33.1 6.0 %collective-permute-start.5 = (f32[104,256]{1,0:T(8,128)S(1)}, f32[104,256]{1,0:T(8,128)S(1)}, u32[]{:S(2)}, u32[]{:S(2)}) collective-permute-start(f32[104,256]{1,0:T(8,128)S(1)} %add.44), channel_id=1, source_target_pairs={{0,2},{1,3},{2,0},{3,1},{4,6},{5,7},{6,4},{7,5},{8,10},{9,11},{10,... | collective-permute-start | bytes 319496 | tf_op jit(solution)/shard_map/ppermute | solution.py:30
  39.0 5.5 %collective-permute-start.6 = (f32[104,256]{1,0:T(8,128)S(1)}, f32[104,256]{1,0:T(8,128)S(1)}, u32[]{:S(2)}, u32[]{:S(2)}) collective-permute-start(f32[104,256]{1,0:T(8,128)S(1)} %add.45), channel_id=1, source_target_pairs={{0,4},{4,0},{8,12},{12,8},{1,5},{5,1},{9,13},{13,9},{2,6},{6,2},{1... | collective-permute-start | bytes 319496 | tf_op jit(solution)/shard_map/ppermute | solution.py:30
  44.5 7.2 %collective-permute-start.7 = (f32[104,256]{1,0:T(8,128)S(1)}, f32[104,256]{1,0:T(8,128)S(1)}, u32[]{:S(2)}, u32[]{:S(2)}) collective-permute-start(f32[104,256]{1,0:T(8,128)S(1)} %add.46), channel_id=1, source_target_pairs={{0,8},{4,12},{8,0},{12,4},{1,9},{5,13},{9,1},{13,5},{2,10},{6,14},... | collective-permute-start | bytes 319496 | tf_op jit(solution)/shard_map/ppermute | solution.py:30
  51.7 1.4 %collective-permute-start.8 = (f32[104,256]{1,0:T(8,128)S(1)}, f32[104,256]{1,0:T(8,128)S(1)}, u32[]{:S(2)}, u32[]{:S(2)}) collective-permute-start(f32[104,256]{1,0:T(8,128)S(1)} %add.47.own), channel_id=1, source_target_pairs={{0,1},{1,0},{2,3},{3,2},{4,5},{5,4},{6,7},{7,6},{8,9},{9,8},{10,11... | collective-permute-start | bytes 319496 | tf_op jit(solution)/shard_map/ppermute | solution.py:30
  62.8 8.8 %collective-permute-start.9 = (f32[272,256]{1,0:T(8,128)S(1)}, f32[272,256]{1,0:T(8,128)S(1)}, u32[]{:S(2)}, u32[]{:S(2)}) collective-permute-start(f32[272,256]{1,0:T(8,128)S(1)} %get-tuple-element.111), channel_id=1, source_target_pairs={{0,16},{16,0},{1,17},{17,1},{2,18},{18,2},{3,19},{19,3},{4,20},{20... | collective-permute-start | bytes 835592 | tf_op jit(solution)/shard_map/ppermute | solution.py:30
  77.1 1.6 %collective-permute-start.10 = (bf16[160,768]{1,0:T(8,128)(2,1)S(1)}, bf16[160,768]{1,0:T(8,128)(2,1)S(1)}, u32[]{:S(2)}, u32[]{:S(2)}) collective-permute-start(bf16[160,768]{1,0:T(8,128)(2,1)S(1)} %select_convert_fusion), channel_id=1, source_target_pairs={{0,1},{1,0},{2,3},{3,2},{4,5},{5,4},{6,7},{7,6},{8,9},{9,8},{10,11... | collective-permute-start | bytes 737288 | tf_op jit(solution)/shard_map/ppermute | solution.py:30
  78.8 5.5 %collective-permute-start.13 = (bf16[40,768]{1,0:T(8,128)(2,1)S(1)}, bf16[40,768]{1,0:T(8,128)(2,1)S(1)}, u32[]{:S(2)}, u32[]{:S(2)}) collective-permute-start(bf16[40,768]{1,0:T(8,128)(2,1)S(1)} %get-tuple-element.126), channel_id=1, source_target_pairs={{0,18},{1,19},{2,16},{3,17},{16,2},{17,3},{18,0},{19,1},{4,22},{5,... | collective-permute-start | bytes 184328 | tf_op jit(solution)/shard_map/ppermute | solution.py:75
  80.0 4.3 %collective-permute-start.12 = (bf16[40,768]{1,0:T(8,128)(2,1)S(1)}, bf16[40,768]{1,0:T(8,128)(2,1)S(1)}, u32[]{:S(2)}, u32[]{:S(2)}) collective-permute-start(bf16[40,768]{1,0:T(8,128)(2,1)S(1)} %get-tuple-element.127), channel_id=1, source_target_pairs={{0,16},{1,17},{2,18},{3,19},{16,0},{17,1},{18,2},{19,3},{4,20},{5,... | collective-permute-start | bytes 184328 | tf_op jit(solution)/shard_map/ppermute | solution.py:75
  80.6 4.6 %collective-permute-start.11 = (bf16[40,768]{1,0:T(8,128)(2,1)S(1)}, bf16[40,768]{1,0:T(8,128)(2,1)S(1)}, u32[]{:S(2)}, u32[]{:S(2)}) collective-permute-start(bf16[40,768]{1,0:T(8,128)(2,1)S(1)} %get-tuple-element.125), channel_id=1, source_target_pairs={{0,2},{1,3},{2,0},{3,1},{16,18},{17,19},{18,16},{19,17},{4,6},{5,7... | collective-permute-start | bytes 184328 | tf_op jit(solution)/shard_map/ppermute | solution.py:75
  85.1 9.2 %collective-permute-start.16 = (bf16[40,768]{1,0:T(8,128)(2,1)S(1)}, bf16[40,768]{1,0:T(8,128)(2,1)S(1)}, u32[]{:S(2)}, u32[]{:S(2)}) collective-permute-start(bf16[40,768]{1,0:T(8,128)(2,1)S(1)} %fusion), channel_id=1, source_target_pairs={{0,12},{4,8},{8,4},{12,0},{1,13},{5,9},{9,5},{13,1},{2,14},{6,10},... | collective-permute-start | bytes 184328 | tf_op jit(solution)/shard_map/ppermute | solution.py:30
  89.8 5.1 %collective-permute-start.15 = (bf16[40,768]{1,0:T(8,128)(2,1)S(1)}, bf16[40,768]{1,0:T(8,128)(2,1)S(1)}, u32[]{:S(2)}, u32[]{:S(2)}) collective-permute-start(bf16[40,768]{1,0:T(8,128)(2,1)S(1)} %fusion), channel_id=1, source_target_pairs={{0,8},{4,12},{8,0},{12,4},{1,9},{5,13},{9,1},{13,5},{2,10},{6,14},... | collective-permute-start | bytes 184328 | tf_op jit(solution)/shard_map/ppermute | solution.py:30
  89.8 5.1 %collective-permute-start.14 = (bf16[40,768]{1,0:T(8,128)(2,1)S(1)}, bf16[40,768]{1,0:T(8,128)(2,1)S(1)}, u32[]{:S(2)}, u32[]{:S(2)}) collective-permute-start(bf16[40,768]{1,0:T(8,128)(2,1)S(1)} %fusion), channel_id=1, source_target_pairs={{0,4},{4,0},{8,12},{12,8},{1,5},{5,1},{9,13},{13,9},{2,6},{6,2},{1... | collective-permute-start | bytes 184328 | tf_op jit(solution)/shard_map/ppermute | solution.py:30
  95.0 4.9 %collective-permute-start.17 = (bf16[40,768]{1,0:T(8,128)(2,1)S(1)}, bf16[40,768]{1,0:T(8,128)(2,1)S(1)}, u32[]{:S(2)}, u32[]{:S(2)}) collective-permute-start(bf16[40,768]{1,0:T(8,128)(2,1)S(1)} %add_convert_fusion), channel_id=1, source_target_pairs={{0,2},{1,3},{2,0},{3,1},{16,18},{17,19},{18,16},{19,17},{4,6},{5,7... | collective-permute-start | bytes 184328 | tf_op jit(solution)/shard_map/ppermute | solution.py:84
  95.9 4.2 %collective-permute-start.18 = (bf16[40,768]{1,0:T(8,128)(2,1)S(1)}, bf16[40,768]{1,0:T(8,128)(2,1)S(1)}, u32[]{:S(2)}, u32[]{:S(2)}) collective-permute-start(bf16[40,768]{1,0:T(8,128)(2,1)S(1)} %add_convert_fusion), channel_id=1, source_target_pairs={{0,16},{1,17},{2,18},{3,19},{16,0},{17,1},{18,2},{19,3},{4,20},{5,... | collective-permute-start | bytes 184328 | tf_op jit(solution)/shard_map/ppermute | solution.py:84
  97.4 5.1 %collective-permute-start.19 = (bf16[40,768]{1,0:T(8,128)(2,1)S(1)}, bf16[40,768]{1,0:T(8,128)(2,1)S(1)}, u32[]{:S(2)}, u32[]{:S(2)}) collective-permute-start(bf16[40,768]{1,0:T(8,128)(2,1)S(1)} %add_convert_fusion), channel_id=1, source_target_pairs={{0,18},{1,19},{2,16},{3,17},{16,2},{17,3},{18,0},{19,1},{4,22},{5,... | collective-permute-start | bytes 184328 | tf_op jit(solution)/shard_map/ppermute | solution.py:84
  102.5 1.6 %collective-permute-start.20 = (bf16[160,768]{1,0:T(8,128)(2,1)S(1)}, bf16[160,768]{1,0:T(8,128)(2,1)S(1)}, u32[]{:S(2)}, u32[]{:S(2)}) collective-permute-start(bf16[160,768]{1,0:T(8,128)(2,1)S(1)} %bitcast.28), channel_id=1, source_target_pairs={{0,1},{1,0},{2,3},{3,2},{4,5},{5,4},{6,7},{7,6},{8,9},{9,8},{10,11... | collective-permute-start | bytes 737288 | tf_op jit(solution)/shard_map/ppermute | solution.py:30

commit v8 on v7

--- a/solution.py
+++ b/solution.py
@@ -14,6 +14,9 @@
 GROUPS = 8
 EDGE = 8
 TAPS_ROWS = 64
+SIDE = 4
+FILL_ROWS = 4
+PARTS = (4, 3, 4)
 
 epsilon = 1e-05
 loss_scale = 64.0
@@ -120,26 +123,105 @@
     return pl.ds(pl.multiple_of(tile * LANES, LANES), LANES)
 
 
-def spread_weights(weight_ref, spread_ref, lanes):
+def part_starts():
+    starts, total = {}, 0
+    for row_part in range(3):
+        for col_part in range(3):
+            starts[row_part, col_part] = total
+            total += PARTS[row_part] * PARTS[col_part]
+    return starts, total
+
+
+FILTERS, PRODUCTS = part_starts()
+
+
+def part_taps(taps):
+    even, odd = taps[0::2], taps[1::2]
+    both = [a + b for a, b in zip(even, odd)] + even[len(odd) :]
+    return even, odd, both
+
+
+def spread_weights(weight_ref, filters, lanes):
+    rows = []
     for row_tap in range(KERNEL):
-        for col_tap in range(KERNEL):
-            scale = weight_ref[row_tap, col_tap : col_tap + 1, lanes]
-            spread_ref[row_tap * KERNEL + col_tap] = jnp.broadcast_to(scale, spread_ref.shape[1:])
-
-
-def conv_rows(load, spread_ref, bias, steps, count):
-    total = [[bias] * steps for _ in range(count)]
-    for place in range(KERNEL + count - 1):
-        windows = [load(place, group) for group in range(steps + KERNEL - 1)]
-        for row in range(count):
-            row_tap = place - row
-            if not 0 <= row_tap < KERNEL:
-                continue
-            for col_tap in range(KERNEL):
-                scale = spread_ref[row_tap * KERNEL + col_tap]
-                for step in range(steps):
-                    total[row][step] = total[row][step] + windows[step + col_tap] * scale
-    return jnp.concatenate([part for row in total for part in row], axis=0).astype(narrow)
+        row = [weight_ref[row_tap, tap : tap + 1, lanes] for tap in range(KERNEL)]
+        rows.append([jnp.broadcast_to(tap, (GROUPS, LANES)) for tap in row])
+    columns = [part_taps([rows[tap][col] for tap in range(KERNEL)]) for col in range(KERNEL)]
+    for row_part, many in enumerate(PARTS):
+        for row in range(many):
+            line = [columns[col][row_part][row] for col in range(KERNEL)]
+            for col_part, taps in enumerate(part_taps(line)):
+                start = FILTERS[row_part, col_part] + row * PARTS[col_part]
+                for col, value in enumerate(taps):
+                    filters[start + col] = value
+
+
+def fill_parts(load, parts, row_pairs, groups):
+    for pair in range(row_pairs):
+        for group in range(groups):
+            middle = load(2 * pair + 1, group)
+            parts[0, pair, group] = load(2 * pair, group) - middle
+            if pair < row_pairs - 1:
+                parts[1, pair, group] = load(2 * pair + 2, group) - middle
+
+
+def part_line(load, parts, row_part, col_part, pair, many):
+    def value(group):
+        return load(2 * pair + 1, group) if row_part == 2 else parts[row_part, pair, group]
+
+    first = (0, 2, 1)[col_part]
+    line = [value(2 * col + first) for col in range(many)]
+    if col_part < 2:
+        line = [side - value(2 * col + 1) for col, side in enumerate(line)]
+    return line
+
+
+def conv_rows(load, filters, bias, steps, count, parts, products):
+    row_pairs, col_pairs = count // 2, steps // 2
+    fill_parts(load, parts, row_pairs + 3, 2 * col_pairs + 6)
+    for row_part in range(3):
+        for col_part in range(3):
+            start = FILTERS[row_part, col_part]
+            many_rows, many_cols = PARTS[row_part], PARTS[col_part]
+            total = [[None] * col_pairs for _ in range(row_pairs)]
+            for place in range(row_pairs + many_rows - 1):
+                line = part_line(
+                    load, parts, row_part, col_part, place, col_pairs + many_cols - 1
+                )
+                for row in range(row_pairs):
+                    tap_row = place - row
+                    if not 0 <= tap_row < many_rows:
+                        continue
+                    for tap_col in range(many_cols):
+                        scale = filters[start + tap_row * many_cols + tap_col]
+                        for col in range(col_pairs):
+                            term = line[col + tap_col] * scale
+                            old = total[row][col]
+                            total[row][col] = term if old is None else old + term
+            for row in range(row_pairs):
+                for col in range(col_pairs):
+                    products[3 * row_part + col_part, row, col] = total[row][col]
+    found = []
+    for row in range(row_pairs):
+        lines = [[], []]
+        for col in range(col_pairs):
+            values = [products[part, row, col] for part in range(9)]
+            shared = [values[6] + values[8] + bias, values[7] + values[8] + bias]
+            for row_part in range(2):
+                for col_part in range(2):
+                    own = values[3 * row_part + col_part] + values[3 * row_part + 2]
+                    lines[row_part].append(own + shared[col_part])
+        found += lines[0] + lines[1]
+    return jnp.concatenate(found, axis=0).astype(narrow)
+
+
+def parts_scratch(count, steps):
+    row_pairs, col_pairs = count // 2, steps // 2
+    return [
+        pltpu.VMEM((PRODUCTS, GROUPS, LANES), wide),
+        pltpu.VMEM((2, row_pairs + 3, 2 * col_pairs + 6, GROUPS, LANES), wide),
+        pltpu.VMEM((9, row_pairs, col_pairs, GROUPS, LANES), wide),
+    ]
 
 
 def reduce_part(conv_out, reduce_ref, reduce_bias_ref, before_out, feat_out):
@@ -155,37 +237,32 @@
 def inner_kernel(
     block, left, right, weight, bias, reduce_weight, reduce_bias,
     spread_out, conv_out, before_out, feat_out, gram_out, colsum_out,
-    wide_row, spread_weight,
+    wide_row, filters, parts, products,
 ):
     rows, cols = block.shape[0], block.shape[1]
     steps = cols // GROUPS
-    inner = rows - 2 * HALF
-    at_once = 2 if inner % 2 == 0 else 1
 
     def one_tile(tile, _):
         lanes = lanes_of(tile)
-        spread_weights(weight, spread_weight, lanes)
+        spread_weights(weight, filters, lanes)
         start_value = jnp.broadcast_to(bias[0:1, lanes], (GROUPS, LANES))
 
-        def fill(row, _):
-            place = wide_row.at[row]
-            fill_row(place, block[row, :, lanes], left[row, :, lanes], right[row, :, lanes])
-            spread_columns(place, spread_out.at[tile, row])
+        def fill(turn, _):
+            for row in range(FILL_ROWS):
+                row = turn * FILL_ROWS + row
+                place = wide_row.at[row]
+                fill_row(place, block[row, :, lanes], left[row, :, lanes], right[row, :, lanes])
+                spread_columns(place, spread_out.at[tile, row])
             return 0
 
-        lax.fori_loop(0, rows, fill, 0)
-
-        def one_row(index, _):
-            def load(row_tap, group):
-                return spread_out[tile, index + row_tap, group]
-
-            start = pl.multiple_of(index * cols, at_once * cols)
-            conv_out[pl.ds(start, at_once * cols), lanes] = conv_rows(
-                load, spread_weight, start_value, steps, at_once
-            )
-            return 0
-
-        lax.fori_loop(0, inner // at_once, lambda turn, _: one_row(turn * at_once, 0), 0)
+        lax.fori_loop(0, rows // FILL_ROWS, fill, 0)
+
+        def load(row, group):
+            return spread_out[tile, row + SIDE - HALF, group]
+
+        conv_out[:, lanes] = conv_rows(
+            load, filters, start_value, steps, rows - 2 * SIDE, parts, products
+        )
         return 0
 
     lax.fori_loop(0, spread_out.shape[0], one_tile, 0)
@@ -197,14 +274,14 @@
 def edge_kernel(
     flag, spread_in, top, bottom, weight, bias, reduce_weight, reduce_bias, gram_in, colsum_in,
     spread_top, spread_bottom, conv_out, before_out, feat_out, kept_out, sent_out,
-    wide_row, corners, spread_weight, sums,
+    wide_row, corners, filters, parts, products, sums,
 ):
     rows, cols = spread_in.shape[1], wide_row.shape[1] - 2 * EDGE
     steps = cols // GROUPS
 
     def one_tile(tile, _):
         lanes = lanes_of(tile)
-        spread_weights(weight, spread_weight, lanes)
+        spread_weights(weight, filters, lanes)
         start_value = jnp.broadcast_to(bias[0:1, lanes], (GROUPS, LANES))
         for side, (strip, spread) in enumerate(((top, spread_top), (bottom, spread_bottom))):
             corners[side] = strip[HALF * cols :, lanes].astype(wide)
@@ -226,10 +303,10 @@
 
             return load
 
-        for side, row in enumerate((0, rows - HALF)):
-            start = side * HALF * cols
-            conv_out[start : start + HALF * cols, lanes] = conv_rows(
-                load_from(row), spread_weight, start_value, steps, HALF
+        for side, row in enumerate((0, rows - SIDE)):
+            start = side * SIDE * cols
+            conv_out[start : start + SIDE * cols, lanes] = conv_rows(
+                load_from(row), filters, start_value, steps, SIDE, parts.at[side], products.at[side]
             )
         return 0
 
@@ -256,7 +333,7 @@
 
 
 def edge_rows(rows):
-    return list(range(HALF)) + list(range(rows - HALF, rows))
+    return list(range(SIDE)) + list(range(rows - SIDE, rows))
 
 
 def shape_of(shape, dtype=wide):
@@ -278,7 +355,7 @@
     width = reduce_weight.shape[1]
     tiles = channels // LANES
     steps = cols // GROUPS
-    pixels = (rows - 2 * HALF) * cols
+    pixels = (rows - 2 * SIDE) * cols
     return pl.pallas_call(
         inner_kernel,
         in_specs=[in_vmem] * 7,
@@ -293,7 +370,7 @@
         ],
         scratch_shapes=[
             pltpu.VMEM((rows, cols + 2 * EDGE, LANES), wide),
-            pltpu.VMEM((KERNEL * KERNEL, GROUPS, LANES), wide),
+            *parts_scratch(rows - 2 * SIDE, steps),
         ],
         compiler_params=params(24),
         cost_estimate=cost(10),
@@ -305,7 +382,8 @@
     tiles, rows, groups = spread.shape[:3]
     cols, channels = (groups - KERNEL + 1) * GROUPS, top.shape[1]
     width = reduce_weight.shape[1]
-    pixels = 2 * HALF * cols
+    pixels = 2 * SIDE * cols
+    filters, parts, products = parts_scratch(SIDE, cols // GROUPS)
     side = (tiles, HALF, groups, GROUPS, LANES)
     sums_rows = 3 * width // 4 + 2 * GROUPS
     return pl.pallas_call(
@@ -324,7 +402,9 @@
         scratch_shapes=[
             pltpu.VMEM((2 * HALF, cols + 2 * EDGE, LANES), wide),
             pltpu.VMEM((2, top.shape[0] - HALF * cols, LANES), wide),
-            pltpu.VMEM((KERNEL * KERNEL, GROUPS, LANES), wide),
+            filters,
+            pltpu.VMEM((2,) + parts.shape, wide),
+            pltpu.VMEM((2,) + products.shape, wide),
             pltpu.VMEM((sums_rows, width), wide),
         ],
         compiler_params=params(24),
@@ -535,11 +615,12 @@
 
 
 def taps_kernel(
-    spread_in, spread_top, spread_bottom, grad_inner, grad_edge, payload_in, payload, grads, out, *,
-    first, last,
+    spread_in, spread_top, spread_bottom, grad_inner, grad_edge, payload_in, payload,
+    parts, grads, products, out, *, first, last,
 ):
     rows = spread_in.shape[1]
-    steps = grads.shape[1]
+    row_pairs, col_pairs = grads.shape[1:3]
+    steps = 2 * col_pairs
     cols = steps * GROUPS
     order = edge_rows(rows)
     taps = KERNEL * KERNEL
@@ -548,47 +629,71 @@
     def one_tile(tile, _):
         lanes = lanes_of(tile)
 
-        for row in range(rows):
+        def grad_row(row):
             if row in order:
                 source, place = grad_edge, order.index(row)
             else:
-                source, place = grad_inner, row - HALF
+                source, place = grad_inner, row - SIDE
             values = source[place * cols : (place + 1) * cols, lanes].astype(wide)
-            for step in range(steps):
-                grads[row, step] = values[step * GROUPS : (step + 1) * GROUPS, :]
+            return [values[step * GROUPS : (step + 1) * GROUPS, :] for step in range(steps)]
+
+        for pair in range(row_pairs):
+            even, odd = grad_row(2 * pair), grad_row(2 * pair + 1)
+            both = [a + b for a, b in zip(even, odd)]
+            for row_part, line in enumerate((even, odd, both)):
+                for col in range(col_pairs):
+                    grads[3 * row_part, pair, col] = line[2 * col]
+                    grads[3 * row_part + 1, pair, col] = line[2 * col + 1]
+                    grads[3 * row_part + 2, pair, col] = line[2 * col] + line[2 * col + 1]
 
         def load(place, group):
+            place = place - HALF
             if place < 0:
                 return spread_top[tile, place + HALF, group]
             if place >= rows:
                 return spread_bottom[tile, place - rows, group]
             return spread_in[tile, place, group]
 
-        for begin in range(0, KERNEL, 2):
-            row_taps = [tap for tap in (begin, begin + 1) if tap < KERNEL]
-            total = {
-                (row_tap, col_tap): jnp.zeros((GROUPS, LANES), wide)
-                for row_tap in row_taps
-                for col_tap in range(KERNEL)
-            }
-            for place in range(begin - HALF, rows + row_taps[-1] - HALF):
-                windows = [load(place, group) for group in range(steps + KERNEL - 1)]
-                for row_tap in row_taps:
-                    row = place - row_tap + HALF
-                    if not 0 <= row < rows:
-                        continue
-                    for step in range(steps):
-                        grad = grads[row, step]
-                        for col_tap in range(KERNEL):
-                            total[row_tap, col_tap] += windows[step + col_tap] * grad
-            for (row_tap, col_tap), value in total.items():
+        fill_parts(load, parts, row_pairs + 3, 2 * col_pairs + 6)
+        for row_part in range(3):
+            for col_part in range(3):
+                part = 3 * row_part + col_part
+                start = FILTERS[row_part, col_part]
+                many_rows, many_cols = PARTS[row_part], PARTS[col_part]
+                total = {}
+                for place in range(row_pairs + many_rows - 1):
+                    line = part_line(
+                        load, parts, row_part, col_part, place, col_pairs + many_cols - 1
+                    )
+                    for tap_row in range(many_rows):
+                        row = place - tap_row
+                        if not 0 <= row < row_pairs:
+                            continue
+                        for col in range(col_pairs):
+                            grad = grads[part, row, col]
+                            for tap_col in range(many_cols):
+                                term = line[col + tap_col] * grad
+                                tap = tap_row * many_cols + tap_col
+                                total[tap] = total[tap] + term if tap in total else term
+                for tap, value in total.items():
+                    products[start + tap] = value
+
+        for row_tap in range(KERNEL):
+            for col_tap in range(KERNEL):
+                place = (row_tap // 2, col_tap // 2)
+                found = None
+                for row_part in (row_tap % 2, 2):
+                    for col_part in (col_tap % 2, 2):
+                        start = FILTERS[row_part, col_part]
+                        value = products[start + place[0] * PARTS[col_part] + place[1]]
+                        found = value if found is None else found + value
                 tap = row_tap * KERNEL + col_tap
-                out[tap : tap + 1, :] = jnp.sum(value, axis=0, keepdims=True)
-        total = [jnp.zeros((GROUPS, LANES), wide) for _ in range(KERNEL)]
-        for index in range(rows * steps):
-            slot = index % KERNEL
-            total[slot] = total[slot] + grads[index // steps, index % steps]
-        out[taps : taps + 1, :] = jnp.sum(sum(total), axis=0, keepdims=True)
+                out[tap : tap + 1, :] = jnp.sum(found, axis=0, keepdims=True)
+        found = [
+            sum(grads[8, pair, col] for col in range(1, col_pairs)) + grads[8, pair, 0]
+            for pair in range(row_pairs)
+        ]
+        out[taps : taps + 1, :] = jnp.sum(sum(found[1:], found[0]), axis=0, keepdims=True)
         payload[pl.ds(base, taps + 1), lanes] = out[: taps + 1, :]
         return 0
 
@@ -597,7 +702,7 @@
 
 def tap_grads(spreads, grads, payload, first, last):
     rows, groups = spreads[0].shape[1:3]
-    steps = groups - KERNEL + 1
+    row_pairs, col_pairs = rows // 2, (groups - KERNEL + 1) // 2
     return pl.pallas_call(
         functools.partial(taps_kernel, first=first, last=last),
         in_specs=[in_vmem] * 6,
@@ -605,7 +710,9 @@
         out_shape=shape_of(payload.shape),
         input_output_aliases={5: 0},
         scratch_shapes=[
-            pltpu.VMEM((rows, steps, GROUPS, LANES), wide),
+            pltpu.VMEM((2, row_pairs + 3, 2 * col_pairs + 6, GROUPS, LANES), wide),
+            pltpu.VMEM((9, row_pairs, col_pairs, GROUPS, LANES), wide),
+            pltpu.VMEM((PRODUCTS, GROUPS, LANES), wide),
             pltpu.VMEM((TAPS_ROWS, LANES), wide),
         ],
         compiler_params=params(16),
@@ -730,9 +837,9 @@
     known = [root] + [swap(root, "dp", shift) for shift in range(1, lax.axis_size("dp"))]
     spreads = (spread, spread_top, spread_bottom)
     tiles = channels // LANES
-    payload = tap_grads(spreads, grads, payload, 0, tiles // 2)
+    payload = tap_grads(spreads, grads, payload, 0, tiles - 1)
     payload, known = together((payload, known))
-    payload = tap_grads(spreads, grads, payload, tiles // 2, tiles)
+    payload = tap_grads(spreads, grads, payload, tiles - 1, tiles)
 
     part = payload.shape[0] // 2
     low, high = payload[:part], payload[part:]
@@ -741,6 +848,9 @@
     axes = ("dp", "sx")
     pairs = square_pairs(axes, (1, 2))
     payload = square_scatter(payload, axes, pairs, places, narrow)
+    for shift in doublings("dp", 2):
+        payload = exchange(payload, "dp", shift, narrow)
+    payload = exchange_all(payload, "sy", narrow).astype(narrow)
     payload, known = together((payload, known))
     class_weight_grad = tree_sum(
         [part[width : width + classes, 0][:, None, None] * part[None, :width] for part in known]
@@ -748,16 +858,11 @@
     totals = tree_sum([part[width:, 0] for part in known])
     class_bias_grad = totals[:classes]
     loss = totals[classes] / image_count
-    for shift in doublings("dp", 2):
-        payload = exchange(payload, "dp", shift, narrow)
-    payload = exchange_all(payload, "sy", narrow).astype(narrow)
-    payload, class_weight_grad, class_bias_grad, loss = together(
-        (payload, class_weight_grad, class_bias_grad, loss)
-    )
     payload = square_gather(payload, axes, pairs, places)
-    weight_grad, depth_grad, depth_bias_grad, bias_grad = finish(
-        flag, payload, swap(payload, "sx", 1), width
-    )
+    other, class_weight_grad, class_bias_grad, loss = together(
+        (swap(payload, "sx", 1), class_weight_grad, class_bias_grad, loss)
+    )
+    weight_grad, depth_grad, depth_bias_grad, bias_grad = finish(flag, payload, other, width)
     return (
         loss,
         depth_grad,

time: 107 us -> 101 us (0.944)
  Pallas kernels: 38.9 us -> 31.5 us
  waiting for transfers between devices: 23 us -> 29.6 us
  starting transfers between devices: 34.1 us -> 28.9 us
    pallas_call x1, Pallas kernels: 11.5 us -> 6.69 us  [conv_inner(): pl.pallas_call(inner_kernel, in_specs=[in_vmem] * 7, out_specs=[in_vmem]...]
    ppermute x2, waiting for transfers between devices: 0.01 us -> 4.83 us  [back_along(): lax.ppermute(value, axis, [(i + 1, i) for i in range(lax.axis_size(axis)...]
    ppermute x11, starting transfers between devices: 16.4 us -> 13.3 us  [swap(): return lax.ppermute(value, axis, [(i, i ^ shift) for i in range(count)])]
    ppermute x11, waiting for transfers between devices: 16.3 us -> 19.1 us  [swap(): return lax.ppermute(value, axis, [(i, i ^ shift) for i in range(count)])]
    pallas_call x2, Pallas kernels: 10.9 us -> 8.06 us  [tap_grads(): pl.pallas_call(functools.partial(taps_kernel, first=first, last=last), in...]
    ppermute x2, starting transfers between devices: 7.98 us -> 5.86 us  [next_along(): lax.ppermute(value, axis, [(i, i + 1) for i in range(lax.axis_size(axis)...]
    ppermute x3, waiting for transfers between devices: 3.9 us -> 1.82 us  [square_gather(): part = lax.ppermute(value, axes, pairs[turn]) if turn else value]
  transfers between devices with their start and end apart: 21 -> 21, of which waited for: 14 -> 16; matrix products, arithmetic and copies ran while one was open for 5% -> 5% of each run, Pallas kernels for 17% -> 14%
where the time goes in v8:
time: 101 us; the launch traced here: 100 us
  Pallas kernels  31.5 us (31%)
  waiting for transfers between devices  29.6 us (29%)
  starting transfers between devices  28.9 us (29%)
  local copies, waits for them, and re-layouts  4.65 us (5%)
  between operations  3.37 us (3%)
  other arithmetic  2.31 us (2%)
    ppermute x11, waiting for transfers between devices, swap(): return lax.ppermute(value, axis, [(i, i ^ shift) for i in range(count)])  19.1 us
    ppermute x11, starting transfers between devices, swap(): return lax.ppermute(value, axis, [(i, i ^ shift) for i in range(count)])  13.3 us
    pallas_call x1, Pallas kernels, head(): pl.pallas_call(functools.partial(head_kernel, count=count, image_count=im...  9.73 us
    pallas_call x2, Pallas kernels, tap_grads(): pl.pallas_call(functools.partial(taps_kernel, first=first, last=last), in...  8.06 us
    pallas_call x1, Pallas kernels, conv_inner(): pl.pallas_call(inner_kernel, in_specs=[in_vmem] * 7, out_specs=[in_vmem]...  6.69 us
    ppermute x2, starting transfers between devices, next_along(): lax.ppermute(value, axis, [(i, i + 1) for i in range(lax.axis_size(axis)...  5.86 us
    pallas_call x1, Pallas kernels, conv_edge(): pl.pallas_call(edge_kernel, in_specs=[in_smem] + [in_vmem] * 9, out_specs...  5.09 us
    ppermute x2, waiting for transfers between devices, back_along(): lax.ppermute(value, axis, [(i + 1, i) for i in range(lax.axis_size(axis)...  4.83 us
  transfers between devices with their start and end apart: 21, of which 16 were waited for; matrix products, arithmetic and copies ran while one was open for 5% of the time, Pallas kernels for 14%

profile of v8, /device:TPU:0, one launch (start us, length us, event | category | flops | bytes accessed | tf_op | source)
XLA Modules:
  0.0 100.3 jit_solution(10304542885586979272)
XLA Ops:
  0.6 0.0 copy-start
  0.6 0.0 copy-start.4
  0.7 1.2 %fusion.6 = (bf16[16,3,768]{2,1,0:T(4,128)(2,1)S(1)}, bf16[16,3,768]{2,1,0:T(4,128)(2,1)S(1)}) fusion(bf16[16,64,768]{2,1,0:T(8,128)(2,1)} %bitcast.28), kind=kLoop, calls=%fused_computation.24 | loop fusion | bytes 294912 | tf_op jit(solution)/shard_map/slice | solution.py:786
  1.9 2.4 %collective-permute-start = (bf16[16,3,768]{2,1,0:T(4,128)(2,1)S(1)}, bf16[16,3,768]{2,1,0:T(4,128)(2,1)S(1)}, u32[]{:S(2)}, u32[]{:S(2)}) collective-permute-start(bf16[16,3,768]{2,1,0:T(4,128)(2,1)S(1)} %get-tuple-element.123), channel_id=1, source_target_pairs={{0,1},{1,2},{2,3},{4,5},{5,6},{6,7},{8,9},{9,10},{10,11},{12,13},{... | collective-permute-start | bytes 221192 | tf_op jit(solution)/shard_map/ppermute | solution.py:103
  4.3 1.3 %collective-permute-start.1 = (bf16[16,3,768]{2,1,0:T(4,128)(2,1)S(1)}, bf16[16,3,768]{2,1,0:T(4,128)(2,1)S(1)}, u32[]{:S(2)}, u32[]{:S(2)}) collective-permute-start(bf16[16,3,768]{2,1,0:T(4,128)(2,1)S(1)} %get-tuple-element.124), channel_id=1, source_target_pairs={{1,0},{2,1},{3,2},{5,4},{6,5},{7,6},{9,8},{10,9},{11,10},{13,12},{... | collective-permute-start | bytes 221192 | tf_op jit(solution)/shard_map/ppermute | solution.py:107
  5.6 1.1 %fusion.5 = (bf16[1,3,64,768]{3,2,1,0:T(8,128)(2,1)S(1)}, bf16[1,3,64,768]{3,2,1,0:T(8,128)(2,1)S(1)}) fusion(bf16[1,16,64,768]{3,2,1,0:T(8,128)(2,1)} %param.8), kind=kLoop, calls=%fused_computation.23 | loop fusion | bytes 1179648 | tf_op jit(solution)/shard_map/slice | solution.py:764
  6.7 0.7 broadcast_in_dim.32.bias
  7.4 0.1 pad.7.clone
  7.5 0.0 collective-permute-done.left
  7.5 2.1 %collective-permute-done.1.right = bf16[16,3,768]{2,1,0:T(4,128)(2,1)S(1)} collective-permute-done((bf16[16,3,768]{2,1,0:T(4,128)(2,1)S(1)}, bf16[16,3,768]{2,1,0:T(4,128)(2,1)S(1)}, u32[]{:S(2)}, u32[]{:S(2)}) %collective-permute-start.1) | collective-permute-done | bytes 73760 | tf_op jit(solution)/shard_map/ppermute | solution.py:107
  9.7 0.2 maximum_maximum_fusion.1
  9.9 3.5 %collective-permute-start.2 = (bf16[224,768]{1,0:T(8,128)(2,1)S(1)}, bf16[224,768]{1,0:T(8,128)(2,1)S(1)}, u32[]{:S(2)}, u32[]{:S(2)}) collective-permute-start(bf16[224,768]{1,0:T(8,128)(2,1)S(1)} %get-tuple-element.71), channel_id=1, source_target_pairs={{0,4},{4,8},{8,12},{1,5},{5,9},{9,13},{2,6},{6,10},{10,14},{3,7},{... | collective-permute-start | bytes 1032200 | tf_op jit(solution)/shard_map/ppermute | solution.py:103
  13.4 1.3 %collective-permute-start.3 = (bf16[224,768]{1,0:T(8,128)(2,1)S(1)}, bf16[224,768]{1,0:T(8,128)(2,1)S(1)}, u32[]{:S(2)}, u32[]{:S(2)}) collective-permute-start(bf16[224,768]{1,0:T(8,128)(2,1)S(1)} %get-tuple-element.72), channel_id=1, source_target_pairs={{4,0},{8,4},{12,8},{5,1},{9,5},{13,9},{6,2},{10,6},{14,10},{7,3},{... | collective-permute-start | bytes 1032200 | tf_op jit(solution)/shard_map/ppermute | solution.py:107
  14.8 6.7 %conv_inner.1 = (f32[6,16,14,8,128]{4,3,2,1,0:T(8,128)S(1)}, bf16[512,768]{1,0:T(8,128)(2,1)S(1)}, f32[512,256]{1,0:T(8,128)S(1)}, bf16[512,256]{1,0:T(8,128)(2,...) custom-call(bf16[16,64,768]{2,1,0:T(8,128)(2,1)S(1)} %bitcast.29, ...), custom_call_target="tpu_custom_call" | custom-call | flops 10000000000 | bytes 10000000 | tf_op jit(solution)/shard_map/conv_inner/pallas_call | solution.py:359
  21.5 0.0 collective-permute-done.2.top
  21.5 2.7 %collective-permute-done.3.bottom = bf16[224,768]{1,0:T(8,128)(2,1)S(1)} collective-permute-done((bf16[224,768]{1,0:T(8,128)(2,1)S(1)}, bf16[224,768]{1,0:T(8,128)(2,1)S(1)}, u32[]{:S(2)}, u32[]{:S(2)}) %collective-permute-start.3) | collective-permute-done | bytes 344096 | tf_op jit(solution)/shard_map/ppermute | solution.py:107
  24.2 5.1 %conv_edge.1 = (f32[6,3,14,8,128]{4,3,2,1,0:T(8,128)S(1)}, f32[6,3,14,8,128]{4,3,2,1,0:T(8,128)S(1)}, bf16[512,768]{1,0:T(8,128)(2,1)S(1)}, f32[512,256]{1,0:T(8...) custom-call(s32[1]{0:T(128)} %bitcast.3.flag, ...), custom_call_target="tpu_custom_call" | custom-call | flops 6000000000 | bytes 6000000 | tf_op jit(solution)/shard_map/conv_edge/pallas_call | solution.py:389
  29.3 0.0 copy-start.1
  29.3 0.0 copy-start.5
  29.3 1.9 %collective-permute-start.4 = (f32[104,256]{1,0:T(8,128)S(1)}, f32[104,256]{1,0:T(8,128)S(1)}, u32[]{:S(2)}, u32[]{:S(2)}) collective-permute-start(f32[104,256]{1,0:T(8,128)S(1)} %get-tuple-element.78), channel_id=1, source_target_pairs={{0,1},{1,0},{2,3},{3,2},{4,5},{5,4},{6,7},{7,6},{8,9},{9,8},{10,11... | collective-permute-start | bytes 319496 | tf_op jit(solution)/shard_map/ppermute | solution.py:33
  31.3 1.0 collective-permute-done.4
  32.2 0.9 collective-permute-start.5
  33.2 0.9 prepare.1
  34.1 3.4 %collective-permute-done.5 = f32[104,256]{1,0:T(8,128)S(1)} collective-permute-done((f32[104,256]{1,0:T(8,128)S(1)}, f32[104,256]{1,0:T(8,128)S(1)}, u32[]{:S(2)}, u32[]{:S(2)}) %collective-permute-start.5) | collective-permute-done | bytes 106528 | tf_op jit(solution)/shard_map/ppermute | solution.py:33
  37.6 1.6 %collective-permute-start.6 = (f32[104,256]{1,0:T(8,128)S(1)}, f32[104,256]{1,0:T(8,128)S(1)}, u32[]{:S(2)}, u32[]{:S(2)}) collective-permute-start(f32[104,256]{1,0:T(8,128)S(1)} %add.45), channel_id=1, source_target_pairs={{0,4},{4,0},{8,12},{12,8},{1,5},{5,1},{9,13},{13,9},{2,6},{6,2},{1... | collective-permute-start | bytes 319496 | tf_op jit(solution)/shard_map/ppermute | solution.py:33
  39.2 3.1 %collective-permute-done.6 = f32[104,256]{1,0:T(8,128)S(1)} collective-permute-done((f32[104,256]{1,0:T(8,128)S(1)}, f32[104,256]{1,0:T(8,128)S(1)}, u32[]{:S(2)}, u32[]{:S(2)}) %collective-permute-start.6) | collective-permute-done | bytes 106528 | tf_op jit(solution)/shard_map/ppermute | solution.py:33
  42.3 2.6 %collective-permute-start.7 = (f32[104,256]{1,0:T(8,128)S(1)}, f32[104,256]{1,0:T(8,128)S(1)}, u32[]{:S(2)}, u32[]{:S(2)}) collective-permute-start(f32[104,256]{1,0:T(8,128)S(1)} %add.46), channel_id=1, source_target_pairs={{0,8},{4,12},{8,0},{12,4},{1,9},{5,13},{9,1},{13,5},{2,10},{6,14},... | collective-permute-start | bytes 319496 | tf_op jit(solution)/shard_map/ppermute | solution.py:33
  45.0 4.2 %collective-permute-done.7 = f32[104,256]{1,0:T(8,128)S(1)} collective-permute-done((f32[104,256]{1,0:T(8,128)S(1)}, f32[104,256]{1,0:T(8,128)S(1)}, u32[]{:S(2)}, u32[]{:S(2)}) %collective-permute-start.7) | collective-permute-done | bytes 106528 | tf_op jit(solution)/shard_map/ppermute | solution.py:33
  49.2 0.1 collective-permute-start.8
  49.9 0.7 collective-permute-done.8.other
  50.6 0.0 copy-done.1
  50.6 9.7 %head.1 = (f32[272,256]{1,0:T(8,128)S(1)}, f32[320,768]{1,0:T(8,128)S(1)}, bf16[512,768]{1,0:T(8,128)(2,1)S(1)}, bf16[512,768]{1,0:T(8,128)(2,1)S(1)}) custom-call(s32[1]{0:T(128)} %bitcast.3.flag, s32[1]{0:T(128)S(6)} %copy.23.label, f32[10]{0:T(128)S(1)} %copy-done.5, f32[104,256]{1,0:T(8,128)S(1)} %add.47.own, ...), custom_call_target="tpu_custom_call" | custom-call | flops 10000000000 | bytes 10000000 | tf_op jit(solution)/shard_map/head/pallas_call | solution.py:561
  60.3 1.6 %collective-permute-start.9 = (f32[272,256]{1,0:T(8,128)S(1)}, f32[272,256]{1,0:T(8,128)S(1)}, u32[]{:S(2)}, u32[]{:S(2)}) collective-permute-start(f32[272,256]{1,0:T(8,128)S(1)} %get-tuple-element.111), channel_id=1, source_target_pairs={{0,16},{16,0},{1,17},{17,1},{2,18},{18,2},{3,19},{19,3},{4,20},{20... | collective-permute-start | bytes 835592 | tf_op jit(solution)/shard_map/ppermute | solution.py:33
  61.9 6.7 %tap_grads.2.payload_in = f32[320,768]{1,0:T(8,128)S(1)} custom-call(f32[6,16,14,8,128]{4,3,2,1,0:T(8,128)S(1)} %get-tuple-element.69.spread_in, f32[6,3,14,8,128]{4,3,2,1,0:T(8,128)S(1)} %get-tuple-element.75.spread_top, f32[6,3,14,8,128]{4,3,2,1,0:T(8,128)S(1)} %get-tuple-element.76.spread_bottom, ...), custom_call_target="tpu_custom_call", output_to_operand_aliasing={{}: (5, {})} | custom-call | flops 10000000000 | bytes 10000000 | tf_op jit(solution)/shard_map/tap_grads/pallas_call | solution.py:706
  68.6 0.5 collective-permute-done.9
  69.1 1.3 %tap_grads.3 = f32[320,768]{1,0:T(8,128)S(1)} custom-call(f32[6,16,14,8,128]{4,3,2,1,0:T(8,128)S(1)} %get-tuple-element.69.spread_in, f32[6,3,14,8,128]{4,3,2,1,0:T(8,128)S(1)} %get-tuple-element.75.spread_top, f32[6,3,14,8,128]{4,3,2,1,0:T(8,128)S(1)} %get-tuple-element.76.spread_bottom, ...), custom_call_target="tpu_custom_call", output_to_operand_aliasing={{}: (5, {})} | custom-call | flops 2000000000 | bytes 2000000 | tf_op jit(solution)/shard_map/tap_grads/pallas_call | solution.py:706
  70.5 0.1 collective-permute-start.10
  70.5 1.5 %collective-permute-done.10 = bf16[160,768]{1,0:T(8,128)(2,1)S(1)} collective-permute-done((bf16[160,768]{1,0:T(8,128)(2,1)S(1)}, bf16[160,768]{1,0:T(8,128)(2,1)S(1)}, u32[]{:S(2)}, u32[]{:S(2)}) %collective-permute-start.10) | collective-permute-done | bytes 245792 | tf_op jit(solution)/shard_map/ppermute | solution.py:33
  72.0 0.1 convert_add_fusion
  72.2 0.7 collective-permute-start.11
  72.9 1.5 %collective-permute-start.12 = (bf16[40,768]{1,0:T(8,128)(2,1)S(1)}, bf16[40,768]{1,0:T(8,128)(2,1)S(1)}, u32[]{:S(2)}, u32[]{:S(2)}) collective-permute-start(bf16[40,768]{1,0:T(8,128)(2,1)S(1)} %get-tuple-element.127), channel_id=1, source_target_pairs={{0,16},{1,17},{2,18},{3,19},{16,0},{17,1},{18,2},{19,3},{4,20},{5,... | collective-permute-start | bytes 184328 | tf_op jit(solution)/shard_map/ppermute | solution.py:78
  74.4 1.4 %collective-permute-start.13 = (bf16[40,768]{1,0:T(8,128)(2,1)S(1)}, bf16[40,768]{1,0:T(8,128)(2,1)S(1)}, u32[]{:S(2)}, u32[]{:S(2)}) collective-permute-start(bf16[40,768]{1,0:T(8,128)(2,1)S(1)} %get-tuple-element.126), channel_id=1, source_target_pairs={{0,18},{1,19},{2,16},{3,17},{16,2},{17,3},{18,0},{19,1},{4,22},{5,... | collective-permute-start | bytes 184328 | tf_op jit(solution)/shard_map/ppermute | solution.py:78
  75.7 0.7 collective-permute-done.11
  76.4 0.7 collective-permute-done.12
  77.1 2.4 %collective-permute-done.13 = bf16[40,768]{1,0:T(8,128)(2,1)S(1)} collective-permute-done((bf16[40,768]{1,0:T(8,128)(2,1)S(1)}, bf16[40,768]{1,0:T(8,128)(2,1)S(1)}, u32[]{:S(2)}, u32[]{:S(2)}) %collective-permute-start.13) | collective-permute-done | bytes 61472 | tf_op jit(solution)/shard_map/ppermute | solution.py:78
  79.5 0.6 collective-permute-start.14
  80.1 2.6 %collective-permute-start.15 = (bf16[40,768]{1,0:T(8,128)(2,1)S(1)}, bf16[40,768]{1,0:T(8,128)(2,1)S(1)}, u32[]{:S(2)}, u32[]{:S(2)}) collective-permute-start(bf16[40,768]{1,0:T(8,128)(2,1)S(1)} %fusion.1), channel_id=1, source_target_pairs={{0,8},{4,12},{8,0},{12,4},{1,9},{5,13},{9,1},{13,5},{2,10},{6,14},... | collective-permute-start | bytes 184328 | tf_op jit(solution)/shard_map/ppermute | solution.py:33
  82.8 1.2 %collective-permute-start.16 = (bf16[40,768]{1,0:T(8,128)(2,1)S(1)}, bf16[40,768]{1,0:T(8,128)(2,1)S(1)}, u32[]{:S(2)}, u32[]{:S(2)}) collective-permute-start(bf16[40,768]{1,0:T(8,128)(2,1)S(1)} %fusion.1), channel_id=1, source_target_pairs={{0,12},{4,8},{8,4},{12,0},{1,13},{5,9},{9,5},{13,1},{2,14},{6,10},... | collective-permute-start | bytes 184328 | tf_op jit(solution)/shard_map/ppermute | solution.py:33
  84.0 0.0 collective-permute-done.14
  84.0 1.3 %collective-permute-done.15 = bf16[40,768]{1,0:T(8,128)(2,1)S(1)} collective-permute-done((bf16[40,768]{1,0:T(8,128)(2,1)S(1)}, bf16[40,768]{1,0:T(8,128)(2,1)S(1)}, u32[]{:S(2)}, u32[]{:S(2)}) %collective-permute-start.15) | collective-permute-done | bytes 61472 | tf_op jit(solution)/shard_map/ppermute | solution.py:33
  85.2 3.5 %collective-permute-done.16 = bf16[40,768]{1,0:T(8,128)(2,1)S(1)} collective-permute-done((bf16[40,768]{1,0:T(8,128)(2,1)S(1)}, bf16[40,768]{1,0:T(8,128)(2,1)S(1)}, u32[]{:S(2)}, u32[]{:S(2)}) %collective-permute-start.16) | collective-permute-done | bytes 61472 | tf_op jit(solution)/shard_map/ppermute | solution.py:33
  88.8 0.1 slice_reduce_fusion.1
  89.0 1.6 %collective-permute-start.17 = (bf16[40,768]{1,0:T(8,128)(2,1)S(1)}, bf16[40,768]{1,0:T(8,128)(2,1)S(1)}, u32[]{:S(2)}, u32[]{:S(2)}) collective-permute-start(bf16[40,768]{1,0:T(8,128)(2,1)S(1)} %add_convert_fusion), channel_id=1, source_target_pairs={{0,2},{1,3},{2,0},{3,1},{16,18},{17,19},{18,16},{19,17},{4,6},{5,7... | collective-permute-start | bytes 184328 | tf_op jit(solution)/shard_map/ppermute | solution.py:87
  90.6 0.5 collective-permute-start.18
  91.1 1.4 %collective-permute-start.19 = (bf16[40,768]{1,0:T(8,128)(2,1)S(1)}, bf16[40,768]{1,0:T(8,128)(2,1)S(1)}, u32[]{:S(2)}, u32[]{:S(2)}) collective-permute-start(bf16[40,768]{1,0:T(8,128)(2,1)S(1)} %add_convert_fusion), channel_id=1, source_target_pairs={{0,18},{1,19},{2,16},{3,17},{16,2},{17,3},{18,0},{19,1},{4,22},{5,... | collective-permute-start | bytes 184328 | tf_op jit(solution)/shard_map/ppermute | solution.py:87
  92.5 0.5 slice.88
  93.7 0.6 slice_reduce_fusion
  94.4 0.0 collective-permute-done.17
  94.4 0.4 collective-permute-done.18
  94.8 1.4 %collective-permute-done.19 = bf16[40,768]{1,0:T(8,128)(2,1)S(1)} collective-permute-done((bf16[40,768]{1,0:T(8,128)(2,1)S(1)}, bf16[40,768]{1,0:T(8,128)(2,1)S(1)}, u32[]{:S(2)}, u32[]{:S(2)}) %collective-permute-start.19) | collective-permute-done | bytes 61472 | tf_op jit(solution)/shard_map/ppermute | solution.py:87
  96.2 0.1 collective-permute-start.20
  96.3 1.9 %multiply_add_fusion = f32[10,256,256]{2,1,0:T(8,128)} fusion(f32[256,256]{1,0:T(8,128)S(1)} %slice.73, f32[10]{0:T(128)S(1)} %get-tuple-element.134, f32[256,256]{1,0:T(8,128)S(1)} %slice.71, f32[10]{0:T(128)S(1)} %get-tuple-element.135), kind=kLoop, calls=%fused_computation | loop fusion | flops 1966080 | bytes 3145808 | tf_op jit(solution)/shard_map/add | solution.py:42
  98.2 0.0 collective-permute-done.20.other
  98.2 1.0 %finish.1 = (f32[768,256]{1,0:T(8,128)}, f32[7,7,768]{2,1,0:T(8,128)}, f32[768]{0:T(1024)}, f32[256]{0:T(256)}) custom-call(s32[1]{0:T(128)} %bitcast.3.flag, bf16[160,768]{1,0:T(8,128)(2,1)S(1)} %bitcast.31, bf16[160,768]{1,0:T(8,128)(2,1)S(1)} %collective-permute-done.20.other), custom_call_target="tpu_custom_call" | custom-call | flops 1000000000 | bytes 1000000 | tf_op jit(solution)/shard_map/finish/pallas_call | solution.py:745
  (30 shorter events, 0.4 us)
Async XLA Ops:
  0.6 14.1 %copy-start = (bf16[1,16,64,768]{3,2,1,0:T(8,128)(2,1)S(1)}, bf16[1,16,64,768]{3,2,1,0:T(8,128)(2,1)}, u32[]{:S(2)}) copy-start(bf16[1,16,64,768]{3,2,1,0:T(8,128)(2,1)} %param.8) | copy-start | bytes 4718596
  0.6 14.1 %copy-start.4 = (f32[256]{0:T(256)S(1)}, f32[256]{0:T(256)}, u32[]{:S(2)}) copy-start(f32[256]{0:T(256)} %param.12) | copy-start | bytes 3076
  0.7 14.1 %copy-start.2 = (bf16[768,256]{1,0:T(8,128)(2,1)S(1)}, bf16[768,256]{1,0:T(8,128)(2,1)}, u32[]{:S(2)}) copy-start(bf16[768,256]{1,0:T(8,128)(2,1)} %reduce_weight.5) | copy-start | bytes 1179652
  0.7 14.1 %copy-start.3 = (f32[7,7,768]{2,1,0:T(8,128)S(1)}, f32[7,7,768]{2,1,0:T(8,128)}, u32[]{:S(2)}) copy-start(f32[7,7,768]{2,1,0:T(8,128)} %weight.3) | copy-start | bytes 451588
  1.9 5.6 %collective-permute-start = (bf16[16,3,768]{2,1,0:T(4,128)(2,1)S(1)}, bf16[16,3,768]{2,1,0:T(4,128)(2,1)S(1)}, u32[]{:S(2)}, u32[]{:S(2)}) collective-permute-start(bf16[16,3,768]{2,1,0:T(4,128)(2,1)S(1)} %get-tuple-element.123), channel_id=1, source_target_pairs={{0,1},{1,2},{2,3},{4,5},{5,6},{6,7},{8,9},{9,10},{10,11},{12,13},{... | collective-permute-start | bytes 221192 | tf_op jit(solution)/shard_map/ppermute | solution.py:103
  4.3 5.3 %collective-permute-start.1 = (bf16[16,3,768]{2,1,0:T(4,128)(2,1)S(1)}, bf16[16,3,768]{2,1,0:T(4,128)(2,1)S(1)}, u32[]{:S(2)}, u32[]{:S(2)}) collective-permute-start(bf16[16,3,768]{2,1,0:T(4,128)(2,1)S(1)} %get-tuple-element.124), channel_id=1, source_target_pairs={{1,0},{2,1},{3,2},{5,4},{6,5},{7,6},{9,8},{10,9},{11,10},{13,12},{... | collective-permute-start | bytes 221192 | tf_op jit(solution)/shard_map/ppermute | solution.py:107
  9.9 11.5 %collective-permute-start.2 = (bf16[224,768]{1,0:T(8,128)(2,1)S(1)}, bf16[224,768]{1,0:T(8,128)(2,1)S(1)}, u32[]{:S(2)}, u32[]{:S(2)}) collective-permute-start(bf16[224,768]{1,0:T(8,128)(2,1)S(1)} %get-tuple-element.71), channel_id=1, source_target_pairs={{0,4},{4,8},{8,12},{1,5},{5,9},{9,13},{2,6},{6,10},{10,14},{3,7},{... | collective-permute-start | bytes 1032200 | tf_op jit(solution)/shard_map/ppermute | solution.py:103
  13.4 10.8 %collective-permute-start.3 = (bf16[224,768]{1,0:T(8,128)(2,1)S(1)}, bf16[224,768]{1,0:T(8,128)(2,1)S(1)}, u32[]{:S(2)}, u32[]{:S(2)}) collective-permute-start(bf16[224,768]{1,0:T(8,128)(2,1)S(1)} %get-tuple-element.72), channel_id=1, source_target_pairs={{4,0},{8,4},{12,8},{5,1},{9,5},{13,9},{6,2},{10,6},{14,10},{7,3},{... | collective-permute-start | bytes 1032200 | tf_op jit(solution)/shard_map/ppermute | solution.py:107
  29.3 21.3 %copy-start.1 = (bf16[10,256,256]{2,1,0:T(8,128)(2,1)S(1)}, bf16[10,256,256]{2,1,0:T(8,128)(2,1)}, u32[]{:S(2)}) copy-start(bf16[10,256,256]{2,1,0:T(8,128)(2,1)} %class_weight.1) | copy-start | bytes 3932164
  29.3 21.2 %copy-start.5 = (f32[10]{0:T(128)S(1)}, f32[10]{0:T(128)}, u32[]{:S(2)}) copy-start(f32[10]{0:T(128)} %class_bias.1) | copy-start | bytes 124
  29.3 2.9 %collective-permute-start.4 = (f32[104,256]{1,0:T(8,128)S(1)}, f32[104,256]{1,0:T(8,128)S(1)}, u32[]{:S(2)}, u32[]{:S(2)}) collective-permute-start(f32[104,256]{1,0:T(8,128)S(1)} %get-tuple-element.78), channel_id=1, source_target_pairs={{0,1},{1,0},{2,3},{3,2},{4,5},{5,4},{6,7},{7,6},{8,9},{9,8},{10,11... | collective-permute-start | bytes 319496 | tf_op jit(solution)/shard_map/ppermute | solution.py:33
  32.2 5.3 %collective-permute-start.5 = (f32[104,256]{1,0:T(8,128)S(1)}, f32[104,256]{1,0:T(8,128)S(1)}, u32[]{:S(2)}, u32[]{:S(2)}) collective-permute-start(f32[104,256]{1,0:T(8,128)S(1)} %add.44), channel_id=1, source_target_pairs={{0,2},{1,3},{2,0},{3,1},{4,6},{5,7},{6,4},{7,5},{8,10},{9,11},{10,... | collective-permute-start | bytes 319496 | tf_op jit(solution)/shard_map/ppermute | solution.py:33
  37.6 4.8 %collective-permute-start.6 = (f32[104,256]{1,0:T(8,128)S(1)}, f32[104,256]{1,0:T(8,128)S(1)}, u32[]{:S(2)}, u32[]{:S(2)}) collective-permute-start(f32[104,256]{1,0:T(8,128)S(1)} %add.45), channel_id=1, source_target_pairs={{0,4},{4,0},{8,12},{12,8},{1,5},{5,1},{9,13},{13,9},{2,6},{6,2},{1... | collective-permute-start | bytes 319496 | tf_op jit(solution)/shard_map/ppermute | solution.py:33
  42.3 6.8 %collective-permute-start.7 = (f32[104,256]{1,0:T(8,128)S(1)}, f32[104,256]{1,0:T(8,128)S(1)}, u32[]{:S(2)}, u32[]{:S(2)}) collective-permute-start(f32[104,256]{1,0:T(8,128)S(1)} %add.46), channel_id=1, source_target_pairs={{0,8},{4,12},{8,0},{12,4},{1,9},{5,13},{9,1},{13,5},{2,10},{6,14},... | collective-permute-start | bytes 319496 | tf_op jit(solution)/shard_map/ppermute | solution.py:33
  49.2 1.4 %collective-permute-start.8 = (f32[104,256]{1,0:T(8,128)S(1)}, f32[104,256]{1,0:T(8,128)S(1)}, u32[]{:S(2)}, u32[]{:S(2)}) collective-permute-start(f32[104,256]{1,0:T(8,128)S(1)} %add.47.own), channel_id=1, source_target_pairs={{0,1},{1,0},{2,3},{3,2},{4,5},{5,4},{6,7},{7,6},{8,9},{9,8},{10,11... | collective-permute-start | bytes 319496 | tf_op jit(solution)/shard_map/ppermute | solution.py:33
  60.3 8.8 %collective-permute-start.9 = (f32[272,256]{1,0:T(8,128)S(1)}, f32[272,256]{1,0:T(8,128)S(1)}, u32[]{:S(2)}, u32[]{:S(2)}) collective-permute-start(f32[272,256]{1,0:T(8,128)S(1)} %get-tuple-element.111), channel_id=1, source_target_pairs={{0,16},{16,0},{1,17},{17,1},{2,18},{18,2},{3,19},{19,3},{4,20},{20... | collective-permute-start | bytes 835592 | tf_op jit(solution)/shard_map/ppermute | solution.py:33
  70.5 1.6 %collective-permute-start.10 = (bf16[160,768]{1,0:T(8,128)(2,1)S(1)}, bf16[160,768]{1,0:T(8,128)(2,1)S(1)}, u32[]{:S(2)}, u32[]{:S(2)}) collective-permute-start(bf16[160,768]{1,0:T(8,128)(2,1)S(1)} %select_convert_fusion), channel_id=1, source_target_pairs={{0,1},{1,0},{2,3},{3,2},{4,5},{5,4},{6,7},{7,6},{8,9},{9,8},{10,11... | collective-permute-start | bytes 737288 | tf_op jit(solution)/shard_map/ppermute | solution.py:33
  72.2 4.3 %collective-permute-start.11 = (bf16[40,768]{1,0:T(8,128)(2,1)S(1)}, bf16[40,768]{1,0:T(8,128)(2,1)S(1)}, u32[]{:S(2)}, u32[]{:S(2)}) collective-permute-start(bf16[40,768]{1,0:T(8,128)(2,1)S(1)} %get-tuple-element.125), channel_id=1, source_target_pairs={{0,2},{1,3},{2,0},{3,1},{16,18},{17,19},{18,16},{19,17},{4,6},{5,7... | collective-permute-start | bytes 184328 | tf_op jit(solution)/shard_map/ppermute | solution.py:78
  72.9 4.2 %collective-permute-start.12 = (bf16[40,768]{1,0:T(8,128)(2,1)S(1)}, bf16[40,768]{1,0:T(8,128)(2,1)S(1)}, u32[]{:S(2)}, u32[]{:S(2)}) collective-permute-start(bf16[40,768]{1,0:T(8,128)(2,1)S(1)} %get-tuple-element.127), channel_id=1, source_target_pairs={{0,16},{1,17},{2,18},{3,19},{16,0},{17,1},{18,2},{19,3},{4,20},{5,... | collective-permute-start | bytes 184328 | tf_op jit(solution)/shard_map/ppermute | solution.py:78
  74.4 5.1 %collective-permute-start.13 = (bf16[40,768]{1,0:T(8,128)(2,1)S(1)}, bf16[40,768]{1,0:T(8,128)(2,1)S(1)}, u32[]{:S(2)}, u32[]{:S(2)}) collective-permute-start(bf16[40,768]{1,0:T(8,128)(2,1)S(1)} %get-tuple-element.126), channel_id=1, source_target_pairs={{0,18},{1,19},{2,16},{3,17},{16,2},{17,3},{18,0},{19,1},{4,22},{5,... | collective-permute-start | bytes 184328 | tf_op jit(solution)/shard_map/ppermute | solution.py:78
  79.5 4.5 %collective-permute-start.14 = (bf16[40,768]{1,0:T(8,128)(2,1)S(1)}, bf16[40,768]{1,0:T(8,128)(2,1)S(1)}, u32[]{:S(2)}, u32[]{:S(2)}) collective-permute-start(bf16[40,768]{1,0:T(8,128)(2,1)S(1)} %fusion.1), channel_id=1, source_target_pairs={{0,4},{4,0},{8,12},{12,8},{1,5},{5,1},{9,13},{13,9},{2,6},{6,2},{1... | collective-permute-start | bytes 184328 | tf_op jit(solution)/shard_map/ppermute | solution.py:33
  80.1 5.1 %collective-permute-start.15 = (bf16[40,768]{1,0:T(8,128)(2,1)S(1)}, bf16[40,768]{1,0:T(8,128)(2,1)S(1)}, u32[]{:S(2)}, u32[]{:S(2)}) collective-permute-start(bf16[40,768]{1,0:T(8,128)(2,1)S(1)} %fusion.1), channel_id=1, source_target_pairs={{0,8},{4,12},{8,0},{12,4},{1,9},{5,13},{9,1},{13,5},{2,10},{6,14},... | collective-permute-start | bytes 184328 | tf_op jit(solution)/shard_map/ppermute | solution.py:33
  82.8 6.0 %collective-permute-start.16 = (bf16[40,768]{1,0:T(8,128)(2,1)S(1)}, bf16[40,768]{1,0:T(8,128)(2,1)S(1)}, u32[]{:S(2)}, u32[]{:S(2)}) collective-permute-start(bf16[40,768]{1,0:T(8,128)(2,1)S(1)} %fusion.1), channel_id=1, source_target_pairs={{0,12},{4,8},{8,4},{12,0},{1,13},{5,9},{9,5},{13,1},{2,14},{6,10},... | collective-permute-start | bytes 184328 | tf_op jit(solution)/shard_map/ppermute | solution.py:33
  89.0 5.4 %collective-permute-start.17 = (bf16[40,768]{1,0:T(8,128)(2,1)S(1)}, bf16[40,768]{1,0:T(8,128)(2,1)S(1)}, u32[]{:S(2)}, u32[]{:S(2)}) collective-permute-start(bf16[40,768]{1,0:T(8,128)(2,1)S(1)} %add_convert_fusion), channel_id=1, source_target_pairs={{0,2},{1,3},{2,0},{3,1},{16,18},{17,19},{18,16},{19,17},{4,6},{5,7... | collective-permute-start | bytes 184328 | tf_op jit(solution)/shard_map/ppermute | solution.py:87
  90.6 4.2 %collective-permute-start.18 = (bf16[40,768]{1,0:T(8,128)(2,1)S(1)}, bf16[40,768]{1,0:T(8,128)(2,1)S(1)}, u32[]{:S(2)}, u32[]{:S(2)}) collective-permute-start(bf16[40,768]{1,0:T(8,128)(2,1)S(1)} %add_convert_fusion), channel_id=1, source_target_pairs={{0,16},{1,17},{2,18},{3,19},{16,0},{17,1},{18,2},{19,3},{4,20},{5,... | collective-permute-start | bytes 184328 | tf_op jit(solution)/shard_map/ppermute | solution.py:87
  91.1 5.1 %collective-permute-start.19 = (bf16[40,768]{1,0:T(8,128)(2,1)S(1)}, bf16[40,768]{1,0:T(8,128)(2,1)S(1)}, u32[]{:S(2)}, u32[]{:S(2)}) collective-permute-start(bf16[40,768]{1,0:T(8,128)(2,1)S(1)} %add_convert_fusion), channel_id=1, source_target_pairs={{0,18},{1,19},{2,16},{3,17},{16,2},{17,3},{18,0},{19,1},{4,22},{5,... | collective-permute-start | bytes 184328 | tf_op jit(solution)/shard_map/ppermute | solution.py:87
  96.2 1.9 %collective-permute-start.20 = (bf16[160,768]{1,0:T(8,128)(2,1)S(1)}, bf16[160,768]{1,0:T(8,128)(2,1)S(1)}, u32[]{:S(2)}, u32[]{:S(2)}) collective-permute-start(bf16[160,768]{1,0:T(8,128)(2,1)S(1)} %bitcast.30), channel_id=1, source_target_pairs={{0,1},{1,0},{2,3},{3,2},{4,5},{5,4},{6,7},{7,6},{8,9},{9,8},{10,11... | collective-permute-start | bytes 737288 | tf_op jit(solution)/shard_map/ppermute | solution.py:33

commit v9 on v8

--- a/solution.py
+++ b/solution.py
@@ -141,7 +141,7 @@
     return even, odd, both
 
 
-def spread_weights(weight_ref, filters, lanes):
+def spread_weights(weight_ref, filters, tile, lanes):
     rows = []
     for row_tap in range(KERNEL):
         row = [weight_ref[row_tap, tap : tap + 1, lanes] for tap in range(KERNEL)]
@@ -153,7 +153,7 @@
             for col_part, taps in enumerate(part_taps(line)):
                 start = FILTERS[row_part, col_part] + row * PARTS[col_part]
                 for col, value in enumerate(taps):
-                    filters[start + col] = value
+                    filters[tile, start + col] = value
 
 
 def fill_parts(load, parts, row_pairs, groups):
@@ -176,7 +176,7 @@
     return line
 
 
-def conv_rows(load, filters, bias, steps, count, parts, products):
+def conv_rows(load, filters, tile, bias, steps, count, parts, products):
     row_pairs, col_pairs = count // 2, steps // 2
     fill_parts(load, parts, row_pairs + 3, 2 * col_pairs + 6)
     for row_part in range(3):
@@ -193,7 +193,7 @@
                     if not 0 <= tap_row < many_rows:
                         continue
                     for tap_col in range(many_cols):
-                        scale = filters[start + tap_row * many_cols + tap_col]
+                        scale = filters[tile, start + tap_row * many_cols + tap_col]
                         for col in range(col_pairs):
                             term = line[col + tap_col] * scale
                             old = total[row][col]
@@ -218,7 +218,6 @@
 def parts_scratch(count, steps):
     row_pairs, col_pairs = count // 2, steps // 2
     return [
-        pltpu.VMEM((PRODUCTS, GROUPS, LANES), wide),
         pltpu.VMEM((2, row_pairs + 3, 2 * col_pairs + 6, GROUPS, LANES), wide),
         pltpu.VMEM((9, row_pairs, col_pairs, GROUPS, LANES), wide),
     ]
@@ -234,34 +233,51 @@
     return gram, jnp.sum(feat.astype(wide), axis=0, keepdims=True)
 
 
-def inner_kernel(
-    block, left, right, weight, bias, reduce_weight, reduce_bias,
-    spread_out, conv_out, before_out, feat_out, gram_out, colsum_out,
-    wide_row, filters, parts, products,
-):
+def spread_kernel(block, weight, spread_out, filters, wide_row):
     rows, cols = block.shape[0], block.shape[1]
-    steps = cols // GROUPS
 
     def one_tile(tile, _):
         lanes = lanes_of(tile)
-        spread_weights(weight, filters, lanes)
-        start_value = jnp.broadcast_to(bias[0:1, lanes], (GROUPS, LANES))
+        spread_weights(weight, filters, tile, lanes)
 
         def fill(turn, _):
             for row in range(FILL_ROWS):
                 row = turn * FILL_ROWS + row
                 place = wide_row.at[row]
-                fill_row(place, block[row, :, lanes], left[row, :, lanes], right[row, :, lanes])
+                nothing = jnp.zeros((HALF, LANES), wide)
+                fill_row(place, block[row, :, lanes], nothing, nothing)
                 spread_columns(place, spread_out.at[tile, row])
             return 0
 
         lax.fori_loop(0, rows // FILL_ROWS, fill, 0)
+        return 0
+
+    lax.fori_loop(0, spread_out.shape[0], one_tile, 0)
+
+
+def inner_kernel(
+    spread_in, left, right, filters, bias, reduce_weight, reduce_bias,
+    spread_out, conv_out, before_out, feat_out, gram_out, colsum_out,
+    parts, products,
+):
+    rows, groups = spread_out.shape[1:3]
+    steps = groups - KERNEL + 1
+
+    def one_tile(tile, _):
+        lanes = lanes_of(tile)
+        start_value = jnp.broadcast_to(bias[0:1, lanes], (GROUPS, LANES))
+        for row in range(rows):
+            start, end = left[row, :, lanes].astype(wide), right[row, :, lanes].astype(wide)
+            for col in range(HALF):
+                spread_out[tile, row, col, 0:1, :] = start[col : col + 1, :]
+                group = groups - HALF + col
+                spread_out[tile, row, group, GROUPS - 1 : GROUPS, :] = end[col : col + 1, :]
 
         def load(row, group):
             return spread_out[tile, row + SIDE - HALF, group]
 
         conv_out[:, lanes] = conv_rows(
-            load, filters, start_value, steps, rows - 2 * SIDE, parts, products
+            load, filters, tile, start_value, steps, rows - 2 * SIDE, parts, products
         )
         return 0
 
@@ -272,24 +288,23 @@
 
 
 def edge_kernel(
-    flag, spread_in, top, bottom, weight, bias, reduce_weight, reduce_bias, gram_in, colsum_in,
+    flag, spread_in, top, bottom, corners_top, corners_bottom, filters, bias, reduce_weight,
+    reduce_bias, gram_in, colsum_in,
     spread_top, spread_bottom, conv_out, before_out, feat_out, kept_out, sent_out,
-    wide_row, corners, filters, parts, products, sums,
+    wide_row, parts, products, sums,
 ):
     rows, cols = spread_in.shape[1], wide_row.shape[1] - 2 * EDGE
     steps = cols // GROUPS
 
     def one_tile(tile, _):
         lanes = lanes_of(tile)
-        spread_weights(weight, filters, lanes)
         start_value = jnp.broadcast_to(bias[0:1, lanes], (GROUPS, LANES))
-        for side, (strip, spread) in enumerate(((top, spread_top), (bottom, spread_bottom))):
-            corners[side] = strip[HALF * cols :, lanes].astype(wide)
+        sides = ((top, corners_top, spread_top), (bottom, corners_bottom, spread_bottom))
+        for side, (strip, ends, spread) in enumerate(sides):
             for row in range(HALF):
                 place = wide_row.at[side * HALF + row]
-                left = corners[side, row * HALF : (row + 1) * HALF, :]
-                right = corners[side, (HALF + row) * HALF : (HALF + row + 1) * HALF, :]
-                fill_row(place, strip[row * cols : (row + 1) * cols, lanes], left, right)
+                left, right = ends[0, row, :, lanes], ends[1, row, :, lanes]
+                fill_row(place, strip[row, :, lanes], left, right)
                 spread_columns(place, spread.at[tile, row])
 
         def load_from(row):
@@ -306,7 +321,8 @@
         for side, row in enumerate((0, rows - SIDE)):
             start = side * SIDE * cols
             conv_out[start : start + SIDE * cols, lanes] = conv_rows(
-                load_from(row), filters, start_value, steps, SIDE, parts.at[side], products.at[side]
+                load_from(row), filters, tile, start_value, steps, SIDE,
+                parts.at[side], products.at[side],
             )
         return 0
 
@@ -314,15 +330,16 @@
     gram, colsum = reduce_part(conv_out, reduce_weight, reduce_bias, before_out, feat_out)
     gram = gram + gram_in[...]
     colsum = colsum + colsum_in[...]
-    width = gram.shape[0]
-    half = width // 2
-    quarter = half // 2
-    sums[:half, :] = gram[:half, :]
-    sums[half : half + quarter, :half] = gram[half : half + quarter, half:]
-    sums[half : half + quarter, half:] = gram[half + quarter :, half:]
-    sums[half + quarter :, :] = jnp.broadcast_to(
-        colsum, (sums.shape[0] - half - quarter, width)
-    )
+    half = gram.shape[0] // 2
+    row = lax.broadcasted_iota(jnp.int32, (half, half), 0)
+    col = lax.broadcasted_iota(jnp.int32, (half, half), 1)
+    last_block = gram[half:, half:]
+    diagonal = jnp.sum(jnp.where(row == col, last_block, 0.0), axis=0, keepdims=True)
+    sums[:half, :half] = gram[:half, half:]
+    sums[:half, half:] = jnp.where(row <= col, gram[:half, :half], last_block)
+    sums[half : half + GROUPS, :] = jnp.broadcast_to(colsum, (GROUPS, 2 * half))
+    sums[half + GROUPS :, :half] = jnp.broadcast_to(diagonal, (GROUPS, half))
+    sums[half + GROUPS :, half:] = jnp.zeros((GROUPS, half), wide)
     part = kept_out.shape[0]
     keep_or_send(flag[0] != 0, sums[:part, :], sums[part:, :], kept_out, sent_out)
 
@@ -350,45 +367,60 @@
     )
 
 
-def conv_inner(block, left, right, weight, bias, reduce_weight, reduce_bias):
+def spread_block(block, weight):
     rows, cols, channels = block.shape
-    width = reduce_weight.shape[1]
     tiles = channels // LANES
-    steps = cols // GROUPS
-    pixels = (rows - 2 * SIDE) * cols
+    return pl.pallas_call(
+        spread_kernel,
+        in_specs=[in_vmem] * 2,
+        out_specs=[in_vmem] * 2,
+        out_shape=[
+            shape_of((tiles, rows, cols // GROUPS + KERNEL - 1, GROUPS, LANES)),
+            shape_of((tiles, PRODUCTS, GROUPS, LANES)),
+        ],
+        scratch_shapes=[pltpu.VMEM((rows, cols + 2 * EDGE, LANES), wide)],
+        compiler_params=params(8),
+        cost_estimate=cost(2),
+        name="spread_block",
+    )(block, weight)
+
+
+def conv_inner(spread, left, right, filters, bias, reduce_weight, reduce_bias):
+    tiles, rows, groups = spread.shape[:3]
+    channels, width = reduce_weight.shape
+    steps = groups - KERNEL + 1
+    pixels = (rows - 2 * SIDE) * steps * GROUPS
     return pl.pallas_call(
         inner_kernel,
         in_specs=[in_vmem] * 7,
         out_specs=[in_vmem] * 6,
         out_shape=[
-            shape_of((tiles, rows, steps + KERNEL - 1, GROUPS, LANES)),
+            shape_of(spread.shape),
             shape_of((pixels, channels), narrow),
             shape_of((pixels, width)),
             shape_of((pixels, width), narrow),
             shape_of((width, width)),
             shape_of((1, width)),
         ],
-        scratch_shapes=[
-            pltpu.VMEM((rows, cols + 2 * EDGE, LANES), wide),
-            *parts_scratch(rows - 2 * SIDE, steps),
-        ],
+        input_output_aliases={0: 0},
+        scratch_shapes=parts_scratch(rows - 2 * SIDE, steps),
         compiler_params=params(24),
         cost_estimate=cost(10),
         name="conv_inner",
-    )(block, left, right, weight, bias, reduce_weight, reduce_bias)
-
-
-def conv_edge(flag, spread, top, bottom, weight, bias, reduce_weight, reduce_bias, gram, colsum):
+    )(spread, left, right, filters, bias, reduce_weight, reduce_bias)
+
+
+def conv_edge(flag, spread, halos, filters, bias, reduce_weight, reduce_bias, gram, colsum):
     tiles, rows, groups = spread.shape[:3]
-    cols, channels = (groups - KERNEL + 1) * GROUPS, top.shape[1]
-    width = reduce_weight.shape[1]
+    cols = (groups - KERNEL + 1) * GROUPS
+    channels, width = reduce_weight.shape
     pixels = 2 * SIDE * cols
-    filters, parts, products = parts_scratch(SIDE, cols // GROUPS)
+    parts, products = parts_scratch(SIDE, cols // GROUPS)
     side = (tiles, HALF, groups, GROUPS, LANES)
-    sums_rows = 3 * width // 4 + 2 * GROUPS
+    sums_rows = width // 2 + 2 * GROUPS
     return pl.pallas_call(
         edge_kernel,
-        in_specs=[in_smem] + [in_vmem] * 9,
+        in_specs=[in_smem] + [in_vmem] * 11,
         out_specs=[in_vmem] * 7,
         out_shape=[
             shape_of(side),
@@ -401,8 +433,6 @@
         ],
         scratch_shapes=[
             pltpu.VMEM((2 * HALF, cols + 2 * EDGE, LANES), wide),
-            pltpu.VMEM((2, top.shape[0] - HALF * cols, LANES), wide),
-            filters,
             pltpu.VMEM((2,) + parts.shape, wide),
             pltpu.VMEM((2,) + products.shape, wide),
             pltpu.VMEM((sums_rows, width), wide),
@@ -410,7 +440,7 @@
         compiler_params=params(24),
         cost_estimate=cost(6),
         name="conv_edge",
-    )(flag, spread, top, bottom, weight, bias, reduce_weight, reduce_bias, gram, colsum)
+    )(flag, spread, *halos, filters, bias, reduce_weight, reduce_bias, gram, colsum)
 
 
 def split(value):
@@ -473,20 +503,26 @@
 ):
     width = root_out.shape[1]
     half = width // 2
-    quarter = half // 2
     rows = own.shape[0]
     upper = flag[0] != 0
     mine, theirs = own[...], other[...]
     sums[:rows, :] = jnp.where(upper, theirs, mine)
     sums[rows:, :] = jnp.where(upper, mine, theirs)
-    low = jnp.concatenate(
-        [sums[half : half + quarter, :half], sums[half : half + quarter, half:]], axis=0
-    )
-    cross = sums[:half, half:]
+    row = lax.broadcasted_iota(jnp.int32, (half, half), 0)
+    col = lax.broadcasted_iota(jnp.int32, (half, half), 1)
+    cross, mixed = sums[:half, :half], sums[:half, half:]
+    turned = mixed.T
+    first = jnp.where(row <= col, mixed, turned)
+    diagonal = jnp.broadcast_to(sums[half + GROUPS : half + GROUPS + 1, :half], (half, half))
+    last = jnp.where(row == col, diagonal, jnp.where(row > col, mixed, turned))
     gram = jnp.concatenate(
-        [sums[:half, :], jnp.concatenate([cross.T, low], axis=1)], axis=0
-    )
-    mean_row = sums[half + quarter : half + quarter + 1, :] / count
+        [
+            jnp.concatenate([first, cross], axis=1),
+            jnp.concatenate([cross.T, last], axis=1),
+        ],
+        axis=0,
+    )
+    mean_row = sums[half : half + 1, :] / count
     mean_col = jnp.broadcast_to(mean_row, (width, width)).T
     sigma = gram / count - mean_col * mean_row
     row = lax.broadcasted_iota(jnp.int32, (width, width), 0)
@@ -759,13 +795,6 @@
     )(flag, own, other)
 
 
-def edge_strip(block, left, right, rows):
-    channels = block.shape[2]
-    parts = [part[rows].reshape(-1, channels) for part in (block, left, right)]
-    short = -(2 * HALF * HALF) % 16
-    return jnp.concatenate(parts + [jnp.zeros((short, channels), block.dtype)])
-
-
 def body(
     features, depth_weight, depth_bias, reduce_weight, reduce_bias, class_weight, class_bias, labels
 ):
@@ -781,30 +810,40 @@
     upper = is_upper("sx", 1)
     corner = 2 * (lax.axis_index("dp") & 1) + ((lax.axis_index("sx") & 2) >> 1)
     places = [corner ^ turn for turn in range(4)]
+    block, flag, upper, places = together((block, flag, upper, places))
     bias_row = depth_bias[None]
     reduce_row = reduce_bias[None]
     left = next_along(block[:, cols - HALF :], "sx")
     right = back_along(block[:, :HALF], "sx")
-    low, high, left, right, flag, upper, places, bias_row, reduce_row = together(
+    top = next_along(block[rows - HALF :], "sy")
+    bottom = back_along(block[:HALF], "sy")
+    spread, filters = spread_block(block, depth_weight)
+    left, right, spread, filters = together((left, right, spread, filters))
+    low, high, left, right, bias_row, reduce_row = together(
         (
-            edge_strip(block, left, right, slice(rows - HALF, rows)),
-            edge_strip(block, left, right, slice(0, HALF)),
+            jnp.stack([left[rows - HALF :], right[rows - HALF :]]),
+            jnp.stack([left[:HALF], right[:HALF]]),
             left,
             right,
-            flag,
-            upper,
-            places,
             bias_row,
             reduce_row,
         )
     )
-    top = next_along(low, "sy")
-    bottom = back_along(high, "sy")
+    corners_top = next_along(low, "sy")
+    corners_bottom = back_along(high, "sy")
     spread, conv_in, before_in, feat_in, gram, colsum = conv_inner(
-        block, left, right, depth_weight, bias_row, reduce_weight, reduce_row
+        spread, left, right, filters, bias_row, reduce_weight, reduce_row
     )
     spread_top, spread_bottom, conv_ed, before_ed, feat_ed, kept, sent = conv_edge(
-        flag, spread, top, bottom, depth_weight, bias_row, reduce_weight, reduce_row, gram, colsum
+        flag,
+        spread,
+        (top, bottom, corners_top, corners_bottom),
+        filters,
+        bias_row,
+        reduce_weight,
+        reduce_row,
+        gram,
+        colsum,
     )
 
     sums = kept + swap(sent, "sx", 1)

time: 101 us -> 106 us (1.050)
  starting transfers between devices: 28.9 us -> 39.6 us
  waiting for transfers between devices: 29.6 us -> 22.9 us
  local copies, waits for them, and re-layouts: 4.65 us -> 6.07 us
    ppermute x2 -> x3, starting transfers between devices: 5.86 us -> 11.2 us  [next_along(): lax.ppermute(value, axis, [(i, i + 1) for i in range(lax.axis_size(axis)...]
    ppermute x2 -> x3, waiting for transfers between devices: 4.83 us -> 0.01 us  [back_along(): lax.ppermute(value, axis, [(i + 1, i) for i in range(lax.axis_size(axis)...]
    ppermute x11, starting transfers between devices: 13.3 us -> 17.3 us  [swap(): return lax.ppermute(value, axis, [(i, i ^ shift) for i in range(count)])]
    ppermute x11, waiting for transfers between devices: 19.1 us -> 15.8 us  [swap(): return lax.ppermute(value, axis, [(i, i ^ shift) for i in range(count)])]
    unnamed x12 -> x14, local copies, waits for them, and re-layouts: 0.03 us -> 2.34 us
    pallas_call x1, Pallas kernels: 6.69 us -> 4.58 us  [conv_inner(): pl.pallas_call(inner_kernel, in_specs=[in_vmem] * 7, out_specs=[in_vmem]...]
    pallas_call x1 -> x2, Pallas kernels: 5.09 us -> 6.76 us  [the longest x1 5.18 us: conv_edge(): pl.pallas_call(edge_kernel, in_specs=[in_smem] + [in_vmem] * 11, out_spec...]
    ppermute x2 -> x3, starting transfers between devices: 2.58 us -> 3.88 us  [back_along(): lax.ppermute(value, axis, [(i + 1, i) for i in range(lax.axis_size(axis)...]
  transfers between devices with their start and end apart: 21 -> 23, of which waited for: 16 -> 14; matrix products, arithmetic and copies ran while one was open for 5% -> 3% of each run, Pallas kernels for 14% -> 13%
where the time goes in v9:
time: 106 us; the launch traced here: 105 us
  starting transfers between devices  39.6 us (37%)
  Pallas kernels  31.1 us (29%)
  waiting for transfers between devices  22.9 us (22%)
  local copies, waits for them, and re-layouts  6.07 us (6%)
  between operations  3.41 us (3%)
  other arithmetic  2.15 us (2%)
    ppermute x11, starting transfers between devices, swap(): return lax.ppermute(value, axis, [(i, i ^ shift) for i in range(count)])  17.3 us
    ppermute x11, waiting for transfers between devices, swap(): return lax.ppermute(value, axis, [(i, i ^ shift) for i in range(count)])  15.8 us
    ppermute x3, starting transfers between devices, next_along(): lax.ppermute(value, axis, [(i, i + 1) for i in range(lax.axis_size(axis)...  11.2 us
    pallas_call x1, Pallas kernels, head(): pl.pallas_call(functools.partial(head_kernel, count=count, image_count=im...  9.75 us
    pallas_call x2, Pallas kernels, tap_grads(): pl.pallas_call(functools.partial(taps_kernel, first=first, last=last), in...  8.04 us
    pallas_call x1, Pallas kernels, conv_edge(): pl.pallas_call(edge_kernel, in_specs=[in_smem] + [in_vmem] * 11, out_spec...  5.18 us
    ppermute x3, waiting for transfers between devices, square_scatter(): lax.ppermute(piece(turn).astype(sent_as), axes, pairs[turn]).astype(wide)  4.88 us
    pallas_call x1, Pallas kernels, conv_inner(): pl.pallas_call(inner_kernel, in_specs=[in_vmem] * 7, out_specs=[in_vmem]...  4.58 us
  transfers between devices with their start and end apart: 23, of which 14 were waited for; matrix products, arithmetic and copies ran while one was open for 3% of the time, Pallas kernels for 13%

profile of v9, /device:TPU:0, one launch (start us, length us, event | category | flops | bytes accessed | tf_op | source)
XLA Modules:
  0.0 105.2 jit_solution(11096482759027476502)
XLA Ops:
  0.6 1.1 %fusion.6 = (bf16[16,3,768]{2,1,0:T(4,128)(2,1)S(1)}, bf16[16,3,768]{2,1,0:T(4,128)(2,1)S(1)}) fusion(bf16[16,64,768]{2,1,0:T(8,128)(2,1)} %bitcast.34), kind=kLoop, calls=%fused_computation.28 | loop fusion | bytes 294912 | tf_op jit(solution)/shard_map/slice | solution.py:817
  1.7 2.4 %collective-permute-start = (bf16[16,3,768]{2,1,0:T(4,128)(2,1)S(1)}, bf16[16,3,768]{2,1,0:T(4,128)(2,1)S(1)}, u32[]{:S(2)}, u32[]{:S(2)}) collective-permute-start(bf16[16,3,768]{2,1,0:T(4,128)(2,1)S(1)} %get-tuple-element.138), channel_id=1, source_target_pairs={{0,1},{1,2},{2,3},{4,5},{5,6},{6,7},{8,9},{9,10},{10,11},{12,13},{... | collective-permute-start | bytes 221192 | tf_op jit(solution)/shard_map/ppermute | solution.py:103
  4.1 1.3 %collective-permute-start.1 = (bf16[16,3,768]{2,1,0:T(4,128)(2,1)S(1)}, bf16[16,3,768]{2,1,0:T(4,128)(2,1)S(1)}, u32[]{:S(2)}, u32[]{:S(2)}) collective-permute-start(bf16[16,3,768]{2,1,0:T(4,128)(2,1)S(1)} %get-tuple-element.137), channel_id=1, source_target_pairs={{1,0},{2,1},{3,2},{5,4},{6,5},{7,6},{9,8},{10,9},{11,10},{13,12},{... | collective-permute-start | bytes 221192 | tf_op jit(solution)/shard_map/ppermute | solution.py:107
  5.4 1.1 %fusion.5 = (bf16[3,64,768]{2,1,0:T(8,128)(2,1)S(1)}, bf16[3,64,768]{2,1,0:T(8,128)(2,1)S(1)}) fusion(bf16[16,64,768]{2,1,0:T(8,128)(2,1)} %bitcast.35), kind=kLoop, calls=%fused_computation.27 | loop fusion | bytes 1179648 | tf_op jit(solution)/shard_map/slice | solution.py:819
  6.5 4.3 %collective-permute-start.2 = (bf16[3,64,768]{2,1,0:T(8,128)(2,1)S(1)}, bf16[3,64,768]{2,1,0:T(8,128)(2,1)S(1)}, u32[]{:S(2)}, u32[]{:S(2)}) collective-permute-start(bf16[3,64,768]{2,1,0:T(8,128)(2,1)S(1)} %get-tuple-element.136), channel_id=1, source_target_pairs={{0,4},{4,8},{8,12},{1,5},{5,9},{9,13},{2,6},{6,10},{10,14},{3,7},{... | collective-permute-start | bytes 884744 | tf_op jit(solution)/shard_map/ppermute | solution.py:103
  10.8 1.3 %collective-permute-start.3 = (bf16[3,64,768]{2,1,0:T(8,128)(2,1)S(1)}, bf16[3,64,768]{2,1,0:T(8,128)(2,1)S(1)}, u32[]{:S(2)}, u32[]{:S(2)}) collective-permute-start(bf16[3,64,768]{2,1,0:T(8,128)(2,1)S(1)} %get-tuple-element.135), channel_id=1, source_target_pairs={{4,0},{8,4},{12,8},{5,1},{9,5},{13,9},{6,2},{10,6},{14,10},{7,3},{... | collective-permute-start | bytes 884744 | tf_op jit(solution)/shard_map/ppermute | solution.py:107
  12.1 0.0 copy-start
  12.2 1.4 %copy-done = bf16[1,16,64,768]{3,2,1,0:T(8,128)(2,1)S(1)} copy-done((bf16[1,16,64,768]{3,2,1,0:T(8,128)(2,1)S(1)}, bf16[1,16,64,768]{3,2,1,0:T(8,128)(2,1)}, u32[]{:S(2)}) %copy-start) | copy-done | bytes 1572888
  13.6 0.9 copy-done.3
  14.5 1.6 %spread_block.1 = (f32[6,16,14,8,128]{4,3,2,1,0:T(8,128)S(1)}, f32[6,121,8,128]{3,2,1,0:T(8,128)S(1)}) custom-call(bf16[16,64,768]{2,1,0:T(8,128)(2,1)S(1)} %bitcast.36, f32[7,7,768]{2,1,0:T(8,128)S(1)} %copy-done.3), custom_call_target="tpu_custom_call" | custom-call | flops 2000000000 | bytes 2000000 | tf_op jit(solution)/shard_map/spread_block/pallas_call | solution.py:373
  16.1 0.0 collective-permute-done.left
  16.1 0.0 collective-permute-done.1.right
  16.2 4.5 %collective-permute-start.4 = (bf16[2,3,3,768]{3,2,1,0:T(4,128)(2,1)S(1)}, bf16[2,3,3,768]{3,2,1,0:T(4,128)(2,1)S(1)}, u32[]{:S(2)}, u32[]{:S(2)}) collective-permute-start(bf16[2,3,3,768]{3,2,1,0:T(4,128)(2,1)S(1)} %pad_maximum_fusion), channel_id=1, source_target_pairs={{0,4},{4,8},{8,12},{1,5},{5,9},{9,13},{2,6},{6,10},{10,14},{3,7},{... | collective-permute-start | bytes 82952 | tf_op jit(solution)/shard_map/ppermute | solution.py:103
  20.8 1.3 %collective-permute-start.5 = (bf16[2,3,3,768]{3,2,1,0:T(4,128)(2,1)S(1)}, bf16[2,3,3,768]{3,2,1,0:T(4,128)(2,1)S(1)}, u32[]{:S(2)}, u32[]{:S(2)}) collective-permute-start(bf16[2,3,3,768]{3,2,1,0:T(4,128)(2,1)S(1)} %pad_maximum_fusion.1), channel_id=1, source_target_pairs={{4,0},{8,4},{12,8},{5,1},{9,5},{13,9},{6,2},{10,6},{14,10},{7,3},{... | collective-permute-start | bytes 82952 | tf_op jit(solution)/shard_map/ppermute | solution.py:107
  22.1 4.6 %conv_inner.1 = (f32[6,16,14,8,128]{4,3,2,1,0:T(8,128)S(1)}, bf16[512,768]{1,0:T(8,128)(2,1)S(1)}, f32[512,256]{1,0:T(8,128)S(1)}, bf16[512,256]{1,0:T(8,128)(2,...) custom-call(f32[6,16,14,8,128]{4,3,2,1,0:T(8,128)S(1)} %get-tuple-element.75.spread_in, ...), custom_call_target="tpu_custom_call", output_to_operand_aliasing={{0}: (0, {})} | custom-call | flops 10000000000 | bytes 10000000 | tf_op jit(solution)/shard_map/conv_inner/pallas_call | solution.py:393
  26.7 0.0 collective-permute-done.5.corners_bottom
  26.7 0.0 collective-permute-done.2.top
  26.7 5.2 %conv_edge.1 = (f32[6,3,14,8,128]{4,3,2,1,0:T(8,128)S(1)}, f32[6,3,14,8,128]{4,3,2,1,0:T(8,128)S(1)}, bf16[512,768]{1,0:T(8,128)(2,1)S(1)}, f32[512,256]{1,0:T(8...) custom-call(s32[1]{0:T(128)} %bitcast.1.flag, ...), custom_call_target="tpu_custom_call" | custom-call | flops 6000000000 | bytes 6000000 | tf_op jit(solution)/shard_map/conv_edge/pallas_call | solution.py:421
  31.9 0.0 copy-start.1
  31.9 0.0 copy-start.5
  31.9 1.7 %collective-permute-start.6 = (f32[72,256]{1,0:T(8,128)S(1)}, f32[72,256]{1,0:T(8,128)S(1)}, u32[]{:S(2)}, u32[]{:S(2)}) collective-permute-start(f32[72,256]{1,0:T(8,128)S(1)} %get-tuple-element.92), channel_id=1, source_target_pairs={{0,1},{1,0},{2,3},{3,2},{4,5},{5,4},{6,7},{7,6},{8,9},{9,8},{10,11... | collective-permute-start | bytes 221192 | tf_op jit(solution)/shard_map/ppermute | solution.py:33
  33.6 0.9 collective-permute-done.6
  34.5 2.9 %collective-permute-start.7 = (f32[72,256]{1,0:T(8,128)S(1)}, f32[72,256]{1,0:T(8,128)S(1)}, u32[]{:S(2)}, u32[]{:S(2)}) collective-permute-start(f32[72,256]{1,0:T(8,128)S(1)} %add.44), channel_id=1, source_target_pairs={{0,2},{1,3},{2,0},{3,1},{4,6},{5,7},{6,4},{7,5},{8,10},{9,11},{10,... | collective-permute-start | bytes 221192 | tf_op jit(solution)/shard_map/ppermute | solution.py:33
  37.4 0.9 prepare.1
  38.3 1.6 %collective-permute-done.7 = f32[72,256]{1,0:T(8,128)S(1)} collective-permute-done((f32[72,256]{1,0:T(8,128)S(1)}, f32[72,256]{1,0:T(8,128)S(1)}, u32[]{:S(2)}, u32[]{:S(2)}) %collective-permute-start.7) | collective-permute-done | bytes 73760 | tf_op jit(solution)/shard_map/ppermute | solution.py:33
  40.0 2.7 %collective-permute-start.8 = (f32[72,256]{1,0:T(8,128)S(1)}, f32[72,256]{1,0:T(8,128)S(1)}, u32[]{:S(2)}, u32[]{:S(2)}) collective-permute-start(f32[72,256]{1,0:T(8,128)S(1)} %add.45), channel_id=1, source_target_pairs={{0,4},{4,0},{8,12},{12,8},{1,5},{5,1},{9,13},{13,9},{2,6},{6,2},{1... | collective-permute-start | bytes 221192 | tf_op jit(solution)/shard_map/ppermute | solution.py:33
  42.7 2.3 %collective-permute-done.8 = f32[72,256]{1,0:T(8,128)S(1)} collective-permute-done((f32[72,256]{1,0:T(8,128)S(1)}, f32[72,256]{1,0:T(8,128)S(1)}, u32[]{:S(2)}, u32[]{:S(2)}) %collective-permute-start.8) | collective-permute-done | bytes 73760 | tf_op jit(solution)/shard_map/ppermute | solution.py:33
  45.0 3.1 %collective-permute-start.9 = (f32[72,256]{1,0:T(8,128)S(1)}, f32[72,256]{1,0:T(8,128)S(1)}, u32[]{:S(2)}, u32[]{:S(2)}) collective-permute-start(f32[72,256]{1,0:T(8,128)S(1)} %add.46), channel_id=1, source_target_pairs={{0,8},{4,12},{8,0},{12,4},{1,9},{5,13},{9,1},{13,5},{2,10},{6,14},... | collective-permute-start | bytes 221192 | tf_op jit(solution)/shard_map/ppermute | solution.py:33
  48.1 2.3 %collective-permute-done.9 = f32[72,256]{1,0:T(8,128)S(1)} collective-permute-done((f32[72,256]{1,0:T(8,128)S(1)}, f32[72,256]{1,0:T(8,128)S(1)}, u32[]{:S(2)}, u32[]{:S(2)}) %collective-permute-start.9) | collective-permute-done | bytes 73760 | tf_op jit(solution)/shard_map/ppermute | solution.py:33
  50.5 0.1 collective-permute-start.10
  51.2 0.6 collective-permute-done.10.other
  51.8 9.8 %head.1 = (f32[272,256]{1,0:T(8,128)S(1)}, f32[320,768]{1,0:T(8,128)S(1)}, bf16[512,768]{1,0:T(8,128)(2,1)S(1)}, bf16[512,768]{1,0:T(8,128)(2,1)S(1)}) custom-call(s32[1]{0:T(128)} %bitcast.1.flag, s32[1]{0:T(128)S(6)} %copy.25.label, f32[10]{0:T(128)S(1)} %copy-done.5, f32[72,256]{1,0:T(8,128)S(1)} %add.47.own, ...), custom_call_target="tpu_custom_call" | custom-call | flops 10000000000 | bytes 10000000 | tf_op jit(solution)/shard_map/head/pallas_call | solution.py:597
  61.6 1.6 %collective-permute-start.11 = (f32[272,256]{1,0:T(8,128)S(1)}, f32[272,256]{1,0:T(8,128)S(1)}, u32[]{:S(2)}, u32[]{:S(2)}) collective-permute-start(f32[272,256]{1,0:T(8,128)S(1)} %get-tuple-element.125), channel_id=1, source_target_pairs={{0,16},{16,0},{1,17},{17,1},{2,18},{18,2},{3,19},{19,3},{4,20},{20... | collective-permute-start | bytes 835592 | tf_op jit(solution)/shard_map/ppermute | solution.py:33
  63.1 6.7 %tap_grads.2.payload_in = f32[320,768]{1,0:T(8,128)S(1)} custom-call(f32[6,16,14,8,128]{4,3,2,1,0:T(8,128)S(1)} %get-tuple-element.83.spread_in, f32[6,3,14,8,128]{4,3,2,1,0:T(8,128)S(1)} %get-tuple-element.89.spread_top, f32[6,3,14,8,128]{4,3,2,1,0:T(8,128)S(1)} %get-tuple-element.90.spread_bottom, ...), custom_call_target="tpu_custom_call", output_to_operand_aliasing={{}: (5, {})} | custom-call | flops 10000000000 | bytes 10000000 | tf_op jit(solution)/shard_map/tap_grads/pallas_call | solution.py:742
  69.9 0.5 collective-permute-done.11
  70.4 1.3 %tap_grads.3 = f32[320,768]{1,0:T(8,128)S(1)} custom-call(f32[6,16,14,8,128]{4,3,2,1,0:T(8,128)S(1)} %get-tuple-element.83.spread_in, f32[6,3,14,8,128]{4,3,2,1,0:T(8,128)S(1)} %get-tuple-element.89.spread_top, f32[6,3,14,8,128]{4,3,2,1,0:T(8,128)S(1)} %get-tuple-element.90.spread_bottom, ...), custom_call_target="tpu_custom_call", output_to_operand_aliasing={{}: (5, {})} | custom-call | flops 2000000000 | bytes 2000000 | tf_op jit(solution)/shard_map/tap_grads/pallas_call | solution.py:742
  71.7 0.1 collective-permute-start.12
  71.8 1.5 %collective-permute-done.12 = bf16[160,768]{1,0:T(8,128)(2,1)S(1)} collective-permute-done((bf16[160,768]{1,0:T(8,128)(2,1)S(1)}, bf16[160,768]{1,0:T(8,128)(2,1)S(1)}, u32[]{:S(2)}, u32[]{:S(2)}) %collective-permute-start.12) | collective-permute-done | bytes 245792 | tf_op jit(solution)/shard_map/ppermute | solution.py:33
  73.3 0.1 convert_add_fusion
  73.4 1.8 %collective-permute-start.13 = (bf16[40,768]{1,0:T(8,128)(2,1)S(1)}, bf16[40,768]{1,0:T(8,128)(2,1)S(1)}, u32[]{:S(2)}, u32[]{:S(2)}) collective-permute-start(bf16[40,768]{1,0:T(8,128)(2,1)S(1)} %get-tuple-element.139), channel_id=1, source_target_pairs={{0,2},{1,3},{2,0},{3,1},{16,18},{17,19},{18,16},{19,17},{4,6},{5,7... | collective-permute-start | bytes 184328 | tf_op jit(solution)/shard_map/ppermute | solution.py:78
  75.2 1.5 %collective-permute-start.14 = (bf16[40,768]{1,0:T(8,128)(2,1)S(1)}, bf16[40,768]{1,0:T(8,128)(2,1)S(1)}, u32[]{:S(2)}, u32[]{:S(2)}) collective-permute-start(bf16[40,768]{1,0:T(8,128)(2,1)S(1)} %get-tuple-element.141), channel_id=1, source_target_pairs={{0,16},{1,17},{2,18},{3,19},{16,0},{17,1},{18,2},{19,3},{4,20},{5,... | collective-permute-start | bytes 184328 | tf_op jit(solution)/shard_map/ppermute | solution.py:78
  76.7 0.2 collective-permute-start.15
  77.0 0.7 collective-permute-done.13
  77.7 2.3 %collective-permute-done.14 = bf16[40,768]{1,0:T(8,128)(2,1)S(1)} collective-permute-done((bf16[40,768]{1,0:T(8,128)(2,1)S(1)}, bf16[40,768]{1,0:T(8,128)(2,1)S(1)}, u32[]{:S(2)}, u32[]{:S(2)}) %collective-permute-start.14) | collective-permute-done | bytes 61472 | tf_op jit(solution)/shard_map/ppermute | solution.py:78
  80.0 1.8 %collective-permute-done.15 = bf16[40,768]{1,0:T(8,128)(2,1)S(1)} collective-permute-done((bf16[40,768]{1,0:T(8,128)(2,1)S(1)}, bf16[40,768]{1,0:T(8,128)(2,1)S(1)}, u32[]{:S(2)}, u32[]{:S(2)}) %collective-permute-start.15) | collective-permute-done | bytes 61472 | tf_op jit(solution)/shard_map/ppermute | solution.py:78
  81.9 2.0 %collective-permute-start.16 = (bf16[40,768]{1,0:T(8,128)(2,1)S(1)}, bf16[40,768]{1,0:T(8,128)(2,1)S(1)}, u32[]{:S(2)}, u32[]{:S(2)}) collective-permute-start(bf16[40,768]{1,0:T(8,128)(2,1)S(1)} %fusion.1), channel_id=1, source_target_pairs={{0,4},{4,0},{8,12},{12,8},{1,5},{5,1},{9,13},{13,9},{2,6},{6,2},{1... | collective-permute-start | bytes 184328 | tf_op jit(solution)/shard_map/ppermute | solution.py:33
  83.9 3.2 %collective-permute-start.17 = (bf16[40,768]{1,0:T(8,128)(2,1)S(1)}, bf16[40,768]{1,0:T(8,128)(2,1)S(1)}, u32[]{:S(2)}, u32[]{:S(2)}) collective-permute-start(bf16[40,768]{1,0:T(8,128)(2,1)S(1)} %fusion.1), channel_id=1, source_target_pairs={{0,8},{4,12},{8,0},{12,4},{1,9},{5,13},{9,1},{13,5},{2,10},{6,14},... | collective-permute-start | bytes 184328 | tf_op jit(solution)/shard_map/ppermute | solution.py:33
  87.1 0.0 collective-permute-start.18
  87.1 3.5 %collective-permute-done.17 = bf16[40,768]{1,0:T(8,128)(2,1)S(1)} collective-permute-done((bf16[40,768]{1,0:T(8,128)(2,1)S(1)}, bf16[40,768]{1,0:T(8,128)(2,1)S(1)}, u32[]{:S(2)}, u32[]{:S(2)}) %collective-permute-start.17) | collective-permute-done | bytes 61472 | tf_op jit(solution)/shard_map/ppermute | solution.py:33
  90.7 2.5 %collective-permute-done.18 = bf16[40,768]{1,0:T(8,128)(2,1)S(1)} collective-permute-done((bf16[40,768]{1,0:T(8,128)(2,1)S(1)}, bf16[40,768]{1,0:T(8,128)(2,1)S(1)}, u32[]{:S(2)}, u32[]{:S(2)}) %collective-permute-start.18) | collective-permute-done | bytes 61472 | tf_op jit(solution)/shard_map/ppermute | solution.py:33
  93.2 0.5 slice.80
  93.7 0.6 slice_reduce_fusion
  94.4 0.1 slice_reduce_fusion.1
  94.5 0.3 collective-permute-start.19
  94.8 1.1 %collective-permute-start.20 = (bf16[40,768]{1,0:T(8,128)(2,1)S(1)}, bf16[40,768]{1,0:T(8,128)(2,1)S(1)}, u32[]{:S(2)}, u32[]{:S(2)}) collective-permute-start(bf16[40,768]{1,0:T(8,128)(2,1)S(1)} %add_convert_fusion), channel_id=1, source_target_pairs={{0,16},{1,17},{2,18},{3,19},{16,0},{17,1},{18,2},{19,3},{4,20},{5,... | collective-permute-start | bytes 184328 | tf_op jit(solution)/shard_map/ppermute | solution.py:87
  96.0 2.1 %collective-permute-start.21 = (bf16[40,768]{1,0:T(8,128)(2,1)S(1)}, bf16[40,768]{1,0:T(8,128)(2,1)S(1)}, u32[]{:S(2)}, u32[]{:S(2)}) collective-permute-start(bf16[40,768]{1,0:T(8,128)(2,1)S(1)} %add_convert_fusion), channel_id=1, source_target_pairs={{0,18},{1,19},{2,16},{3,17},{16,2},{17,3},{18,0},{19,1},{4,22},{5,... | collective-permute-start | bytes 184328 | tf_op jit(solution)/shard_map/ppermute | solution.py:87
  98.7 0.1 slice_reduce_fusion.2
  98.9 0.0 collective-permute-done.19
  98.9 0.2 collective-permute-done.20
  99.1 2.0 %collective-permute-done.21 = bf16[40,768]{1,0:T(8,128)(2,1)S(1)} collective-permute-done((bf16[40,768]{1,0:T(8,128)(2,1)S(1)}, bf16[40,768]{1,0:T(8,128)(2,1)S(1)}, u32[]{:S(2)}, u32[]{:S(2)}) %collective-permute-start.21) | collective-permute-done | bytes 61472 | tf_op jit(solution)/shard_map/ppermute | solution.py:87
  101.1 0.1 collective-permute-start.22
  101.2 1.9 %multiply_add_fusion = f32[10,256,256]{2,1,0:T(8,128)} fusion(f32[256,256]{1,0:T(8,128)S(1)} %slice.71, f32[10]{0:T(128)S(1)} %slice_reduce_fusion.1, f32[256,256]{1,0:T(8,128)S(1)} %slice.69, f32[10]{0:T(128)S(1)} %slice_reduce_fusion.2), kind=kLoop, calls=%fused_computation | loop fusion | flops 1966080 | bytes 3145808 | tf_op jit(solution)/shard_map/add | solution.py:42
  103.1 0.0 collective-permute-done.22.other
  103.1 1.0 finish.1
  (32 shorter events, 0.4 us)
Async XLA Ops:
  1.7 14.3 %collective-permute-start = (bf16[16,3,768]{2,1,0:T(4,128)(2,1)S(1)}, bf16[16,3,768]{2,1,0:T(4,128)(2,1)S(1)}, u32[]{:S(2)}, u32[]{:S(2)}) collective-permute-start(bf16[16,3,768]{2,1,0:T(4,128)(2,1)S(1)} %get-tuple-element.138), channel_id=1, source_target_pairs={{0,1},{1,2},{2,3},{4,5},{5,6},{6,7},{8,9},{9,10},{10,11},{12,13},{... | collective-permute-start | bytes 221192 | tf_op jit(solution)/shard_map/ppermute | solution.py:103
  4.1 12.0 %collective-permute-start.1 = (bf16[16,3,768]{2,1,0:T(4,128)(2,1)S(1)}, bf16[16,3,768]{2,1,0:T(4,128)(2,1)S(1)}, u32[]{:S(2)}, u32[]{:S(2)}) collective-permute-start(bf16[16,3,768]{2,1,0:T(4,128)(2,1)S(1)} %get-tuple-element.137), channel_id=1, source_target_pairs={{1,0},{2,1},{3,2},{5,4},{6,5},{7,6},{9,8},{10,9},{11,10},{13,12},{... | collective-permute-start | bytes 221192 | tf_op jit(solution)/shard_map/ppermute | solution.py:107
  6.5 20.2 %collective-permute-start.2 = (bf16[3,64,768]{2,1,0:T(8,128)(2,1)S(1)}, bf16[3,64,768]{2,1,0:T(8,128)(2,1)S(1)}, u32[]{:S(2)}, u32[]{:S(2)}) collective-permute-start(bf16[3,64,768]{2,1,0:T(8,128)(2,1)S(1)} %get-tuple-element.136), channel_id=1, source_target_pairs={{0,4},{4,8},{8,12},{1,5},{5,9},{9,13},{2,6},{6,10},{10,14},{3,7},{... | collective-permute-start | bytes 884744 | tf_op jit(solution)/shard_map/ppermute | solution.py:103
  10.8 15.9 %collective-permute-start.3 = (bf16[3,64,768]{2,1,0:T(8,128)(2,1)S(1)}, bf16[3,64,768]{2,1,0:T(8,128)(2,1)S(1)}, u32[]{:S(2)}, u32[]{:S(2)}) collective-permute-start(bf16[3,64,768]{2,1,0:T(8,128)(2,1)S(1)} %get-tuple-element.135), channel_id=1, source_target_pairs={{4,0},{8,4},{12,8},{5,1},{9,5},{13,9},{6,2},{10,6},{14,10},{7,3},{... | collective-permute-start | bytes 884744 | tf_op jit(solution)/shard_map/ppermute | solution.py:107
  12.1 1.4 %copy-start = (bf16[1,16,64,768]{3,2,1,0:T(8,128)(2,1)S(1)}, bf16[1,16,64,768]{3,2,1,0:T(8,128)(2,1)}, u32[]{:S(2)}) copy-start(bf16[1,16,64,768]{3,2,1,0:T(8,128)(2,1)} %param.8) | copy-start | bytes 4718596
  13.6 0.9 copy-start.3
  14.5 1.6 %copy-start.6 = (f32[768]{0:T(1024)S(1)}, f32[768]{0:T(1024)}, u32[]{:S(2)}) copy-start(f32[768]{0:T(1024)} %param.10) | copy-start | bytes 9220
  14.5 7.6 %copy-start.2 = (bf16[768,256]{1,0:T(8,128)(2,1)S(1)}, bf16[768,256]{1,0:T(8,128)(2,1)}, u32[]{:S(2)}) copy-start(bf16[768,256]{1,0:T(8,128)(2,1)} %reduce_weight.5) | copy-start | bytes 1179652
  14.5 7.6 %copy-start.4 = (f32[256]{0:T(256)S(1)}, f32[256]{0:T(256)}, u32[]{:S(2)}) copy-start(f32[256]{0:T(256)} %param.12) | copy-start | bytes 3076
  16.2 10.5 %collective-permute-start.4 = (bf16[2,3,3,768]{3,2,1,0:T(4,128)(2,1)S(1)}, bf16[2,3,3,768]{3,2,1,0:T(4,128)(2,1)S(1)}, u32[]{:S(2)}, u32[]{:S(2)}) collective-permute-start(bf16[2,3,3,768]{3,2,1,0:T(4,128)(2,1)S(1)} %pad_maximum_fusion), channel_id=1, source_target_pairs={{0,4},{4,8},{8,12},{1,5},{5,9},{9,13},{2,6},{6,10},{10,14},{3,7},{... | collective-permute-start | bytes 82952 | tf_op jit(solution)/shard_map/ppermute | solution.py:103
  20.8 5.9 %collective-permute-start.5 = (bf16[2,3,3,768]{3,2,1,0:T(4,128)(2,1)S(1)}, bf16[2,3,3,768]{3,2,1,0:T(4,128)(2,1)S(1)}, u32[]{:S(2)}, u32[]{:S(2)}) collective-permute-start(bf16[2,3,3,768]{3,2,1,0:T(4,128)(2,1)S(1)} %pad_maximum_fusion.1), channel_id=1, source_target_pairs={{4,0},{8,4},{12,8},{5,1},{9,5},{13,9},{6,2},{10,6},{14,10},{7,3},{... | collective-permute-start | bytes 82952 | tf_op jit(solution)/shard_map/ppermute | solution.py:107
  31.9 19.9 %copy-start.1 = (bf16[10,256,256]{2,1,0:T(8,128)(2,1)S(1)}, bf16[10,256,256]{2,1,0:T(8,128)(2,1)}, u32[]{:S(2)}) copy-start(bf16[10,256,256]{2,1,0:T(8,128)(2,1)} %class_weight.1) | copy-start | bytes 3932164
  31.9 19.9 %copy-start.5 = (f32[10]{0:T(128)S(1)}, f32[10]{0:T(128)}, u32[]{:S(2)}) copy-start(f32[10]{0:T(128)} %class_bias.1) | copy-start | bytes 124
  31.9 2.6 %collective-permute-start.6 = (f32[72,256]{1,0:T(8,128)S(1)}, f32[72,256]{1,0:T(8,128)S(1)}, u32[]{:S(2)}, u32[]{:S(2)}) collective-permute-start(f32[72,256]{1,0:T(8,128)S(1)} %get-tuple-element.92), channel_id=1, source_target_pairs={{0,1},{1,0},{2,3},{3,2},{4,5},{5,4},{6,7},{7,6},{8,9},{9,8},{10,11... | collective-permute-start | bytes 221192 | tf_op jit(solution)/shard_map/ppermute | solution.py:33
  34.5 5.5 %collective-permute-start.7 = (f32[72,256]{1,0:T(8,128)S(1)}, f32[72,256]{1,0:T(8,128)S(1)}, u32[]{:S(2)}, u32[]{:S(2)}) collective-permute-start(f32[72,256]{1,0:T(8,128)S(1)} %add.44), channel_id=1, source_target_pairs={{0,2},{1,3},{2,0},{3,1},{4,6},{5,7},{6,4},{7,5},{8,10},{9,11},{10,... | collective-permute-start | bytes 221192 | tf_op jit(solution)/shard_map/ppermute | solution.py:33
  40.0 5.0 %collective-permute-start.8 = (f32[72,256]{1,0:T(8,128)S(1)}, f32[72,256]{1,0:T(8,128)S(1)}, u32[]{:S(2)}, u32[]{:S(2)}) collective-permute-start(f32[72,256]{1,0:T(8,128)S(1)} %add.45), channel_id=1, source_target_pairs={{0,4},{4,0},{8,12},{12,8},{1,5},{5,1},{9,13},{13,9},{2,6},{6,2},{1... | collective-permute-start | bytes 221192 | tf_op jit(solution)/shard_map/ppermute | solution.py:33
  45.0 5.4 %collective-permute-start.9 = (f32[72,256]{1,0:T(8,128)S(1)}, f32[72,256]{1,0:T(8,128)S(1)}, u32[]{:S(2)}, u32[]{:S(2)}) collective-permute-start(f32[72,256]{1,0:T(8,128)S(1)} %add.46), channel_id=1, source_target_pairs={{0,8},{4,12},{8,0},{12,4},{1,9},{5,13},{9,1},{13,5},{2,10},{6,14},... | collective-permute-start | bytes 221192 | tf_op jit(solution)/shard_map/ppermute | solution.py:33
  50.5 1.3 %collective-permute-start.10 = (f32[72,256]{1,0:T(8,128)S(1)}, f32[72,256]{1,0:T(8,128)S(1)}, u32[]{:S(2)}, u32[]{:S(2)}) collective-permute-start(f32[72,256]{1,0:T(8,128)S(1)} %add.47.own), channel_id=1, source_target_pairs={{0,1},{1,0},{2,3},{3,2},{4,5},{5,4},{6,7},{7,6},{8,9},{9,8},{10,11... | collective-permute-start | bytes 221192 | tf_op jit(solution)/shard_map/ppermute | solution.py:33
  61.6 8.8 %collective-permute-start.11 = (f32[272,256]{1,0:T(8,128)S(1)}, f32[272,256]{1,0:T(8,128)S(1)}, u32[]{:S(2)}, u32[]{:S(2)}) collective-permute-start(f32[272,256]{1,0:T(8,128)S(1)} %get-tuple-element.125), channel_id=1, source_target_pairs={{0,16},{16,0},{1,17},{17,1},{2,18},{18,2},{3,19},{19,3},{4,20},{20... | collective-permute-start | bytes 835592 | tf_op jit(solution)/shard_map/ppermute | solution.py:33
  71.7 1.6 %collective-permute-start.12 = (bf16[160,768]{1,0:T(8,128)(2,1)S(1)}, bf16[160,768]{1,0:T(8,128)(2,1)S(1)}, u32[]{:S(2)}, u32[]{:S(2)}) collective-permute-start(bf16[160,768]{1,0:T(8,128)(2,1)S(1)} %select_convert_fusion), channel_id=1, source_target_pairs={{0,1},{1,0},{2,3},{3,2},{4,5},{5,4},{6,7},{7,6},{8,9},{9,8},{10,11... | collective-permute-start | bytes 737288 | tf_op jit(solution)/shard_map/ppermute | solution.py:33
  73.4 4.3 %collective-permute-start.13 = (bf16[40,768]{1,0:T(8,128)(2,1)S(1)}, bf16[40,768]{1,0:T(8,128)(2,1)S(1)}, u32[]{:S(2)}, u32[]{:S(2)}) collective-permute-start(bf16[40,768]{1,0:T(8,128)(2,1)S(1)} %get-tuple-element.139), channel_id=1, source_target_pairs={{0,2},{1,3},{2,0},{3,1},{16,18},{17,19},{18,16},{19,17},{4,6},{5,7... | collective-permute-start | bytes 184328 | tf_op jit(solution)/shard_map/ppermute | solution.py:78
  75.2 4.8 %collective-permute-start.14 = (bf16[40,768]{1,0:T(8,128)(2,1)S(1)}, bf16[40,768]{1,0:T(8,128)(2,1)S(1)}, u32[]{:S(2)}, u32[]{:S(2)}) collective-permute-start(bf16[40,768]{1,0:T(8,128)(2,1)S(1)} %get-tuple-element.141), channel_id=1, source_target_pairs={{0,16},{1,17},{2,18},{3,19},{16,0},{17,1},{18,2},{19,3},{4,20},{5,... | collective-permute-start | bytes 184328 | tf_op jit(solution)/shard_map/ppermute | solution.py:78
  76.7 5.1 %collective-permute-start.15 = (bf16[40,768]{1,0:T(8,128)(2,1)S(1)}, bf16[40,768]{1,0:T(8,128)(2,1)S(1)}, u32[]{:S(2)}, u32[]{:S(2)}) collective-permute-start(bf16[40,768]{1,0:T(8,128)(2,1)S(1)} %get-tuple-element.140), channel_id=1, source_target_pairs={{0,18},{1,19},{2,16},{3,17},{16,2},{17,3},{18,0},{19,1},{4,22},{5,... | collective-permute-start | bytes 184328 | tf_op jit(solution)/shard_map/ppermute | solution.py:78
  81.9 5.3 %collective-permute-start.16 = (bf16[40,768]{1,0:T(8,128)(2,1)S(1)}, bf16[40,768]{1,0:T(8,128)(2,1)S(1)}, u32[]{:S(2)}, u32[]{:S(2)}) collective-permute-start(bf16[40,768]{1,0:T(8,128)(2,1)S(1)} %fusion.1), channel_id=1, source_target_pairs={{0,4},{4,0},{8,12},{12,8},{1,5},{5,1},{9,13},{13,9},{2,6},{6,2},{1... | collective-permute-start | bytes 184328 | tf_op jit(solution)/shard_map/ppermute | solution.py:33
  83.9 6.8 %collective-permute-start.17 = (bf16[40,768]{1,0:T(8,128)(2,1)S(1)}, bf16[40,768]{1,0:T(8,128)(2,1)S(1)}, u32[]{:S(2)}, u32[]{:S(2)}) collective-permute-start(bf16[40,768]{1,0:T(8,128)(2,1)S(1)} %fusion.1), channel_id=1, source_target_pairs={{0,8},{4,12},{8,0},{12,4},{1,9},{5,13},{9,1},{13,5},{2,10},{6,14},... | collective-permute-start | bytes 184328 | tf_op jit(solution)/shard_map/ppermute | solution.py:33
  87.1 6.0 %collective-permute-start.18 = (bf16[40,768]{1,0:T(8,128)(2,1)S(1)}, bf16[40,768]{1,0:T(8,128)(2,1)S(1)}, u32[]{:S(2)}, u32[]{:S(2)}) collective-permute-start(bf16[40,768]{1,0:T(8,128)(2,1)S(1)} %fusion.1), channel_id=1, source_target_pairs={{0,12},{4,8},{8,4},{12,0},{1,13},{5,9},{9,5},{13,1},{2,14},{6,10},... | collective-permute-start | bytes 184328 | tf_op jit(solution)/shard_map/ppermute | solution.py:33
  94.5 4.4 %collective-permute-start.19 = (bf16[40,768]{1,0:T(8,128)(2,1)S(1)}, bf16[40,768]{1,0:T(8,128)(2,1)S(1)}, u32[]{:S(2)}, u32[]{:S(2)}) collective-permute-start(bf16[40,768]{1,0:T(8,128)(2,1)S(1)} %add_convert_fusion), channel_id=1, source_target_pairs={{0,2},{1,3},{2,0},{3,1},{16,18},{17,19},{18,16},{19,17},{4,6},{5,7... | collective-permute-start | bytes 184328 | tf_op jit(solution)/shard_map/ppermute | solution.py:87
  94.8 4.2 %collective-permute-start.20 = (bf16[40,768]{1,0:T(8,128)(2,1)S(1)}, bf16[40,768]{1,0:T(8,128)(2,1)S(1)}, u32[]{:S(2)}, u32[]{:S(2)}) collective-permute-start(bf16[40,768]{1,0:T(8,128)(2,1)S(1)} %add_convert_fusion), channel_id=1, source_target_pairs={{0,16},{1,17},{2,18},{3,19},{16,0},{17,1},{18,2},{19,3},{4,20},{5,... | collective-permute-start | bytes 184328 | tf_op jit(solution)/shard_map/ppermute | solution.py:87
  96.0 5.1 %collective-permute-start.21 = (bf16[40,768]{1,0:T(8,128)(2,1)S(1)}, bf16[40,768]{1,0:T(8,128)(2,1)S(1)}, u32[]{:S(2)}, u32[]{:S(2)}) collective-permute-start(bf16[40,768]{1,0:T(8,128)(2,1)S(1)} %add_convert_fusion), channel_id=1, source_target_pairs={{0,18},{1,19},{2,16},{3,17},{16,2},{17,3},{18,0},{19,1},{4,22},{5,... | collective-permute-start | bytes 184328 | tf_op jit(solution)/shard_map/ppermute | solution.py:87
  101.1 1.9 %collective-permute-start.22 = (bf16[160,768]{1,0:T(8,128)(2,1)S(1)}, bf16[160,768]{1,0:T(8,128)(2,1)S(1)}, u32[]{:S(2)}, u32[]{:S(2)}) collective-permute-start(bf16[160,768]{1,0:T(8,128)(2,1)S(1)} %bitcast.37), channel_id=1, source_target_pairs={{0,1},{1,0},{2,3},{3,2},{4,5},{5,4},{6,7},{7,6},{8,9},{9,8},{10,11... | collective-permute-start | bytes 737288 | tf_op jit(solution)/shard_map/ppermute | solution.py:33

commit v10 on v8

--- a/solution.py
+++ b/solution.py
@@ -141,7 +141,7 @@
     return even, odd, both
 
 
-def spread_weights(weight_ref, filters, lanes):
+def spread_weights(weight_ref, filters, tile, lanes):
     rows = []
     for row_tap in range(KERNEL):
         row = [weight_ref[row_tap, tap : tap + 1, lanes] for tap in range(KERNEL)]
@@ -153,7 +153,7 @@
             for col_part, taps in enumerate(part_taps(line)):
                 start = FILTERS[row_part, col_part] + row * PARTS[col_part]
                 for col, value in enumerate(taps):
-                    filters[start + col] = value
+                    filters[tile, start + col] = value
 
 
 def fill_parts(load, parts, row_pairs, groups):
@@ -176,7 +176,7 @@
     return line
 
 
-def conv_rows(load, filters, bias, steps, count, parts, products):
+def conv_rows(load, filters, tile, bias, steps, count, parts, products):
     row_pairs, col_pairs = count // 2, steps // 2
     fill_parts(load, parts, row_pairs + 3, 2 * col_pairs + 6)
     for row_part in range(3):
@@ -193,7 +193,7 @@
                     if not 0 <= tap_row < many_rows:
                         continue
                     for tap_col in range(many_cols):
-                        scale = filters[start + tap_row * many_cols + tap_col]
+                        scale = filters[tile, start + tap_row * many_cols + tap_col]
                         for col in range(col_pairs):
                             term = line[col + tap_col] * scale
                             old = total[row][col]
@@ -218,7 +218,6 @@
 def parts_scratch(count, steps):
     row_pairs, col_pairs = count // 2, steps // 2
     return [
-        pltpu.VMEM((PRODUCTS, GROUPS, LANES), wide),
         pltpu.VMEM((2, row_pairs + 3, 2 * col_pairs + 6, GROUPS, LANES), wide),
         pltpu.VMEM((9, row_pairs, col_pairs, GROUPS, LANES), wide),
     ]
@@ -236,15 +235,15 @@
 
 def inner_kernel(
     block, left, right, weight, bias, reduce_weight, reduce_bias,
-    spread_out, conv_out, before_out, feat_out, gram_out, colsum_out,
-    wide_row, filters, parts, products,
+    spread_out, filters, conv_out, before_out, feat_out, gram_out, colsum_out,
+    wide_row, parts, products,
 ):
     rows, cols = block.shape[0], block.shape[1]
     steps = cols // GROUPS
 
     def one_tile(tile, _):
         lanes = lanes_of(tile)
-        spread_weights(weight, filters, lanes)
+        spread_weights(weight, filters, tile, lanes)
         start_value = jnp.broadcast_to(bias[0:1, lanes], (GROUPS, LANES))
 
         def fill(turn, _):
@@ -261,7 +260,7 @@
             return spread_out[tile, row + SIDE - HALF, group]
 
         conv_out[:, lanes] = conv_rows(
-            load, filters, start_value, steps, rows - 2 * SIDE, parts, products
+            load, filters, tile, start_value, steps, rows - 2 * SIDE, parts, products
         )
         return 0
 
@@ -272,24 +271,29 @@
 
 
 def edge_kernel(
-    flag, spread_in, top, bottom, weight, bias, reduce_weight, reduce_bias, gram_in, colsum_in,
+    flag, spread_in, top, bottom, filters, bias, reduce_weight,
+    reduce_bias, gram_in, colsum_in,
     spread_top, spread_bottom, conv_out, before_out, feat_out, kept_out, sent_out,
-    wide_row, corners, filters, parts, products, sums,
+    wide_row, stage, parts, products, sums,
 ):
     rows, cols = spread_in.shape[1], wide_row.shape[1] - 2 * EDGE
     steps = cols // GROUPS
 
     def one_tile(tile, _):
         lanes = lanes_of(tile)
-        spread_weights(weight, filters, lanes)
         start_value = jnp.broadcast_to(bias[0:1, lanes], (GROUPS, LANES))
         for side, (strip, spread) in enumerate(((top, spread_top), (bottom, spread_bottom))):
-            corners[side] = strip[HALF * cols :, lanes].astype(wide)
+            stage[side] = strip[:, lanes].astype(wide)
             for row in range(HALF):
                 place = wide_row.at[side * HALF + row]
-                left = corners[side, row * HALF : (row + 1) * HALF, :]
-                right = corners[side, (HALF + row) * HALF : (HALF + row + 1) * HALF, :]
-                fill_row(place, strip[row * cols : (row + 1) * cols, lanes], left, right)
+                left = HALF * cols + row * HALF
+                right = left + HALF * HALF
+                fill_row(
+                    place,
+                    stage[side, row * cols : (row + 1) * cols, :],
+                    stage[side, left : left + HALF, :],
+                    stage[side, right : right + HALF, :],
+                )
                 spread_columns(place, spread.at[tile, row])
 
         def load_from(row):
@@ -306,7 +310,8 @@
         for side, row in enumerate((0, rows - SIDE)):
             start = side * SIDE * cols
             conv_out[start : start + SIDE * cols, lanes] = conv_rows(
-                load_from(row), filters, start_value, steps, SIDE, parts.at[side], products.at[side]
+                load_from(row), filters, tile, start_value, steps, SIDE,
+                parts.at[side], products.at[side],
             )
         return 0
 
@@ -314,15 +319,16 @@
     gram, colsum = reduce_part(conv_out, reduce_weight, reduce_bias, before_out, feat_out)
     gram = gram + gram_in[...]
     colsum = colsum + colsum_in[...]
-    width = gram.shape[0]
-    half = width // 2
-    quarter = half // 2
-    sums[:half, :] = gram[:half, :]
-    sums[half : half + quarter, :half] = gram[half : half + quarter, half:]
-    sums[half : half + quarter, half:] = gram[half + quarter :, half:]
-    sums[half + quarter :, :] = jnp.broadcast_to(
-        colsum, (sums.shape[0] - half - quarter, width)
-    )
+    half = gram.shape[0] // 2
+    row = lax.broadcasted_iota(jnp.int32, (half, half), 0)
+    col = lax.broadcasted_iota(jnp.int32, (half, half), 1)
+    last_block = gram[half:, half:]
+    diagonal = jnp.sum(jnp.where(row == col, last_block, 0.0), axis=0, keepdims=True)
+    sums[:half, :half] = gram[:half, half:]
+    sums[:half, half:] = jnp.where(row <= col, gram[:half, :half], last_block)
+    sums[half : half + GROUPS, :] = jnp.broadcast_to(colsum, (GROUPS, 2 * half))
+    sums[half + GROUPS :, :half] = jnp.broadcast_to(diagonal, (GROUPS, half))
+    sums[half + GROUPS :, half:] = jnp.zeros((GROUPS, half), wide)
     part = kept_out.shape[0]
     keep_or_send(flag[0] != 0, sums[:part, :], sums[part:, :], kept_out, sent_out)
 
@@ -359,9 +365,10 @@
     return pl.pallas_call(
         inner_kernel,
         in_specs=[in_vmem] * 7,
-        out_specs=[in_vmem] * 6,
+        out_specs=[in_vmem] * 7,
         out_shape=[
             shape_of((tiles, rows, steps + KERNEL - 1, GROUPS, LANES)),
+            shape_of((tiles, PRODUCTS, GROUPS, LANES)),
             shape_of((pixels, channels), narrow),
             shape_of((pixels, width)),
             shape_of((pixels, width), narrow),
@@ -378,14 +385,14 @@
     )(block, left, right, weight, bias, reduce_weight, reduce_bias)
 
 
-def conv_edge(flag, spread, top, bottom, weight, bias, reduce_weight, reduce_bias, gram, colsum):
+def conv_edge(flag, spread, halos, filters, bias, reduce_weight, reduce_bias, gram, colsum):
     tiles, rows, groups = spread.shape[:3]
-    cols, channels = (groups - KERNEL + 1) * GROUPS, top.shape[1]
-    width = reduce_weight.shape[1]
+    cols = (groups - KERNEL + 1) * GROUPS
+    channels, width = reduce_weight.shape
     pixels = 2 * SIDE * cols
-    filters, parts, products = parts_scratch(SIDE, cols // GROUPS)
+    parts, products = parts_scratch(SIDE, cols // GROUPS)
     side = (tiles, HALF, groups, GROUPS, LANES)
-    sums_rows = 3 * width // 4 + 2 * GROUPS
+    sums_rows = width // 2 + 2 * GROUPS
     return pl.pallas_call(
         edge_kernel,
         in_specs=[in_smem] + [in_vmem] * 9,
@@ -401,8 +408,7 @@
         ],
         scratch_shapes=[
             pltpu.VMEM((2 * HALF, cols + 2 * EDGE, LANES), wide),
-            pltpu.VMEM((2, top.shape[0] - HALF * cols, LANES), wide),
-            filters,
+            pltpu.VMEM((2,) + (halos[0].shape[0], LANES), wide),
             pltpu.VMEM((2,) + parts.shape, wide),
             pltpu.VMEM((2,) + products.shape, wide),
             pltpu.VMEM((sums_rows, width), wide),
@@ -410,7 +416,7 @@
         compiler_params=params(24),
         cost_estimate=cost(6),
         name="conv_edge",
-    )(flag, spread, top, bottom, weight, bias, reduce_weight, reduce_bias, gram, colsum)
+    )(flag, spread, *halos, filters, bias, reduce_weight, reduce_bias, gram, colsum)
 
 
 def split(value):
@@ -473,20 +479,26 @@
 ):
     width = root_out.shape[1]
     half = width // 2
-    quarter = half // 2
     rows = own.shape[0]
     upper = flag[0] != 0
     mine, theirs = own[...], other[...]
     sums[:rows, :] = jnp.where(upper, theirs, mine)
     sums[rows:, :] = jnp.where(upper, mine, theirs)
-    low = jnp.concatenate(
-        [sums[half : half + quarter, :half], sums[half : half + quarter, half:]], axis=0
-    )
-    cross = sums[:half, half:]
+    row = lax.broadcasted_iota(jnp.int32, (half, half), 0)
+    col = lax.broadcasted_iota(jnp.int32, (half, half), 1)
+    cross, mixed = sums[:half, :half], sums[:half, half:]
+    turned = mixed.T
+    first = jnp.where(row <= col, mixed, turned)
+    diagonal = jnp.broadcast_to(sums[half + GROUPS : half + GROUPS + 1, :half], (half, half))
+    last = jnp.where(row == col, diagonal, jnp.where(row > col, mixed, turned))
     gram = jnp.concatenate(
-        [sums[:half, :], jnp.concatenate([cross.T, low], axis=1)], axis=0
-    )
-    mean_row = sums[half + quarter : half + quarter + 1, :] / count
+        [
+            jnp.concatenate([first, cross], axis=1),
+            jnp.concatenate([cross.T, last], axis=1),
+        ],
+        axis=0,
+    )
+    mean_row = sums[half : half + 1, :] / count
     mean_col = jnp.broadcast_to(mean_row, (width, width)).T
     sigma = gram / count - mean_col * mean_row
     row = lax.broadcasted_iota(jnp.int32, (width, width), 0)
@@ -519,6 +531,11 @@
     root_out[width:, :] = jnp.broadcast_to(
         jnp.where(place == classes, loss_part, logit_grad), (slots, width)
     )
+    across = lax.broadcasted_iota(jnp.int32, (slots, width), 1)
+    facts = jnp.where(place == classes, loss_part, logit_grad)
+    root_out[width + slots - 1 :, :] = jnp.sum(
+        jnp.where(across == place, facts, 0.0), axis=0, keepdims=True
+    )
 
     root_grad = jnp.zeros((width, width), wide)
     for index in range(classes):
@@ -557,7 +574,7 @@
     feat_inner, feat_edge, gate_inner, gate_edge, conv_turned, reduce_turned = prepared
     width, channels = reduce_turned.shape
     inner, edge = feat_inner.shape[0], feat_edge.shape[0]
-    slots = -(-(class_weight.shape[0] + 1) // GROUPS) * GROUPS
+    slots = -(-(class_weight.shape[0] + 2) // GROUPS) * GROUPS
     return pl.pallas_call(
         functools.partial(head_kernel, count=count, image_count=image_count),
         in_specs=[in_smem] * 3 + [in_vmem] * 9,
@@ -721,9 +738,9 @@
     )(*spreads, *grads, payload)
 
 
-def finish_kernel(
-    flag, own, other, weight_out, depth_out, depth_bias_out, bias_out, payload,
-):
+def finish_kernel(flag, own, other, *refs, image_count):
+    known = refs[:-7]
+    weight_out, depth_out, depth_bias_out, bias_out, class_bias_out, loss_out, payload = refs[-7:]
     part = own.shape[0]
     upper = flag[0] != 0
     mine, theirs = own[...].astype(wide), other[...].astype(wide)
@@ -738,32 +755,37 @@
     taps = KERNEL * KERNEL
     depth_bias_out[...] = payload[width + taps, :]
     bias_out[...] = payload[width + taps + 1, :width]
-
-
-def finish(flag, own, other, width):
+    totals = tree_sum([part[part.shape[0] - 1 :, :] for part in known])
+    classes = class_bias_out.shape[0]
+    class_bias_out[...] = totals[0, :classes]
+    across = lax.broadcasted_iota(jnp.int32, totals.shape, 1)
+    loss_out[0] = jnp.sum(jnp.where(across == classes, totals, 0.0)) / image_count
+
+
+def finish(flag, own, other, known, width, classes, image_count):
     part, channels = own.shape
     return pl.pallas_call(
-        finish_kernel,
-        in_specs=[in_smem] + [in_vmem] * 2,
-        out_specs=[in_vmem] * 4,
+        functools.partial(finish_kernel, image_count=image_count),
+        in_specs=[in_smem] + [in_vmem] * (2 + len(known)),
+        out_specs=[in_vmem] * 5 + [in_smem],
         out_shape=[
             shape_of((channels, width)),
             shape_of((KERNEL, KERNEL, channels)),
             shape_of((channels,)),
             shape_of((width,)),
+            shape_of((classes,)),
+            shape_of((1,)),
         ],
         scratch_shapes=[pltpu.VMEM((2 * part, channels), wide)],
         compiler_params=params(8),
         cost_estimate=cost(1),
         name="finish",
-    )(flag, own, other)
+    )(flag, own, other, *known)
 
 
 def edge_strip(block, left, right, rows):
     channels = block.shape[2]
-    parts = [part[rows].reshape(-1, channels) for part in (block, left, right)]
-    short = -(2 * HALF * HALF) % 16
-    return jnp.concatenate(parts + [jnp.zeros((short, channels), block.dtype)])
+    return jnp.concatenate([part[rows].reshape(-1, channels) for part in (block, left, right)])
 
 
 def body(
@@ -800,11 +822,11 @@
     )
     top = next_along(low, "sy")
     bottom = back_along(high, "sy")
-    spread, conv_in, before_in, feat_in, gram, colsum = conv_inner(
+    spread, filters, conv_in, before_in, feat_in, gram, colsum = conv_inner(
         block, left, right, depth_weight, bias_row, reduce_weight, reduce_row
     )
     spread_top, spread_bottom, conv_ed, before_ed, feat_ed, kept, sent = conv_edge(
-        flag, spread, top, bottom, depth_weight, bias_row, reduce_weight, reduce_row, gram, colsum
+        flag, spread, (top, bottom), filters, bias_row, reduce_weight, reduce_row, gram, colsum
     )
 
     sums = kept + swap(sent, "sx", 1)
@@ -855,16 +877,13 @@
     class_weight_grad = tree_sum(
         [part[width : width + classes, 0][:, None, None] * part[None, :width] for part in known]
     )
-    totals = tree_sum([part[width:, 0] for part in known])
-    class_bias_grad = totals[:classes]
-    loss = totals[classes] / image_count
     payload = square_gather(payload, axes, pairs, places)
-    other, class_weight_grad, class_bias_grad, loss = together(
-        (swap(payload, "sx", 1), class_weight_grad, class_bias_grad, loss)
-    )
-    weight_grad, depth_grad, depth_bias_grad, bias_grad = finish(flag, payload, other, width)
+    other, class_weight_grad = together((swap(payload, "sx", 1), class_weight_grad))
+    weight_grad, depth_grad, depth_bias_grad, bias_grad, class_bias_grad, loss = finish(
+        flag, payload, other, known, width, classes, image_count
+    )
     return (
-        loss,
+        loss[0],
         depth_grad,
         depth_bias_grad,
         weight_grad,

time: 101 us -> 97.9 us (0.969)
  between operations: 3.37 us -> 1.74 us
  local copies, waits for them, and re-layouts: 4.65 us -> 3.54 us
    ppermute x3, waiting for transfers between devices: 1.82 us -> 3.43 us  [square_gather(): part = lax.ppermute(value, axes, pairs[turn]) if turn else value]
    ppermute x11, waiting for transfers between devices: 19.1 us -> 17.8 us  [swap(): return lax.ppermute(value, axis, [(i, i ^ shift) for i in range(count)])]
    slice x5 -> x3, local copies, waits for them, and re-layouts: 2.26 us -> 1.12 us  [edge_strip(): part[rows].reshape(-1, channels)]
  transfers between devices with their start and end apart: 21 -> 21, of which waited for: 16 -> 18; matrix products, arithmetic and copies ran while one was open for 5% -> 4% of each run, Pallas kernels for 14% -> 15%
where the time goes in v10:
time: 97.9 us; the launch traced here: 97.5 us
  Pallas kernels  31.7 us (32%)
  waiting for transfers between devices  29.5 us (30%)
  starting transfers between devices  28.9 us (30%)
  local copies, waits for them, and re-layouts  3.54 us (4%)
  other arithmetic  2.14 us (2%)
  between operations  1.74 us (2%)
    ppermute x11, waiting for transfers between devices, swap(): return lax.ppermute(value, axis, [(i, i ^ shift) for i in range(count)])  17.8 us
    ppermute x11, starting transfers between devices, swap(): return lax.ppermute(value, axis, [(i, i ^ shift) for i in range(count)])  13.3 us
    pallas_call x1, Pallas kernels, head(): pl.pallas_call(functools.partial(head_kernel, count=count, image_count=im...  9.77 us
    pallas_call x2, Pallas kernels, tap_grads(): pl.pallas_call(functools.partial(taps_kernel, first=first, last=last), in...  8.04 us
    pallas_call x1, Pallas kernels, conv_inner(): pl.pallas_call(inner_kernel, in_specs=[in_vmem] * 7, out_specs=[in_vmem]...  6.79 us
    ppermute x2, starting transfers between devices, next_along(): lax.ppermute(value, axis, [(i, i + 1) for i in range(lax.axis_size(axis)...  5.86 us
    pallas_call x1, Pallas kernels, conv_edge(): pl.pallas_call(edge_kernel, in_specs=[in_smem] + [in_vmem] * 9, out_specs...  5.16 us
    ppermute x2, waiting for transfers between devices, back_along(): lax.ppermute(value, axis, [(i + 1, i) for i in range(lax.axis_size(axis)...  4.54 us
  transfers between devices with their start and end apart: 21, of which 18 were waited for; matrix products, arithmetic and copies ran while one was open for 4% of the time, Pallas kernels for 15%

profile of v10, /device:TPU:0, one launch (start us, length us, event | category | flops | bytes accessed | tf_op | source)
XLA Modules:
  0.0 97.5 jit_solution(2051886384362303262)
XLA Ops:
  0.6 0.0 copy-start
  0.6 0.0 copy-start.4
  0.7 0.0 copy-start.2
  0.7 0.0 copy-start.3
  0.7 1.2 %fusion.6 = (bf16[16,3,768]{2,1,0:T(4,128)(2,1)S(1)}, bf16[16,3,768]{2,1,0:T(4,128)(2,1)S(1)}) fusion(bf16[16,64,768]{2,1,0:T(8,128)(2,1)} %bitcast.28), kind=kLoop, calls=%fused_computation.22 | loop fusion | bytes 294912 | tf_op jit(solution)/shard_map/slice | solution.py:808
  1.9 2.4 %collective-permute-start = (bf16[16,3,768]{2,1,0:T(4,128)(2,1)S(1)}, bf16[16,3,768]{2,1,0:T(4,128)(2,1)S(1)}, u32[]{:S(2)}, u32[]{:S(2)}) collective-permute-start(bf16[16,3,768]{2,1,0:T(4,128)(2,1)S(1)} %get-tuple-element.125), channel_id=1, source_target_pairs={{0,1},{1,2},{2,3},{4,5},{5,6},{6,7},{8,9},{9,10},{10,11},{12,13},{... | collective-permute-start | bytes 221192 | tf_op jit(solution)/shard_map/ppermute | solution.py:103
  4.3 1.3 %collective-permute-start.1 = (bf16[16,3,768]{2,1,0:T(4,128)(2,1)S(1)}, bf16[16,3,768]{2,1,0:T(4,128)(2,1)S(1)}, u32[]{:S(2)}, u32[]{:S(2)}) collective-permute-start(bf16[16,3,768]{2,1,0:T(4,128)(2,1)S(1)} %get-tuple-element.126), channel_id=1, source_target_pairs={{1,0},{2,1},{3,2},{5,4},{6,5},{7,6},{9,8},{10,9},{11,10},{13,12},{... | collective-permute-start | bytes 221192 | tf_op jit(solution)/shard_map/ppermute | solution.py:107
  5.6 1.1 %fusion.5 = (bf16[1,3,64,768]{3,2,1,0:T(8,128)(2,1)S(1)}, bf16[1,3,64,768]{3,2,1,0:T(8,128)(2,1)S(1)}) fusion(bf16[1,16,64,768]{3,2,1,0:T(8,128)(2,1)} %param.8), kind=kLoop, calls=%fused_computation.21 | loop fusion | bytes 1179648 | tf_op jit(solution)/shard_map/slice | solution.py:788
  6.7 0.7 broadcast_in_dim.31.bias
  7.4 0.0 collective-permute-done.left
  7.4 2.2 %collective-permute-done.1.right = bf16[16,3,768]{2,1,0:T(4,128)(2,1)S(1)} collective-permute-done((bf16[16,3,768]{2,1,0:T(4,128)(2,1)S(1)}, bf16[16,3,768]{2,1,0:T(4,128)(2,1)S(1)}, u32[]{:S(2)}, u32[]{:S(2)}) %collective-permute-start.1) | collective-permute-done | bytes 73760 | tf_op jit(solution)/shard_map/ppermute | solution.py:107
  9.8 3.5 %collective-permute-start.2 = (bf16[210,768]{1,0:T(8,128)(2,1)S(1)}, bf16[210,768]{1,0:T(8,128)(2,1)S(1)}, u32[]{:S(2)}, u32[]{:S(2)}) collective-permute-start(bf16[210,768]{1,0:T(8,128)(2,1)S(1)} %get-tuple-element.72), channel_id=1, source_target_pairs={{0,4},{4,8},{8,12},{1,5},{5,9},{9,13},{2,6},{6,10},{10,14},{3,7},{... | collective-permute-start | bytes 967688 | tf_op jit(solution)/shard_map/ppermute | solution.py:103
  13.3 1.3 %collective-permute-start.3 = (bf16[210,768]{1,0:T(8,128)(2,1)S(1)}, bf16[210,768]{1,0:T(8,128)(2,1)S(1)}, u32[]{:S(2)}, u32[]{:S(2)}) collective-permute-start(bf16[210,768]{1,0:T(8,128)(2,1)S(1)} %get-tuple-element.73), channel_id=1, source_target_pairs={{4,0},{8,4},{12,8},{5,1},{9,5},{13,9},{6,2},{10,6},{14,10},{7,3},{... | collective-permute-start | bytes 967688 | tf_op jit(solution)/shard_map/ppermute | solution.py:107
  14.6 0.0 copy-done
  14.6 0.0 copy-done.4
  14.6 6.8 %conv_inner.1 = (f32[6,16,14,8,128]{4,3,2,1,0:T(8,128)S(1)}, f32[6,121,8,128]{3,2,1,0:T(8,128)S(1)}, bf16[512,768]{1,0:T(8,128)(2,1)S(1)}, f32[512,256]{1,0:T(8,...) custom-call(bf16[16,64,768]{2,1,0:T(8,128)(2,1)S(1)} %bitcast.29, ...), custom_call_target="tpu_custom_call" | custom-call | flops 10000000000 | bytes 10000000 | tf_op jit(solution)/shard_map/conv_inner/pallas_call | solution.py:365
  21.4 0.0 collective-permute-done.2.top
  21.4 2.4 %collective-permute-done.3.bottom = bf16[210,768]{1,0:T(8,128)(2,1)S(1)} collective-permute-done((bf16[210,768]{1,0:T(8,128)(2,1)S(1)}, bf16[210,768]{1,0:T(8,128)(2,1)S(1)}, u32[]{:S(2)}, u32[]{:S(2)}) %collective-permute-start.3) | collective-permute-done | bytes 322592 | tf_op jit(solution)/shard_map/ppermute | solution.py:107
  23.8 5.2 %conv_edge.1 = (f32[6,3,14,8,128]{4,3,2,1,0:T(8,128)S(1)}, f32[6,3,14,8,128]{4,3,2,1,0:T(8,128)S(1)}, bf16[512,768]{1,0:T(8,128)(2,1)S(1)}, f32[512,256]{1,0:T(8...) custom-call(s32[1]{0:T(128)} %bitcast.3.flag, ...), custom_call_target="tpu_custom_call" | custom-call | flops 6000000000 | bytes 6000000 | tf_op jit(solution)/shard_map/conv_edge/pallas_call | solution.py:396
  29.0 0.0 copy-start.1
  29.0 0.0 copy-start.5
  29.0 1.9 %collective-permute-start.4 = (f32[72,256]{1,0:T(8,128)S(1)}, f32[72,256]{1,0:T(8,128)S(1)}, u32[]{:S(2)}, u32[]{:S(2)}) collective-permute-start(f32[72,256]{1,0:T(8,128)S(1)} %get-tuple-element.80), channel_id=1, source_target_pairs={{0,1},{1,0},{2,3},{3,2},{4,5},{5,4},{6,7},{7,6},{8,9},{9,8},{10,11... | collective-permute-start | bytes 221192 | tf_op jit(solution)/shard_map/ppermute | solution.py:33
  30.9 0.9 collective-permute-done.4
  31.9 0.8 collective-permute-start.5
  32.7 0.9 prepare.1
  33.6 2.8 %collective-permute-done.5 = f32[72,256]{1,0:T(8,128)S(1)} collective-permute-done((f32[72,256]{1,0:T(8,128)S(1)}, f32[72,256]{1,0:T(8,128)S(1)}, u32[]{:S(2)}, u32[]{:S(2)}) %collective-permute-start.5) | collective-permute-done | bytes 73760 | tf_op jit(solution)/shard_map/ppermute | solution.py:33
  36.5 1.6 %collective-permute-start.6 = (f32[72,256]{1,0:T(8,128)S(1)}, f32[72,256]{1,0:T(8,128)S(1)}, u32[]{:S(2)}, u32[]{:S(2)}) collective-permute-start(f32[72,256]{1,0:T(8,128)S(1)} %add.41), channel_id=1, source_target_pairs={{0,4},{4,0},{8,12},{12,8},{1,5},{5,1},{9,13},{13,9},{2,6},{6,2},{1... | collective-permute-start | bytes 221192 | tf_op jit(solution)/shard_map/ppermute | solution.py:33
  38.1 2.8 %collective-permute-done.6 = f32[72,256]{1,0:T(8,128)S(1)} collective-permute-done((f32[72,256]{1,0:T(8,128)S(1)}, f32[72,256]{1,0:T(8,128)S(1)}, u32[]{:S(2)}, u32[]{:S(2)}) %collective-permute-start.6) | collective-permute-done | bytes 73760 | tf_op jit(solution)/shard_map/ppermute | solution.py:33
  40.9 2.6 %collective-permute-start.7 = (f32[72,256]{1,0:T(8,128)S(1)}, f32[72,256]{1,0:T(8,128)S(1)}, u32[]{:S(2)}, u32[]{:S(2)}) collective-permute-start(f32[72,256]{1,0:T(8,128)S(1)} %add.42), channel_id=1, source_target_pairs={{0,8},{4,12},{8,0},{12,4},{1,9},{5,13},{9,1},{13,5},{2,10},{6,14},... | collective-permute-start | bytes 221192 | tf_op jit(solution)/shard_map/ppermute | solution.py:33
  43.5 2.7 %collective-permute-done.7 = f32[72,256]{1,0:T(8,128)S(1)} collective-permute-done((f32[72,256]{1,0:T(8,128)S(1)}, f32[72,256]{1,0:T(8,128)S(1)}, u32[]{:S(2)}, u32[]{:S(2)}) %collective-permute-start.7) | collective-permute-done | bytes 73760 | tf_op jit(solution)/shard_map/ppermute | solution.py:33
  46.2 0.1 collective-permute-start.8
  47.0 0.6 collective-permute-done.8.other
  47.6 9.8 %head.1 = (f32[272,256]{1,0:T(8,128)S(1)}, f32[320,768]{1,0:T(8,128)S(1)}, bf16[512,768]{1,0:T(8,128)(2,1)S(1)}, bf16[512,768]{1,0:T(8,128)(2,1)S(1)}) custom-call(s32[1]{0:T(128)} %bitcast.3.flag, s32[1]{0:T(128)S(6)} %copy.23.label, f32[10]{0:T(128)S(1)} %copy-done.5, f32[72,256]{1,0:T(8,128)S(1)} %add.43.own, f32[72,256]{1,0:T(8,128)S(1)} %collective-permute-done.8.other, ...), custom_call_target="tpu_custom_call" | custom-call | flops 10000000000 | bytes 10000000 | tf_op jit(solution)/shard_map/head/pallas_call | solution.py:578
  57.3 1.6 %collective-permute-start.9 = (f32[272,256]{1,0:T(8,128)S(1)}, f32[272,256]{1,0:T(8,128)S(1)}, u32[]{:S(2)}, u32[]{:S(2)}) collective-permute-start(f32[272,256]{1,0:T(8,128)S(1)} %get-tuple-element.113.refs_0_), channel_id=1, source_target_pairs={{0,16},{16,0},{1,17},{17,1},{2,18},{18,2},{3,19},{19,3},{4,20},{20... | collective-permute-start | bytes 835592 | tf_op jit(solution)/shard_map/ppermute | solution.py:33
  58.9 6.7 %tap_grads.2.payload_in = f32[320,768]{1,0:T(8,128)S(1)} custom-call(f32[6,16,14,8,128]{4,3,2,1,0:T(8,128)S(1)} %get-tuple-element.71.spread_in, f32[6,3,14,8,128]{4,3,2,1,0:T(8,128)S(1)} %get-tuple-element.77.spread_top, f32[6,3,14,8,128]{4,3,2,1,0:T(8,128)S(1)} %get-tuple-element.78.spread_bottom, ...), custom_call_target="tpu_custom_call", output_to_operand_aliasing={{}: (5, {})} | custom-call | flops 10000000000 | bytes 10000000 | tf_op jit(solution)/shard_map/tap_grads/pallas_call | solution.py:723
  65.6 0.5 collective-permute-done.9.refs_1_
  66.1 1.3 %tap_grads.3 = f32[320,768]{1,0:T(8,128)S(1)} custom-call(f32[6,16,14,8,128]{4,3,2,1,0:T(8,128)S(1)} %get-tuple-element.71.spread_in, f32[6,3,14,8,128]{4,3,2,1,0:T(8,128)S(1)} %get-tuple-element.77.spread_top, f32[6,3,14,8,128]{4,3,2,1,0:T(8,128)S(1)} %get-tuple-element.78.spread_bottom, ...), custom_call_target="tpu_custom_call", output_to_operand_aliasing={{}: (5, {})} | custom-call | flops 2000000000 | bytes 2000000 | tf_op jit(solution)/shard_map/tap_grads/pallas_call | solution.py:723
  67.5 0.1 collective-permute-start.10
  67.6 1.5 %collective-permute-done.10 = bf16[160,768]{1,0:T(8,128)(2,1)S(1)} collective-permute-done((bf16[160,768]{1,0:T(8,128)(2,1)S(1)}, bf16[160,768]{1,0:T(8,128)(2,1)S(1)}, u32[]{:S(2)}, u32[]{:S(2)}) %collective-permute-start.10) | collective-permute-done | bytes 245792 | tf_op jit(solution)/shard_map/ppermute | solution.py:33
  69.1 0.1 convert_add_fusion
  69.2 0.7 collective-permute-start.11
  69.8 1.5 %collective-permute-start.12 = (bf16[40,768]{1,0:T(8,128)(2,1)S(1)}, bf16[40,768]{1,0:T(8,128)(2,1)S(1)}, u32[]{:S(2)}, u32[]{:S(2)}) collective-permute-start(bf16[40,768]{1,0:T(8,128)(2,1)S(1)} %get-tuple-element.129), channel_id=1, source_target_pairs={{0,16},{1,17},{2,18},{3,19},{16,0},{17,1},{18,2},{19,3},{4,20},{5,... | collective-permute-start | bytes 184328 | tf_op jit(solution)/shard_map/ppermute | solution.py:78
  71.3 1.4 %collective-permute-start.13 = (bf16[40,768]{1,0:T(8,128)(2,1)S(1)}, bf16[40,768]{1,0:T(8,128)(2,1)S(1)}, u32[]{:S(2)}, u32[]{:S(2)}) collective-permute-start(bf16[40,768]{1,0:T(8,128)(2,1)S(1)} %get-tuple-element.128), channel_id=1, source_target_pairs={{0,18},{1,19},{2,16},{3,17},{16,2},{17,3},{18,0},{19,1},{4,22},{5,... | collective-permute-start | bytes 184328 | tf_op jit(solution)/shard_map/ppermute | solution.py:78
  72.7 0.7 collective-permute-done.11
  73.5 0.6 collective-permute-done.12
  74.1 2.4 %collective-permute-done.13 = bf16[40,768]{1,0:T(8,128)(2,1)S(1)} collective-permute-done((bf16[40,768]{1,0:T(8,128)(2,1)S(1)}, bf16[40,768]{1,0:T(8,128)(2,1)S(1)}, u32[]{:S(2)}, u32[]{:S(2)}) %collective-permute-start.13) | collective-permute-done | bytes 61472 | tf_op jit(solution)/shard_map/ppermute | solution.py:78
  76.5 1.6 %collective-permute-start.14 = (bf16[40,768]{1,0:T(8,128)(2,1)S(1)}, bf16[40,768]{1,0:T(8,128)(2,1)S(1)}, u32[]{:S(2)}, u32[]{:S(2)}) collective-permute-start(bf16[40,768]{1,0:T(8,128)(2,1)S(1)} %fusion.1), channel_id=1, source_target_pairs={{0,4},{4,0},{8,12},{12,8},{1,5},{5,1},{9,13},{13,9},{2,6},{6,2},{1... | collective-permute-start | bytes 184328 | tf_op jit(solution)/shard_map/ppermute | solution.py:33
  78.1 2.9 %collective-permute-start.15 = (bf16[40,768]{1,0:T(8,128)(2,1)S(1)}, bf16[40,768]{1,0:T(8,128)(2,1)S(1)}, u32[]{:S(2)}, u32[]{:S(2)}) collective-permute-start(bf16[40,768]{1,0:T(8,128)(2,1)S(1)} %fusion.1), channel_id=1, source_target_pairs={{0,8},{4,12},{8,0},{12,4},{1,9},{5,13},{9,1},{13,5},{2,10},{6,14},... | collective-permute-start | bytes 184328 | tf_op jit(solution)/shard_map/ppermute | solution.py:33
  81.0 0.0 collective-permute-start.16
  81.0 0.3 collective-permute-done.14
  81.2 3.3 %collective-permute-done.15 = bf16[40,768]{1,0:T(8,128)(2,1)S(1)} collective-permute-done((bf16[40,768]{1,0:T(8,128)(2,1)S(1)}, bf16[40,768]{1,0:T(8,128)(2,1)S(1)}, u32[]{:S(2)}, u32[]{:S(2)}) %collective-permute-start.15) | collective-permute-done | bytes 61472 | tf_op jit(solution)/shard_map/ppermute | solution.py:33
  84.5 2.5 %collective-permute-done.16 = bf16[40,768]{1,0:T(8,128)(2,1)S(1)} collective-permute-done((bf16[40,768]{1,0:T(8,128)(2,1)S(1)}, bf16[40,768]{1,0:T(8,128)(2,1)S(1)}, u32[]{:S(2)}, u32[]{:S(2)}) %collective-permute-start.16) | collective-permute-done | bytes 61472 | tf_op jit(solution)/shard_map/ppermute | solution.py:33
  87.1 0.1 slice_reduce_fusion
  87.2 1.5 %collective-permute-start.17 = (bf16[40,768]{1,0:T(8,128)(2,1)S(1)}, bf16[40,768]{1,0:T(8,128)(2,1)S(1)}, u32[]{:S(2)}, u32[]{:S(2)}) collective-permute-start(bf16[40,768]{1,0:T(8,128)(2,1)S(1)} %add_convert_fusion), channel_id=1, source_target_pairs={{0,2},{1,3},{2,0},{3,1},{16,18},{17,19},{18,16},{19,17},{4,6},{5,7... | collective-permute-start | bytes 184328 | tf_op jit(solution)/shard_map/ppermute | solution.py:87
  88.7 0.5 collective-permute-start.18
  89.2 1.5 %collective-permute-start.19 = (bf16[40,768]{1,0:T(8,128)(2,1)S(1)}, bf16[40,768]{1,0:T(8,128)(2,1)S(1)}, u32[]{:S(2)}, u32[]{:S(2)}) collective-permute-start(bf16[40,768]{1,0:T(8,128)(2,1)S(1)} %add_convert_fusion), channel_id=1, source_target_pairs={{0,18},{1,19},{2,16},{3,17},{16,2},{17,3},{18,0},{19,1},{4,22},{5,... | collective-permute-start | bytes 184328 | tf_op jit(solution)/shard_map/ppermute | solution.py:87
  90.8 0.1 slice_reduce_fusion.1
  90.9 0.6 collective-permute-done.17
  91.5 1.5 %collective-permute-done.18 = bf16[40,768]{1,0:T(8,128)(2,1)S(1)} collective-permute-done((bf16[40,768]{1,0:T(8,128)(2,1)S(1)}, bf16[40,768]{1,0:T(8,128)(2,1)S(1)}, u32[]{:S(2)}, u32[]{:S(2)}) %collective-permute-start.18) | collective-permute-done | bytes 61472 | tf_op jit(solution)/shard_map/ppermute | solution.py:87
  92.9 1.4 %collective-permute-done.19 = bf16[40,768]{1,0:T(8,128)(2,1)S(1)} collective-permute-done((bf16[40,768]{1,0:T(8,128)(2,1)S(1)}, bf16[40,768]{1,0:T(8,128)(2,1)S(1)}, u32[]{:S(2)}, u32[]{:S(2)}) %collective-permute-start.19) | collective-permute-done | bytes 61472 | tf_op jit(solution)/shard_map/ppermute | solution.py:87
  94.4 0.1 collective-permute-start.20
  94.5 1.9 %multiply_add_fusion = f32[10,256,256]{2,1,0:T(8,128)} fusion(f32[256,256]{1,0:T(8,128)S(1)} %slice.57, f32[10]{0:T(128)S(1)} %slice_reduce_fusion, f32[256,256]{1,0:T(8,128)S(1)} %slice.55, f32[10]{0:T(128)S(1)} %slice_reduce_fusion.1), kind=kLoop, calls=%fused_computation | loop fusion | flops 1966080 | bytes 3145808 | tf_op jit(solution)/shard_map/add | solution.py:42
  96.3 0.0 collective-permute-done.20.other
  96.3 1.0 %finish.1 = (f32[768,256]{1,0:T(8,128)}, f32[7,7,768]{2,1,0:T(8,128)}, f32[768]{0:T(1024)}, f32[256]{0:T(256)}, f32[10]{0:T(128)}, /*index=5*/f32[1]{0:T(128)}) custom-call(s32[1]{0:T(128)} %bitcast.3.flag, bf16[160,768]{1,0:T(8,128)(2,1)S(1)} %bitcast.31, bf16[160,768]{1,0:T(8,128)(2,1)S(1)} %collective-permute-done.20.other, ...), custom_call_target="tpu_custom_call" | custom-call | flops 1000000000 | bytes 1000000 | tf_op jit(solution)/shard_map/finish/pallas_call | solution.py:767
  (26 shorter events, 0.5 us)
Async XLA Ops:
  0.6 14.0 %copy-start = (bf16[1,16,64,768]{3,2,1,0:T(8,128)(2,1)S(1)}, bf16[1,16,64,768]{3,2,1,0:T(8,128)(2,1)}, u32[]{:S(2)}) copy-start(bf16[1,16,64,768]{3,2,1,0:T(8,128)(2,1)} %param.8) | copy-start | bytes 4718596
  0.6 14.0 %copy-start.4 = (f32[256]{0:T(256)S(1)}, f32[256]{0:T(256)}, u32[]{:S(2)}) copy-start(f32[256]{0:T(256)} %param.12) | copy-start | bytes 3076
  0.7 14.0 %copy-start.2 = (bf16[768,256]{1,0:T(8,128)(2,1)S(1)}, bf16[768,256]{1,0:T(8,128)(2,1)}, u32[]{:S(2)}) copy-start(bf16[768,256]{1,0:T(8,128)(2,1)} %reduce_weight.5) | copy-start | bytes 1179652
  0.7 14.0 %copy-start.3 = (f32[7,7,768]{2,1,0:T(8,128)S(1)}, f32[7,7,768]{2,1,0:T(8,128)}, u32[]{:S(2)}) copy-start(f32[7,7,768]{2,1,0:T(8,128)} %weight.1) | copy-start | bytes 451588
  1.9 5.5 %collective-permute-start = (bf16[16,3,768]{2,1,0:T(4,128)(2,1)S(1)}, bf16[16,3,768]{2,1,0:T(4,128)(2,1)S(1)}, u32[]{:S(2)}, u32[]{:S(2)}) collective-permute-start(bf16[16,3,768]{2,1,0:T(4,128)(2,1)S(1)} %get-tuple-element.125), channel_id=1, source_target_pairs={{0,1},{1,2},{2,3},{4,5},{5,6},{6,7},{8,9},{9,10},{10,11},{12,13},{... | collective-permute-start | bytes 221192 | tf_op jit(solution)/shard_map/ppermute | solution.py:103
  4.3 5.3 %collective-permute-start.1 = (bf16[16,3,768]{2,1,0:T(4,128)(2,1)S(1)}, bf16[16,3,768]{2,1,0:T(4,128)(2,1)S(1)}, u32[]{:S(2)}, u32[]{:S(2)}) collective-permute-start(bf16[16,3,768]{2,1,0:T(4,128)(2,1)S(1)} %get-tuple-element.126), channel_id=1, source_target_pairs={{1,0},{2,1},{3,2},{5,4},{6,5},{7,6},{9,8},{10,9},{11,10},{13,12},{... | collective-permute-start | bytes 221192 | tf_op jit(solution)/shard_map/ppermute | solution.py:107
  9.8 11.6 %collective-permute-start.2 = (bf16[210,768]{1,0:T(8,128)(2,1)S(1)}, bf16[210,768]{1,0:T(8,128)(2,1)S(1)}, u32[]{:S(2)}, u32[]{:S(2)}) collective-permute-start(bf16[210,768]{1,0:T(8,128)(2,1)S(1)} %get-tuple-element.72), channel_id=1, source_target_pairs={{0,4},{4,8},{8,12},{1,5},{5,9},{9,13},{2,6},{6,10},{10,14},{3,7},{... | collective-permute-start | bytes 967688 | tf_op jit(solution)/shard_map/ppermute | solution.py:103
  13.3 10.5 %collective-permute-start.3 = (bf16[210,768]{1,0:T(8,128)(2,1)S(1)}, bf16[210,768]{1,0:T(8,128)(2,1)S(1)}, u32[]{:S(2)}, u32[]{:S(2)}) collective-permute-start(bf16[210,768]{1,0:T(8,128)(2,1)S(1)} %get-tuple-element.73), channel_id=1, source_target_pairs={{4,0},{8,4},{12,8},{5,1},{9,5},{13,9},{6,2},{10,6},{14,10},{7,3},{... | collective-permute-start | bytes 967688 | tf_op jit(solution)/shard_map/ppermute | solution.py:107
  29.0 18.6 %copy-start.1 = (bf16[10,256,256]{2,1,0:T(8,128)(2,1)S(1)}, bf16[10,256,256]{2,1,0:T(8,128)(2,1)}, u32[]{:S(2)}) copy-start(bf16[10,256,256]{2,1,0:T(8,128)(2,1)} %class_weight.1) | copy-start | bytes 3932164
  29.0 18.6 %copy-start.5 = (f32[10]{0:T(128)S(1)}, f32[10]{0:T(128)}, u32[]{:S(2)}) copy-start(f32[10]{0:T(128)} %class_bias.1) | copy-start | bytes 124
  29.0 2.9 %collective-permute-start.4 = (f32[72,256]{1,0:T(8,128)S(1)}, f32[72,256]{1,0:T(8,128)S(1)}, u32[]{:S(2)}, u32[]{:S(2)}) collective-permute-start(f32[72,256]{1,0:T(8,128)S(1)} %get-tuple-element.80), channel_id=1, source_target_pairs={{0,1},{1,0},{2,3},{3,2},{4,5},{5,4},{6,7},{7,6},{8,9},{9,8},{10,11... | collective-permute-start | bytes 221192 | tf_op jit(solution)/shard_map/ppermute | solution.py:33
  31.9 4.6 %collective-permute-start.5 = (f32[72,256]{1,0:T(8,128)S(1)}, f32[72,256]{1,0:T(8,128)S(1)}, u32[]{:S(2)}, u32[]{:S(2)}) collective-permute-start(f32[72,256]{1,0:T(8,128)S(1)} %add.40), channel_id=1, source_target_pairs={{0,2},{1,3},{2,0},{3,1},{4,6},{5,7},{6,4},{7,5},{8,10},{9,11},{10,... | collective-permute-start | bytes 221192 | tf_op jit(solution)/shard_map/ppermute | solution.py:33
  36.5 4.4 %collective-permute-start.6 = (f32[72,256]{1,0:T(8,128)S(1)}, f32[72,256]{1,0:T(8,128)S(1)}, u32[]{:S(2)}, u32[]{:S(2)}) collective-permute-start(f32[72,256]{1,0:T(8,128)S(1)} %add.41), channel_id=1, source_target_pairs={{0,4},{4,0},{8,12},{12,8},{1,5},{5,1},{9,13},{13,9},{2,6},{6,2},{1... | collective-permute-start | bytes 221192 | tf_op jit(solution)/shard_map/ppermute | solution.py:33
  40.9 5.3 %collective-permute-start.7 = (f32[72,256]{1,0:T(8,128)S(1)}, f32[72,256]{1,0:T(8,128)S(1)}, u32[]{:S(2)}, u32[]{:S(2)}) collective-permute-start(f32[72,256]{1,0:T(8,128)S(1)} %add.42), channel_id=1, source_target_pairs={{0,8},{4,12},{8,0},{12,4},{1,9},{5,13},{9,1},{13,5},{2,10},{6,14},... | collective-permute-start | bytes 221192 | tf_op jit(solution)/shard_map/ppermute | solution.py:33
  46.2 1.3 %collective-permute-start.8 = (f32[72,256]{1,0:T(8,128)S(1)}, f32[72,256]{1,0:T(8,128)S(1)}, u32[]{:S(2)}, u32[]{:S(2)}) collective-permute-start(f32[72,256]{1,0:T(8,128)S(1)} %add.43.own), channel_id=1, source_target_pairs={{0,1},{1,0},{2,3},{3,2},{4,5},{5,4},{6,7},{7,6},{8,9},{9,8},{10,11... | collective-permute-start | bytes 221192 | tf_op jit(solution)/shard_map/ppermute | solution.py:33
  57.3 8.8 %collective-permute-start.9 = (f32[272,256]{1,0:T(8,128)S(1)}, f32[272,256]{1,0:T(8,128)S(1)}, u32[]{:S(2)}, u32[]{:S(2)}) collective-permute-start(f32[272,256]{1,0:T(8,128)S(1)} %get-tuple-element.113.refs_0_), channel_id=1, source_target_pairs={{0,16},{16,0},{1,17},{17,1},{2,18},{18,2},{3,19},{19,3},{4,20},{20... | collective-permute-start | bytes 835592 | tf_op jit(solution)/shard_map/ppermute | solution.py:33
  67.5 1.6 %collective-permute-start.10 = (bf16[160,768]{1,0:T(8,128)(2,1)S(1)}, bf16[160,768]{1,0:T(8,128)(2,1)S(1)}, u32[]{:S(2)}, u32[]{:S(2)}) collective-permute-start(bf16[160,768]{1,0:T(8,128)(2,1)S(1)} %select_convert_fusion), channel_id=1, source_target_pairs={{0,1},{1,0},{2,3},{3,2},{4,5},{5,4},{6,7},{7,6},{8,9},{9,8},{10,11... | collective-permute-start | bytes 737288 | tf_op jit(solution)/shard_map/ppermute | solution.py:33
  69.2 4.3 %collective-permute-start.11 = (bf16[40,768]{1,0:T(8,128)(2,1)S(1)}, bf16[40,768]{1,0:T(8,128)(2,1)S(1)}, u32[]{:S(2)}, u32[]{:S(2)}) collective-permute-start(bf16[40,768]{1,0:T(8,128)(2,1)S(1)} %get-tuple-element.127), channel_id=1, source_target_pairs={{0,2},{1,3},{2,0},{3,1},{16,18},{17,19},{18,16},{19,17},{4,6},{5,7... | collective-permute-start | bytes 184328 | tf_op jit(solution)/shard_map/ppermute | solution.py:78
  69.8 4.2 %collective-permute-start.12 = (bf16[40,768]{1,0:T(8,128)(2,1)S(1)}, bf16[40,768]{1,0:T(8,128)(2,1)S(1)}, u32[]{:S(2)}, u32[]{:S(2)}) collective-permute-start(bf16[40,768]{1,0:T(8,128)(2,1)S(1)} %get-tuple-element.129), channel_id=1, source_target_pairs={{0,16},{1,17},{2,18},{3,19},{16,0},{17,1},{18,2},{19,3},{4,20},{5,... | collective-permute-start | bytes 184328 | tf_op jit(solution)/shard_map/ppermute | solution.py:78
  71.3 5.1 %collective-permute-start.13 = (bf16[40,768]{1,0:T(8,128)(2,1)S(1)}, bf16[40,768]{1,0:T(8,128)(2,1)S(1)}, u32[]{:S(2)}, u32[]{:S(2)}) collective-permute-start(bf16[40,768]{1,0:T(8,128)(2,1)S(1)} %get-tuple-element.128), channel_id=1, source_target_pairs={{0,18},{1,19},{2,16},{3,17},{16,2},{17,3},{18,0},{19,1},{4,22},{5,... | collective-permute-start | bytes 184328 | tf_op jit(solution)/shard_map/ppermute | solution.py:78
  76.5 4.8 %collective-permute-start.14 = (bf16[40,768]{1,0:T(8,128)(2,1)S(1)}, bf16[40,768]{1,0:T(8,128)(2,1)S(1)}, u32[]{:S(2)}, u32[]{:S(2)}) collective-permute-start(bf16[40,768]{1,0:T(8,128)(2,1)S(1)} %fusion.1), channel_id=1, source_target_pairs={{0,4},{4,0},{8,12},{12,8},{1,5},{5,1},{9,13},{13,9},{2,6},{6,2},{1... | collective-permute-start | bytes 184328 | tf_op jit(solution)/shard_map/ppermute | solution.py:33
  78.1 6.4 %collective-permute-start.15 = (bf16[40,768]{1,0:T(8,128)(2,1)S(1)}, bf16[40,768]{1,0:T(8,128)(2,1)S(1)}, u32[]{:S(2)}, u32[]{:S(2)}) collective-permute-start(bf16[40,768]{1,0:T(8,128)(2,1)S(1)} %fusion.1), channel_id=1, source_target_pairs={{0,8},{4,12},{8,0},{12,4},{1,9},{5,13},{9,1},{13,5},{2,10},{6,14},... | collective-permute-start | bytes 184328 | tf_op jit(solution)/shard_map/ppermute | solution.py:33
  81.0 6.0 %collective-permute-start.16 = (bf16[40,768]{1,0:T(8,128)(2,1)S(1)}, bf16[40,768]{1,0:T(8,128)(2,1)S(1)}, u32[]{:S(2)}, u32[]{:S(2)}) collective-permute-start(bf16[40,768]{1,0:T(8,128)(2,1)S(1)} %fusion.1), channel_id=1, source_target_pairs={{0,12},{4,8},{8,4},{12,0},{1,13},{5,9},{9,5},{13,1},{2,14},{6,10},... | collective-permute-start | bytes 184328 | tf_op jit(solution)/shard_map/ppermute | solution.py:33
  87.2 4.3 %collective-permute-start.17 = (bf16[40,768]{1,0:T(8,128)(2,1)S(1)}, bf16[40,768]{1,0:T(8,128)(2,1)S(1)}, u32[]{:S(2)}, u32[]{:S(2)}) collective-permute-start(bf16[40,768]{1,0:T(8,128)(2,1)S(1)} %add_convert_fusion), channel_id=1, source_target_pairs={{0,2},{1,3},{2,0},{3,1},{16,18},{17,19},{18,16},{19,17},{4,6},{5,7... | collective-permute-start | bytes 184328 | tf_op jit(solution)/shard_map/ppermute | solution.py:87
  88.7 4.2 %collective-permute-start.18 = (bf16[40,768]{1,0:T(8,128)(2,1)S(1)}, bf16[40,768]{1,0:T(8,128)(2,1)S(1)}, u32[]{:S(2)}, u32[]{:S(2)}) collective-permute-start(bf16[40,768]{1,0:T(8,128)(2,1)S(1)} %add_convert_fusion), channel_id=1, source_target_pairs={{0,16},{1,17},{2,18},{3,19},{16,0},{17,1},{18,2},{19,3},{4,20},{5,... | collective-permute-start | bytes 184328 | tf_op jit(solution)/shard_map/ppermute | solution.py:87
  89.2 5.1 %collective-permute-start.19 = (bf16[40,768]{1,0:T(8,128)(2,1)S(1)}, bf16[40,768]{1,0:T(8,128)(2,1)S(1)}, u32[]{:S(2)}, u32[]{:S(2)}) collective-permute-start(bf16[40,768]{1,0:T(8,128)(2,1)S(1)} %add_convert_fusion), channel_id=1, source_target_pairs={{0,18},{1,19},{2,16},{3,17},{16,2},{17,3},{18,0},{19,1},{4,22},{5,... | collective-permute-start | bytes 184328 | tf_op jit(solution)/shard_map/ppermute | solution.py:87
  94.4 1.9 %collective-permute-start.20 = (bf16[160,768]{1,0:T(8,128)(2,1)S(1)}, bf16[160,768]{1,0:T(8,128)(2,1)S(1)}, u32[]{:S(2)}, u32[]{:S(2)}) collective-permute-start(bf16[160,768]{1,0:T(8,128)(2,1)S(1)} %bitcast.30), channel_id=1, source_target_pairs={{0,1},{1,0},{2,3},{3,2},{4,5},{5,4},{6,7},{7,6},{8,9},{9,8},{10,11... | collective-permute-start | bytes 737288 | tf_op jit(solution)/shard_map/ppermute | solution.py:33

commit v11 on v10

--- a/solution.py
+++ b/solution.py
@@ -46,12 +46,6 @@
 def exchange(value, axis, shift, sent_as):
     sent = value.astype(sent_as)
     return sent.astype(wide) + swap(sent, axis, shift).astype(wide)
-
-
-def exchange_all(value, axis, sent_as):
-    sent = value.astype(sent_as)
-    moved = [sent] + [swap(sent, axis, shift) for shift in range(1, lax.axis_size(axis))]
-    return tree_sum([part.astype(wide) for part in moved])
 
 
 def square_pairs(axes, shifts):
@@ -211,8 +205,12 @@
                 for col_part in range(2):
                     own = values[3 * row_part + col_part] + values[3 * row_part + 2]
                     lines[row_part].append(own + shared[col_part])
-        found += lines[0] + lines[1]
-    return jnp.concatenate(found, axis=0).astype(narrow)
+        found += lines
+    return found
+
+
+def rounded(lines):
+    return jnp.concatenate([part for line in lines for part in line], axis=0).astype(narrow)
 
 
 def parts_scratch(count, steps):
@@ -235,7 +233,7 @@
 
 def inner_kernel(
     block, left, right, weight, bias, reduce_weight, reduce_bias,
-    spread_out, filters, conv_out, before_out, feat_out, gram_out, colsum_out,
+    spread_out, filters, conv_out, before_out, feat_out, gram_out, colsum_out, partial_out,
     wide_row, parts, products,
 ):
     rows, cols = block.shape[0], block.shape[1]
@@ -256,12 +254,27 @@
 
         lax.fori_loop(0, rows // FILL_ROWS, fill, 0)
 
-        def load(row, group):
-            return spread_out[tile, row + SIDE - HALF, group]
-
-        conv_out[:, lanes] = conv_rows(
-            load, filters, tile, start_value, steps, rows - 2 * SIDE, parts, products
+        def load_from(first):
+            def load(row, group):
+                place = first + row - HALF
+                if 0 <= place < rows:
+                    return spread_out[tile, place, group]
+                return jnp.zeros((GROUPS, LANES), wide)
+
+            return load
+
+        conv_out[:, lanes] = rounded(
+            conv_rows(
+                load_from(SIDE), filters, tile, start_value, steps, rows - 2 * SIDE, parts, products
+            )
         )
+        for side, first in enumerate((0, rows - SIDE)):
+            lines = conv_rows(
+                load_from(first), filters, tile, start_value, steps, SIDE, parts, products
+            )
+            for row, line in enumerate(lines):
+                for step, value in enumerate(line):
+                    partial_out[tile, side * SIDE + row, step] = value
         return 0
 
     lax.fori_loop(0, spread_out.shape[0], one_tile, 0)
@@ -271,17 +284,15 @@
 
 
 def edge_kernel(
-    flag, spread_in, top, bottom, filters, bias, reduce_weight,
-    reduce_bias, gram_in, colsum_in,
+    flag, partial, top, bottom, filters, reduce_weight, reduce_bias, gram_in, colsum_in,
     spread_top, spread_bottom, conv_out, before_out, feat_out, kept_out, sent_out,
-    wide_row, stage, parts, products, sums,
+    wide_row, stage, sums,
 ):
-    rows, cols = spread_in.shape[1], wide_row.shape[1] - 2 * EDGE
+    cols = wide_row.shape[1] - 2 * EDGE
     steps = cols // GROUPS
 
     def one_tile(tile, _):
         lanes = lanes_of(tile)
-        start_value = jnp.broadcast_to(bias[0:1, lanes], (GROUPS, LANES))
         for side, (strip, spread) in enumerate(((top, spread_top), (bottom, spread_bottom))):
             stage[side] = strip[:, lanes].astype(wide)
             for row in range(HALF):
@@ -296,26 +307,30 @@
                 )
                 spread_columns(place, spread.at[tile, row])
 
-        def load_from(row):
-            def load(row_tap, group):
-                place = row + row_tap - HALF
-                if place < 0:
-                    return spread_top[tile, place + HALF, group]
-                if place >= rows:
-                    return spread_bottom[tile, place - rows, group]
-                return spread_in[tile, place, group]
-
-            return load
-
-        for side, row in enumerate((0, rows - SIDE)):
+        def filter_of(row_tap, col_tap):
+            start = FILTERS[row_tap % 2, col_tap % 2]
+            return filters[tile, start + row_tap // 2 * PARTS[col_tap % 2] + col_tap // 2]
+
+        for side, spread in enumerate((spread_top, spread_bottom)):
+            lines = [
+                [partial[tile, side * SIDE + row, step] for step in range(steps)]
+                for row in range(SIDE)
+            ]
+            for place in range(HALF):
+                windows = [spread[tile, place, group] for group in range(steps + KERNEL - 1)]
+                for row in range(SIDE):
+                    row_tap = place - row if side == 0 else place + HALF + SIDE - row
+                    if not 0 <= row_tap < KERNEL:
+                        continue
+                    for col_tap in range(KERNEL):
+                        scale = filter_of(row_tap, col_tap)
+                        for step in range(steps):
+                            lines[row][step] = lines[row][step] + windows[step + col_tap] * scale
             start = side * SIDE * cols
-            conv_out[start : start + SIDE * cols, lanes] = conv_rows(
-                load_from(row), filters, tile, start_value, steps, SIDE,
-                parts.at[side], products.at[side],
-            )
+            conv_out[start : start + SIDE * cols, lanes] = rounded(lines)
         return 0
 
-    lax.fori_loop(0, spread_in.shape[0], one_tile, 0)
+    lax.fori_loop(0, partial.shape[0], one_tile, 0)
     gram, colsum = reduce_part(conv_out, reduce_weight, reduce_bias, before_out, feat_out)
     gram = gram + gram_in[...]
     colsum = colsum + colsum_in[...]
@@ -365,7 +380,7 @@
     return pl.pallas_call(
         inner_kernel,
         in_specs=[in_vmem] * 7,
-        out_specs=[in_vmem] * 7,
+        out_specs=[in_vmem] * 8,
         out_shape=[
             shape_of((tiles, rows, steps + KERNEL - 1, GROUPS, LANES)),
             shape_of((tiles, PRODUCTS, GROUPS, LANES)),
@@ -374,6 +389,7 @@
             shape_of((pixels, width), narrow),
             shape_of((width, width)),
             shape_of((1, width)),
+            shape_of((tiles, 2 * SIDE, steps, GROUPS, LANES)),
         ],
         scratch_shapes=[
             pltpu.VMEM((rows, cols + 2 * EDGE, LANES), wide),
@@ -385,17 +401,16 @@
     )(block, left, right, weight, bias, reduce_weight, reduce_bias)
 
 
-def conv_edge(flag, spread, halos, filters, bias, reduce_weight, reduce_bias, gram, colsum):
-    tiles, rows, groups = spread.shape[:3]
-    cols = (groups - KERNEL + 1) * GROUPS
+def conv_edge(flag, partial, halos, filters, reduce_weight, reduce_bias, gram, colsum):
+    tiles, _, steps = partial.shape[:3]
+    cols, groups = steps * GROUPS, steps + KERNEL - 1
     channels, width = reduce_weight.shape
     pixels = 2 * SIDE * cols
-    parts, products = parts_scratch(SIDE, cols // GROUPS)
     side = (tiles, HALF, groups, GROUPS, LANES)
     sums_rows = width // 2 + 2 * GROUPS
     return pl.pallas_call(
         edge_kernel,
-        in_specs=[in_smem] + [in_vmem] * 9,
+        in_specs=[in_smem] + [in_vmem] * 8,
         out_specs=[in_vmem] * 7,
         out_shape=[
             shape_of(side),
@@ -409,14 +424,12 @@
         scratch_shapes=[
             pltpu.VMEM((2 * HALF, cols + 2 * EDGE, LANES), wide),
             pltpu.VMEM((2,) + (halos[0].shape[0], LANES), wide),
-            pltpu.VMEM((2,) + parts.shape, wide),
-            pltpu.VMEM((2,) + products.shape, wide),
             pltpu.VMEM((sums_rows, width), wide),
         ],
         compiler_params=params(24),
         cost_estimate=cost(6),
         name="conv_edge",
-    )(flag, spread, *halos, filters, bias, reduce_weight, reduce_bias, gram, colsum)
+    )(flag, partial, *halos, filters, reduce_weight, reduce_bias, gram, colsum)
 
 
 def split(value):
@@ -822,11 +835,11 @@
     )
     top = next_along(low, "sy")
     bottom = back_along(high, "sy")
-    spread, filters, conv_in, before_in, feat_in, gram, colsum = conv_inner(
+    spread, filters, conv_in, before_in, feat_in, gram, colsum, partial = conv_inner(
         block, left, right, depth_weight, bias_row, reduce_weight, reduce_row
     )
     spread_top, spread_bottom, conv_ed, before_ed, feat_ed, kept, sent = conv_edge(
-        flag, spread, (top, bottom), filters, bias_row, reduce_weight, reduce_row, gram, colsum
+        flag, partial, (top, bottom), filters, reduce_weight, reduce_row, gram, colsum
     )
 
     sums = kept + swap(sent, "sx", 1)
@@ -872,13 +885,17 @@
     payload = square_scatter(payload, axes, pairs, places, narrow)
     for shift in doublings("dp", 2):
         payload = exchange(payload, "dp", shift, narrow)
-    payload = exchange_all(payload, "sy", narrow).astype(narrow)
+    for shift in doublings("sy"):
+        payload = exchange(payload, "sy", shift, narrow)
+    payload = payload.astype(narrow)
     payload, known = together((payload, known))
     class_weight_grad = tree_sum(
         [part[width : width + classes, 0][:, None, None] * part[None, :width] for part in known]
     )
-    payload = square_gather(payload, axes, pairs, places)
-    other, class_weight_grad = together((swap(payload, "sx", 1), class_weight_grad))
+    payload, class_weight_grad = together(
+        (square_gather(payload, axes, pairs, places), class_weight_grad)
+    )
+    other = swap(payload, "sx", 1)
     weight_grad, depth_grad, depth_bias_grad, bias_grad, class_bias_grad, loss = finish(
         flag, payload, other, known, width, classes, image_count
     )

time: 97.9 us -> 97.9 us (level)
  waiting for transfers between devices: 29.5 us -> 24.8 us
  starting transfers between devices: 28.9 us -> 31.6 us
  Pallas kernels: 31.7 us -> 33.7 us
    pallas_call x1, Pallas kernels: 6.79 us -> 11.5 us  [conv_inner(): pl.pallas_call(inner_kernel, in_specs=[in_vmem] * 7, out_specs=[in_vmem]...]
    pallas_call x1, Pallas kernels: 5.16 us -> 2.39 us  [conv_edge(): pl.pallas_call(edge_kernel, in_specs=[in_smem] + [in_vmem] * 8, out_specs...]
    ppermute x11 -> x10, starting transfers between devices: 13.3 us -> 16 us  [swap(): return lax.ppermute(value, axis, [(i, i ^ shift) for i in range(count)])]
    ppermute x2, waiting for transfers between devices: 4.54 us -> 2.18 us  [back_along(): lax.ppermute(value, axis, [(i + 1, i) for i in range(lax.axis_size(axis)...]
    ppermute x3, waiting for transfers between devices: 3.43 us -> 1.7 us  [square_gather(): part = lax.ppermute(value, axes, pairs[turn]) if turn else value]
    ppermute x11 -> x10, waiting for transfers between devices: 17.8 us -> 17.3 us  [swap(): return lax.ppermute(value, axis, [(i, i ^ shift) for i in range(count)])]
  transfers between devices with their start and end apart: 21 -> 20, of which waited for: 18 -> 16; matrix products, arithmetic and copies ran while one was open for 4% -> 4% of each run, Pallas kernels for 15% -> 20%
where the time goes in v11:
time: 97.9 us; the launch traced here: 97.6 us
  Pallas kernels  33.7 us (34%)
  starting transfers between devices  31.6 us (32%)
  waiting for transfers between devices  24.8 us (25%)
  local copies, waits for them, and re-layouts  3.55 us (4%)
  other arithmetic  2.13 us (2%)
  between operations  1.77 us (2%)
    ppermute x10, waiting for transfers between devices, swap(): return lax.ppermute(value, axis, [(i, i ^ shift) for i in range(count)])  17.3 us
    ppermute x10, starting transfers between devices, swap(): return lax.ppermute(value, axis, [(i, i ^ shift) for i in range(count)])  16 us
    pallas_call x1, Pallas kernels, conv_inner(): pl.pallas_call(inner_kernel, in_specs=[in_vmem] * 7, out_specs=[in_vmem]...  11.5 us
    pallas_call x1, Pallas kernels, head(): pl.pallas_call(functools.partial(head_kernel, count=count, image_count=im...  9.77 us
    pallas_call x2, Pallas kernels, tap_grads(): pl.pallas_call(functools.partial(taps_kernel, first=first, last=last), in...  8.07 us
    ppermute x2, starting transfers between devices, next_along(): lax.ppermute(value, axis, [(i, i + 1) for i in range(lax.axis_size(axis)...  5.86 us
    ppermute x3, waiting for transfers between devices, square_scatter(): lax.ppermute(piece(turn).astype(sent_as), axes, pairs[turn]).astype(wide)  3.67 us
    ppermute x3, starting transfers between devices, square_scatter(): lax.ppermute(piece(turn).astype(sent_as), axes, pairs[turn]).astype(wide)  3.55 us
  transfers between devices with their start and end apart: 20, of which 16 were waited for; matrix products, arithmetic and copies ran while one was open for 4% of the time, Pallas kernels for 20%

profile of v11, /device:TPU:0, one launch (start us, length us, event | category | flops | bytes accessed | tf_op | source)
XLA Modules:
  0.0 97.6 jit_solution(9223295558916438814)
XLA Ops:
  0.6 0.0 copy-start
  0.6 0.0 copy-start.4
  0.7 0.0 copy-start.2
  0.7 0.0 copy-start.3
  0.7 1.2 %fusion.6 = (bf16[16,3,768]{2,1,0:T(4,128)(2,1)S(1)}, bf16[16,3,768]{2,1,0:T(4,128)(2,1)S(1)}) fusion(bf16[16,64,768]{2,1,0:T(8,128)(2,1)} %bitcast.28), kind=kLoop, calls=%fused_computation.23 | loop fusion | bytes 294912 | tf_op jit(solution)/shard_map/slice | solution.py:821
  1.9 2.4 %collective-permute-start = (bf16[16,3,768]{2,1,0:T(4,128)(2,1)S(1)}, bf16[16,3,768]{2,1,0:T(4,128)(2,1)S(1)}, u32[]{:S(2)}, u32[]{:S(2)}) collective-permute-start(bf16[16,3,768]{2,1,0:T(4,128)(2,1)S(1)} %get-tuple-element.127), channel_id=1, source_target_pairs={{0,1},{1,2},{2,3},{4,5},{5,6},{6,7},{8,9},{9,10},{10,11},{12,13},{... | collective-permute-start | bytes 221192 | tf_op jit(solution)/shard_map/ppermute | solution.py:97
  4.3 1.3 %collective-permute-start.1 = (bf16[16,3,768]{2,1,0:T(4,128)(2,1)S(1)}, bf16[16,3,768]{2,1,0:T(4,128)(2,1)S(1)}, u32[]{:S(2)}, u32[]{:S(2)}) collective-permute-start(bf16[16,3,768]{2,1,0:T(4,128)(2,1)S(1)} %get-tuple-element.128), channel_id=1, source_target_pairs={{1,0},{2,1},{3,2},{5,4},{6,5},{7,6},{9,8},{10,9},{11,10},{13,12},{... | collective-permute-start | bytes 221192 | tf_op jit(solution)/shard_map/ppermute | solution.py:101
  5.6 1.1 %fusion.5 = (bf16[1,3,64,768]{3,2,1,0:T(8,128)(2,1)S(1)}, bf16[1,3,64,768]{3,2,1,0:T(8,128)(2,1)S(1)}) fusion(bf16[1,16,64,768]{3,2,1,0:T(8,128)(2,1)} %param.8), kind=kLoop, calls=%fused_computation.22 | loop fusion | bytes 1179648 | tf_op jit(solution)/shard_map/slice | solution.py:801
  6.7 0.7 broadcast_in_dim.31.bias
  7.4 0.0 collective-permute-done.left
  7.4 2.2 %collective-permute-done.1.right = bf16[16,3,768]{2,1,0:T(4,128)(2,1)S(1)} collective-permute-done((bf16[16,3,768]{2,1,0:T(4,128)(2,1)S(1)}, bf16[16,3,768]{2,1,0:T(4,128)(2,1)S(1)}, u32[]{:S(2)}, u32[]{:S(2)}) %collective-permute-start.1) | collective-permute-done | bytes 73760 | tf_op jit(solution)/shard_map/ppermute | solution.py:101
  9.8 3.5 %collective-permute-start.2 = (bf16[210,768]{1,0:T(8,128)(2,1)S(1)}, bf16[210,768]{1,0:T(8,128)(2,1)S(1)}, u32[]{:S(2)}, u32[]{:S(2)}) collective-permute-start(bf16[210,768]{1,0:T(8,128)(2,1)S(1)} %get-tuple-element.74), channel_id=1, source_target_pairs={{0,4},{4,8},{8,12},{1,5},{5,9},{9,13},{2,6},{6,10},{10,14},{3,7},{... | collective-permute-start | bytes 967688 | tf_op jit(solution)/shard_map/ppermute | solution.py:97
  13.3 1.3 %collective-permute-start.3 = (bf16[210,768]{1,0:T(8,128)(2,1)S(1)}, bf16[210,768]{1,0:T(8,128)(2,1)S(1)}, u32[]{:S(2)}, u32[]{:S(2)}) collective-permute-start(bf16[210,768]{1,0:T(8,128)(2,1)S(1)} %get-tuple-element.75), channel_id=1, source_target_pairs={{4,0},{8,4},{12,8},{5,1},{9,5},{13,9},{6,2},{10,6},{14,10},{7,3},{... | collective-permute-start | bytes 967688 | tf_op jit(solution)/shard_map/ppermute | solution.py:101
  14.6 0.0 copy-done
  14.6 0.0 copy-done.4
  14.6 0.0 copy-done.2
  14.6 0.0 copy-done.3
  14.6 11.5 %conv_inner.1 = (f32[6,16,14,8,128]{4,3,2,1,0:T(8,128)S(1)}, f32[6,121,8,128]{3,2,1,0:T(8,128)S(1)}, bf16[512,768]{1,0:T(8,128)(2,1)S(1)}, f32[512,256]{1,0:T(8,...) custom-call(bf16[16,64,768]{2,1,0:T(8,128)(2,1)S(1)} %bitcast.29, ...), custom_call_target="tpu_custom_call" | custom-call | flops 10000000000 | bytes 10000000 | tf_op jit(solution)/shard_map/conv_inner/pallas_call | solution.py:380
  26.2 0.0 collective-permute-done.2.top
  26.2 0.0 collective-permute-done.3.bottom
  26.2 2.4 %conv_edge.1 = (f32[6,3,14,8,128]{4,3,2,1,0:T(8,128)S(1)}, f32[6,3,14,8,128]{4,3,2,1,0:T(8,128)S(1)}, bf16[512,768]{1,0:T(8,128)(2,1)S(1)}, f32[512,256]{1,0:T(8...) custom-call(s32[1]{0:T(128)} %bitcast.3.flag, ...), custom_call_target="tpu_custom_call" | custom-call | flops 6000000000 | bytes 6000000 | tf_op jit(solution)/shard_map/conv_edge/pallas_call | solution.py:411
  28.6 0.0 copy-start.1
  28.6 0.0 copy-start.5
  28.6 3.0 %collective-permute-start.4 = (f32[72,256]{1,0:T(8,128)S(1)}, f32[72,256]{1,0:T(8,128)S(1)}, u32[]{:S(2)}, u32[]{:S(2)}) collective-permute-start(f32[72,256]{1,0:T(8,128)S(1)} %get-tuple-element.82), channel_id=1, source_target_pairs={{0,1},{1,0},{2,3},{3,2},{4,5},{5,4},{6,7},{7,6},{8,9},{9,8},{10,11... | collective-permute-start | bytes 221192 | tf_op jit(solution)/shard_map/ppermute | solution.py:33
  31.6 0.9 collective-permute-done.4
  32.5 0.5 collective-permute-start.5
  33.0 0.9 prepare.1
  34.0 3.1 %collective-permute-done.5 = f32[72,256]{1,0:T(8,128)S(1)} collective-permute-done((f32[72,256]{1,0:T(8,128)S(1)}, f32[72,256]{1,0:T(8,128)S(1)}, u32[]{:S(2)}, u32[]{:S(2)}) %collective-permute-start.5) | collective-permute-done | bytes 73760 | tf_op jit(solution)/shard_map/ppermute | solution.py:33
  37.2 2.4 %collective-permute-start.6 = (f32[72,256]{1,0:T(8,128)S(1)}, f32[72,256]{1,0:T(8,128)S(1)}, u32[]{:S(2)}, u32[]{:S(2)}) collective-permute-start(f32[72,256]{1,0:T(8,128)S(1)} %add.38), channel_id=1, source_target_pairs={{0,4},{4,0},{8,12},{12,8},{1,5},{5,1},{9,13},{13,9},{2,6},{6,2},{1... | collective-permute-start | bytes 221192 | tf_op jit(solution)/shard_map/ppermute | solution.py:33
  39.6 2.3 %collective-permute-done.6 = f32[72,256]{1,0:T(8,128)S(1)} collective-permute-done((f32[72,256]{1,0:T(8,128)S(1)}, f32[72,256]{1,0:T(8,128)S(1)}, u32[]{:S(2)}, u32[]{:S(2)}) %collective-permute-start.6) | collective-permute-done | bytes 73760 | tf_op jit(solution)/shard_map/ppermute | solution.py:33
  41.9 3.1 %collective-permute-start.7 = (f32[72,256]{1,0:T(8,128)S(1)}, f32[72,256]{1,0:T(8,128)S(1)}, u32[]{:S(2)}, u32[]{:S(2)}) collective-permute-start(f32[72,256]{1,0:T(8,128)S(1)} %add.39), channel_id=1, source_target_pairs={{0,8},{4,12},{8,0},{12,4},{1,9},{5,13},{9,1},{13,5},{2,10},{6,14},... | collective-permute-start | bytes 221192 | tf_op jit(solution)/shard_map/ppermute | solution.py:33
  45.0 2.3 %collective-permute-done.7 = f32[72,256]{1,0:T(8,128)S(1)} collective-permute-done((f32[72,256]{1,0:T(8,128)S(1)}, f32[72,256]{1,0:T(8,128)S(1)}, u32[]{:S(2)}, u32[]{:S(2)}) %collective-permute-start.7) | collective-permute-done | bytes 73760 | tf_op jit(solution)/shard_map/ppermute | solution.py:33
  47.4 0.1 collective-permute-start.8
  48.1 0.6 collective-permute-done.8.other
  48.7 9.8 %head.1 = (f32[272,256]{1,0:T(8,128)S(1)}, f32[320,768]{1,0:T(8,128)S(1)}, bf16[512,768]{1,0:T(8,128)(2,1)S(1)}, bf16[512,768]{1,0:T(8,128)(2,1)S(1)}) custom-call(s32[1]{0:T(128)} %bitcast.3.flag, s32[1]{0:T(128)S(6)} %copy.23.label, f32[10]{0:T(128)S(1)} %copy-done.5, f32[72,256]{1,0:T(8,128)S(1)} %add.40.own, f32[72,256]{1,0:T(8,128)S(1)} %collective-permute-done.8.other, ...), custom_call_target="tpu_custom_call" | custom-call | flops 10000000000 | bytes 10000000 | tf_op jit(solution)/shard_map/head/pallas_call | solution.py:591
  58.5 1.6 %collective-permute-start.9 = (f32[272,256]{1,0:T(8,128)S(1)}, f32[272,256]{1,0:T(8,128)S(1)}, u32[]{:S(2)}, u32[]{:S(2)}) collective-permute-start(f32[272,256]{1,0:T(8,128)S(1)} %get-tuple-element.115.refs_0_), channel_id=1, source_target_pairs={{0,16},{16,0},{1,17},{17,1},{2,18},{18,2},{3,19},{19,3},{4,20},{20... | collective-permute-start | bytes 835592 | tf_op jit(solution)/shard_map/ppermute | solution.py:33
  60.0 6.8 %tap_grads.2.payload_in = f32[320,768]{1,0:T(8,128)S(1)} custom-call(f32[6,16,14,8,128]{4,3,2,1,0:T(8,128)S(1)} %get-tuple-element.72.spread_in, f32[6,3,14,8,128]{4,3,2,1,0:T(8,128)S(1)} %get-tuple-element.79.spread_top, f32[6,3,14,8,128]{4,3,2,1,0:T(8,128)S(1)} %get-tuple-element.80.spread_bottom, ...), custom_call_target="tpu_custom_call", output_to_operand_aliasing={{}: (5, {})} | custom-call | flops 10000000000 | bytes 10000000 | tf_op jit(solution)/shard_map/tap_grads/pallas_call | solution.py:736
  66.8 0.4 collective-permute-done.9.refs_1_
  67.2 1.3 %tap_grads.3 = f32[320,768]{1,0:T(8,128)S(1)} custom-call(f32[6,16,14,8,128]{4,3,2,1,0:T(8,128)S(1)} %get-tuple-element.72.spread_in, f32[6,3,14,8,128]{4,3,2,1,0:T(8,128)S(1)} %get-tuple-element.79.spread_top, f32[6,3,14,8,128]{4,3,2,1,0:T(8,128)S(1)} %get-tuple-element.80.spread_bottom, ...), custom_call_target="tpu_custom_call", output_to_operand_aliasing={{}: (5, {})} | custom-call | flops 2000000000 | bytes 2000000 | tf_op jit(solution)/shard_map/tap_grads/pallas_call | solution.py:736
  68.6 0.1 collective-permute-start.10
  68.7 1.5 %collective-permute-done.10 = bf16[160,768]{1,0:T(8,128)(2,1)S(1)} collective-permute-done((bf16[160,768]{1,0:T(8,128)(2,1)S(1)}, bf16[160,768]{1,0:T(8,128)(2,1)S(1)}, u32[]{:S(2)}, u32[]{:S(2)}) %collective-permute-start.10) | collective-permute-done | bytes 245792 | tf_op jit(solution)/shard_map/ppermute | solution.py:33
  70.2 0.1 convert_add_fusion
  70.3 0.6 collective-permute-start.11
  70.9 1.5 %collective-permute-start.12 = (bf16[40,768]{1,0:T(8,128)(2,1)S(1)}, bf16[40,768]{1,0:T(8,128)(2,1)S(1)}, u32[]{:S(2)}, u32[]{:S(2)}) collective-permute-start(bf16[40,768]{1,0:T(8,128)(2,1)S(1)} %get-tuple-element.131), channel_id=1, source_target_pairs={{0,16},{1,17},{2,18},{3,19},{16,0},{17,1},{18,2},{19,3},{4,20},{5,... | collective-permute-start | bytes 184328 | tf_op jit(solution)/shard_map/ppermute | solution.py:72
  72.4 1.4 %collective-permute-start.13 = (bf16[40,768]{1,0:T(8,128)(2,1)S(1)}, bf16[40,768]{1,0:T(8,128)(2,1)S(1)}, u32[]{:S(2)}, u32[]{:S(2)}) collective-permute-start(bf16[40,768]{1,0:T(8,128)(2,1)S(1)} %get-tuple-element.130), channel_id=1, source_target_pairs={{0,18},{1,19},{2,16},{3,17},{16,2},{17,3},{18,0},{19,1},{4,22},{5,... | collective-permute-start | bytes 184328 | tf_op jit(solution)/shard_map/ppermute | solution.py:72
  73.9 0.7 collective-permute-done.11
  74.6 0.6 collective-permute-done.12
  75.1 2.4 %collective-permute-done.13 = bf16[40,768]{1,0:T(8,128)(2,1)S(1)} collective-permute-done((bf16[40,768]{1,0:T(8,128)(2,1)S(1)}, bf16[40,768]{1,0:T(8,128)(2,1)S(1)}, u32[]{:S(2)}, u32[]{:S(2)}) %collective-permute-start.13) | collective-permute-done | bytes 61472 | tf_op jit(solution)/shard_map/ppermute | solution.py:72
  77.6 2.0 %collective-permute-start.14 = (bf16[40,768]{1,0:T(8,128)(2,1)S(1)}, bf16[40,768]{1,0:T(8,128)(2,1)S(1)}, u32[]{:S(2)}, u32[]{:S(2)}) collective-permute-start(bf16[40,768]{1,0:T(8,128)(2,1)S(1)} %fusion.1), channel_id=1, source_target_pairs={{0,4},{4,0},{8,12},{12,8},{1,5},{5,1},{9,13},{13,9},{2,6},{6,2},{1... | collective-permute-start | bytes 184328 | tf_op jit(solution)/shard_map/ppermute | solution.py:33
  79.5 2.3 %collective-permute-done.14 = bf16[40,768]{1,0:T(8,128)(2,1)S(1)} collective-permute-done((bf16[40,768]{1,0:T(8,128)(2,1)S(1)}, bf16[40,768]{1,0:T(8,128)(2,1)S(1)}, u32[]{:S(2)}, u32[]{:S(2)}) %collective-permute-start.14) | collective-permute-done | bytes 61472 | tf_op jit(solution)/shard_map/ppermute | solution.py:33
  81.9 3.2 %collective-permute-start.15 = (bf16[40,768]{1,0:T(8,128)(2,1)S(1)}, bf16[40,768]{1,0:T(8,128)(2,1)S(1)}, u32[]{:S(2)}, u32[]{:S(2)}) collective-permute-start(bf16[40,768]{1,0:T(8,128)(2,1)S(1)} %add_convert_fusion.1), channel_id=1, source_target_pairs={{0,8},{4,12},{8,0},{12,4},{1,9},{5,13},{9,1},{13,5},{2,10},{6,14},... | collective-permute-start | bytes 184328 | tf_op jit(solution)/shard_map/ppermute | solution.py:33
  85.1 2.2 %collective-permute-done.15 = bf16[40,768]{1,0:T(8,128)(2,1)S(1)} collective-permute-done((bf16[40,768]{1,0:T(8,128)(2,1)S(1)}, bf16[40,768]{1,0:T(8,128)(2,1)S(1)}, u32[]{:S(2)}, u32[]{:S(2)}) %collective-permute-start.15) | collective-permute-done | bytes 61472 | tf_op jit(solution)/shard_map/ppermute | solution.py:33
  87.3 0.1 slice_reduce_fusion
  87.5 0.1 slice_reduce_fusion.1
  87.6 1.6 %collective-permute-start.16 = (bf16[40,768]{1,0:T(8,128)(2,1)S(1)}, bf16[40,768]{1,0:T(8,128)(2,1)S(1)}, u32[]{:S(2)}, u32[]{:S(2)}) collective-permute-start(bf16[40,768]{1,0:T(8,128)(2,1)S(1)} %add_convert_fusion), channel_id=1, source_target_pairs={{0,2},{1,3},{2,0},{3,1},{16,18},{17,19},{18,16},{19,17},{4,6},{5,7... | collective-permute-start | bytes 184328 | tf_op jit(solution)/shard_map/ppermute | solution.py:81
  89.1 0.5 collective-permute-start.17
  89.7 1.5 %collective-permute-start.18 = (bf16[40,768]{1,0:T(8,128)(2,1)S(1)}, bf16[40,768]{1,0:T(8,128)(2,1)S(1)}, u32[]{:S(2)}, u32[]{:S(2)}) collective-permute-start(bf16[40,768]{1,0:T(8,128)(2,1)S(1)} %add_convert_fusion), channel_id=1, source_target_pairs={{0,18},{1,19},{2,16},{3,17},{16,2},{17,3},{18,0},{19,1},{4,22},{5,... | collective-permute-start | bytes 184328 | tf_op jit(solution)/shard_map/ppermute | solution.py:81
  91.1 1.9 %multiply_add_fusion = f32[10,256,256]{2,1,0:T(8,128)} fusion(f32[256,256]{1,0:T(8,128)S(1)} %slice.57, f32[10]{0:T(128)S(1)} %slice_reduce_fusion, f32[256,256]{1,0:T(8,128)S(1)} %slice.55, f32[10]{0:T(128)S(1)} %slice_reduce_fusion.1), kind=kLoop, calls=%fused_computation | loop fusion | flops 1966080 | bytes 3145808 | tf_op jit(solution)/shard_map/add | solution.py:42
  93.0 0.0 collective-permute-done.16
  93.1 0.3 collective-permute-done.17
  93.4 1.4 %collective-permute-done.18 = bf16[40,768]{1,0:T(8,128)(2,1)S(1)} collective-permute-done((bf16[40,768]{1,0:T(8,128)(2,1)S(1)}, bf16[40,768]{1,0:T(8,128)(2,1)S(1)}, u32[]{:S(2)}, u32[]{:S(2)}) %collective-permute-start.18) | collective-permute-done | bytes 61472 | tf_op jit(solution)/shard_map/ppermute | solution.py:81
  94.8 0.1 collective-permute-start.19
  94.9 1.5 %collective-permute-done.19.other = bf16[160,768]{1,0:T(8,128)(2,1)S(1)} collective-permute-done((bf16[160,768]{1,0:T(8,128)(2,1)S(1)}, bf16[160,768]{1,0:T(8,128)(2,1)S(1)}, u32[]{:S(2)}, u32[]{:S(2)}) %collective-permute-start.19) | collective-permute-done | bytes 245792 | tf_op jit(solution)/shard_map/ppermute | solution.py:33
  96.4 1.0 %finish.1 = (f32[768,256]{1,0:T(8,128)}, f32[7,7,768]{2,1,0:T(8,128)}, f32[768]{0:T(1024)}, f32[256]{0:T(256)}, f32[10]{0:T(128)}, /*index=5*/f32[1]{0:T(128)}) custom-call(s32[1]{0:T(128)} %bitcast.3.flag, bf16[160,768]{1,0:T(8,128)(2,1)S(1)} %bitcast.31, bf16[160,768]{1,0:T(8,128)(2,1)S(1)} %collective-permute-done.19.other, ...), custom_call_target="tpu_custom_call" | custom-call | flops 1000000000 | bytes 1000000 | tf_op jit(solution)/shard_map/finish/pallas_call | solution.py:780
  (25 shorter events, 0.5 us)
Async XLA Ops:
  0.6 14.0 %copy-start = (bf16[1,16,64,768]{3,2,1,0:T(8,128)(2,1)S(1)}, bf16[1,16,64,768]{3,2,1,0:T(8,128)(2,1)}, u32[]{:S(2)}) copy-start(bf16[1,16,64,768]{3,2,1,0:T(8,128)(2,1)} %param.8) | copy-start | bytes 4718596
  0.6 14.0 %copy-start.4 = (f32[256]{0:T(256)S(1)}, f32[256]{0:T(256)}, u32[]{:S(2)}) copy-start(f32[256]{0:T(256)} %param.12) | copy-start | bytes 3076
  0.7 14.0 %copy-start.2 = (bf16[768,256]{1,0:T(8,128)(2,1)S(1)}, bf16[768,256]{1,0:T(8,128)(2,1)}, u32[]{:S(2)}) copy-start(bf16[768,256]{1,0:T(8,128)(2,1)} %reduce_weight.5) | copy-start | bytes 1179652
  0.7 14.0 %copy-start.3 = (f32[7,7,768]{2,1,0:T(8,128)S(1)}, f32[7,7,768]{2,1,0:T(8,128)}, u32[]{:S(2)}) copy-start(f32[7,7,768]{2,1,0:T(8,128)} %weight.1) | copy-start | bytes 451588
  1.9 5.5 %collective-permute-start = (bf16[16,3,768]{2,1,0:T(4,128)(2,1)S(1)}, bf16[16,3,768]{2,1,0:T(4,128)(2,1)S(1)}, u32[]{:S(2)}, u32[]{:S(2)}) collective-permute-start(bf16[16,3,768]{2,1,0:T(4,128)(2,1)S(1)} %get-tuple-element.127), channel_id=1, source_target_pairs={{0,1},{1,2},{2,3},{4,5},{5,6},{6,7},{8,9},{9,10},{10,11},{12,13},{... | collective-permute-start | bytes 221192 | tf_op jit(solution)/shard_map/ppermute | solution.py:97
  4.3 5.3 %collective-permute-start.1 = (bf16[16,3,768]{2,1,0:T(4,128)(2,1)S(1)}, bf16[16,3,768]{2,1,0:T(4,128)(2,1)S(1)}, u32[]{:S(2)}, u32[]{:S(2)}) collective-permute-start(bf16[16,3,768]{2,1,0:T(4,128)(2,1)S(1)} %get-tuple-element.128), channel_id=1, source_target_pairs={{1,0},{2,1},{3,2},{5,4},{6,5},{7,6},{9,8},{10,9},{11,10},{13,12},{... | collective-permute-start | bytes 221192 | tf_op jit(solution)/shard_map/ppermute | solution.py:101
  9.8 16.4 %collective-permute-start.2 = (bf16[210,768]{1,0:T(8,128)(2,1)S(1)}, bf16[210,768]{1,0:T(8,128)(2,1)S(1)}, u32[]{:S(2)}, u32[]{:S(2)}) collective-permute-start(bf16[210,768]{1,0:T(8,128)(2,1)S(1)} %get-tuple-element.74), channel_id=1, source_target_pairs={{0,4},{4,8},{8,12},{1,5},{5,9},{9,13},{2,6},{6,10},{10,14},{3,7},{... | collective-permute-start | bytes 967688 | tf_op jit(solution)/shard_map/ppermute | solution.py:97
  13.3 12.9 %collective-permute-start.3 = (bf16[210,768]{1,0:T(8,128)(2,1)S(1)}, bf16[210,768]{1,0:T(8,128)(2,1)S(1)}, u32[]{:S(2)}, u32[]{:S(2)}) collective-permute-start(bf16[210,768]{1,0:T(8,128)(2,1)S(1)} %get-tuple-element.75), channel_id=1, source_target_pairs={{4,0},{8,4},{12,8},{5,1},{9,5},{13,9},{6,2},{10,6},{14,10},{7,3},{... | collective-permute-start | bytes 967688 | tf_op jit(solution)/shard_map/ppermute | solution.py:101
  28.6 20.1 %copy-start.1 = (bf16[10,256,256]{2,1,0:T(8,128)(2,1)S(1)}, bf16[10,256,256]{2,1,0:T(8,128)(2,1)}, u32[]{:S(2)}) copy-start(bf16[10,256,256]{2,1,0:T(8,128)(2,1)} %class_weight.1) | copy-start | bytes 3932164
  28.6 20.1 %copy-start.5 = (f32[10]{0:T(128)S(1)}, f32[10]{0:T(128)}, u32[]{:S(2)}) copy-start(f32[10]{0:T(128)} %class_bias.1) | copy-start | bytes 124
  28.6 3.9 %collective-permute-start.4 = (f32[72,256]{1,0:T(8,128)S(1)}, f32[72,256]{1,0:T(8,128)S(1)}, u32[]{:S(2)}, u32[]{:S(2)}) collective-permute-start(f32[72,256]{1,0:T(8,128)S(1)} %get-tuple-element.82), channel_id=1, source_target_pairs={{0,1},{1,0},{2,3},{3,2},{4,5},{5,4},{6,7},{7,6},{8,9},{9,8},{10,11... | collective-permute-start | bytes 221192 | tf_op jit(solution)/shard_map/ppermute | solution.py:33
  32.5 4.6 %collective-permute-start.5 = (f32[72,256]{1,0:T(8,128)S(1)}, f32[72,256]{1,0:T(8,128)S(1)}, u32[]{:S(2)}, u32[]{:S(2)}) collective-permute-start(f32[72,256]{1,0:T(8,128)S(1)} %add.37), channel_id=1, source_target_pairs={{0,2},{1,3},{2,0},{3,1},{4,6},{5,7},{6,4},{7,5},{8,10},{9,11},{10,... | collective-permute-start | bytes 221192 | tf_op jit(solution)/shard_map/ppermute | solution.py:33
  37.2 4.8 %collective-permute-start.6 = (f32[72,256]{1,0:T(8,128)S(1)}, f32[72,256]{1,0:T(8,128)S(1)}, u32[]{:S(2)}, u32[]{:S(2)}) collective-permute-start(f32[72,256]{1,0:T(8,128)S(1)} %add.38), channel_id=1, source_target_pairs={{0,4},{4,0},{8,12},{12,8},{1,5},{5,1},{9,13},{13,9},{2,6},{6,2},{1... | collective-permute-start | bytes 221192 | tf_op jit(solution)/shard_map/ppermute | solution.py:33
  41.9 5.4 %collective-permute-start.7 = (f32[72,256]{1,0:T(8,128)S(1)}, f32[72,256]{1,0:T(8,128)S(1)}, u32[]{:S(2)}, u32[]{:S(2)}) collective-permute-start(f32[72,256]{1,0:T(8,128)S(1)} %add.39), channel_id=1, source_target_pairs={{0,8},{4,12},{8,0},{12,4},{1,9},{5,13},{9,1},{13,5},{2,10},{6,14},... | collective-permute-start | bytes 221192 | tf_op jit(solution)/shard_map/ppermute | solution.py:33
  47.4 1.3 %collective-permute-start.8 = (f32[72,256]{1,0:T(8,128)S(1)}, f32[72,256]{1,0:T(8,128)S(1)}, u32[]{:S(2)}, u32[]{:S(2)}) collective-permute-start(f32[72,256]{1,0:T(8,128)S(1)} %add.40.own), channel_id=1, source_target_pairs={{0,1},{1,0},{2,3},{3,2},{4,5},{5,4},{6,7},{7,6},{8,9},{9,8},{10,11... | collective-permute-start | bytes 221192 | tf_op jit(solution)/shard_map/ppermute | solution.py:33
  58.5 8.8 %collective-permute-start.9 = (f32[272,256]{1,0:T(8,128)S(1)}, f32[272,256]{1,0:T(8,128)S(1)}, u32[]{:S(2)}, u32[]{:S(2)}) collective-permute-start(f32[272,256]{1,0:T(8,128)S(1)} %get-tuple-element.115.refs_0_), channel_id=1, source_target_pairs={{0,16},{16,0},{1,17},{17,1},{2,18},{18,2},{3,19},{19,3},{4,20},{20... | collective-permute-start | bytes 835592 | tf_op jit(solution)/shard_map/ppermute | solution.py:33
  68.6 1.6 %collective-permute-start.10 = (bf16[160,768]{1,0:T(8,128)(2,1)S(1)}, bf16[160,768]{1,0:T(8,128)(2,1)S(1)}, u32[]{:S(2)}, u32[]{:S(2)}) collective-permute-start(bf16[160,768]{1,0:T(8,128)(2,1)S(1)} %select_convert_fusion), channel_id=1, source_target_pairs={{0,1},{1,0},{2,3},{3,2},{4,5},{5,4},{6,7},{7,6},{8,9},{9,8},{10,11... | collective-permute-start | bytes 737288 | tf_op jit(solution)/shard_map/ppermute | solution.py:33
  70.3 4.3 %collective-permute-start.11 = (bf16[40,768]{1,0:T(8,128)(2,1)S(1)}, bf16[40,768]{1,0:T(8,128)(2,1)S(1)}, u32[]{:S(2)}, u32[]{:S(2)}) collective-permute-start(bf16[40,768]{1,0:T(8,128)(2,1)S(1)} %get-tuple-element.129), channel_id=1, source_target_pairs={{0,2},{1,3},{2,0},{3,1},{16,18},{17,19},{18,16},{19,17},{4,6},{5,7... | collective-permute-start | bytes 184328 | tf_op jit(solution)/shard_map/ppermute | solution.py:72
  70.9 4.2 %collective-permute-start.12 = (bf16[40,768]{1,0:T(8,128)(2,1)S(1)}, bf16[40,768]{1,0:T(8,128)(2,1)S(1)}, u32[]{:S(2)}, u32[]{:S(2)}) collective-permute-start(bf16[40,768]{1,0:T(8,128)(2,1)S(1)} %get-tuple-element.131), channel_id=1, source_target_pairs={{0,16},{1,17},{2,18},{3,19},{16,0},{17,1},{18,2},{19,3},{4,20},{5,... | collective-permute-start | bytes 184328 | tf_op jit(solution)/shard_map/ppermute | solution.py:72
  72.4 5.1 %collective-permute-start.13 = (bf16[40,768]{1,0:T(8,128)(2,1)S(1)}, bf16[40,768]{1,0:T(8,128)(2,1)S(1)}, u32[]{:S(2)}, u32[]{:S(2)}) collective-permute-start(bf16[40,768]{1,0:T(8,128)(2,1)S(1)} %get-tuple-element.130), channel_id=1, source_target_pairs={{0,18},{1,19},{2,16},{3,17},{16,2},{17,3},{18,0},{19,1},{4,22},{5,... | collective-permute-start | bytes 184328 | tf_op jit(solution)/shard_map/ppermute | solution.py:72
  77.6 4.3 %collective-permute-start.14 = (bf16[40,768]{1,0:T(8,128)(2,1)S(1)}, bf16[40,768]{1,0:T(8,128)(2,1)S(1)}, u32[]{:S(2)}, u32[]{:S(2)}) collective-permute-start(bf16[40,768]{1,0:T(8,128)(2,1)S(1)} %fusion.1), channel_id=1, source_target_pairs={{0,4},{4,0},{8,12},{12,8},{1,5},{5,1},{9,13},{13,9},{2,6},{6,2},{1... | collective-permute-start | bytes 184328 | tf_op jit(solution)/shard_map/ppermute | solution.py:33
  81.9 5.4 %collective-permute-start.15 = (bf16[40,768]{1,0:T(8,128)(2,1)S(1)}, bf16[40,768]{1,0:T(8,128)(2,1)S(1)}, u32[]{:S(2)}, u32[]{:S(2)}) collective-permute-start(bf16[40,768]{1,0:T(8,128)(2,1)S(1)} %add_convert_fusion.1), channel_id=1, source_target_pairs={{0,8},{4,12},{8,0},{12,4},{1,9},{5,13},{9,1},{13,5},{2,10},{6,14},... | collective-permute-start | bytes 184328 | tf_op jit(solution)/shard_map/ppermute | solution.py:33
  87.6 5.5 %collective-permute-start.16 = (bf16[40,768]{1,0:T(8,128)(2,1)S(1)}, bf16[40,768]{1,0:T(8,128)(2,1)S(1)}, u32[]{:S(2)}, u32[]{:S(2)}) collective-permute-start(bf16[40,768]{1,0:T(8,128)(2,1)S(1)} %add_convert_fusion), channel_id=1, source_target_pairs={{0,2},{1,3},{2,0},{3,1},{16,18},{17,19},{18,16},{19,17},{4,6},{5,7... | collective-permute-start | bytes 184328 | tf_op jit(solution)/shard_map/ppermute | solution.py:81
  89.1 4.2 %collective-permute-start.17 = (bf16[40,768]{1,0:T(8,128)(2,1)S(1)}, bf16[40,768]{1,0:T(8,128)(2,1)S(1)}, u32[]{:S(2)}, u32[]{:S(2)}) collective-permute-start(bf16[40,768]{1,0:T(8,128)(2,1)S(1)} %add_convert_fusion), channel_id=1, source_target_pairs={{0,16},{1,17},{2,18},{3,19},{16,0},{17,1},{18,2},{19,3},{4,20},{5,... | collective-permute-start | bytes 184328 | tf_op jit(solution)/shard_map/ppermute | solution.py:81
  89.7 5.1 %collective-permute-start.18 = (bf16[40,768]{1,0:T(8,128)(2,1)S(1)}, bf16[40,768]{1,0:T(8,128)(2,1)S(1)}, u32[]{:S(2)}, u32[]{:S(2)}) collective-permute-start(bf16[40,768]{1,0:T(8,128)(2,1)S(1)} %add_convert_fusion), channel_id=1, source_target_pairs={{0,18},{1,19},{2,16},{3,17},{16,2},{17,3},{18,0},{19,1},{4,22},{5,... | collective-permute-start | bytes 184328 | tf_op jit(solution)/shard_map/ppermute | solution.py:81
  94.8 1.6 %collective-permute-start.19 = (bf16[160,768]{1,0:T(8,128)(2,1)S(1)}, bf16[160,768]{1,0:T(8,128)(2,1)S(1)}, u32[]{:S(2)}, u32[]{:S(2)}) collective-permute-start(bf16[160,768]{1,0:T(8,128)(2,1)S(1)} %bitcast.30), channel_id=1, source_target_pairs={{0,1},{1,0},{2,3},{3,2},{4,5},{5,4},{6,7},{7,6},{8,9},{9,8},{10,11... | collective-permute-start | bytes 737288 | tf_op jit(solution)/shard_map/ppermute | solution.py:33

commit v12 on v11

--- a/solution.py
+++ b/solution.py
@@ -486,9 +486,9 @@
 
 def head_kernel(
     flag, label, class_bias, own, other, class_weight,
-    feat_inner, feat_edge, gate_inner, gate_edge, conv_turned, reduce_turned,
-    root_out, payload, conv_inner_out, conv_edge_out,
-    sums, pre, *, count, image_count,
+    feat_inner, feat_edge, gate_inner, gate_edge,
+    root_out, payload, pre,
+    sums, *, count, image_count,
 ):
     width = root_out.shape[1]
     half = width // 2
@@ -573,42 +573,27 @@
     payload[width + taps + 1 : width + taps + 2, :width] = jnp.sum(
         pre_grad.astype(wide), axis=0, keepdims=True
     )
-    for first in range(0, conv_turned.shape[0], width):
-        payload[:width, first : first + width] = jnp.dot(
-            conv_turned[first : first + width, :], pre_grad, preferred_element_type=wide
-        )
-    for out, start in ((conv_inner_out, 0), (conv_edge_out, inner)):
-        out[...] = jnp.dot(
-            pre[start : start + out.shape[0], :], reduce_turned[...], preferred_element_type=wide
-        ).astype(narrow)
-
-
-def head(flag, label, class_bias, own, other, class_weight, prepared, count, image_count):
-    feat_inner, feat_edge, gate_inner, gate_edge, conv_turned, reduce_turned = prepared
-    width, channels = reduce_turned.shape
+
+
+def head(flag, label, class_bias, own, other, class_weight, prepared, channels, count, image_count):
+    feat_inner, feat_edge = prepared[:2]
+    width = feat_inner.shape[1]
     inner, edge = feat_inner.shape[0], feat_edge.shape[0]
     slots = -(-(class_weight.shape[0] + 2) // GROUPS) * GROUPS
     return pl.pallas_call(
         functools.partial(head_kernel, count=count, image_count=image_count),
-        in_specs=[in_smem] * 3 + [in_vmem] * 9,
-        out_specs=[in_vmem] * 4,
+        in_specs=[in_smem] * 3 + [in_vmem] * 7,
+        out_specs=[in_vmem] * 3,
         out_shape=[
             shape_of((width + slots, width)),
             shape_of((width + TAPS_ROWS, channels)),
-            shape_of((inner, channels), narrow),
-            shape_of((edge, channels), narrow),
+            shape_of((inner + edge, width), narrow),
         ],
-        scratch_shapes=[
-            pltpu.VMEM((2 * own.shape[0], width), wide),
-            pltpu.VMEM((inner + edge, width), narrow),
-        ],
+        scratch_shapes=[pltpu.VMEM((2 * own.shape[0], width), wide)],
         compiler_params=params(24),
         cost_estimate=cost(10),
         name="head",
-    )(
-        flag, label, class_bias, own, other, class_weight,
-        feat_inner, feat_edge, gate_inner, gate_edge, conv_turned, reduce_turned,
-    )
+    )(flag, label, class_bias, own, other, class_weight, *prepared)
 
 
 def prepare_kernel(
@@ -645,8 +630,8 @@
 
 
 def taps_kernel(
-    spread_in, spread_top, spread_bottom, grad_inner, grad_edge, payload_in, payload,
-    parts, grads, products, out, *, first, last,
+    spread_in, spread_top, spread_bottom, pre, conv_turned, reduce_turned, payload_in, payload,
+    parts, grads, products, out, conv_grad, *, first, last,
 ):
     rows = spread_in.shape[1]
     row_pairs, col_pairs = grads.shape[1:3]
@@ -655,16 +640,22 @@
     order = edge_rows(rows)
     taps = KERNEL * KERNEL
     base = payload.shape[0] - TAPS_ROWS
+    width = pre.shape[1]
+    halves = width // LANES
+
+    def fill_conv_grad(tile):
+        product = jnp.dot(pre[...], reduce_turned[:, lanes_of(tile)], preferred_element_type=wide)
+        conv_grad[tile % 2] = product.astype(narrow)
+
+    fill_conv_grad(first)
 
     def one_tile(tile, _):
         lanes = lanes_of(tile)
+        slot = tile % 2
 
         def grad_row(row):
-            if row in order:
-                source, place = grad_edge, order.index(row)
-            else:
-                source, place = grad_inner, row - SIDE
-            values = source[place * cols : (place + 1) * cols, lanes].astype(wide)
+            place = rows - 2 * SIDE + order.index(row) if row in order else row - SIDE
+            values = conv_grad[slot, place * cols : (place + 1) * cols, :].astype(wide)
             return [values[step * GROUPS : (step + 1) * GROUPS, :] for step in range(steps)]
 
         for pair in range(row_pairs):
@@ -725,30 +716,39 @@
         ]
         out[taps : taps + 1, :] = jnp.sum(sum(found[1:], found[0]), axis=0, keepdims=True)
         payload[pl.ds(base, taps + 1), lanes] = out[: taps + 1, :]
+        fill_conv_grad(jnp.minimum(tile + 1, last - 1))
+        weight_rows = pl.ds(pl.multiple_of(tile % halves * LANES, LANES), LANES)
+        weight_lanes = pl.ds(pl.multiple_of(tile // halves * width, width), width)
+        payload[weight_rows, weight_lanes] = jnp.dot(
+            conv_turned[pl.ds(pl.multiple_of(tile * LANES, LANES), LANES), :],
+            pre[...],
+            preferred_element_type=wide,
+        )
         return 0
 
     lax.fori_loop(first, last, one_tile, 0)
 
 
-def tap_grads(spreads, grads, payload, first, last):
+def tap_grads(spreads, pre, conv_turned, reduce_turned, payload, first, last):
     rows, groups = spreads[0].shape[1:3]
     row_pairs, col_pairs = rows // 2, (groups - KERNEL + 1) // 2
     return pl.pallas_call(
         functools.partial(taps_kernel, first=first, last=last),
-        in_specs=[in_vmem] * 6,
+        in_specs=[in_vmem] * 7,
         out_specs=in_vmem,
         out_shape=shape_of(payload.shape),
-        input_output_aliases={5: 0},
+        input_output_aliases={6: 0},
         scratch_shapes=[
             pltpu.VMEM((2, row_pairs + 3, 2 * col_pairs + 6, GROUPS, LANES), wide),
             pltpu.VMEM((9, row_pairs, col_pairs, GROUPS, LANES), wide),
             pltpu.VMEM((PRODUCTS, GROUPS, LANES), wide),
             pltpu.VMEM((TAPS_ROWS, LANES), wide),
+            pltpu.VMEM((2, pre.shape[0], LANES), narrow),
         ],
         compiler_params=params(16),
         cost_estimate=cost(2 * (last - first)),
         name="tap_grads",
-    )(*spreads, *grads, payload)
+    )(*spreads, pre, conv_turned, reduce_turned, payload)
 
 
 def finish_kernel(flag, own, other, *refs, image_count):
@@ -858,23 +858,24 @@
         sums = exchange(sums, "sy", shift, wide)
     other = swap(sums, "sx", 1)
 
-    root, payload, *grads = head(
+    root, payload, pre = head(
         flag,
         labels,
         class_bias,
         sums,
         other,
         class_weight,
-        (feat_in, feat_ed, gate_in, gate_ed, conv_turned, reduce_turned),
+        (feat_in, feat_ed, gate_in, gate_ed),
+        channels,
         count,
         image_count,
     )
     known = [root] + [swap(root, "dp", shift) for shift in range(1, lax.axis_size("dp"))]
     spreads = (spread, spread_top, spread_bottom)
     tiles = channels // LANES
-    payload = tap_grads(spreads, grads, payload, 0, tiles - 1)
+    payload = tap_grads(spreads, pre, conv_turned, reduce_turned, payload, 0, tiles - 1)
     payload, known = together((payload, known))
-    payload = tap_grads(spreads, grads, payload, tiles - 1, tiles)
+    payload = tap_grads(spreads, pre, conv_turned, reduce_turned, payload, tiles - 1, tiles)
 
     part = payload.shape[0] // 2
     low, high = payload[:part], payload[part:]

time: 97.9 us -> 99.8 us (1.019)
  Pallas kernels: 33.7 us -> 36.1 us
    pallas_call x2, Pallas kernels: 8.07 us -> 11.3 us  [tap_grads(): pl.pallas_call(functools.partial(taps_kernel, first=first, last=last), in...]
  transfers between devices with their start and end apart: 20 -> 20, of which waited for: 16 -> 14; matrix products, arithmetic and copies ran while one was open for 4% -> 4% of each run, Pallas kernels for 20% -> 22%
where the time goes in v12:
time: 99.8 us; the launch traced here: 99.5 us
  Pallas kernels  36.1 us (36%)
  starting transfers between devices  31.6 us (32%)
  waiting for transfers between devices  24.4 us (24%)
  local copies, waits for them, and re-layouts  3.56 us (4%)
  other arithmetic  2.14 us (2%)
  between operations  1.79 us (2%)
    ppermute x10, waiting for transfers between devices, swap(): return lax.ppermute(value, axis, [(i, i ^ shift) for i in range(count)])  16.8 us
    ppermute x10, starting transfers between devices, swap(): return lax.ppermute(value, axis, [(i, i ^ shift) for i in range(count)])  16 us
    pallas_call x1, Pallas kernels, conv_inner(): pl.pallas_call(inner_kernel, in_specs=[in_vmem] * 7, out_specs=[in_vmem]...  11.5 us
    pallas_call x2, Pallas kernels, tap_grads(): pl.pallas_call(functools.partial(taps_kernel, first=first, last=last), in...  11.3 us
    pallas_call x1, Pallas kernels, head(): pl.pallas_call(functools.partial(head_kernel, count=count, image_count=im...  8.89 us
    ppermute x2, starting transfers between devices, next_along(): lax.ppermute(value, axis, [(i, i + 1) for i in range(lax.axis_size(axis)...  5.86 us
    ppermute x3, starting transfers between devices, square_scatter(): lax.ppermute(piece(turn).astype(sent_as), axes, pairs[turn]).astype(wide)  3.55 us
    ppermute x3, starting transfers between devices, square_gather(): part = lax.ppermute(value, axes, pairs[turn]) if turn else value  3.55 us
  transfers between devices with their start and end apart: 20, of which 14 were waited for; matrix products, arithmetic and copies ran while one was open for 4% of the time, Pallas kernels for 22%

profile of v12, /device:TPU:0, one launch (start us, length us, event | category | flops | bytes accessed | tf_op | source)
XLA Modules:
  0.0 99.5 jit_solution(15245814546240354585)
XLA Ops:
  0.6 0.0 copy-start
  0.6 0.0 copy-start.4
  0.7 0.0 copy-start.2
  0.7 0.0 copy-start.3
  0.7 1.2 %fusion.6 = (bf16[16,3,768]{2,1,0:T(4,128)(2,1)S(1)}, bf16[16,3,768]{2,1,0:T(4,128)(2,1)S(1)}) fusion(bf16[16,64,768]{2,1,0:T(8,128)(2,1)} %bitcast.28), kind=kLoop, calls=%fused_computation.23 | loop fusion | bytes 294912 | tf_op jit(solution)/shard_map/slice | solution.py:821
  1.9 2.4 %collective-permute-start = (bf16[16,3,768]{2,1,0:T(4,128)(2,1)S(1)}, bf16[16,3,768]{2,1,0:T(4,128)(2,1)S(1)}, u32[]{:S(2)}, u32[]{:S(2)}) collective-permute-start(bf16[16,3,768]{2,1,0:T(4,128)(2,1)S(1)} %get-tuple-element.125), channel_id=1, source_target_pairs={{0,1},{1,2},{2,3},{4,5},{5,6},{6,7},{8,9},{9,10},{10,11},{12,13},{... | collective-permute-start | bytes 221192 | tf_op jit(solution)/shard_map/ppermute | solution.py:97
  4.3 1.3 %collective-permute-start.1 = (bf16[16,3,768]{2,1,0:T(4,128)(2,1)S(1)}, bf16[16,3,768]{2,1,0:T(4,128)(2,1)S(1)}, u32[]{:S(2)}, u32[]{:S(2)}) collective-permute-start(bf16[16,3,768]{2,1,0:T(4,128)(2,1)S(1)} %get-tuple-element.126), channel_id=1, source_target_pairs={{1,0},{2,1},{3,2},{5,4},{6,5},{7,6},{9,8},{10,9},{11,10},{13,12},{... | collective-permute-start | bytes 221192 | tf_op jit(solution)/shard_map/ppermute | solution.py:101
  5.6 1.1 %fusion.5 = (bf16[1,3,64,768]{3,2,1,0:T(8,128)(2,1)S(1)}, bf16[1,3,64,768]{3,2,1,0:T(8,128)(2,1)S(1)}) fusion(bf16[1,16,64,768]{3,2,1,0:T(8,128)(2,1)} %param.8), kind=kLoop, calls=%fused_computation.22 | loop fusion | bytes 1179648 | tf_op jit(solution)/shard_map/slice | solution.py:801
  6.7 0.7 broadcast_in_dim.31.bias
  7.4 0.0 collective-permute-done.left
  7.4 2.2 %collective-permute-done.1.right = bf16[16,3,768]{2,1,0:T(4,128)(2,1)S(1)} collective-permute-done((bf16[16,3,768]{2,1,0:T(4,128)(2,1)S(1)}, bf16[16,3,768]{2,1,0:T(4,128)(2,1)S(1)}, u32[]{:S(2)}, u32[]{:S(2)}) %collective-permute-start.1) | collective-permute-done | bytes 73760 | tf_op jit(solution)/shard_map/ppermute | solution.py:101
  9.8 3.5 %collective-permute-start.2 = (bf16[210,768]{1,0:T(8,128)(2,1)S(1)}, bf16[210,768]{1,0:T(8,128)(2,1)S(1)}, u32[]{:S(2)}, u32[]{:S(2)}) collective-permute-start(bf16[210,768]{1,0:T(8,128)(2,1)S(1)} %get-tuple-element.73), channel_id=1, source_target_pairs={{0,4},{4,8},{8,12},{1,5},{5,9},{9,13},{2,6},{6,10},{10,14},{3,7},{... | collective-permute-start | bytes 967688 | tf_op jit(solution)/shard_map/ppermute | solution.py:97
  13.3 1.3 %collective-permute-start.3 = (bf16[210,768]{1,0:T(8,128)(2,1)S(1)}, bf16[210,768]{1,0:T(8,128)(2,1)S(1)}, u32[]{:S(2)}, u32[]{:S(2)}) collective-permute-start(bf16[210,768]{1,0:T(8,128)(2,1)S(1)} %get-tuple-element.74), channel_id=1, source_target_pairs={{4,0},{8,4},{12,8},{5,1},{9,5},{13,9},{6,2},{10,6},{14,10},{7,3},{... | collective-permute-start | bytes 967688 | tf_op jit(solution)/shard_map/ppermute | solution.py:101
  14.6 0.0 copy-done
  14.6 0.0 copy-done.4
  14.6 0.0 copy-done.2
  14.6 0.0 copy-done.3
  14.6 11.5 %conv_inner.1 = (f32[6,16,14,8,128]{4,3,2,1,0:T(8,128)S(1)}, f32[6,121,8,128]{3,2,1,0:T(8,128)S(1)}, bf16[512,768]{1,0:T(8,128)(2,1)S(1)}, f32[512,256]{1,0:T(8,...) custom-call(bf16[16,64,768]{2,1,0:T(8,128)(2,1)S(1)} %bitcast.29, ...), custom_call_target="tpu_custom_call" | custom-call | flops 10000000000 | bytes 10000000 | tf_op jit(solution)/shard_map/conv_inner/pallas_call | solution.py:380
  26.2 0.0 collective-permute-done.2.top
  26.2 0.0 collective-permute-done.3.bottom
  26.2 2.4 %conv_edge.1 = (f32[6,3,14,8,128]{4,3,2,1,0:T(8,128)S(1)}, f32[6,3,14,8,128]{4,3,2,1,0:T(8,128)S(1)}, bf16[512,768]{1,0:T(8,128)(2,1)S(1)}, f32[512,256]{1,0:T(8...) custom-call(s32[1]{0:T(128)} %bitcast.3.flag, ...), custom_call_target="tpu_custom_call" | custom-call | flops 6000000000 | bytes 6000000 | tf_op jit(solution)/shard_map/conv_edge/pallas_call | solution.py:411
  28.6 0.0 copy-start.1
  28.6 0.0 copy-start.5
  28.6 3.0 %collective-permute-start.4 = (f32[72,256]{1,0:T(8,128)S(1)}, f32[72,256]{1,0:T(8,128)S(1)}, u32[]{:S(2)}, u32[]{:S(2)}) collective-permute-start(f32[72,256]{1,0:T(8,128)S(1)} %get-tuple-element.81), channel_id=1, source_target_pairs={{0,1},{1,0},{2,3},{3,2},{4,5},{5,4},{6,7},{7,6},{8,9},{9,8},{10,11... | collective-permute-start | bytes 221192 | tf_op jit(solution)/shard_map/ppermute | solution.py:33
  31.6 0.9 collective-permute-done.4
  32.5 0.5 collective-permute-start.5
  33.0 0.9 prepare.1
  34.0 3.1 %collective-permute-done.5 = f32[72,256]{1,0:T(8,128)S(1)} collective-permute-done((f32[72,256]{1,0:T(8,128)S(1)}, f32[72,256]{1,0:T(8,128)S(1)}, u32[]{:S(2)}, u32[]{:S(2)}) %collective-permute-start.5) | collective-permute-done | bytes 73760 | tf_op jit(solution)/shard_map/ppermute | solution.py:33
  37.2 2.4 %collective-permute-start.6 = (f32[72,256]{1,0:T(8,128)S(1)}, f32[72,256]{1,0:T(8,128)S(1)}, u32[]{:S(2)}, u32[]{:S(2)}) collective-permute-start(f32[72,256]{1,0:T(8,128)S(1)} %add.38), channel_id=1, source_target_pairs={{0,4},{4,0},{8,12},{12,8},{1,5},{5,1},{9,13},{13,9},{2,6},{6,2},{1... | collective-permute-start | bytes 221192 | tf_op jit(solution)/shard_map/ppermute | solution.py:33
  39.6 2.3 %collective-permute-done.6 = f32[72,256]{1,0:T(8,128)S(1)} collective-permute-done((f32[72,256]{1,0:T(8,128)S(1)}, f32[72,256]{1,0:T(8,128)S(1)}, u32[]{:S(2)}, u32[]{:S(2)}) %collective-permute-start.6) | collective-permute-done | bytes 73760 | tf_op jit(solution)/shard_map/ppermute | solution.py:33
  41.9 3.1 %collective-permute-start.7 = (f32[72,256]{1,0:T(8,128)S(1)}, f32[72,256]{1,0:T(8,128)S(1)}, u32[]{:S(2)}, u32[]{:S(2)}) collective-permute-start(f32[72,256]{1,0:T(8,128)S(1)} %add.39), channel_id=1, source_target_pairs={{0,8},{4,12},{8,0},{12,4},{1,9},{5,13},{9,1},{13,5},{2,10},{6,14},... | collective-permute-start | bytes 221192 | tf_op jit(solution)/shard_map/ppermute | solution.py:33
  45.0 2.3 %collective-permute-done.7 = f32[72,256]{1,0:T(8,128)S(1)} collective-permute-done((f32[72,256]{1,0:T(8,128)S(1)}, f32[72,256]{1,0:T(8,128)S(1)}, u32[]{:S(2)}, u32[]{:S(2)}) %collective-permute-start.7) | collective-permute-done | bytes 73760 | tf_op jit(solution)/shard_map/ppermute | solution.py:33
  47.4 0.1 collective-permute-start.8
  48.1 0.6 collective-permute-done.8.other
  48.7 8.9 %head.1 = (f32[272,256]{1,0:T(8,128)S(1)}, f32[320,768]{1,0:T(8,128)S(1)}, bf16[1024,256]{1,0:T(8,128)(2,1)S(1)}) custom-call(s32[1]{0:T(128)} %bitcast.3.flag, s32[1]{0:T(128)S(6)} %copy.23.label, f32[10]{0:T(128)S(1)} %copy-done.5, f32[72,256]{1,0:T(8,128)S(1)} %add.40.own, f32[72,256]{1,0:T(8,128)S(1)} %collective-permute-done.8.other, ...), custom_call_target="tpu_custom_call" | custom-call | flops 10000000000 | bytes 10000000 | tf_op jit(solution)/shard_map/head/pallas_call | solution.py:583
  57.6 1.6 %collective-permute-start.9 = (f32[272,256]{1,0:T(8,128)S(1)}, f32[272,256]{1,0:T(8,128)S(1)}, u32[]{:S(2)}, u32[]{:S(2)}) collective-permute-start(f32[272,256]{1,0:T(8,128)S(1)} %get-tuple-element.113.refs_0_), channel_id=1, source_target_pairs={{0,16},{16,0},{1,17},{17,1},{2,18},{18,2},{3,19},{19,3},{4,20},{20... | collective-permute-start | bytes 835592 | tf_op jit(solution)/shard_map/ppermute | solution.py:33
  59.2 9.4 %tap_grads.2.payload_in = f32[320,768]{1,0:T(8,128)S(1)} custom-call(f32[6,16,14,8,128]{4,3,2,1,0:T(8,128)S(1)} %get-tuple-element.71.spread_in, f32[6,3,14,8,128]{4,3,2,1,0:T(8,128)S(1)} %get-tuple-element.78.spread_top, f32[6,3,14,8,128]{4,3,2,1,0:T(8,128)S(1)} %get-tuple-element.79.spread_bottom, ...), custom_call_target="tpu_custom_call", output_to_operand_aliasing={{}: (6, {})} | custom-call | flops 10000000000 | bytes 10000000 | tf_op jit(solution)/shard_map/tap_grads/pallas_call | solution.py:735
  68.5 0.0 collective-permute-done.9.refs_1_
  68.5 1.9 %tap_grads.3 = f32[320,768]{1,0:T(8,128)S(1)} custom-call(f32[6,16,14,8,128]{4,3,2,1,0:T(8,128)S(1)} %get-tuple-element.71.spread_in, f32[6,3,14,8,128]{4,3,2,1,0:T(8,128)S(1)} %get-tuple-element.78.spread_top, f32[6,3,14,8,128]{4,3,2,1,0:T(8,128)S(1)} %get-tuple-element.79.spread_bottom, ...), custom_call_target="tpu_custom_call", output_to_operand_aliasing={{}: (6, {})} | custom-call | flops 2000000000 | bytes 2000000 | tf_op jit(solution)/shard_map/tap_grads/pallas_call | solution.py:735
  70.5 0.1 collective-permute-start.10
  70.6 1.5 %collective-permute-done.10 = bf16[160,768]{1,0:T(8,128)(2,1)S(1)} collective-permute-done((bf16[160,768]{1,0:T(8,128)(2,1)S(1)}, bf16[160,768]{1,0:T(8,128)(2,1)S(1)}, u32[]{:S(2)}, u32[]{:S(2)}) %collective-permute-start.10) | collective-permute-done | bytes 245792 | tf_op jit(solution)/shard_map/ppermute | solution.py:33
  72.1 0.1 convert_add_fusion
  72.2 0.6 collective-permute-start.11
  72.8 0.5 collective-permute-start.12
  73.3 2.4 %collective-permute-start.13 = (bf16[40,768]{1,0:T(8,128)(2,1)S(1)}, bf16[40,768]{1,0:T(8,128)(2,1)S(1)}, u32[]{:S(2)}, u32[]{:S(2)}) collective-permute-start(bf16[40,768]{1,0:T(8,128)(2,1)S(1)} %get-tuple-element.128), channel_id=1, source_target_pairs={{0,18},{1,19},{2,16},{3,17},{16,2},{17,3},{18,0},{19,1},{4,22},{5,... | collective-permute-start | bytes 184328 | tf_op jit(solution)/shard_map/ppermute | solution.py:72
  75.8 0.7 collective-permute-done.11
  76.5 1.2 %collective-permute-done.12 = bf16[40,768]{1,0:T(8,128)(2,1)S(1)} collective-permute-done((bf16[40,768]{1,0:T(8,128)(2,1)S(1)}, bf16[40,768]{1,0:T(8,128)(2,1)S(1)}, u32[]{:S(2)}, u32[]{:S(2)}) %collective-permute-start.12) | collective-permute-done | bytes 61472 | tf_op jit(solution)/shard_map/ppermute | solution.py:72
  77.6 1.2 %collective-permute-done.13 = bf16[40,768]{1,0:T(8,128)(2,1)S(1)} collective-permute-done((bf16[40,768]{1,0:T(8,128)(2,1)S(1)}, bf16[40,768]{1,0:T(8,128)(2,1)S(1)}, u32[]{:S(2)}, u32[]{:S(2)}) %collective-permute-start.13) | collective-permute-done | bytes 61472 | tf_op jit(solution)/shard_map/ppermute | solution.py:72
  78.8 2.0 %collective-permute-start.14 = (bf16[40,768]{1,0:T(8,128)(2,1)S(1)}, bf16[40,768]{1,0:T(8,128)(2,1)S(1)}, u32[]{:S(2)}, u32[]{:S(2)}) collective-permute-start(bf16[40,768]{1,0:T(8,128)(2,1)S(1)} %fusion.1), channel_id=1, source_target_pairs={{0,4},{4,0},{8,12},{12,8},{1,5},{5,1},{9,13},{13,9},{2,6},{6,2},{1... | collective-permute-start | bytes 184328 | tf_op jit(solution)/shard_map/ppermute | solution.py:33
  80.8 2.3 %collective-permute-done.14 = bf16[40,768]{1,0:T(8,128)(2,1)S(1)} collective-permute-done((bf16[40,768]{1,0:T(8,128)(2,1)S(1)}, bf16[40,768]{1,0:T(8,128)(2,1)S(1)}, u32[]{:S(2)}, u32[]{:S(2)}) %collective-permute-start.14) | collective-permute-done | bytes 61472 | tf_op jit(solution)/shard_map/ppermute | solution.py:33
  83.2 3.2 %collective-permute-start.15 = (bf16[40,768]{1,0:T(8,128)(2,1)S(1)}, bf16[40,768]{1,0:T(8,128)(2,1)S(1)}, u32[]{:S(2)}, u32[]{:S(2)}) collective-permute-start(bf16[40,768]{1,0:T(8,128)(2,1)S(1)} %add_convert_fusion.1), channel_id=1, source_target_pairs={{0,8},{4,12},{8,0},{12,4},{1,9},{5,13},{9,1},{13,5},{2,10},{6,14},... | collective-permute-start | bytes 184328 | tf_op jit(solution)/shard_map/ppermute | solution.py:33
  86.4 2.2 %collective-permute-done.15 = bf16[40,768]{1,0:T(8,128)(2,1)S(1)} collective-permute-done((bf16[40,768]{1,0:T(8,128)(2,1)S(1)}, bf16[40,768]{1,0:T(8,128)(2,1)S(1)}, u32[]{:S(2)}, u32[]{:S(2)}) %collective-permute-start.15) | collective-permute-done | bytes 61472 | tf_op jit(solution)/shard_map/ppermute | solution.py:33
  88.6 0.1 slice_reduce_fusion
  88.8 0.1 slice_reduce_fusion.1
  88.9 1.2 %collective-permute-start.16 = (bf16[40,768]{1,0:T(8,128)(2,1)S(1)}, bf16[40,768]{1,0:T(8,128)(2,1)S(1)}, u32[]{:S(2)}, u32[]{:S(2)}) collective-permute-start(bf16[40,768]{1,0:T(8,128)(2,1)S(1)} %add_convert_fusion), channel_id=1, source_target_pairs={{0,2},{1,3},{2,0},{3,1},{16,18},{17,19},{18,16},{19,17},{4,6},{5,7... | collective-permute-start | bytes 184328 | tf_op jit(solution)/shard_map/ppermute | solution.py:81
  90.1 1.5 %collective-permute-start.17 = (bf16[40,768]{1,0:T(8,128)(2,1)S(1)}, bf16[40,768]{1,0:T(8,128)(2,1)S(1)}, u32[]{:S(2)}, u32[]{:S(2)}) collective-permute-start(bf16[40,768]{1,0:T(8,128)(2,1)S(1)} %add_convert_fusion), channel_id=1, source_target_pairs={{0,16},{1,17},{2,18},{3,19},{16,0},{17,1},{18,2},{19,3},{4,20},{5,... | collective-permute-start | bytes 184328 | tf_op jit(solution)/shard_map/ppermute | solution.py:81
  91.6 0.9 collective-permute-start.18
  92.4 1.9 %multiply_add_fusion = f32[10,256,256]{2,1,0:T(8,128)} fusion(f32[256,256]{1,0:T(8,128)S(1)} %slice.57, f32[10]{0:T(128)S(1)} %slice_reduce_fusion, f32[256,256]{1,0:T(8,128)S(1)} %slice.55, f32[10]{0:T(128)S(1)} %slice_reduce_fusion.1), kind=kLoop, calls=%fused_computation | loop fusion | flops 1966080 | bytes 3145808 | tf_op jit(solution)/shard_map/add | solution.py:42
  94.3 0.0 collective-permute-done.16
  94.4 0.0 collective-permute-done.17
  94.4 2.3 %collective-permute-done.18 = bf16[40,768]{1,0:T(8,128)(2,1)S(1)} collective-permute-done((bf16[40,768]{1,0:T(8,128)(2,1)S(1)}, bf16[40,768]{1,0:T(8,128)(2,1)S(1)}, u32[]{:S(2)}, u32[]{:S(2)}) %collective-permute-start.18) | collective-permute-done | bytes 61472 | tf_op jit(solution)/shard_map/ppermute | solution.py:81
  96.7 0.1 collective-permute-start.19
  96.8 1.5 %collective-permute-done.19.other = bf16[160,768]{1,0:T(8,128)(2,1)S(1)} collective-permute-done((bf16[160,768]{1,0:T(8,128)(2,1)S(1)}, bf16[160,768]{1,0:T(8,128)(2,1)S(1)}, u32[]{:S(2)}, u32[]{:S(2)}) %collective-permute-start.19) | collective-permute-done | bytes 245792 | tf_op jit(solution)/shard_map/ppermute | solution.py:33
  98.3 1.0 %finish.1 = (f32[768,256]{1,0:T(8,128)}, f32[7,7,768]{2,1,0:T(8,128)}, f32[768]{0:T(1024)}, f32[256]{0:T(256)}, f32[10]{0:T(128)}, /*index=5*/f32[1]{0:T(128)}) custom-call(s32[1]{0:T(128)} %bitcast.3.flag, bf16[160,768]{1,0:T(8,128)(2,1)S(1)} %bitcast.31, bf16[160,768]{1,0:T(8,128)(2,1)S(1)} %collective-permute-done.19.other, ...), custom_call_target="tpu_custom_call" | custom-call | flops 1000000000 | bytes 1000000 | tf_op jit(solution)/shard_map/finish/pallas_call | solution.py:780
  (25 shorter events, 0.5 us)
Async XLA Ops:
  0.6 14.0 %copy-start = (bf16[1,16,64,768]{3,2,1,0:T(8,128)(2,1)S(1)}, bf16[1,16,64,768]{3,2,1,0:T(8,128)(2,1)}, u32[]{:S(2)}) copy-start(bf16[1,16,64,768]{3,2,1,0:T(8,128)(2,1)} %param.8) | copy-start | bytes 4718596
  0.6 14.0 %copy-start.4 = (f32[256]{0:T(256)S(1)}, f32[256]{0:T(256)}, u32[]{:S(2)}) copy-start(f32[256]{0:T(256)} %param.12) | copy-start | bytes 3076
  0.7 14.0 %copy-start.2 = (bf16[768,256]{1,0:T(8,128)(2,1)S(1)}, bf16[768,256]{1,0:T(8,128)(2,1)}, u32[]{:S(2)}) copy-start(bf16[768,256]{1,0:T(8,128)(2,1)} %reduce_weight.5) | copy-start | bytes 1179652
  0.7 14.0 %copy-start.3 = (f32[7,7,768]{2,1,0:T(8,128)S(1)}, f32[7,7,768]{2,1,0:T(8,128)}, u32[]{:S(2)}) copy-start(f32[7,7,768]{2,1,0:T(8,128)} %weight.1) | copy-start | bytes 451588
  1.9 5.5 %collective-permute-start = (bf16[16,3,768]{2,1,0:T(4,128)(2,1)S(1)}, bf16[16,3,768]{2,1,0:T(4,128)(2,1)S(1)}, u32[]{:S(2)}, u32[]{:S(2)}) collective-permute-start(bf16[16,3,768]{2,1,0:T(4,128)(2,1)S(1)} %get-tuple-element.125), channel_id=1, source_target_pairs={{0,1},{1,2},{2,3},{4,5},{5,6},{6,7},{8,9},{9,10},{10,11},{12,13},{... | collective-permute-start | bytes 221192 | tf_op jit(solution)/shard_map/ppermute | solution.py:97
  4.3 5.3 %collective-permute-start.1 = (bf16[16,3,768]{2,1,0:T(4,128)(2,1)S(1)}, bf16[16,3,768]{2,1,0:T(4,128)(2,1)S(1)}, u32[]{:S(2)}, u32[]{:S(2)}) collective-permute-start(bf16[16,3,768]{2,1,0:T(4,128)(2,1)S(1)} %get-tuple-element.126), channel_id=1, source_target_pairs={{1,0},{2,1},{3,2},{5,4},{6,5},{7,6},{9,8},{10,9},{11,10},{13,12},{... | collective-permute-start | bytes 221192 | tf_op jit(solution)/shard_map/ppermute | solution.py:101
  9.8 16.4 %collective-permute-start.2 = (bf16[210,768]{1,0:T(8,128)(2,1)S(1)}, bf16[210,768]{1,0:T(8,128)(2,1)S(1)}, u32[]{:S(2)}, u32[]{:S(2)}) collective-permute-start(bf16[210,768]{1,0:T(8,128)(2,1)S(1)} %get-tuple-element.73), channel_id=1, source_target_pairs={{0,4},{4,8},{8,12},{1,5},{5,9},{9,13},{2,6},{6,10},{10,14},{3,7},{... | collective-permute-start | bytes 967688 | tf_op jit(solution)/shard_map/ppermute | solution.py:97
  13.3 12.9 %collective-permute-start.3 = (bf16[210,768]{1,0:T(8,128)(2,1)S(1)}, bf16[210,768]{1,0:T(8,128)(2,1)S(1)}, u32[]{:S(2)}, u32[]{:S(2)}) collective-permute-start(bf16[210,768]{1,0:T(8,128)(2,1)S(1)} %get-tuple-element.74), channel_id=1, source_target_pairs={{4,0},{8,4},{12,8},{5,1},{9,5},{13,9},{6,2},{10,6},{14,10},{7,3},{... | collective-permute-start | bytes 967688 | tf_op jit(solution)/shard_map/ppermute | solution.py:101
  28.6 20.1 %copy-start.1 = (bf16[10,256,256]{2,1,0:T(8,128)(2,1)S(1)}, bf16[10,256,256]{2,1,0:T(8,128)(2,1)}, u32[]{:S(2)}) copy-start(bf16[10,256,256]{2,1,0:T(8,128)(2,1)} %class_weight.1) | copy-start | bytes 3932164
  28.6 20.1 %copy-start.5 = (f32[10]{0:T(128)S(1)}, f32[10]{0:T(128)}, u32[]{:S(2)}) copy-start(f32[10]{0:T(128)} %class_bias.1) | copy-start | bytes 124
  28.6 3.9 %collective-permute-start.4 = (f32[72,256]{1,0:T(8,128)S(1)}, f32[72,256]{1,0:T(8,128)S(1)}, u32[]{:S(2)}, u32[]{:S(2)}) collective-permute-start(f32[72,256]{1,0:T(8,128)S(1)} %get-tuple-element.81), channel_id=1, source_target_pairs={{0,1},{1,0},{2,3},{3,2},{4,5},{5,4},{6,7},{7,6},{8,9},{9,8},{10,11... | collective-permute-start | bytes 221192 | tf_op jit(solution)/shard_map/ppermute | solution.py:33
  32.5 4.6 %collective-permute-start.5 = (f32[72,256]{1,0:T(8,128)S(1)}, f32[72,256]{1,0:T(8,128)S(1)}, u32[]{:S(2)}, u32[]{:S(2)}) collective-permute-start(f32[72,256]{1,0:T(8,128)S(1)} %add.37), channel_id=1, source_target_pairs={{0,2},{1,3},{2,0},{3,1},{4,6},{5,7},{6,4},{7,5},{8,10},{9,11},{10,... | collective-permute-start | bytes 221192 | tf_op jit(solution)/shard_map/ppermute | solution.py:33
  37.2 4.8 %collective-permute-start.6 = (f32[72,256]{1,0:T(8,128)S(1)}, f32[72,256]{1,0:T(8,128)S(1)}, u32[]{:S(2)}, u32[]{:S(2)}) collective-permute-start(f32[72,256]{1,0:T(8,128)S(1)} %add.38), channel_id=1, source_target_pairs={{0,4},{4,0},{8,12},{12,8},{1,5},{5,1},{9,13},{13,9},{2,6},{6,2},{1... | collective-permute-start | bytes 221192 | tf_op jit(solution)/shard_map/ppermute | solution.py:33
  41.9 5.4 %collective-permute-start.7 = (f32[72,256]{1,0:T(8,128)S(1)}, f32[72,256]{1,0:T(8,128)S(1)}, u32[]{:S(2)}, u32[]{:S(2)}) collective-permute-start(f32[72,256]{1,0:T(8,128)S(1)} %add.39), channel_id=1, source_target_pairs={{0,8},{4,12},{8,0},{12,4},{1,9},{5,13},{9,1},{13,5},{2,10},{6,14},... | collective-permute-start | bytes 221192 | tf_op jit(solution)/shard_map/ppermute | solution.py:33
  47.4 1.3 %collective-permute-start.8 = (f32[72,256]{1,0:T(8,128)S(1)}, f32[72,256]{1,0:T(8,128)S(1)}, u32[]{:S(2)}, u32[]{:S(2)}) collective-permute-start(f32[72,256]{1,0:T(8,128)S(1)} %add.40.own), channel_id=1, source_target_pairs={{0,1},{1,0},{2,3},{3,2},{4,5},{5,4},{6,7},{7,6},{8,9},{9,8},{10,11... | collective-permute-start | bytes 221192 | tf_op jit(solution)/shard_map/ppermute | solution.py:33
  57.6 10.9 %collective-permute-start.9 = (f32[272,256]{1,0:T(8,128)S(1)}, f32[272,256]{1,0:T(8,128)S(1)}, u32[]{:S(2)}, u32[]{:S(2)}) collective-permute-start(f32[272,256]{1,0:T(8,128)S(1)} %get-tuple-element.113.refs_0_), channel_id=1, source_target_pairs={{0,16},{16,0},{1,17},{17,1},{2,18},{18,2},{3,19},{19,3},{4,20},{20... | collective-permute-start | bytes 835592 | tf_op jit(solution)/shard_map/ppermute | solution.py:33
  70.5 1.6 %collective-permute-start.10 = (bf16[160,768]{1,0:T(8,128)(2,1)S(1)}, bf16[160,768]{1,0:T(8,128)(2,1)S(1)}, u32[]{:S(2)}, u32[]{:S(2)}) collective-permute-start(bf16[160,768]{1,0:T(8,128)(2,1)S(1)} %select_convert_fusion), channel_id=1, source_target_pairs={{0,1},{1,0},{2,3},{3,2},{4,5},{5,4},{6,7},{7,6},{8,9},{9,8},{10,11... | collective-permute-start | bytes 737288 | tf_op jit(solution)/shard_map/ppermute | solution.py:33
  72.2 4.3 %collective-permute-start.11 = (bf16[40,768]{1,0:T(8,128)(2,1)S(1)}, bf16[40,768]{1,0:T(8,128)(2,1)S(1)}, u32[]{:S(2)}, u32[]{:S(2)}) collective-permute-start(bf16[40,768]{1,0:T(8,128)(2,1)S(1)} %get-tuple-element.127), channel_id=1, source_target_pairs={{0,2},{1,3},{2,0},{3,1},{16,18},{17,19},{18,16},{19,17},{4,6},{5,7... | collective-permute-start | bytes 184328 | tf_op jit(solution)/shard_map/ppermute | solution.py:72
  72.8 4.8 %collective-permute-start.12 = (bf16[40,768]{1,0:T(8,128)(2,1)S(1)}, bf16[40,768]{1,0:T(8,128)(2,1)S(1)}, u32[]{:S(2)}, u32[]{:S(2)}) collective-permute-start(bf16[40,768]{1,0:T(8,128)(2,1)S(1)} %get-tuple-element.129), channel_id=1, source_target_pairs={{0,16},{1,17},{2,18},{3,19},{16,0},{17,1},{18,2},{19,3},{4,20},{5,... | collective-permute-start | bytes 184328 | tf_op jit(solution)/shard_map/ppermute | solution.py:72
  73.3 5.5 %collective-permute-start.13 = (bf16[40,768]{1,0:T(8,128)(2,1)S(1)}, bf16[40,768]{1,0:T(8,128)(2,1)S(1)}, u32[]{:S(2)}, u32[]{:S(2)}) collective-permute-start(bf16[40,768]{1,0:T(8,128)(2,1)S(1)} %get-tuple-element.128), channel_id=1, source_target_pairs={{0,18},{1,19},{2,16},{3,17},{16,2},{17,3},{18,0},{19,1},{4,22},{5,... | collective-permute-start | bytes 184328 | tf_op jit(solution)/shard_map/ppermute | solution.py:72
  78.8 4.3 %collective-permute-start.14 = (bf16[40,768]{1,0:T(8,128)(2,1)S(1)}, bf16[40,768]{1,0:T(8,128)(2,1)S(1)}, u32[]{:S(2)}, u32[]{:S(2)}) collective-permute-start(bf16[40,768]{1,0:T(8,128)(2,1)S(1)} %fusion.1), channel_id=1, source_target_pairs={{0,4},{4,0},{8,12},{12,8},{1,5},{5,1},{9,13},{13,9},{2,6},{6,2},{1... | collective-permute-start | bytes 184328 | tf_op jit(solution)/shard_map/ppermute | solution.py:33
  83.2 5.4 %collective-permute-start.15 = (bf16[40,768]{1,0:T(8,128)(2,1)S(1)}, bf16[40,768]{1,0:T(8,128)(2,1)S(1)}, u32[]{:S(2)}, u32[]{:S(2)}) collective-permute-start(bf16[40,768]{1,0:T(8,128)(2,1)S(1)} %add_convert_fusion.1), channel_id=1, source_target_pairs={{0,8},{4,12},{8,0},{12,4},{1,9},{5,13},{9,1},{13,5},{2,10},{6,14},... | collective-permute-start | bytes 184328 | tf_op jit(solution)/shard_map/ppermute | solution.py:33
  88.9 5.5 %collective-permute-start.16 = (bf16[40,768]{1,0:T(8,128)(2,1)S(1)}, bf16[40,768]{1,0:T(8,128)(2,1)S(1)}, u32[]{:S(2)}, u32[]{:S(2)}) collective-permute-start(bf16[40,768]{1,0:T(8,128)(2,1)S(1)} %add_convert_fusion), channel_id=1, source_target_pairs={{0,2},{1,3},{2,0},{3,1},{16,18},{17,19},{18,16},{19,17},{4,6},{5,7... | collective-permute-start | bytes 184328 | tf_op jit(solution)/shard_map/ppermute | solution.py:81
  90.1 4.3 %collective-permute-start.17 = (bf16[40,768]{1,0:T(8,128)(2,1)S(1)}, bf16[40,768]{1,0:T(8,128)(2,1)S(1)}, u32[]{:S(2)}, u32[]{:S(2)}) collective-permute-start(bf16[40,768]{1,0:T(8,128)(2,1)S(1)} %add_convert_fusion), channel_id=1, source_target_pairs={{0,16},{1,17},{2,18},{3,19},{16,0},{17,1},{18,2},{19,3},{4,20},{5,... | collective-permute-start | bytes 184328 | tf_op jit(solution)/shard_map/ppermute | solution.py:81
  91.6 5.1 %collective-permute-start.18 = (bf16[40,768]{1,0:T(8,128)(2,1)S(1)}, bf16[40,768]{1,0:T(8,128)(2,1)S(1)}, u32[]{:S(2)}, u32[]{:S(2)}) collective-permute-start(bf16[40,768]{1,0:T(8,128)(2,1)S(1)} %add_convert_fusion), channel_id=1, source_target_pairs={{0,18},{1,19},{2,16},{3,17},{16,2},{17,3},{18,0},{19,1},{4,22},{5,... | collective-permute-start | bytes 184328 | tf_op jit(solution)/shard_map/ppermute | solution.py:81
  96.7 1.6 %collective-permute-start.19 = (bf16[160,768]{1,0:T(8,128)(2,1)S(1)}, bf16[160,768]{1,0:T(8,128)(2,1)S(1)}, u32[]{:S(2)}, u32[]{:S(2)}) collective-permute-start(bf16[160,768]{1,0:T(8,128)(2,1)S(1)} %bitcast.30), channel_id=1, source_target_pairs={{0,1},{1,0},{2,3},{3,2},{4,5},{5,4},{6,7},{7,6},{8,9},{9,8},{10,11... | collective-permute-start | bytes 737288 | tf_op jit(solution)/shard_map/ppermute | solution.py:33

commit v13 on v11

--- a/solution.py
+++ b/solution.py
@@ -170,7 +170,7 @@
     return line
 
 
-def conv_rows(load, filters, tile, bias, steps, count, parts, products):
+def conv_rows(load, filters, tile, bias, steps, count, parts, products, skipped=()):
     row_pairs, col_pairs = count // 2, steps // 2
     fill_parts(load, parts, row_pairs + 3, 2 * col_pairs + 6)
     for row_part in range(3):
@@ -179,6 +179,8 @@
             many_rows, many_cols = PARTS[row_part], PARTS[col_part]
             total = [[None] * col_pairs for _ in range(row_pairs)]
             for place in range(row_pairs + many_rows - 1):
+                if (row_part, place) in skipped:
+                    continue
                 line = part_line(
                     load, parts, row_part, col_part, place, col_pairs + many_cols - 1
                 )
@@ -268,9 +270,15 @@
                 load_from(SIDE), filters, tile, start_value, steps, rows - 2 * SIDE, parts, products
             )
         )
+        last = SIDE // 2 + 2
+        beyond = (
+            [(row_part, 0) for row_part in range(3)],
+            [(0, last), (1, last - 1), (2, last)],
+        )
         for side, first in enumerate((0, rows - SIDE)):
             lines = conv_rows(
-                load_from(first), filters, tile, start_value, steps, SIDE, parts, products
+                load_from(first), filters, tile, start_value, steps, SIDE, parts, products,
+                beyond[side],
             )
             for row, line in enumerate(lines):
                 for step, value in enumerate(line):

time: 97.9 us -> 97.5 us (level)
  transfers between devices with their start and end apart: 20 -> 20, of which waited for: 16 -> 16; matrix products, arithmetic and copies ran while one was open for 4% -> 4% of each run, Pallas kernels for 20% -> 19%
where the time goes in v13:
time: 97.5 us; the launch traced here: 97.2 us
  Pallas kernels  33.4 us (34%)
  starting transfers between devices  31.5 us (32%)
  waiting for transfers between devices  24.9 us (26%)
  local copies, waits for them, and re-layouts  3.55 us (4%)
  other arithmetic  2.13 us (2%)
  between operations  1.77 us (2%)
    ppermute x10, waiting for transfers between devices, swap(): return lax.ppermute(value, axis, [(i, i ^ shift) for i in range(count)])  17.3 us
    ppermute x10, starting transfers between devices, swap(): return lax.ppermute(value, axis, [(i, i ^ shift) for i in range(count)])  16 us
    pallas_call x1, Pallas kernels, conv_inner(): pl.pallas_call(inner_kernel, in_specs=[in_vmem] * 7, out_specs=[in_vmem]...  11.2 us
    pallas_call x1, Pallas kernels, head(): pl.pallas_call(functools.partial(head_kernel, count=count, image_count=im...  9.77 us
    pallas_call x2, Pallas kernels, tap_grads(): pl.pallas_call(functools.partial(taps_kernel, first=first, last=last), in...  8.07 us
    ppermute x2, starting transfers between devices, next_along(): lax.ppermute(value, axis, [(i, i + 1) for i in range(lax.axis_size(axis)...  5.86 us
    ppermute x3, waiting for transfers between devices, square_scatter(): lax.ppermute(piece(turn).astype(sent_as), axes, pairs[turn]).astype(wide)  3.68 us
    ppermute x3, starting transfers between devices, square_scatter(): lax.ppermute(piece(turn).astype(sent_as), axes, pairs[turn]).astype(wide)  3.55 us
  transfers between devices with their start and end apart: 20, of which 16 were waited for; matrix products, arithmetic and copies ran while one was open for 4% of the time, Pallas kernels for 19%

profile of v13, /device:TPU:0, one launch (start us, length us, event | category | flops | bytes accessed | tf_op | source)
XLA Modules:
  0.0 97.2 jit_solution(5028507244064694328)
XLA Ops:
  0.6 0.0 copy-start
  0.6 0.0 copy-start.4
  0.7 0.0 copy-start.2
  0.7 0.0 copy-start.3
  0.7 1.2 %fusion.6 = (bf16[16,3,768]{2,1,0:T(4,128)(2,1)S(1)}, bf16[16,3,768]{2,1,0:T(4,128)(2,1)S(1)}) fusion(bf16[16,64,768]{2,1,0:T(8,128)(2,1)} %bitcast.28), kind=kLoop, calls=%fused_computation.23 | loop fusion | bytes 294912 | tf_op jit(solution)/shard_map/slice | solution.py:829
  1.9 2.4 %collective-permute-start = (bf16[16,3,768]{2,1,0:T(4,128)(2,1)S(1)}, bf16[16,3,768]{2,1,0:T(4,128)(2,1)S(1)}, u32[]{:S(2)}, u32[]{:S(2)}) collective-permute-start(bf16[16,3,768]{2,1,0:T(4,128)(2,1)S(1)} %get-tuple-element.127), channel_id=1, source_target_pairs={{0,1},{1,2},{2,3},{4,5},{5,6},{6,7},{8,9},{9,10},{10,11},{12,13},{... | collective-permute-start | bytes 221192 | tf_op jit(solution)/shard_map/ppermute | solution.py:97
  4.3 1.3 %collective-permute-start.1 = (bf16[16,3,768]{2,1,0:T(4,128)(2,1)S(1)}, bf16[16,3,768]{2,1,0:T(4,128)(2,1)S(1)}, u32[]{:S(2)}, u32[]{:S(2)}) collective-permute-start(bf16[16,3,768]{2,1,0:T(4,128)(2,1)S(1)} %get-tuple-element.128), channel_id=1, source_target_pairs={{1,0},{2,1},{3,2},{5,4},{6,5},{7,6},{9,8},{10,9},{11,10},{13,12},{... | collective-permute-start | bytes 221192 | tf_op jit(solution)/shard_map/ppermute | solution.py:101
  5.6 1.1 %fusion.5 = (bf16[1,3,64,768]{3,2,1,0:T(8,128)(2,1)S(1)}, bf16[1,3,64,768]{3,2,1,0:T(8,128)(2,1)S(1)}) fusion(bf16[1,16,64,768]{3,2,1,0:T(8,128)(2,1)} %param.8), kind=kLoop, calls=%fused_computation.22 | loop fusion | bytes 1179648 | tf_op jit(solution)/shard_map/slice | solution.py:809
  6.7 0.7 broadcast_in_dim.31.bias
  7.4 0.0 collective-permute-done.left
  7.4 2.2 %collective-permute-done.1.right = bf16[16,3,768]{2,1,0:T(4,128)(2,1)S(1)} collective-permute-done((bf16[16,3,768]{2,1,0:T(4,128)(2,1)S(1)}, bf16[16,3,768]{2,1,0:T(4,128)(2,1)S(1)}, u32[]{:S(2)}, u32[]{:S(2)}) %collective-permute-start.1) | collective-permute-done | bytes 73760 | tf_op jit(solution)/shard_map/ppermute | solution.py:101
  9.8 3.5 %collective-permute-start.2 = (bf16[210,768]{1,0:T(8,128)(2,1)S(1)}, bf16[210,768]{1,0:T(8,128)(2,1)S(1)}, u32[]{:S(2)}, u32[]{:S(2)}) collective-permute-start(bf16[210,768]{1,0:T(8,128)(2,1)S(1)} %get-tuple-element.74), channel_id=1, source_target_pairs={{0,4},{4,8},{8,12},{1,5},{5,9},{9,13},{2,6},{6,10},{10,14},{3,7},{... | collective-permute-start | bytes 967688 | tf_op jit(solution)/shard_map/ppermute | solution.py:97
  13.3 1.3 %collective-permute-start.3 = (bf16[210,768]{1,0:T(8,128)(2,1)S(1)}, bf16[210,768]{1,0:T(8,128)(2,1)S(1)}, u32[]{:S(2)}, u32[]{:S(2)}) collective-permute-start(bf16[210,768]{1,0:T(8,128)(2,1)S(1)} %get-tuple-element.75), channel_id=1, source_target_pairs={{4,0},{8,4},{12,8},{5,1},{9,5},{13,9},{6,2},{10,6},{14,10},{7,3},{... | collective-permute-start | bytes 967688 | tf_op jit(solution)/shard_map/ppermute | solution.py:101
  14.6 0.0 copy-done
  14.6 0.0 copy-done.4
  14.6 0.0 copy-done.2
  14.6 11.2 %conv_inner.1 = (f32[6,16,14,8,128]{4,3,2,1,0:T(8,128)S(1)}, f32[6,121,8,128]{3,2,1,0:T(8,128)S(1)}, bf16[512,768]{1,0:T(8,128)(2,1)S(1)}, f32[512,256]{1,0:T(8,...) custom-call(bf16[16,64,768]{2,1,0:T(8,128)(2,1)S(1)} %bitcast.29, ...), custom_call_target="tpu_custom_call" | custom-call | flops 10000000000 | bytes 10000000 | tf_op jit(solution)/shard_map/conv_inner/pallas_call | solution.py:388
  25.8 0.0 collective-permute-done.2.top
  25.8 0.0 collective-permute-done.3.bottom
  25.8 2.4 %conv_edge.1 = (f32[6,3,14,8,128]{4,3,2,1,0:T(8,128)S(1)}, f32[6,3,14,8,128]{4,3,2,1,0:T(8,128)S(1)}, bf16[512,768]{1,0:T(8,128)(2,1)S(1)}, f32[512,256]{1,0:T(8...) custom-call(s32[1]{0:T(128)} %bitcast.3.flag, ...), custom_call_target="tpu_custom_call" | custom-call | flops 6000000000 | bytes 6000000 | tf_op jit(solution)/shard_map/conv_edge/pallas_call | solution.py:419
  28.2 0.0 copy-start.1
  28.2 0.0 copy-start.5
  28.2 3.0 %collective-permute-start.4 = (f32[72,256]{1,0:T(8,128)S(1)}, f32[72,256]{1,0:T(8,128)S(1)}, u32[]{:S(2)}, u32[]{:S(2)}) collective-permute-start(f32[72,256]{1,0:T(8,128)S(1)} %get-tuple-element.82), channel_id=1, source_target_pairs={{0,1},{1,0},{2,3},{3,2},{4,5},{5,4},{6,7},{7,6},{8,9},{9,8},{10,11... | collective-permute-start | bytes 221192 | tf_op jit(solution)/shard_map/ppermute | solution.py:33
  31.3 0.9 collective-permute-done.4
  32.2 0.5 collective-permute-start.5
  32.7 0.9 prepare.1
  33.7 3.1 %collective-permute-done.5 = f32[72,256]{1,0:T(8,128)S(1)} collective-permute-done((f32[72,256]{1,0:T(8,128)S(1)}, f32[72,256]{1,0:T(8,128)S(1)}, u32[]{:S(2)}, u32[]{:S(2)}) %collective-permute-start.5) | collective-permute-done | bytes 73760 | tf_op jit(solution)/shard_map/ppermute | solution.py:33
  36.8 2.4 %collective-permute-start.6 = (f32[72,256]{1,0:T(8,128)S(1)}, f32[72,256]{1,0:T(8,128)S(1)}, u32[]{:S(2)}, u32[]{:S(2)}) collective-permute-start(f32[72,256]{1,0:T(8,128)S(1)} %add.38), channel_id=1, source_target_pairs={{0,4},{4,0},{8,12},{12,8},{1,5},{5,1},{9,13},{13,9},{2,6},{6,2},{1... | collective-permute-start | bytes 221192 | tf_op jit(solution)/shard_map/ppermute | solution.py:33
  39.2 2.3 %collective-permute-done.6 = f32[72,256]{1,0:T(8,128)S(1)} collective-permute-done((f32[72,256]{1,0:T(8,128)S(1)}, f32[72,256]{1,0:T(8,128)S(1)}, u32[]{:S(2)}, u32[]{:S(2)}) %collective-permute-start.6) | collective-permute-done | bytes 73760 | tf_op jit(solution)/shard_map/ppermute | solution.py:33
  41.6 3.1 %collective-permute-start.7 = (f32[72,256]{1,0:T(8,128)S(1)}, f32[72,256]{1,0:T(8,128)S(1)}, u32[]{:S(2)}, u32[]{:S(2)}) collective-permute-start(f32[72,256]{1,0:T(8,128)S(1)} %add.39), channel_id=1, source_target_pairs={{0,8},{4,12},{8,0},{12,4},{1,9},{5,13},{9,1},{13,5},{2,10},{6,14},... | collective-permute-start | bytes 221192 | tf_op jit(solution)/shard_map/ppermute | solution.py:33
  44.7 2.3 %collective-permute-done.7 = f32[72,256]{1,0:T(8,128)S(1)} collective-permute-done((f32[72,256]{1,0:T(8,128)S(1)}, f32[72,256]{1,0:T(8,128)S(1)}, u32[]{:S(2)}, u32[]{:S(2)}) %collective-permute-start.7) | collective-permute-done | bytes 73760 | tf_op jit(solution)/shard_map/ppermute | solution.py:33
  47.0 0.1 collective-permute-start.8
  47.7 0.6 collective-permute-done.8.other
  48.3 0.0 copy-done.5
  48.3 9.8 %head.1 = (f32[272,256]{1,0:T(8,128)S(1)}, f32[320,768]{1,0:T(8,128)S(1)}, bf16[512,768]{1,0:T(8,128)(2,1)S(1)}, bf16[512,768]{1,0:T(8,128)(2,1)S(1)}) custom-call(s32[1]{0:T(128)} %bitcast.3.flag, s32[1]{0:T(128)S(6)} %copy.23.label, f32[10]{0:T(128)S(1)} %copy-done.5, f32[72,256]{1,0:T(8,128)S(1)} %add.40.own, f32[72,256]{1,0:T(8,128)S(1)} %collective-permute-done.8.other, ...), custom_call_target="tpu_custom_call" | custom-call | flops 10000000000 | bytes 10000000 | tf_op jit(solution)/shard_map/head/pallas_call | solution.py:599
  58.1 1.6 %collective-permute-start.9 = (f32[272,256]{1,0:T(8,128)S(1)}, f32[272,256]{1,0:T(8,128)S(1)}, u32[]{:S(2)}, u32[]{:S(2)}) collective-permute-start(f32[272,256]{1,0:T(8,128)S(1)} %get-tuple-element.115.refs_0_), channel_id=1, source_target_pairs={{0,16},{16,0},{1,17},{17,1},{2,18},{18,2},{3,19},{19,3},{4,20},{20... | collective-permute-start | bytes 835592 | tf_op jit(solution)/shard_map/ppermute | solution.py:33
  59.7 6.8 %tap_grads.2.payload_in = f32[320,768]{1,0:T(8,128)S(1)} custom-call(f32[6,16,14,8,128]{4,3,2,1,0:T(8,128)S(1)} %get-tuple-element.72.spread_in, f32[6,3,14,8,128]{4,3,2,1,0:T(8,128)S(1)} %get-tuple-element.79.spread_top, f32[6,3,14,8,128]{4,3,2,1,0:T(8,128)S(1)} %get-tuple-element.80.spread_bottom, ...), custom_call_target="tpu_custom_call", output_to_operand_aliasing={{}: (5, {})} | custom-call | flops 10000000000 | bytes 10000000 | tf_op jit(solution)/shard_map/tap_grads/pallas_call | solution.py:744
  66.4 0.5 collective-permute-done.9.refs_1_
  66.9 1.3 %tap_grads.3 = f32[320,768]{1,0:T(8,128)S(1)} custom-call(f32[6,16,14,8,128]{4,3,2,1,0:T(8,128)S(1)} %get-tuple-element.72.spread_in, f32[6,3,14,8,128]{4,3,2,1,0:T(8,128)S(1)} %get-tuple-element.79.spread_top, f32[6,3,14,8,128]{4,3,2,1,0:T(8,128)S(1)} %get-tuple-element.80.spread_bottom, ...), custom_call_target="tpu_custom_call", output_to_operand_aliasing={{}: (5, {})} | custom-call | flops 2000000000 | bytes 2000000 | tf_op jit(solution)/shard_map/tap_grads/pallas_call | solution.py:744
  68.3 0.1 collective-permute-start.10
  68.3 1.5 %collective-permute-done.10 = bf16[160,768]{1,0:T(8,128)(2,1)S(1)} collective-permute-done((bf16[160,768]{1,0:T(8,128)(2,1)S(1)}, bf16[160,768]{1,0:T(8,128)(2,1)S(1)}, u32[]{:S(2)}, u32[]{:S(2)}) %collective-permute-start.10) | collective-permute-done | bytes 245792 | tf_op jit(solution)/shard_map/ppermute | solution.py:33
  69.8 0.1 convert_add_fusion
  69.9 0.6 collective-permute-start.11
  70.6 1.5 %collective-permute-start.12 = (bf16[40,768]{1,0:T(8,128)(2,1)S(1)}, bf16[40,768]{1,0:T(8,128)(2,1)S(1)}, u32[]{:S(2)}, u32[]{:S(2)}) collective-permute-start(bf16[40,768]{1,0:T(8,128)(2,1)S(1)} %get-tuple-element.131), channel_id=1, source_target_pairs={{0,16},{1,17},{2,18},{3,19},{16,0},{17,1},{18,2},{19,3},{4,20},{5,... | collective-permute-start | bytes 184328 | tf_op jit(solution)/shard_map/ppermute | solution.py:72
  72.1 1.4 %collective-permute-start.13 = (bf16[40,768]{1,0:T(8,128)(2,1)S(1)}, bf16[40,768]{1,0:T(8,128)(2,1)S(1)}, u32[]{:S(2)}, u32[]{:S(2)}) collective-permute-start(bf16[40,768]{1,0:T(8,128)(2,1)S(1)} %get-tuple-element.130), channel_id=1, source_target_pairs={{0,18},{1,19},{2,16},{3,17},{16,2},{17,3},{18,0},{19,1},{4,22},{5,... | collective-permute-start | bytes 184328 | tf_op jit(solution)/shard_map/ppermute | solution.py:72
  73.5 0.7 collective-permute-done.11
  74.2 0.5 collective-permute-done.12
  74.8 2.4 %collective-permute-done.13 = bf16[40,768]{1,0:T(8,128)(2,1)S(1)} collective-permute-done((bf16[40,768]{1,0:T(8,128)(2,1)S(1)}, bf16[40,768]{1,0:T(8,128)(2,1)S(1)}, u32[]{:S(2)}, u32[]{:S(2)}) %collective-permute-start.13) | collective-permute-done | bytes 61472 | tf_op jit(solution)/shard_map/ppermute | solution.py:72
  77.2 2.0 %collective-permute-start.14 = (bf16[40,768]{1,0:T(8,128)(2,1)S(1)}, bf16[40,768]{1,0:T(8,128)(2,1)S(1)}, u32[]{:S(2)}, u32[]{:S(2)}) collective-permute-start(bf16[40,768]{1,0:T(8,128)(2,1)S(1)} %fusion.1), channel_id=1, source_target_pairs={{0,4},{4,0},{8,12},{12,8},{1,5},{5,1},{9,13},{13,9},{2,6},{6,2},{1... | collective-permute-start | bytes 184328 | tf_op jit(solution)/shard_map/ppermute | solution.py:33
  79.2 2.3 %collective-permute-done.14 = bf16[40,768]{1,0:T(8,128)(2,1)S(1)} collective-permute-done((bf16[40,768]{1,0:T(8,128)(2,1)S(1)}, bf16[40,768]{1,0:T(8,128)(2,1)S(1)}, u32[]{:S(2)}, u32[]{:S(2)}) %collective-permute-start.14) | collective-permute-done | bytes 61472 | tf_op jit(solution)/shard_map/ppermute | solution.py:33
  81.5 3.2 %collective-permute-start.15 = (bf16[40,768]{1,0:T(8,128)(2,1)S(1)}, bf16[40,768]{1,0:T(8,128)(2,1)S(1)}, u32[]{:S(2)}, u32[]{:S(2)}) collective-permute-start(bf16[40,768]{1,0:T(8,128)(2,1)S(1)} %add_convert_fusion.1), channel_id=1, source_target_pairs={{0,8},{4,12},{8,0},{12,4},{1,9},{5,13},{9,1},{13,5},{2,10},{6,14},... | collective-permute-start | bytes 184328 | tf_op jit(solution)/shard_map/ppermute | solution.py:33
  84.7 2.2 %collective-permute-done.15 = bf16[40,768]{1,0:T(8,128)(2,1)S(1)} collective-permute-done((bf16[40,768]{1,0:T(8,128)(2,1)S(1)}, bf16[40,768]{1,0:T(8,128)(2,1)S(1)}, u32[]{:S(2)}, u32[]{:S(2)}) %collective-permute-start.15) | collective-permute-done | bytes 61472 | tf_op jit(solution)/shard_map/ppermute | solution.py:33
  87.0 0.1 slice_reduce_fusion
  87.1 0.1 slice_reduce_fusion.1
  87.2 1.5 %collective-permute-start.16 = (bf16[40,768]{1,0:T(8,128)(2,1)S(1)}, bf16[40,768]{1,0:T(8,128)(2,1)S(1)}, u32[]{:S(2)}, u32[]{:S(2)}) collective-permute-start(bf16[40,768]{1,0:T(8,128)(2,1)S(1)} %add_convert_fusion), channel_id=1, source_target_pairs={{0,2},{1,3},{2,0},{3,1},{16,18},{17,19},{18,16},{19,17},{4,6},{5,7... | collective-permute-start | bytes 184328 | tf_op jit(solution)/shard_map/ppermute | solution.py:81
  88.8 0.5 collective-permute-start.17
  89.3 1.5 %collective-permute-start.18 = (bf16[40,768]{1,0:T(8,128)(2,1)S(1)}, bf16[40,768]{1,0:T(8,128)(2,1)S(1)}, u32[]{:S(2)}, u32[]{:S(2)}) collective-permute-start(bf16[40,768]{1,0:T(8,128)(2,1)S(1)} %add_convert_fusion), channel_id=1, source_target_pairs={{0,18},{1,19},{2,16},{3,17},{16,2},{17,3},{18,0},{19,1},{4,22},{5,... | collective-permute-start | bytes 184328 | tf_op jit(solution)/shard_map/ppermute | solution.py:81
  90.8 1.9 %multiply_add_fusion = f32[10,256,256]{2,1,0:T(8,128)} fusion(f32[256,256]{1,0:T(8,128)S(1)} %slice.57, f32[10]{0:T(128)S(1)} %slice_reduce_fusion, f32[256,256]{1,0:T(8,128)S(1)} %slice.55, f32[10]{0:T(128)S(1)} %slice_reduce_fusion.1), kind=kLoop, calls=%fused_computation | loop fusion | flops 1966080 | bytes 3145808 | tf_op jit(solution)/shard_map/add | solution.py:42
  92.7 0.0 collective-permute-done.16
  92.7 0.3 collective-permute-done.17
  93.0 1.4 %collective-permute-done.18 = bf16[40,768]{1,0:T(8,128)(2,1)S(1)} collective-permute-done((bf16[40,768]{1,0:T(8,128)(2,1)S(1)}, bf16[40,768]{1,0:T(8,128)(2,1)S(1)}, u32[]{:S(2)}, u32[]{:S(2)}) %collective-permute-start.18) | collective-permute-done | bytes 61472 | tf_op jit(solution)/shard_map/ppermute | solution.py:81
  94.4 0.1 collective-permute-start.19
  94.5 1.5 %collective-permute-done.19.other = bf16[160,768]{1,0:T(8,128)(2,1)S(1)} collective-permute-done((bf16[160,768]{1,0:T(8,128)(2,1)S(1)}, bf16[160,768]{1,0:T(8,128)(2,1)S(1)}, u32[]{:S(2)}, u32[]{:S(2)}) %collective-permute-start.19) | collective-permute-done | bytes 245792 | tf_op jit(solution)/shard_map/ppermute | solution.py:33
  96.0 1.0 %finish.1 = (f32[768,256]{1,0:T(8,128)}, f32[7,7,768]{2,1,0:T(8,128)}, f32[768]{0:T(1024)}, f32[256]{0:T(256)}, f32[10]{0:T(128)}, /*index=5*/f32[1]{0:T(128)}) custom-call(s32[1]{0:T(128)} %bitcast.3.flag, bf16[160,768]{1,0:T(8,128)(2,1)S(1)} %bitcast.31, bf16[160,768]{1,0:T(8,128)(2,1)S(1)} %collective-permute-done.19.other, ...), custom_call_target="tpu_custom_call" | custom-call | flops 1000000000 | bytes 1000000 | tf_op jit(solution)/shard_map/finish/pallas_call | solution.py:788
  (25 shorter events, 0.5 us)
Async XLA Ops:
  0.6 14.0 %copy-start = (bf16[1,16,64,768]{3,2,1,0:T(8,128)(2,1)S(1)}, bf16[1,16,64,768]{3,2,1,0:T(8,128)(2,1)}, u32[]{:S(2)}) copy-start(bf16[1,16,64,768]{3,2,1,0:T(8,128)(2,1)} %param.8) | copy-start | bytes 4718596
  0.6 14.0 %copy-start.4 = (f32[256]{0:T(256)S(1)}, f32[256]{0:T(256)}, u32[]{:S(2)}) copy-start(f32[256]{0:T(256)} %param.12) | copy-start | bytes 3076
  0.7 14.0 %copy-start.2 = (bf16[768,256]{1,0:T(8,128)(2,1)S(1)}, bf16[768,256]{1,0:T(8,128)(2,1)}, u32[]{:S(2)}) copy-start(bf16[768,256]{1,0:T(8,128)(2,1)} %reduce_weight.5) | copy-start | bytes 1179652
  0.7 14.0 %copy-start.3 = (f32[7,7,768]{2,1,0:T(8,128)S(1)}, f32[7,7,768]{2,1,0:T(8,128)}, u32[]{:S(2)}) copy-start(f32[7,7,768]{2,1,0:T(8,128)} %weight.1) | copy-start | bytes 451588
  1.9 5.5 %collective-permute-start = (bf16[16,3,768]{2,1,0:T(4,128)(2,1)S(1)}, bf16[16,3,768]{2,1,0:T(4,128)(2,1)S(1)}, u32[]{:S(2)}, u32[]{:S(2)}) collective-permute-start(bf16[16,3,768]{2,1,0:T(4,128)(2,1)S(1)} %get-tuple-element.127), channel_id=1, source_target_pairs={{0,1},{1,2},{2,3},{4,5},{5,6},{6,7},{8,9},{9,10},{10,11},{12,13},{... | collective-permute-start | bytes 221192 | tf_op jit(solution)/shard_map/ppermute | solution.py:97
  4.3 5.3 %collective-permute-start.1 = (bf16[16,3,768]{2,1,0:T(4,128)(2,1)S(1)}, bf16[16,3,768]{2,1,0:T(4,128)(2,1)S(1)}, u32[]{:S(2)}, u32[]{:S(2)}) collective-permute-start(bf16[16,3,768]{2,1,0:T(4,128)(2,1)S(1)} %get-tuple-element.128), channel_id=1, source_target_pairs={{1,0},{2,1},{3,2},{5,4},{6,5},{7,6},{9,8},{10,9},{11,10},{13,12},{... | collective-permute-start | bytes 221192 | tf_op jit(solution)/shard_map/ppermute | solution.py:101
  9.8 16.0 %collective-permute-start.2 = (bf16[210,768]{1,0:T(8,128)(2,1)S(1)}, bf16[210,768]{1,0:T(8,128)(2,1)S(1)}, u32[]{:S(2)}, u32[]{:S(2)}) collective-permute-start(bf16[210,768]{1,0:T(8,128)(2,1)S(1)} %get-tuple-element.74), channel_id=1, source_target_pairs={{0,4},{4,8},{8,12},{1,5},{5,9},{9,13},{2,6},{6,10},{10,14},{3,7},{... | collective-permute-start | bytes 967688 | tf_op jit(solution)/shard_map/ppermute | solution.py:97
  13.3 12.5 %collective-permute-start.3 = (bf16[210,768]{1,0:T(8,128)(2,1)S(1)}, bf16[210,768]{1,0:T(8,128)(2,1)S(1)}, u32[]{:S(2)}, u32[]{:S(2)}) collective-permute-start(bf16[210,768]{1,0:T(8,128)(2,1)S(1)} %get-tuple-element.75), channel_id=1, source_target_pairs={{4,0},{8,4},{12,8},{5,1},{9,5},{13,9},{6,2},{10,6},{14,10},{7,3},{... | collective-permute-start | bytes 967688 | tf_op jit(solution)/shard_map/ppermute | solution.py:101
  28.2 20.1 %copy-start.1 = (bf16[10,256,256]{2,1,0:T(8,128)(2,1)S(1)}, bf16[10,256,256]{2,1,0:T(8,128)(2,1)}, u32[]{:S(2)}) copy-start(bf16[10,256,256]{2,1,0:T(8,128)(2,1)} %class_weight.1) | copy-start | bytes 3932164
  28.2 20.1 %copy-start.5 = (f32[10]{0:T(128)S(1)}, f32[10]{0:T(128)}, u32[]{:S(2)}) copy-start(f32[10]{0:T(128)} %class_bias.1) | copy-start | bytes 124
  28.2 3.9 %collective-permute-start.4 = (f32[72,256]{1,0:T(8,128)S(1)}, f32[72,256]{1,0:T(8,128)S(1)}, u32[]{:S(2)}, u32[]{:S(2)}) collective-permute-start(f32[72,256]{1,0:T(8,128)S(1)} %get-tuple-element.82), channel_id=1, source_target_pairs={{0,1},{1,0},{2,3},{3,2},{4,5},{5,4},{6,7},{7,6},{8,9},{9,8},{10,11... | collective-permute-start | bytes 221192 | tf_op jit(solution)/shard_map/ppermute | solution.py:33
  32.2 4.6 %collective-permute-start.5 = (f32[72,256]{1,0:T(8,128)S(1)}, f32[72,256]{1,0:T(8,128)S(1)}, u32[]{:S(2)}, u32[]{:S(2)}) collective-permute-start(f32[72,256]{1,0:T(8,128)S(1)} %add.37), channel_id=1, source_target_pairs={{0,2},{1,3},{2,0},{3,1},{4,6},{5,7},{6,4},{7,5},{8,10},{9,11},{10,... | collective-permute-start | bytes 221192 | tf_op jit(solution)/shard_map/ppermute | solution.py:33
  36.8 4.8 %collective-permute-start.6 = (f32[72,256]{1,0:T(8,128)S(1)}, f32[72,256]{1,0:T(8,128)S(1)}, u32[]{:S(2)}, u32[]{:S(2)}) collective-permute-start(f32[72,256]{1,0:T(8,128)S(1)} %add.38), channel_id=1, source_target_pairs={{0,4},{4,0},{8,12},{12,8},{1,5},{5,1},{9,13},{13,9},{2,6},{6,2},{1... | collective-permute-start | bytes 221192 | tf_op jit(solution)/shard_map/ppermute | solution.py:33
  41.6 5.4 %collective-permute-start.7 = (f32[72,256]{1,0:T(8,128)S(1)}, f32[72,256]{1,0:T(8,128)S(1)}, u32[]{:S(2)}, u32[]{:S(2)}) collective-permute-start(f32[72,256]{1,0:T(8,128)S(1)} %add.39), channel_id=1, source_target_pairs={{0,8},{4,12},{8,0},{12,4},{1,9},{5,13},{9,1},{13,5},{2,10},{6,14},... | collective-permute-start | bytes 221192 | tf_op jit(solution)/shard_map/ppermute | solution.py:33
  47.0 1.3 %collective-permute-start.8 = (f32[72,256]{1,0:T(8,128)S(1)}, f32[72,256]{1,0:T(8,128)S(1)}, u32[]{:S(2)}, u32[]{:S(2)}) collective-permute-start(f32[72,256]{1,0:T(8,128)S(1)} %add.40.own), channel_id=1, source_target_pairs={{0,1},{1,0},{2,3},{3,2},{4,5},{5,4},{6,7},{7,6},{8,9},{9,8},{10,11... | collective-permute-start | bytes 221192 | tf_op jit(solution)/shard_map/ppermute | solution.py:33
  58.1 8.8 %collective-permute-start.9 = (f32[272,256]{1,0:T(8,128)S(1)}, f32[272,256]{1,0:T(8,128)S(1)}, u32[]{:S(2)}, u32[]{:S(2)}) collective-permute-start(f32[272,256]{1,0:T(8,128)S(1)} %get-tuple-element.115.refs_0_), channel_id=1, source_target_pairs={{0,16},{16,0},{1,17},{17,1},{2,18},{18,2},{3,19},{19,3},{4,20},{20... | collective-permute-start | bytes 835592 | tf_op jit(solution)/shard_map/ppermute | solution.py:33
  68.3 1.6 %collective-permute-start.10 = (bf16[160,768]{1,0:T(8,128)(2,1)S(1)}, bf16[160,768]{1,0:T(8,128)(2,1)S(1)}, u32[]{:S(2)}, u32[]{:S(2)}) collective-permute-start(bf16[160,768]{1,0:T(8,128)(2,1)S(1)} %select_convert_fusion), channel_id=1, source_target_pairs={{0,1},{1,0},{2,3},{3,2},{4,5},{5,4},{6,7},{7,6},{8,9},{9,8},{10,11... | collective-permute-start | bytes 737288 | tf_op jit(solution)/shard_map/ppermute | solution.py:33
  69.9 4.3 %collective-permute-start.11 = (bf16[40,768]{1,0:T(8,128)(2,1)S(1)}, bf16[40,768]{1,0:T(8,128)(2,1)S(1)}, u32[]{:S(2)}, u32[]{:S(2)}) collective-permute-start(bf16[40,768]{1,0:T(8,128)(2,1)S(1)} %get-tuple-element.129), channel_id=1, source_target_pairs={{0,2},{1,3},{2,0},{3,1},{16,18},{17,19},{18,16},{19,17},{4,6},{5,7... | collective-permute-start | bytes 184328 | tf_op jit(solution)/shard_map/ppermute | solution.py:72
  70.6 4.2 %collective-permute-start.12 = (bf16[40,768]{1,0:T(8,128)(2,1)S(1)}, bf16[40,768]{1,0:T(8,128)(2,1)S(1)}, u32[]{:S(2)}, u32[]{:S(2)}) collective-permute-start(bf16[40,768]{1,0:T(8,128)(2,1)S(1)} %get-tuple-element.131), channel_id=1, source_target_pairs={{0,16},{1,17},{2,18},{3,19},{16,0},{17,1},{18,2},{19,3},{4,20},{5,... | collective-permute-start | bytes 184328 | tf_op jit(solution)/shard_map/ppermute | solution.py:72
  72.1 5.1 %collective-permute-start.13 = (bf16[40,768]{1,0:T(8,128)(2,1)S(1)}, bf16[40,768]{1,0:T(8,128)(2,1)S(1)}, u32[]{:S(2)}, u32[]{:S(2)}) collective-permute-start(bf16[40,768]{1,0:T(8,128)(2,1)S(1)} %get-tuple-element.130), channel_id=1, source_target_pairs={{0,18},{1,19},{2,16},{3,17},{16,2},{17,3},{18,0},{19,1},{4,22},{5,... | collective-permute-start | bytes 184328 | tf_op jit(solution)/shard_map/ppermute | solution.py:72
  77.2 4.3 %collective-permute-start.14 = (bf16[40,768]{1,0:T(8,128)(2,1)S(1)}, bf16[40,768]{1,0:T(8,128)(2,1)S(1)}, u32[]{:S(2)}, u32[]{:S(2)}) collective-permute-start(bf16[40,768]{1,0:T(8,128)(2,1)S(1)} %fusion.1), channel_id=1, source_target_pairs={{0,4},{4,0},{8,12},{12,8},{1,5},{5,1},{9,13},{13,9},{2,6},{6,2},{1... | collective-permute-start | bytes 184328 | tf_op jit(solution)/shard_map/ppermute | solution.py:33
  81.5 5.4 %collective-permute-start.15 = (bf16[40,768]{1,0:T(8,128)(2,1)S(1)}, bf16[40,768]{1,0:T(8,128)(2,1)S(1)}, u32[]{:S(2)}, u32[]{:S(2)}) collective-permute-start(bf16[40,768]{1,0:T(8,128)(2,1)S(1)} %add_convert_fusion.1), channel_id=1, source_target_pairs={{0,8},{4,12},{8,0},{12,4},{1,9},{5,13},{9,1},{13,5},{2,10},{6,14},... | collective-permute-start | bytes 184328 | tf_op jit(solution)/shard_map/ppermute | solution.py:33
  87.2 5.5 %collective-permute-start.16 = (bf16[40,768]{1,0:T(8,128)(2,1)S(1)}, bf16[40,768]{1,0:T(8,128)(2,1)S(1)}, u32[]{:S(2)}, u32[]{:S(2)}) collective-permute-start(bf16[40,768]{1,0:T(8,128)(2,1)S(1)} %add_convert_fusion), channel_id=1, source_target_pairs={{0,2},{1,3},{2,0},{3,1},{16,18},{17,19},{18,16},{19,17},{4,6},{5,7... | collective-permute-start | bytes 184328 | tf_op jit(solution)/shard_map/ppermute | solution.py:81
  88.8 4.2 %collective-permute-start.17 = (bf16[40,768]{1,0:T(8,128)(2,1)S(1)}, bf16[40,768]{1,0:T(8,128)(2,1)S(1)}, u32[]{:S(2)}, u32[]{:S(2)}) collective-permute-start(bf16[40,768]{1,0:T(8,128)(2,1)S(1)} %add_convert_fusion), channel_id=1, source_target_pairs={{0,16},{1,17},{2,18},{3,19},{16,0},{17,1},{18,2},{19,3},{4,20},{5,... | collective-permute-start | bytes 184328 | tf_op jit(solution)/shard_map/ppermute | solution.py:81
  89.3 5.1 %collective-permute-start.18 = (bf16[40,768]{1,0:T(8,128)(2,1)S(1)}, bf16[40,768]{1,0:T(8,128)(2,1)S(1)}, u32[]{:S(2)}, u32[]{:S(2)}) collective-permute-start(bf16[40,768]{1,0:T(8,128)(2,1)S(1)} %add_convert_fusion), channel_id=1, source_target_pairs={{0,18},{1,19},{2,16},{3,17},{16,2},{17,3},{18,0},{19,1},{4,22},{5,... | collective-permute-start | bytes 184328 | tf_op jit(solution)/shard_map/ppermute | solution.py:81
  94.4 1.6 %collective-permute-start.19 = (bf16[160,768]{1,0:T(8,128)(2,1)S(1)}, bf16[160,768]{1,0:T(8,128)(2,1)S(1)}, u32[]{:S(2)}, u32[]{:S(2)}) collective-permute-start(bf16[160,768]{1,0:T(8,128)(2,1)S(1)} %bitcast.30), channel_id=1, source_target_pairs={{0,1},{1,0},{2,3},{3,2},{4,5},{5,4},{6,7},{7,6},{8,9},{9,8},{10,11... | collective-permute-start | bytes 737288 | tf_op jit(solution)/shard_map/ppermute | solution.py:33

commit v14 on v11

--- a/solution.py
+++ b/solution.py
@@ -288,8 +288,8 @@
     spread_top, spread_bottom, conv_out, before_out, feat_out, kept_out, sent_out,
     wide_row, stage, sums,
 ):
-    cols = wide_row.shape[1] - 2 * EDGE
-    steps = cols // GROUPS
+    steps = partial.shape[2]
+    cols = steps * GROUPS
 
     def one_tile(tile, _):
         lanes = lanes_of(tile)
@@ -392,7 +392,7 @@
             shape_of((tiles, 2 * SIDE, steps, GROUPS, LANES)),
         ],
         scratch_shapes=[
-            pltpu.VMEM((rows, cols + 2 * EDGE, LANES), wide),
+            pltpu.VMEM((rows, cols + 3 * EDGE, LANES), wide),
             *parts_scratch(rows - 2 * SIDE, steps),
         ],
         compiler_params=params(24),
@@ -422,7 +422,7 @@
             shape_of((sums_rows // 2, width)),
         ],
         scratch_shapes=[
-            pltpu.VMEM((2 * HALF, cols + 2 * EDGE, LANES), wide),
+            pltpu.VMEM((2 * HALF, cols + 3 * EDGE, LANES), wide),
             pltpu.VMEM((2,) + (halos[0].shape[0], LANES), wide),
             pltpu.VMEM((sums_rows, width), wide),
         ],

time: 97.9 us -> 97.9 us (level)
  no operation moved by 1% of the time
where the time goes in v14:
time: 97.9 us; the launch traced here: 97.6 us
  Pallas kernels  33.8 us (35%)
  starting transfers between devices  31.5 us (32%)
  waiting for transfers between devices  24.9 us (25%)
  local copies, waits for them, and re-layouts  3.55 us (4%)
  other arithmetic  2.13 us (2%)
  between operations  1.77 us (2%)
    ppermute x10, waiting for transfers between devices, swap(): return lax.ppermute(value, axis, [(i, i ^ shift) for i in range(count)])  17.3 us
    ppermute x10, starting transfers between devices, swap(): return lax.ppermute(value, axis, [(i, i ^ shift) for i in range(count)])  16 us
    pallas_call x1, Pallas kernels, conv_inner(): pl.pallas_call(inner_kernel, in_specs=[in_vmem] * 7, out_specs=[in_vmem]...  11.5 us
    pallas_call x1, Pallas kernels, head(): pl.pallas_call(functools.partial(head_kernel, count=count, image_count=im...  9.78 us
    pallas_call x2, Pallas kernels, tap_grads(): pl.pallas_call(functools.partial(taps_kernel, first=first, last=last), in...  8.07 us
    ppermute x2, starting transfers between devices, next_along(): lax.ppermute(value, axis, [(i, i + 1) for i in range(lax.axis_size(axis)...  5.86 us
    ppermute x3, waiting for transfers between devices, square_scatter(): lax.ppermute(piece(turn).astype(sent_as), axes, pairs[turn]).astype(wide)  3.67 us
    ppermute x3, starting transfers between devices, square_scatter(): lax.ppermute(piece(turn).astype(sent_as), axes, pairs[turn]).astype(wide)  3.55 us
  transfers between devices with their start and end apart: 20, of which 16 were waited for; matrix products, arithmetic and copies ran while one was open for 4% of the time, Pallas kernels for 20%

profile of v14, /device:TPU:0, one launch (start us, length us, event | category | flops | bytes accessed | tf_op | source)
XLA Modules:
  0.0 97.6 jit_solution(16263872202317500967)
XLA Ops:
  0.6 0.0 copy-start
  0.6 0.0 copy-start.4
  0.7 0.0 copy-start.2
  0.7 0.0 copy-start.3
  0.7 1.2 %fusion.6 = (bf16[16,3,768]{2,1,0:T(4,128)(2,1)S(1)}, bf16[16,3,768]{2,1,0:T(4,128)(2,1)S(1)}) fusion(bf16[16,64,768]{2,1,0:T(8,128)(2,1)} %bitcast.28), kind=kLoop, calls=%fused_computation.23 | loop fusion | bytes 294912 | tf_op jit(solution)/shard_map/slice | solution.py:821
  1.9 2.4 %collective-permute-start = (bf16[16,3,768]{2,1,0:T(4,128)(2,1)S(1)}, bf16[16,3,768]{2,1,0:T(4,128)(2,1)S(1)}, u32[]{:S(2)}, u32[]{:S(2)}) collective-permute-start(bf16[16,3,768]{2,1,0:T(4,128)(2,1)S(1)} %get-tuple-element.127), channel_id=1, source_target_pairs={{0,1},{1,2},{2,3},{4,5},{5,6},{6,7},{8,9},{9,10},{10,11},{12,13},{... | collective-permute-start | bytes 221192 | tf_op jit(solution)/shard_map/ppermute | solution.py:97
  4.3 1.3 %collective-permute-start.1 = (bf16[16,3,768]{2,1,0:T(4,128)(2,1)S(1)}, bf16[16,3,768]{2,1,0:T(4,128)(2,1)S(1)}, u32[]{:S(2)}, u32[]{:S(2)}) collective-permute-start(bf16[16,3,768]{2,1,0:T(4,128)(2,1)S(1)} %get-tuple-element.128), channel_id=1, source_target_pairs={{1,0},{2,1},{3,2},{5,4},{6,5},{7,6},{9,8},{10,9},{11,10},{13,12},{... | collective-permute-start | bytes 221192 | tf_op jit(solution)/shard_map/ppermute | solution.py:101
  5.6 1.1 %fusion.5 = (bf16[1,3,64,768]{3,2,1,0:T(8,128)(2,1)S(1)}, bf16[1,3,64,768]{3,2,1,0:T(8,128)(2,1)S(1)}) fusion(bf16[1,16,64,768]{3,2,1,0:T(8,128)(2,1)} %param.8), kind=kLoop, calls=%fused_computation.22 | loop fusion | bytes 1179648 | tf_op jit(solution)/shard_map/slice | solution.py:801
  6.7 0.7 broadcast_in_dim.31.bias
  7.4 0.0 collective-permute-done.left
  7.4 2.2 %collective-permute-done.1.right = bf16[16,3,768]{2,1,0:T(4,128)(2,1)S(1)} collective-permute-done((bf16[16,3,768]{2,1,0:T(4,128)(2,1)S(1)}, bf16[16,3,768]{2,1,0:T(4,128)(2,1)S(1)}, u32[]{:S(2)}, u32[]{:S(2)}) %collective-permute-start.1) | collective-permute-done | bytes 73760 | tf_op jit(solution)/shard_map/ppermute | solution.py:101
  9.8 3.5 %collective-permute-start.2 = (bf16[210,768]{1,0:T(8,128)(2,1)S(1)}, bf16[210,768]{1,0:T(8,128)(2,1)S(1)}, u32[]{:S(2)}, u32[]{:S(2)}) collective-permute-start(bf16[210,768]{1,0:T(8,128)(2,1)S(1)} %get-tuple-element.74), channel_id=1, source_target_pairs={{0,4},{4,8},{8,12},{1,5},{5,9},{9,13},{2,6},{6,10},{10,14},{3,7},{... | collective-permute-start | bytes 967688 | tf_op jit(solution)/shard_map/ppermute | solution.py:97
  13.3 1.3 %collective-permute-start.3 = (bf16[210,768]{1,0:T(8,128)(2,1)S(1)}, bf16[210,768]{1,0:T(8,128)(2,1)S(1)}, u32[]{:S(2)}, u32[]{:S(2)}) collective-permute-start(bf16[210,768]{1,0:T(8,128)(2,1)S(1)} %get-tuple-element.75), channel_id=1, source_target_pairs={{4,0},{8,4},{12,8},{5,1},{9,5},{13,9},{6,2},{10,6},{14,10},{7,3},{... | collective-permute-start | bytes 967688 | tf_op jit(solution)/shard_map/ppermute | solution.py:101
  14.6 0.0 copy-done
  14.6 0.0 copy-done.4
  14.6 0.0 copy-done.2
  14.6 11.5 %conv_inner.1 = (f32[6,16,14,8,128]{4,3,2,1,0:T(8,128)S(1)}, f32[6,121,8,128]{3,2,1,0:T(8,128)S(1)}, bf16[512,768]{1,0:T(8,128)(2,1)S(1)}, f32[512,256]{1,0:T(8,...) custom-call(bf16[16,64,768]{2,1,0:T(8,128)(2,1)S(1)} %bitcast.29, ...), custom_call_target="tpu_custom_call" | custom-call | flops 10000000000 | bytes 10000000 | tf_op jit(solution)/shard_map/conv_inner/pallas_call | solution.py:380
  26.1 0.0 collective-permute-done.2.top
  26.2 0.0 collective-permute-done.3.bottom
  26.2 2.4 %conv_edge.1 = (f32[6,3,14,8,128]{4,3,2,1,0:T(8,128)S(1)}, f32[6,3,14,8,128]{4,3,2,1,0:T(8,128)S(1)}, bf16[512,768]{1,0:T(8,128)(2,1)S(1)}, f32[512,256]{1,0:T(8...) custom-call(s32[1]{0:T(128)} %bitcast.3.flag, ...), custom_call_target="tpu_custom_call" | custom-call | flops 6000000000 | bytes 6000000 | tf_op jit(solution)/shard_map/conv_edge/pallas_call | solution.py:411
  28.6 0.0 copy-start.1
  28.6 0.0 copy-start.5
  28.6 3.0 %collective-permute-start.4 = (f32[72,256]{1,0:T(8,128)S(1)}, f32[72,256]{1,0:T(8,128)S(1)}, u32[]{:S(2)}, u32[]{:S(2)}) collective-permute-start(f32[72,256]{1,0:T(8,128)S(1)} %get-tuple-element.82), channel_id=1, source_target_pairs={{0,1},{1,0},{2,3},{3,2},{4,5},{5,4},{6,7},{7,6},{8,9},{9,8},{10,11... | collective-permute-start | bytes 221192 | tf_op jit(solution)/shard_map/ppermute | solution.py:33
  31.6 0.9 collective-permute-done.4
  32.5 0.5 collective-permute-start.5
  33.0 0.9 prepare.1
  34.0 3.1 %collective-permute-done.5 = f32[72,256]{1,0:T(8,128)S(1)} collective-permute-done((f32[72,256]{1,0:T(8,128)S(1)}, f32[72,256]{1,0:T(8,128)S(1)}, u32[]{:S(2)}, u32[]{:S(2)}) %collective-permute-start.5) | collective-permute-done | bytes 73760 | tf_op jit(solution)/shard_map/ppermute | solution.py:33
  37.1 2.4 %collective-permute-start.6 = (f32[72,256]{1,0:T(8,128)S(1)}, f32[72,256]{1,0:T(8,128)S(1)}, u32[]{:S(2)}, u32[]{:S(2)}) collective-permute-start(f32[72,256]{1,0:T(8,128)S(1)} %add.38), channel_id=1, source_target_pairs={{0,4},{4,0},{8,12},{12,8},{1,5},{5,1},{9,13},{13,9},{2,6},{6,2},{1... | collective-permute-start | bytes 221192 | tf_op jit(solution)/shard_map/ppermute | solution.py:33
  39.6 2.3 %collective-permute-done.6 = f32[72,256]{1,0:T(8,128)S(1)} collective-permute-done((f32[72,256]{1,0:T(8,128)S(1)}, f32[72,256]{1,0:T(8,128)S(1)}, u32[]{:S(2)}, u32[]{:S(2)}) %collective-permute-start.6) | collective-permute-done | bytes 73760 | tf_op jit(solution)/shard_map/ppermute | solution.py:33
  41.9 3.1 %collective-permute-start.7 = (f32[72,256]{1,0:T(8,128)S(1)}, f32[72,256]{1,0:T(8,128)S(1)}, u32[]{:S(2)}, u32[]{:S(2)}) collective-permute-start(f32[72,256]{1,0:T(8,128)S(1)} %add.39), channel_id=1, source_target_pairs={{0,8},{4,12},{8,0},{12,4},{1,9},{5,13},{9,1},{13,5},{2,10},{6,14},... | collective-permute-start | bytes 221192 | tf_op jit(solution)/shard_map/ppermute | solution.py:33
  45.0 2.3 %collective-permute-done.7 = f32[72,256]{1,0:T(8,128)S(1)} collective-permute-done((f32[72,256]{1,0:T(8,128)S(1)}, f32[72,256]{1,0:T(8,128)S(1)}, u32[]{:S(2)}, u32[]{:S(2)}) %collective-permute-start.7) | collective-permute-done | bytes 73760 | tf_op jit(solution)/shard_map/ppermute | solution.py:33
  47.3 0.1 collective-permute-start.8
  48.1 0.6 collective-permute-done.8.other
  48.7 0.0 copy-done.1
  48.7 9.8 %head.1 = (f32[272,256]{1,0:T(8,128)S(1)}, f32[320,768]{1,0:T(8,128)S(1)}, bf16[512,768]{1,0:T(8,128)(2,1)S(1)}, bf16[512,768]{1,0:T(8,128)(2,1)S(1)}) custom-call(s32[1]{0:T(128)} %bitcast.3.flag, s32[1]{0:T(128)S(6)} %copy.23.label, f32[10]{0:T(128)S(1)} %copy-done.5, f32[72,256]{1,0:T(8,128)S(1)} %add.40.own, f32[72,256]{1,0:T(8,128)S(1)} %collective-permute-done.8.other, ...), custom_call_target="tpu_custom_call" | custom-call | flops 10000000000 | bytes 10000000 | tf_op jit(solution)/shard_map/head/pallas_call | solution.py:591
  58.5 1.6 %collective-permute-start.9 = (f32[272,256]{1,0:T(8,128)S(1)}, f32[272,256]{1,0:T(8,128)S(1)}, u32[]{:S(2)}, u32[]{:S(2)}) collective-permute-start(f32[272,256]{1,0:T(8,128)S(1)} %get-tuple-element.115.refs_0_), channel_id=1, source_target_pairs={{0,16},{16,0},{1,17},{17,1},{2,18},{18,2},{3,19},{19,3},{4,20},{20... | collective-permute-start | bytes 835592 | tf_op jit(solution)/shard_map/ppermute | solution.py:33
  60.0 6.8 %tap_grads.2.payload_in = f32[320,768]{1,0:T(8,128)S(1)} custom-call(f32[6,16,14,8,128]{4,3,2,1,0:T(8,128)S(1)} %get-tuple-element.72.spread_in, f32[6,3,14,8,128]{4,3,2,1,0:T(8,128)S(1)} %get-tuple-element.79.spread_top, f32[6,3,14,8,128]{4,3,2,1,0:T(8,128)S(1)} %get-tuple-element.80.spread_bottom, ...), custom_call_target="tpu_custom_call", output_to_operand_aliasing={{}: (5, {})} | custom-call | flops 10000000000 | bytes 10000000 | tf_op jit(solution)/shard_map/tap_grads/pallas_call | solution.py:736
  66.8 0.5 collective-permute-done.9.refs_1_
  67.3 1.3 %tap_grads.3 = f32[320,768]{1,0:T(8,128)S(1)} custom-call(f32[6,16,14,8,128]{4,3,2,1,0:T(8,128)S(1)} %get-tuple-element.72.spread_in, f32[6,3,14,8,128]{4,3,2,1,0:T(8,128)S(1)} %get-tuple-element.79.spread_top, f32[6,3,14,8,128]{4,3,2,1,0:T(8,128)S(1)} %get-tuple-element.80.spread_bottom, ...), custom_call_target="tpu_custom_call", output_to_operand_aliasing={{}: (5, {})} | custom-call | flops 2000000000 | bytes 2000000 | tf_op jit(solution)/shard_map/tap_grads/pallas_call | solution.py:736
  68.6 0.1 collective-permute-start.10
  68.7 1.5 %collective-permute-done.10 = bf16[160,768]{1,0:T(8,128)(2,1)S(1)} collective-permute-done((bf16[160,768]{1,0:T(8,128)(2,1)S(1)}, bf16[160,768]{1,0:T(8,128)(2,1)S(1)}, u32[]{:S(2)}, u32[]{:S(2)}) %collective-permute-start.10) | collective-permute-done | bytes 245792 | tf_op jit(solution)/shard_map/ppermute | solution.py:33
  70.2 0.1 convert_add_fusion
  70.3 0.6 collective-permute-start.11
  70.9 1.5 %collective-permute-start.12 = (bf16[40,768]{1,0:T(8,128)(2,1)S(1)}, bf16[40,768]{1,0:T(8,128)(2,1)S(1)}, u32[]{:S(2)}, u32[]{:S(2)}) collective-permute-start(bf16[40,768]{1,0:T(8,128)(2,1)S(1)} %get-tuple-element.131), channel_id=1, source_target_pairs={{0,16},{1,17},{2,18},{3,19},{16,0},{17,1},{18,2},{19,3},{4,20},{5,... | collective-permute-start | bytes 184328 | tf_op jit(solution)/shard_map/ppermute | solution.py:72
  72.4 1.4 %collective-permute-start.13 = (bf16[40,768]{1,0:T(8,128)(2,1)S(1)}, bf16[40,768]{1,0:T(8,128)(2,1)S(1)}, u32[]{:S(2)}, u32[]{:S(2)}) collective-permute-start(bf16[40,768]{1,0:T(8,128)(2,1)S(1)} %get-tuple-element.130), channel_id=1, source_target_pairs={{0,18},{1,19},{2,16},{3,17},{16,2},{17,3},{18,0},{19,1},{4,22},{5,... | collective-permute-start | bytes 184328 | tf_op jit(solution)/shard_map/ppermute | solution.py:72
  73.9 0.7 collective-permute-done.11
  74.6 0.5 collective-permute-done.12
  75.1 2.4 %collective-permute-done.13 = bf16[40,768]{1,0:T(8,128)(2,1)S(1)} collective-permute-done((bf16[40,768]{1,0:T(8,128)(2,1)S(1)}, bf16[40,768]{1,0:T(8,128)(2,1)S(1)}, u32[]{:S(2)}, u32[]{:S(2)}) %collective-permute-start.13) | collective-permute-done | bytes 61472 | tf_op jit(solution)/shard_map/ppermute | solution.py:72
  77.6 2.0 %collective-permute-start.14 = (bf16[40,768]{1,0:T(8,128)(2,1)S(1)}, bf16[40,768]{1,0:T(8,128)(2,1)S(1)}, u32[]{:S(2)}, u32[]{:S(2)}) collective-permute-start(bf16[40,768]{1,0:T(8,128)(2,1)S(1)} %fusion.1), channel_id=1, source_target_pairs={{0,4},{4,0},{8,12},{12,8},{1,5},{5,1},{9,13},{13,9},{2,6},{6,2},{1... | collective-permute-start | bytes 184328 | tf_op jit(solution)/shard_map/ppermute | solution.py:33
  79.5 2.3 %collective-permute-done.14 = bf16[40,768]{1,0:T(8,128)(2,1)S(1)} collective-permute-done((bf16[40,768]{1,0:T(8,128)(2,1)S(1)}, bf16[40,768]{1,0:T(8,128)(2,1)S(1)}, u32[]{:S(2)}, u32[]{:S(2)}) %collective-permute-start.14) | collective-permute-done | bytes 61472 | tf_op jit(solution)/shard_map/ppermute | solution.py:33
  81.9 3.2 %collective-permute-start.15 = (bf16[40,768]{1,0:T(8,128)(2,1)S(1)}, bf16[40,768]{1,0:T(8,128)(2,1)S(1)}, u32[]{:S(2)}, u32[]{:S(2)}) collective-permute-start(bf16[40,768]{1,0:T(8,128)(2,1)S(1)} %add_convert_fusion.1), channel_id=1, source_target_pairs={{0,8},{4,12},{8,0},{12,4},{1,9},{5,13},{9,1},{13,5},{2,10},{6,14},... | collective-permute-start | bytes 184328 | tf_op jit(solution)/shard_map/ppermute | solution.py:33
  85.1 2.2 %collective-permute-done.15 = bf16[40,768]{1,0:T(8,128)(2,1)S(1)} collective-permute-done((bf16[40,768]{1,0:T(8,128)(2,1)S(1)}, bf16[40,768]{1,0:T(8,128)(2,1)S(1)}, u32[]{:S(2)}, u32[]{:S(2)}) %collective-permute-start.15) | collective-permute-done | bytes 61472 | tf_op jit(solution)/shard_map/ppermute | solution.py:33
  87.3 0.1 slice_reduce_fusion
  87.5 0.1 slice_reduce_fusion.1
  87.6 1.5 %collective-permute-start.16 = (bf16[40,768]{1,0:T(8,128)(2,1)S(1)}, bf16[40,768]{1,0:T(8,128)(2,1)S(1)}, u32[]{:S(2)}, u32[]{:S(2)}) collective-permute-start(bf16[40,768]{1,0:T(8,128)(2,1)S(1)} %add_convert_fusion), channel_id=1, source_target_pairs={{0,2},{1,3},{2,0},{3,1},{16,18},{17,19},{18,16},{19,17},{4,6},{5,7... | collective-permute-start | bytes 184328 | tf_op jit(solution)/shard_map/ppermute | solution.py:81
  89.1 0.6 collective-permute-start.17
  89.7 1.5 %collective-permute-start.18 = (bf16[40,768]{1,0:T(8,128)(2,1)S(1)}, bf16[40,768]{1,0:T(8,128)(2,1)S(1)}, u32[]{:S(2)}, u32[]{:S(2)}) collective-permute-start(bf16[40,768]{1,0:T(8,128)(2,1)S(1)} %add_convert_fusion), channel_id=1, source_target_pairs={{0,18},{1,19},{2,16},{3,17},{16,2},{17,3},{18,0},{19,1},{4,22},{5,... | collective-permute-start | bytes 184328 | tf_op jit(solution)/shard_map/ppermute | solution.py:81
  91.1 1.9 %multiply_add_fusion = f32[10,256,256]{2,1,0:T(8,128)} fusion(f32[256,256]{1,0:T(8,128)S(1)} %slice.57, f32[10]{0:T(128)S(1)} %slice_reduce_fusion, f32[256,256]{1,0:T(8,128)S(1)} %slice.55, f32[10]{0:T(128)S(1)} %slice_reduce_fusion.1), kind=kLoop, calls=%fused_computation | loop fusion | flops 1966080 | bytes 3145808 | tf_op jit(solution)/shard_map/add | solution.py:42
  93.1 0.0 collective-permute-done.16
  93.1 0.3 collective-permute-done.17
  93.3 1.4 %collective-permute-done.18 = bf16[40,768]{1,0:T(8,128)(2,1)S(1)} collective-permute-done((bf16[40,768]{1,0:T(8,128)(2,1)S(1)}, bf16[40,768]{1,0:T(8,128)(2,1)S(1)}, u32[]{:S(2)}, u32[]{:S(2)}) %collective-permute-start.18) | collective-permute-done | bytes 61472 | tf_op jit(solution)/shard_map/ppermute | solution.py:81
  94.8 0.1 collective-permute-start.19
  94.9 1.5 %collective-permute-done.19.other = bf16[160,768]{1,0:T(8,128)(2,1)S(1)} collective-permute-done((bf16[160,768]{1,0:T(8,128)(2,1)S(1)}, bf16[160,768]{1,0:T(8,128)(2,1)S(1)}, u32[]{:S(2)}, u32[]{:S(2)}) %collective-permute-start.19) | collective-permute-done | bytes 245792 | tf_op jit(solution)/shard_map/ppermute | solution.py:33
  96.4 1.0 %finish.1 = (f32[768,256]{1,0:T(8,128)}, f32[7,7,768]{2,1,0:T(8,128)}, f32[768]{0:T(1024)}, f32[256]{0:T(256)}, f32[10]{0:T(128)}, /*index=5*/f32[1]{0:T(128)}) custom-call(s32[1]{0:T(128)} %bitcast.3.flag, bf16[160,768]{1,0:T(8,128)(2,1)S(1)} %bitcast.31, bf16[160,768]{1,0:T(8,128)(2,1)S(1)} %collective-permute-done.19.other, ...), custom_call_target="tpu_custom_call" | custom-call | flops 1000000000 | bytes 1000000 | tf_op jit(solution)/shard_map/finish/pallas_call | solution.py:780
  (25 shorter events, 0.5 us)
Async XLA Ops:
  0.6 14.0 %copy-start = (bf16[1,16,64,768]{3,2,1,0:T(8,128)(2,1)S(1)}, bf16[1,16,64,768]{3,2,1,0:T(8,128)(2,1)}, u32[]{:S(2)}) copy-start(bf16[1,16,64,768]{3,2,1,0:T(8,128)(2,1)} %param.8) | copy-start | bytes 4718596
  0.6 14.0 %copy-start.4 = (f32[256]{0:T(256)S(1)}, f32[256]{0:T(256)}, u32[]{:S(2)}) copy-start(f32[256]{0:T(256)} %param.12) | copy-start | bytes 3076
  0.7 14.0 %copy-start.2 = (bf16[768,256]{1,0:T(8,128)(2,1)S(1)}, bf16[768,256]{1,0:T(8,128)(2,1)}, u32[]{:S(2)}) copy-start(bf16[768,256]{1,0:T(8,128)(2,1)} %reduce_weight.5) | copy-start | bytes 1179652
  0.7 14.0 %copy-start.3 = (f32[7,7,768]{2,1,0:T(8,128)S(1)}, f32[7,7,768]{2,1,0:T(8,128)}, u32[]{:S(2)}) copy-start(f32[7,7,768]{2,1,0:T(8,128)} %weight.1) | copy-start | bytes 451588
  1.9 5.5 %collective-permute-start = (bf16[16,3,768]{2,1,0:T(4,128)(2,1)S(1)}, bf16[16,3,768]{2,1,0:T(4,128)(2,1)S(1)}, u32[]{:S(2)}, u32[]{:S(2)}) collective-permute-start(bf16[16,3,768]{2,1,0:T(4,128)(2,1)S(1)} %get-tuple-element.127), channel_id=1, source_target_pairs={{0,1},{1,2},{2,3},{4,5},{5,6},{6,7},{8,9},{9,10},{10,11},{12,13},{... | collective-permute-start | bytes 221192 | tf_op jit(solution)/shard_map/ppermute | solution.py:97
  4.3 5.3 %collective-permute-start.1 = (bf16[16,3,768]{2,1,0:T(4,128)(2,1)S(1)}, bf16[16,3,768]{2,1,0:T(4,128)(2,1)S(1)}, u32[]{:S(2)}, u32[]{:S(2)}) collective-permute-start(bf16[16,3,768]{2,1,0:T(4,128)(2,1)S(1)} %get-tuple-element.128), channel_id=1, source_target_pairs={{1,0},{2,1},{3,2},{5,4},{6,5},{7,6},{9,8},{10,9},{11,10},{13,12},{... | collective-permute-start | bytes 221192 | tf_op jit(solution)/shard_map/ppermute | solution.py:101
  9.8 16.4 %collective-permute-start.2 = (bf16[210,768]{1,0:T(8,128)(2,1)S(1)}, bf16[210,768]{1,0:T(8,128)(2,1)S(1)}, u32[]{:S(2)}, u32[]{:S(2)}) collective-permute-start(bf16[210,768]{1,0:T(8,128)(2,1)S(1)} %get-tuple-element.74), channel_id=1, source_target_pairs={{0,4},{4,8},{8,12},{1,5},{5,9},{9,13},{2,6},{6,10},{10,14},{3,7},{... | collective-permute-start | bytes 967688 | tf_op jit(solution)/shard_map/ppermute | solution.py:97
  13.3 12.9 %collective-permute-start.3 = (bf16[210,768]{1,0:T(8,128)(2,1)S(1)}, bf16[210,768]{1,0:T(8,128)(2,1)S(1)}, u32[]{:S(2)}, u32[]{:S(2)}) collective-permute-start(bf16[210,768]{1,0:T(8,128)(2,1)S(1)} %get-tuple-element.75), channel_id=1, source_target_pairs={{4,0},{8,4},{12,8},{5,1},{9,5},{13,9},{6,2},{10,6},{14,10},{7,3},{... | collective-permute-start | bytes 967688 | tf_op jit(solution)/shard_map/ppermute | solution.py:101
  28.6 20.1 %copy-start.1 = (bf16[10,256,256]{2,1,0:T(8,128)(2,1)S(1)}, bf16[10,256,256]{2,1,0:T(8,128)(2,1)}, u32[]{:S(2)}) copy-start(bf16[10,256,256]{2,1,0:T(8,128)(2,1)} %class_weight.1) | copy-start | bytes 3932164
  28.6 20.1 %copy-start.5 = (f32[10]{0:T(128)S(1)}, f32[10]{0:T(128)}, u32[]{:S(2)}) copy-start(f32[10]{0:T(128)} %class_bias.1) | copy-start | bytes 124
  28.6 3.9 %collective-permute-start.4 = (f32[72,256]{1,0:T(8,128)S(1)}, f32[72,256]{1,0:T(8,128)S(1)}, u32[]{:S(2)}, u32[]{:S(2)}) collective-permute-start(f32[72,256]{1,0:T(8,128)S(1)} %get-tuple-element.82), channel_id=1, source_target_pairs={{0,1},{1,0},{2,3},{3,2},{4,5},{5,4},{6,7},{7,6},{8,9},{9,8},{10,11... | collective-permute-start | bytes 221192 | tf_op jit(solution)/shard_map/ppermute | solution.py:33
  32.5 4.6 %collective-permute-start.5 = (f32[72,256]{1,0:T(8,128)S(1)}, f32[72,256]{1,0:T(8,128)S(1)}, u32[]{:S(2)}, u32[]{:S(2)}) collective-permute-start(f32[72,256]{1,0:T(8,128)S(1)} %add.37), channel_id=1, source_target_pairs={{0,2},{1,3},{2,0},{3,1},{4,6},{5,7},{6,4},{7,5},{8,10},{9,11},{10,... | collective-permute-start | bytes 221192 | tf_op jit(solution)/shard_map/ppermute | solution.py:33
  37.1 4.8 %collective-permute-start.6 = (f32[72,256]{1,0:T(8,128)S(1)}, f32[72,256]{1,0:T(8,128)S(1)}, u32[]{:S(2)}, u32[]{:S(2)}) collective-permute-start(f32[72,256]{1,0:T(8,128)S(1)} %add.38), channel_id=1, source_target_pairs={{0,4},{4,0},{8,12},{12,8},{1,5},{5,1},{9,13},{13,9},{2,6},{6,2},{1... | collective-permute-start | bytes 221192 | tf_op jit(solution)/shard_map/ppermute | solution.py:33
  41.9 5.4 %collective-permute-start.7 = (f32[72,256]{1,0:T(8,128)S(1)}, f32[72,256]{1,0:T(8,128)S(1)}, u32[]{:S(2)}, u32[]{:S(2)}) collective-permute-start(f32[72,256]{1,0:T(8,128)S(1)} %add.39), channel_id=1, source_target_pairs={{0,8},{4,12},{8,0},{12,4},{1,9},{5,13},{9,1},{13,5},{2,10},{6,14},... | collective-permute-start | bytes 221192 | tf_op jit(solution)/shard_map/ppermute | solution.py:33
  47.3 1.3 %collective-permute-start.8 = (f32[72,256]{1,0:T(8,128)S(1)}, f32[72,256]{1,0:T(8,128)S(1)}, u32[]{:S(2)}, u32[]{:S(2)}) collective-permute-start(f32[72,256]{1,0:T(8,128)S(1)} %add.40.own), channel_id=1, source_target_pairs={{0,1},{1,0},{2,3},{3,2},{4,5},{5,4},{6,7},{7,6},{8,9},{9,8},{10,11... | collective-permute-start | bytes 221192 | tf_op jit(solution)/shard_map/ppermute | solution.py:33
  58.5 8.8 %collective-permute-start.9 = (f32[272,256]{1,0:T(8,128)S(1)}, f32[272,256]{1,0:T(8,128)S(1)}, u32[]{:S(2)}, u32[]{:S(2)}) collective-permute-start(f32[272,256]{1,0:T(8,128)S(1)} %get-tuple-element.115.refs_0_), channel_id=1, source_target_pairs={{0,16},{16,0},{1,17},{17,1},{2,18},{18,2},{3,19},{19,3},{4,20},{20... | collective-permute-start | bytes 835592 | tf_op jit(solution)/shard_map/ppermute | solution.py:33
  68.6 1.6 %collective-permute-start.10 = (bf16[160,768]{1,0:T(8,128)(2,1)S(1)}, bf16[160,768]{1,0:T(8,128)(2,1)S(1)}, u32[]{:S(2)}, u32[]{:S(2)}) collective-permute-start(bf16[160,768]{1,0:T(8,128)(2,1)S(1)} %select_convert_fusion), channel_id=1, source_target_pairs={{0,1},{1,0},{2,3},{3,2},{4,5},{5,4},{6,7},{7,6},{8,9},{9,8},{10,11... | collective-permute-start | bytes 737288 | tf_op jit(solution)/shard_map/ppermute | solution.py:33
  70.3 4.3 %collective-permute-start.11 = (bf16[40,768]{1,0:T(8,128)(2,1)S(1)}, bf16[40,768]{1,0:T(8,128)(2,1)S(1)}, u32[]{:S(2)}, u32[]{:S(2)}) collective-permute-start(bf16[40,768]{1,0:T(8,128)(2,1)S(1)} %get-tuple-element.129), channel_id=1, source_target_pairs={{0,2},{1,3},{2,0},{3,1},{16,18},{17,19},{18,16},{19,17},{4,6},{5,7... | collective-permute-start | bytes 184328 | tf_op jit(solution)/shard_map/ppermute | solution.py:72
  70.9 4.2 %collective-permute-start.12 = (bf16[40,768]{1,0:T(8,128)(2,1)S(1)}, bf16[40,768]{1,0:T(8,128)(2,1)S(1)}, u32[]{:S(2)}, u32[]{:S(2)}) collective-permute-start(bf16[40,768]{1,0:T(8,128)(2,1)S(1)} %get-tuple-element.131), channel_id=1, source_target_pairs={{0,16},{1,17},{2,18},{3,19},{16,0},{17,1},{18,2},{19,3},{4,20},{5,... | collective-permute-start | bytes 184328 | tf_op jit(solution)/shard_map/ppermute | solution.py:72
  72.4 5.1 %collective-permute-start.13 = (bf16[40,768]{1,0:T(8,128)(2,1)S(1)}, bf16[40,768]{1,0:T(8,128)(2,1)S(1)}, u32[]{:S(2)}, u32[]{:S(2)}) collective-permute-start(bf16[40,768]{1,0:T(8,128)(2,1)S(1)} %get-tuple-element.130), channel_id=1, source_target_pairs={{0,18},{1,19},{2,16},{3,17},{16,2},{17,3},{18,0},{19,1},{4,22},{5,... | collective-permute-start | bytes 184328 | tf_op jit(solution)/shard_map/ppermute | solution.py:72
  77.6 4.3 %collective-permute-start.14 = (bf16[40,768]{1,0:T(8,128)(2,1)S(1)}, bf16[40,768]{1,0:T(8,128)(2,1)S(1)}, u32[]{:S(2)}, u32[]{:S(2)}) collective-permute-start(bf16[40,768]{1,0:T(8,128)(2,1)S(1)} %fusion.1), channel_id=1, source_target_pairs={{0,4},{4,0},{8,12},{12,8},{1,5},{5,1},{9,13},{13,9},{2,6},{6,2},{1... | collective-permute-start | bytes 184328 | tf_op jit(solution)/shard_map/ppermute | solution.py:33
  81.9 5.4 %collective-permute-start.15 = (bf16[40,768]{1,0:T(8,128)(2,1)S(1)}, bf16[40,768]{1,0:T(8,128)(2,1)S(1)}, u32[]{:S(2)}, u32[]{:S(2)}) collective-permute-start(bf16[40,768]{1,0:T(8,128)(2,1)S(1)} %add_convert_fusion.1), channel_id=1, source_target_pairs={{0,8},{4,12},{8,0},{12,4},{1,9},{5,13},{9,1},{13,5},{2,10},{6,14},... | collective-permute-start | bytes 184328 | tf_op jit(solution)/shard_map/ppermute | solution.py:33
  87.6 5.5 %collective-permute-start.16 = (bf16[40,768]{1,0:T(8,128)(2,1)S(1)}, bf16[40,768]{1,0:T(8,128)(2,1)S(1)}, u32[]{:S(2)}, u32[]{:S(2)}) collective-permute-start(bf16[40,768]{1,0:T(8,128)(2,1)S(1)} %add_convert_fusion), channel_id=1, source_target_pairs={{0,2},{1,3},{2,0},{3,1},{16,18},{17,19},{18,16},{19,17},{4,6},{5,7... | collective-permute-start | bytes 184328 | tf_op jit(solution)/shard_map/ppermute | solution.py:81
  89.1 4.2 %collective-permute-start.17 = (bf16[40,768]{1,0:T(8,128)(2,1)S(1)}, bf16[40,768]{1,0:T(8,128)(2,1)S(1)}, u32[]{:S(2)}, u32[]{:S(2)}) collective-permute-start(bf16[40,768]{1,0:T(8,128)(2,1)S(1)} %add_convert_fusion), channel_id=1, source_target_pairs={{0,16},{1,17},{2,18},{3,19},{16,0},{17,1},{18,2},{19,3},{4,20},{5,... | collective-permute-start | bytes 184328 | tf_op jit(solution)/shard_map/ppermute | solution.py:81
  89.7 5.1 %collective-permute-start.18 = (bf16[40,768]{1,0:T(8,128)(2,1)S(1)}, bf16[40,768]{1,0:T(8,128)(2,1)S(1)}, u32[]{:S(2)}, u32[]{:S(2)}) collective-permute-start(bf16[40,768]{1,0:T(8,128)(2,1)S(1)} %add_convert_fusion), channel_id=1, source_target_pairs={{0,18},{1,19},{2,16},{3,17},{16,2},{17,3},{18,0},{19,1},{4,22},{5,... | collective-permute-start | bytes 184328 | tf_op jit(solution)/shard_map/ppermute | solution.py:81
  94.8 1.6 %collective-permute-start.19 = (bf16[160,768]{1,0:T(8,128)(2,1)S(1)}, bf16[160,768]{1,0:T(8,128)(2,1)S(1)}, u32[]{:S(2)}, u32[]{:S(2)}) collective-permute-start(bf16[160,768]{1,0:T(8,128)(2,1)S(1)} %bitcast.30), channel_id=1, source_target_pairs={{0,1},{1,0},{2,3},{3,2},{4,5},{5,4},{6,7},{7,6},{8,9},{9,8},{10,11... | collective-permute-start | bytes 737288 | tf_op jit(solution)/shard_map/ppermute | solution.py:33
